TPU v7x, 512 devices: a whole 4x4x16 slice. The times are simulated.
512 devices in a mesh: row: 32 (over x, z_hi, core), col: 16 (over z_lo, y).
Axes of the slice: x: 4, y: 4, z: 16 (z_hi: 4, z_lo: 4; z = z_hi * 4 + z_lo), core: 2. Of those that a mesh axis runs over, the one named last changes fastest.
Arguments:
- tokens: bfloat16 [4096, 6144], P('row', 'col'), may hold values from -40 to 40
- ln_gain: bfloat16 [6144], P('col'), may hold values from 0.5 to 1.5
- w_qkv: bfloat16 [6144, 3, 4096], P('row', None, 'col'), may hold values from -1 to 1
- q_gain: float32 [4096], P('col'), may hold values from 0.8 to 6
- k_gain: float32 [4096], P('col'), may hold values from 0.8 to 6
Outputs:
- attended: bfloat16 [4096, 4096], P('row', 'col')
All inputs are finite; a program needn't handle non-finite values.
Results may differ from a plain program's by a relative error of at most 0.03.
Values may be sent and summed in bfloat16 or wider, within the bound.
No kernel may reach another device: no remote copies, remote signals or barrier semaphores. Data moves between devices by JAX's collectives and lax.ppermute only.
A program may use at most 64 MiB of HBM per device.

v0:
```python
import jax
import jax.numpy as jnp
from jax import lax
from jax.sharding import PartitionSpec as P

DH = 128


EPSILON = 1e-06


def head_norm(values, gain_row, head_count, head_width):
    row_count = values.shape[0]
    grouped = values.reshape(row_count, head_count, head_width)
    center = jnp.mean(grouped, axis=2, keepdims=True)
    spread = jnp.mean(grouped * grouped, axis=2, keepdims=True) - center * center
    scaled = (
        (grouped - center)
        * lax.rsqrt(spread + EPSILON)
        * gain_row.reshape(1, head_count, head_width)
    )
    return scaled.reshape(row_count, head_count * head_width).astype(jnp.bfloat16)


def body(tokens, ln_gain, w_qkv, q_gain, k_gain):
    rows_here = tokens.shape[0]
    width_here = w_qkv.shape[2]
    heads_here = width_here // DH
    values = tokens.astype(jnp.float32)
    feature_count = lax.axis_size("col") * tokens.shape[1]
    row_sums, row_squares = lax.psum(
        (jnp.sum(values, axis=1), jnp.sum(values * values, axis=1)), "col"
    )
    center = (row_sums / feature_count)[:, None]
    spread = (row_squares / feature_count)[:, None] - center * center
    normed_local = (
        (values - center) * lax.rsqrt(spread + EPSILON) * ln_gain.astype(jnp.float32)
    ).astype(jnp.bfloat16)
    normed = lax.all_gather(normed_local, "col", axis=1, tiled=True)

    def project(panel):
        return jnp.einsum("td,dsh->tsh", normed, panel, preferred_element_type=jnp.float32)

    query_proj = project(lax.all_gather(w_qkv[:, 0:1], "row", axis=0, tiled=True))[:, 0]
    key_value = project(lax.all_gather(w_qkv[:, 1:3], "row", axis=0, tiled=True))
    key_proj = key_value[:, 0]
    value_proj = key_value[:, 1]
    query_normed = head_norm(query_proj, q_gain, heads_here, DH)
    key_normed = head_norm(key_proj, k_gain, heads_here, DH)
    value_rows = value_proj.astype(jnp.bfloat16)
    queries_split = query_normed.reshape(rows_here, heads_here, DH)
    score_scale = DH ** (-0.5)
    running_max = jnp.full((heads_here, rows_here), -1e30, jnp.float32)
    key_panel = lax.all_gather(key_normed, "row", axis=0, tiled=True).reshape(-1, heads_here, DH)
    value_panel = lax.all_gather(value_rows, "row", axis=0, tiled=True).reshape(-1, heads_here, DH)
    scores = (
        jnp.einsum("qhd,khd->hqk", queries_split, key_panel, preferred_element_type=jnp.float32)
        * score_scale
    )
    new_max = jnp.maximum(running_max, jnp.max(scores, axis=2))
    weights = jnp.exp(scores - new_max[:, :, None])
    new_sum = jnp.sum(weights, axis=2)
    new_weighted = jnp.einsum(
        "hqk,khd->hqd",
        weights.astype(jnp.bfloat16),
        value_panel,
        preferred_element_type=jnp.float32,
    )
    output = new_weighted / new_sum[:, :, None]
    return jnp.transpose(output, (1, 0, 2)).reshape(rows_here, width_here).astype(jnp.bfloat16)


def solution(mesh):
    in_specs = (P("row", "col"), P("col"), P("row", None, "col"), P("col"), P("col"))
    out_specs = P("row", "col")
    return jax.shard_map(body, mesh=mesh, in_specs=in_specs, out_specs=out_specs, check_vma=False)
```

profile of v0, /device:TPU:1, one launch (start us, length us, event | category | flops | bytes accessed | tf_op | source)
XLA Modules:
  0.0 513.6 jit_solution(3748479847157437421)
XLA Ops:
  6.5 1.0 convert_reduce_fusion
  7.5 0.7 convert_element_type.30
  8.2 38.4 %all-reduce = (f32[128]{0:T(128)S(1)}, f32[128]{0:T(128)S(1)}) all-reduce(f32[128]{0:T(128)S(1)} %get-tuple-element.10, f32[128]{0:T(128)S(1)} %get-tuple-element.9), channel_id=1, replica_groups=mesh['row'=32,'col'=16] {'col'}, use_global_device_ids=true, to_apply=%region_3.0 | all-reduce | flops 256 | bytes 2048 | tf_op jit(solution)/shard_map/psum | solution.py:31
  46.7 1.6 fusion.22
  48.3 0.0 all-gather.11.cloned.1.call-start
  48.4 1.6 slice.14
  50.1 1.5 slice.13
  51.7 0.0 all-gather.13.cloned.1.call-start
  51.7 80.6 %all-gather.7.cloned.1.call-done = bf16[128,6144]{1,0:T(8,128)(2,1)} async-done(((bf16[128,384]{1,0:T(8,128)(2,1)}), bf16[128,6144]{1,0:T(8,128)(2,1)}) %all-gather.7.cloned.1.call-update) | async-done | bytes 1572880 | tf_op jit(solution)/shard_map/all_gather | solution.py:39
  132.4 128.3 %all-gather.11.cloned.1.call-done = bf16[6144,2,256]{2,0,1:T(8,128)(2,1)} async-done(((bf16[192,2,256]{2,0,1:T(8,128)(2,1)}), bf16[6144,2,256]{2,0,1:T(8,128)(2,1)}) %all-gather.11.cloned.1.call-update) | async-done | bytes 6291472 | tf_op jit(solution)/shard_map/all_gather | solution.py:45
  260.6 4.2 fusion.7
  264.9 0.1 reshape_squeeze.7
  265.0 0.3 fusion.30
  265.3 0.1 copy.21
  265.4 0.1 copy.23
  265.5 0.1 copy.22
  265.6 0.1 copy.24
  265.7 0.2 sub.61
  265.9 0.2 mul.108
  266.1 0.6 fusion.25
  266.9 0.6 slice.21
  267.5 80.0 %all-gather.9.cloned.1.call-done = bf16[6144,1,256]{2,0,1:T(8,128)(2,1)} async-done(((bf16[192,1,256]{2,0,1:T(8,128)(2,1)}), bf16[6144,1,256]{2,0,1:T(8,128)(2,1)}) %all-gather.9.cloned.1.call-update) | async-done | bytes 3145744 | tf_op jit(solution)/shard_map/all_gather | solution.py:44
  347.5 3.2 copy.20
  350.7 2.4 fusion.29
  353.1 71.1 %all-gather.13.cloned.1.call-done = bf16[4096,256]{1,0:T(8,128)(2,1)} async-done(((bf16[128,256]{1,0:T(8,128)(2,1)}), bf16[4096,256]{1,0:T(8,128)(2,1)}) %all-gather.13.cloned.1.call-update) | async-done | bytes 2097168 | tf_op jit(solution)/shard_map/all_gather | solution.py:54
  424.2 2.5 fusion.31
  426.8 1.9 copy-done
  428.7 0.7 fusion
  429.4 71.0 %all-gather.15.cloned.1.call-done = bf16[4096,1,256]{2,0,1:T(8,128)(2,1)} async-done(((bf16[128,1,256]{2,0,1:T(8,128)(2,1)}), bf16[4096,1,256]{2,0,1:T(8,128)(2,1)}) %all-gather.15.cloned.1.call-update) | async-done | bytes 2097168 | tf_op jit(solution)/shard_map/all_gather | solution.py:55
  500.4 2.9 copy.30
  503.3 3.0 fusion.17
  506.3 0.7 copy.28
  (18 shorter events, 0.2 us)
Async XLA Ops:
  6.5 125.8 %all-gather.7.cloned.1.call-start = ((), (), s32[]{:S(2)}) async-start(), calls=%async_computation | async-start | bytes 1671168 | tf_op jit(solution)/shard_map/all_gather | solution.py:39
  48.3 212.3 %all-gather.11.cloned.1.call-start = ((), (), s32[]{:S(2)}) async-start(), calls=%async_computation.2 | async-start | bytes 6488064 | tf_op jit(solution)/shard_map/all_gather | solution.py:45
  50.1 297.4 %all-gather.9.cloned.1.call-start = ((), (), s32[]{:S(2)}) async-start(), calls=%async_computation.1 | async-start | bytes 3244032 | tf_op jit(solution)/shard_map/all_gather | solution.py:44
  51.7 214.5 %copy-start.1 = (f32[256]{0:T(256)S(1)}, f32[256]{0:T(256)}, u32[]{:S(2)}) copy-start(f32[256]{0:T(256)} %param.9) | copy-start | bytes 3076
  51.7 372.6 %all-gather.13.cloned.1.call-start = ((), (), s32[]{:S(2)}) async-start(), calls=%async_computation.3 | async-start | bytes 2162688 | tf_op jit(solution)/shard_map/all_gather | solution.py:54
  266.8 233.6 %all-gather.15.cloned.1.call-start = ((), (), s32[]{:S(2)}) async-start(), calls=%async_computation.4 | async-start | bytes 2162688 | tf_op jit(solution)/shard_map/all_gather | solution.py:55
  350.7 73.6 %copy-start.2 = (f32[256]{0:T(256)S(1)}, f32[256]{0:T(256)}, u32[]{:S(2)}) copy-start(f32[256]{0:T(256)} %param.8) | copy-start | bytes 3076
  426.7 1.9 copy-start
Sparse Core Ops, SparseCore 0:
  48.5 83.8 all-gather.6
  135.5 125.0 all-gather.10
  263.8 83.6 all-gather.8
  350.5 73.7 all-gather.12
  427.2 73.1 all-gather.14
where the time goes:
time: 514 us
  waiting for transfers between devices  431 us (84%)
  blocking collectives  38.4 us (7%)
  local copies, waits for them, and re-layouts  13.4 us (3%)
  between operations  13.3 us (3%)
  matrix products  12.1 us (2%)
    all_gather x1, waiting for transfers between devices, body(): lax.all_gather(w_qkv[:, 1:3], 'row', axis=0, tiled=True)  128 us
    all_gather x1, waiting for transfers between devices, body(): normed = lax.all_gather(normed_local, 'col', axis=1, tiled=True)  80.6 us
    all_gather x1, waiting for transfers between devices, body(): lax.all_gather(w_qkv[:, 0:1], 'row', axis=0, tiled=True)  80 us
    all_gather x1, waiting for transfers between devices, body(): lax.all_gather(key_normed, 'row', axis=0, tiled=True)  71.1 us
    all_gather x1, waiting for transfers between devices, body(): lax.all_gather(value_rows, 'row', axis=0, tiled=True)  71 us
    psum x1, blocking collectives, body(): lax.psum((jnp.sum(values, axis=1), jnp.sum(values * values, axis=1)), 'col')  38.4 us
  transfers between devices with their start and end apart: 5, of which 5 were waited for; matrix products, arithmetic and copies ran while one was open for 4% of the time, Pallas kernels for 0%

commit v1 on v0

v1 whole, which is shorter than its diff:
```python
import numpy as np
import jax
import jax.numpy as jnp
from jax import lax
from jax.experimental import pallas as pl
from jax.experimental.pallas import tpu as pltpu
from jax.sharding import Mesh, PartitionSpec as P

DH = 128
EPSILON = 1e-06
NX = NZH = NZL = NY = 4
CORES = 2
AXES = ("x", "zh", "core", "zl", "y")
SIZES = (NX, NZH, CORES, NZL, NY)
VMEM_LIMIT = 56 * 1024 * 1024


def shift(values, axes, move):
    sizes = [SIZES[AXES.index(axis)] for axis in axes]
    pairs = [
        (int(np.ravel_multi_index(src, sizes)), int(np.ravel_multi_index(move(src), sizes)))
        for src in np.ndindex(*sizes)
    ]
    return lax.ppermute(values, axes, pairs)


def relabel(values):
    return shift(values, ("zh", "core", "zl", "y"), lambda i: (i[3], i[1], i[2], i[0]))


def relabel_cross(values):
    return shift(values, ("zh", "core", "zl", "y"), lambda i: (i[3], 1 - i[1], i[2], i[0]))


def along_z(values, step):
    return shift(values, ("zh", "zl"), lambda i: divmod((i[0] * NZL + i[1] + step) % 16, NZL))


def swap_cores(values):
    return shift(values, ("core",), lambda i: (1 - i[0],))


def spread(values, axes, count):
    return lax.all_to_all(jnp.broadcast_to(values[None], (count,) + values.shape), axes, 0, 0)


def project_kernel(
    where, t0, t1, t2a, t2b, t3, p0, p1, p2a, p2b, p3, gain, head_gain, w, kv_out, q_out, normed
):
    zl = where[0]
    pieces = (
        ((t0, 0, 128), (p0, 128, 128)),
        ((t1, 0, 128), (p1, 128, 128)),
        ((t2a, 0, 64), (t2b, 64, 64), (p2a, 128, 64), (p2b, 192, 64)),
        ((t3, 0, 128), (p3, 128, 128)),
    )
    rows = 256
    features = 6144

    def block(slot, y):
        return jnp.concatenate([ref[y] for ref, _, _ in pieces[slot]], axis=0).astype(jnp.float32)

    total = jnp.zeros((rows, 1), jnp.float32)
    squares = jnp.zeros((rows, 1), jnp.float32)
    for slot in range(4):
        for y in range(NY):
            x = block(slot, y)
            total += jnp.sum(x, axis=1, keepdims=True)
            squares += jnp.sum(x * x, axis=1, keepdims=True)
    center = total / features
    scale = lax.rsqrt(squares / features - center * center + EPSILON)
    acc = jnp.zeros((rows, 3 * DH), jnp.float32)
    for slot in range(4):
        for y in range(NY):
            c = lax.rem(zl + slot, NZL) * NY + y
            x = block(slot, y)
            n = ((x - center) * scale * gain[c]).astype(jnp.bfloat16)
            acc += jnp.dot(n, w[c], preferred_element_type=jnp.float32)

    def head_norm(values, row):
        mid = jnp.mean(values, axis=1, keepdims=True)
        var = jnp.mean(values * values, axis=1, keepdims=True) - mid * mid
        return ((values - mid) * lax.rsqrt(var + EPSILON) * row).astype(jnp.bfloat16)

    q_out[...] = head_norm(acc[:, :DH], head_gain[0])
    kv_out[:, :DH] = head_norm(acc[:, DH : 2 * DH], head_gain[1])
    kv_out[:, DH:] = acc[:, 2 * DH :].astype(jnp.bfloat16)


def attend_kernel(q, kv, out):
    keys = kv[:, :, :DH].reshape(-1, DH)
    values = kv[:, :, DH:].reshape(-1, DH)
    scores = lax.dot_general(
        q[...], keys, (((1,), (1,)), ((), ())), preferred_element_type=jnp.float32
    ) * (DH ** -0.5)
    top = jnp.max(scores, axis=1, keepdims=True)
    weights = jnp.exp(scores - top)
    total = jnp.sum(weights, axis=1, keepdims=True)
    mixed = jnp.dot(weights.astype(jnp.bfloat16), values, preferred_element_type=jnp.float32)
    out[...] = (mixed / total).astype(jnp.bfloat16)


def body(tokens, ln_gain, w_qkv, q_gain, k_gain):
    core = lax.axis_index("core")
    zl = lax.axis_index("zl")
    zh = lax.axis_index("zh")

    with jax.named_scope("weights"):
        w_mine = lax.dynamic_slice_in_dim(w_qkv, core * DH, DH, axis=2).reshape(192, 3 * DH)
        w_other = lax.dynamic_slice_in_dim(w_qkv, (1 - core) * DH, DH, axis=2).reshape(192, 3 * DH)
        w_same = relabel(w_mine)
        w_cross = relabel_cross(w_other)
        w_block = jnp.where(
            core == 0,
            jnp.concatenate([w_same, w_cross], axis=0),
            jnp.concatenate([w_cross, w_same], axis=0),
        )
        w_all = lax.all_gather(w_block, ("x", "y"), axis=0)

    with jax.named_scope("tokens"):
        line = spread(tokens, "y", NY)
        t0 = relabel(line)
        t1 = along_z(t0, -1)
        t3 = along_z(t0, 1)
        t2a = along_z(t0[:, :64], 2)
        t2b = along_z(t0[:, 64:], -2)
        mine = (t0, t1, t2a, t2b, t3)
        theirs = tuple(swap_cores(t) for t in mine)

    with jax.named_scope("gains"):
        gains = spread(
            jnp.concatenate([ln_gain.astype(jnp.float32), q_gain, k_gain]), ("zl", "y"), NZL * NY
        )
        gain = gains[:, None, :384]
        head = lax.dynamic_slice_in_dim(gains, zl * NY + zh, 1, axis=0)
        head = lax.dynamic_slice_in_dim(head[:, 384:].reshape(2, 2, DH), core, 1, axis=1)

    with jax.named_scope("project"):
        kv, q = pl.pallas_call(
            project_kernel,
            out_shape=(
                jax.ShapeDtypeStruct((256, 2 * DH), jnp.bfloat16),
                jax.ShapeDtypeStruct((256, DH), jnp.bfloat16),
            ),
            in_specs=[pl.BlockSpec(memory_space=pltpu.SMEM)]
            + [pl.BlockSpec(memory_space=pltpu.VMEM)] * 13,
            out_specs=(pl.BlockSpec(memory_space=pltpu.VMEM),) * 2,
            scratch_shapes=[pltpu.VMEM((8, 128), jnp.float32)],
            compiler_params=pltpu.CompilerParams(vmem_limit_bytes=VMEM_LIMIT),
        )(zl.reshape(1).astype(jnp.int32), *mine, *theirs, gain, head, w_all)

    with jax.named_scope("keys"):
        kv_all = spread(kv, ("x", "y"), NX * NY)

    with jax.named_scope("attend"):
        out = pl.pallas_call(
            attend_kernel,
            out_shape=jax.ShapeDtypeStruct((256, DH), jnp.bfloat16),
            in_specs=[pl.BlockSpec(memory_space=pltpu.VMEM)] * 2,
            out_specs=pl.BlockSpec(memory_space=pltpu.VMEM),
            compiler_params=pltpu.CompilerParams(vmem_limit_bytes=VMEM_LIMIT),
        )(q, kv_all)

    with jax.named_scope("home"):
        same = relabel(out[:128])
        cross = relabel_cross(out[128:])
        return jnp.where(
            core == 0,
            jnp.concatenate([same, cross], axis=1),
            jnp.concatenate([cross, same], axis=1),
        )


def solution(mesh):
    fine = Mesh(mesh.devices.reshape(SIZES), AXES)
    rows = ("x", "zh", "core")
    cols = ("zl", "y")
    in_specs = (P(rows, cols), P(cols), P(rows, None, cols), P(cols), P(cols))
    return jax.shard_map(body, mesh=fine, in_specs=in_specs, out_specs=P(rows, cols), check_vma=False)
```

time: 514 us -> 243 us (0.47)
  the two profiles are of different devices: /device:TPU:1 before, /device:TPU:16 now
where the time goes in v1:
time: 243 us
  starting transfers between devices  113 us (47%)
  blocking collectives  59.9 us (25%)
  waiting for transfers between devices  36.6 us (15%)
  between operations  13.8 us (6%)
  Pallas kernels  11.7 us (5%)
  local copies, waits for them, and re-layouts  5.88 us (2%)
    ppermute x14, starting transfers between devices, shift(): return lax.ppermute(values, axes, pairs)  108 us
    all_to_all x2, blocking collectives, spread(): lax.all_to_all(jnp.broadcast_to(values[None], (count,) + values.shape), a...  59.9 us
    ppermute x14, waiting for transfers between devices, shift(): return lax.ppermute(values, axes, pairs)  36.6 us
    pallas_call x1, Pallas kernels, body(): pl.pallas_call(project_kernel, out_shape=(jax.ShapeDtypeStruct((256, 2 *...  7.41 us
    all_to_all x1, starting transfers between devices, spread(): lax.all_to_all(jnp.broadcast_to(values[None], (count,) + values.shape), a...  5.05 us
  transfers between devices with their start and end apart: 16, of which 7 were waited for; matrix products, arithmetic and copies ran while one was open for 1% of the time, Pallas kernels for 0%

profile of v1, /device:TPU:16, one launch (start us, length us, event | category | flops | bytes accessed | tf_op | source)
XLA Modules:
  0.0 242.6 jit_solution(4589325222835847578)
XLA Ops:
  6.6 1.0 dynamic-slice_bitcast_fusion.1
  7.7 14.9 %collective-permute-start.11 = (bf16[192,384]{1,0:T(8,128)(2,1)S(1)}, bf16[192,384]{1,0:T(8,128)(2,1)S(1)}, u32[]{:S(2)}, u32[]{:S(2)}) collective-permute-start(bf16[192,384]{1,0:T(8,128)(2,1)S(1)} %bitcast.19), channel_id=1, source_target_pairs={{0,16},{1,48},{2,80},{3,112},{4,20},{5,52},{6,84},{7,116},{8,24},{... | collective-permute-start | bytes 442376 | tf_op jit(solution)/shard_map/weights/ppermute | solution.py:24
  22.6 2.5 %collective-permute-start.10 = (bf16[192,384]{1,0:T(8,128)(2,1)S(1)}, bf16[192,384]{1,0:T(8,128)(2,1)S(1)}, u32[]{:S(2)}, u32[]{:S(2)}) collective-permute-start(bf16[192,384]{1,0:T(8,128)(2,1)S(1)} %bitcast.20), channel_id=1, source_target_pairs={{0,0},{1,32},{2,64},{3,96},{4,4},{5,36},{6,68},{7,100},{8,8},{9,40... | collective-permute-start | bytes 442376 | tf_op jit(solution)/shard_map/weights/ppermute | solution.py:24
  25.1 1.7 collective-permute-done.11
  26.8 15.6 %collective-permute-done.10 = bf16[192,384]{1,0:T(8,128)(2,1)S(1)} collective-permute-done((bf16[192,384]{1,0:T(8,128)(2,1)S(1)}, bf16[192,384]{1,0:T(8,128)(2,1)S(1)}, u32[]{:S(2)}, u32[]{:S(2)}) %collective-permute-start.10) | collective-permute-done | bytes 147488 | tf_op jit(solution)/shard_map/weights/ppermute | solution.py:24
  42.4 0.8 maximum_select_fusion
  43.3 26.1 %all_to_all.19 = bf16[4,128,384]{2,1,0:T(8,128)(2,1)S(1)} all-to-all(bf16[4,128,384]{2,1,0:T(8,128)(2,1)S(1)} %broadcast_in_dim.8), channel_id=1, replica_groups=mesh['x'=4,'zh'=4,'core'=2,'zl'=4,'y'=4] {'y'}, dimensions={0} | all-to-all | bytes 786432 | tf_op jit(solution)/shard_map/tokens/all_to_all | solution.py:44
  69.4 14.6 %collective-permute-start = (bf16[4,128,384]{2,1,0:T(8,128)(2,1)S(1)}, bf16[4,128,384]{2,1,0:T(8,128)(2,1)S(1)}, u32[]{:S(2)}, u32[]{:S(2)}) collective-permute-start(bf16[4,128,384]{2,1,0:T(8,128)(2,1)S(1)} %all_to_all.19), channel_id=1, source_target_pairs={{0,0},{1,32},{2,64},{3,96},{4,4},{5,36},{6,68},{7,100},{8,8},{9,40... | collective-permute-start | bytes 1179656 | tf_op jit(solution)/shard_map/tokens/ppermute | solution.py:24
  84.1 9.0 %collective-permute-done.t0 = bf16[4,128,384]{2,1,0:T(8,128)(2,1)S(1)} collective-permute-done((bf16[4,128,384]{2,1,0:T(8,128)(2,1)S(1)}, bf16[4,128,384]{2,1,0:T(8,128)(2,1)S(1)}, u32[]{:S(2)}, u32[]{:S(2)}) %collective-permute-start) | collective-permute-done | bytes 393248 | tf_op jit(solution)/shard_map/tokens/ppermute | solution.py:24
  93.1 3.3 %collective-permute-start.4 = (bf16[4,128,384]{2,1,0:T(8,128)(2,1)S(1)}, bf16[4,128,384]{2,1,0:T(8,128)(2,1)S(1)}, u32[]{:S(2)}, u32[]{:S(2)}) collective-permute-start(bf16[4,128,384]{2,1,0:T(8,128)(2,1)S(1)} %collective-permute-done.t0), channel_id=1, source_target_pairs={{0,4},{4,8},{8,12},{12,32},{32,36},{36,40},{40,44},{44,64},{64,68}... | collective-permute-start | bytes 1179656 | tf_op jit(solution)/shard_map/tokens/ppermute | solution.py:24
  96.4 36.1 %collective-permute-start.1 = (bf16[4,128,384]{2,1,0:T(8,128)(2,1)S(1)}, bf16[4,128,384]{2,1,0:T(8,128)(2,1)S(1)}, u32[]{:S(2)}, u32[]{:S(2)}) collective-permute-start(bf16[4,128,384]{2,1,0:T(8,128)(2,1)S(1)} %collective-permute-done.t0), channel_id=1, source_target_pairs={{0,108},{4,0},{8,4},{12,8},{32,12},{36,32},{40,36},{44,40},{64,44}... | collective-permute-start | bytes 1179656 | tf_op jit(solution)/shard_map/tokens/ppermute | solution.py:24
  132.6 0.7 broadcast_in_dim.9
  133.2 5.0 %all-to-all-start.1 = ((f32[16,1,896]{2,1,0:T(1,128)}), f32[16,1,896]{2,1,0:T(1,128)S(1)}, u32[]{:S(2)}, u32[]{:S(2)}) async-start(f32[16,1,896]{2,1,0:T(1,128)} %broadcast_in_dim.9), calls=%async_computation.1 | async-start | bytes 114688 | tf_op jit(solution)/shard_map/gains/all_to_all | solution.py:44
  138.3 8.8 %collective-permute-start.3 = (bf16[4,64,384]{2,1,0:T(8,128)(2,1)S(1)}, bf16[4,64,384]{2,1,0:T(8,128)(2,1)S(1)}, u32[]{:S(2)}, u32[]{:S(2)}) collective-permute-start(bf16[4,64,384]{2,1,0:T(8,128)(2,1)S(1)} %get-tuple-element.9), channel_id=1, source_target_pairs={{0,104},{4,108},{8,0},{12,4},{32,8},{36,12},{40,32},{44,36},{64,40... | collective-permute-start | bytes 589832 | tf_op jit(solution)/shard_map/tokens/ppermute | solution.py:24
  147.2 1.9 collective-permute-start.2
  149.1 1.9 collective-permute-start.5
  151.0 2.4 collective-permute-start.9
  153.5 1.9 collective-permute-start.6
  155.4 2.4 collective-permute-start.8
  157.8 3.1 %collective-permute-done.2.t2a = bf16[4,64,384]{2,1,0:T(8,128)(2,1)S(1)} collective-permute-done((bf16[4,64,384]{2,1,0:T(8,128)(2,1)S(1)}, bf16[4,64,384]{2,1,0:T(8,128)(2,1)S(1)}, u32[]{:S(2)}, u32[]{:S(2)}) %collective-permute-start.2) | collective-permute-done | bytes 196640 | tf_op jit(solution)/shard_map/tokens/ppermute | solution.py:24
  161.0 1.9 collective-permute-start.7
  163.0 0.6 broadcast_in_dim.10.gain
  165.4 7.4 %project.1 = (bf16[256,256]{1,0:T(8,128)(2,1)}, bf16[256,128]{1,0:T(8,128)(2,1)}) custom-call(s32[1]{0:T(128)} %bitcast.where, bf16[4,128,384]{2,1,0:T(8,128)(2,1)} %copy-done, bf16[4,128,384]{2,1,0:T(8,128)(2,1)} %copy-done.2, bf16[4,64,384]{2,1,0:T(8,128)(2,1)} %copy-done.7, bf16[4,64,384]{2,1,0:T(8,128)(2,1)} %copy-done.6, ...), custom_call_target="tpu_custom_call" | custom-call | tf_op jit(solution)/shard_map/project/pallas_call | solution.py:139
  172.8 1.1 broadcast_in_dim.11
  173.9 33.8 %all_to_all.20.kv = bf16[16,256,256]{2,1,0:T(8,128)(2,1)} all-to-all(bf16[16,256,256]{2,1,0:T(8,128)(2,1)S(1)} %broadcast_in_dim.11), channel_id=1, replica_groups=mesh['x'=4,'zh'=4,'core'=2,'zl'=4,'y'=4] {'x','y'}, dimensions={0} | all-to-all | bytes 4194304 | tf_op jit(solution)/shard_map/keys/all_to_all | solution.py:44
  207.7 4.3 %attend.1 = bf16[256,128]{1,0:T(8,128)(2,1)} custom-call(bf16[256,128]{1,0:T(8,128)(2,1)} %get-tuple-element.7.q, bf16[16,256,256]{2,1,0:T(8,128)(2,1)} %all_to_all.20.kv), custom_call_target="tpu_custom_call" | custom-call | tf_op jit(solution)/shard_map/attend/pallas_call | solution.py:156
  212.0 0.8 fusion.1
  212.8 6.0 %collective-permute-start.12 = (bf16[128,128]{1,0:T(8,128)(2,1)S(1)}, bf16[128,128]{1,0:T(8,128)(2,1)S(1)}, u32[]{:S(2)}, u32[]{:S(2)}) collective-permute-start(bf16[128,128]{1,0:T(8,128)(2,1)S(1)} %get-tuple-element.13), channel_id=1, source_target_pairs={{0,0},{1,32},{2,64},{3,96},{4,4},{5,36},{6,68},{7,100},{8,8},{9,40... | collective-permute-start | bytes 98312 | tf_op jit(solution)/shard_map/home/ppermute | solution.py:24
  218.8 9.3 %collective-permute-start.13 = (bf16[128,128]{1,0:T(8,128)(2,1)S(1)}, bf16[128,128]{1,0:T(8,128)(2,1)S(1)}, u32[]{:S(2)}, u32[]{:S(2)}) collective-permute-start(bf16[128,128]{1,0:T(8,128)(2,1)S(1)} %get-tuple-element.14), channel_id=1, source_target_pairs={{0,16},{1,48},{2,80},{3,112},{4,20},{5,52},{6,84},{7,116},{8,24},{... | collective-permute-start | bytes 98312 | tf_op jit(solution)/shard_map/home/ppermute | solution.py:24
  228.1 1.6 collective-permute-done.12
  229.7 5.4 %collective-permute-done.13 = bf16[128,128]{1,0:T(8,128)(2,1)S(1)} collective-permute-done((bf16[128,128]{1,0:T(8,128)(2,1)S(1)}, bf16[128,128]{1,0:T(8,128)(2,1)S(1)}, u32[]{:S(2)}, u32[]{:S(2)}) %collective-permute-start.13) | collective-permute-done | bytes 32800 | tf_op jit(solution)/shard_map/home/ppermute | solution.py:24
  235.1 0.6 maximum_select_fusion.1
  (51 shorter events, 2.0 us)
Async XLA Ops:
  6.5 36.7 %copy-start.10 = (bf16[128,384]{1,0:T(8,128)(2,1)S(1)}, bf16[128,384]{1,0:T(8,128)(2,1)}, u32[]{:S(2)}) copy-start(bf16[128,384]{1,0:T(8,128)(2,1)} %param.5) | copy-start | bytes 294916
  6.5 126.0 %copy-start.11 = (bf16[384]{0:T(512)(128)(2,1)S(1)}, bf16[384]{0:T(512)(128)(2,1)}, u32[]{:S(2)}) copy-start(bf16[384]{0:T(512)(128)(2,1)} %param.6) | copy-start | bytes 2308
  6.5 126.0 %copy-start.12 = (f32[256]{0:T(256)S(1)}, f32[256]{0:T(256)}, u32[]{:S(2)}) copy-start(f32[256]{0:T(256)} %param.9) | copy-start | bytes 3076
  6.5 126.0 %copy-start.13 = (f32[256]{0:T(256)S(1)}, f32[256]{0:T(256)}, u32[]{:S(2)}) copy-start(f32[256]{0:T(256)} %param.8) | copy-start | bytes 3076
  6.5 157.8 %all-gather.2.cloned.1.call-start = ((), (), s32[]{:S(2)}) async-start(), calls=%async_computation.3 | async-start | bytes 5013504 | tf_op jit(solution)/shard_map/weights/all_gather | solution.py:118
  7.7 19.2 %collective-permute-start.11 = (bf16[192,384]{1,0:T(8,128)(2,1)S(1)}, bf16[192,384]{1,0:T(8,128)(2,1)S(1)}, u32[]{:S(2)}, u32[]{:S(2)}) collective-permute-start(bf16[192,384]{1,0:T(8,128)(2,1)S(1)} %bitcast.19), channel_id=1, source_target_pairs={{0,16},{1,48},{2,80},{3,112},{4,20},{5,52},{6,84},{7,116},{8,24},{... | collective-permute-start | bytes 442376 | tf_op jit(solution)/shard_map/weights/ppermute | solution.py:24
  22.6 19.8 %collective-permute-start.10 = (bf16[192,384]{1,0:T(8,128)(2,1)S(1)}, bf16[192,384]{1,0:T(8,128)(2,1)S(1)}, u32[]{:S(2)}, u32[]{:S(2)}) collective-permute-start(bf16[192,384]{1,0:T(8,128)(2,1)S(1)} %bitcast.20), channel_id=1, source_target_pairs={{0,0},{1,32},{2,64},{3,96},{4,4},{5,36},{6,68},{7,100},{8,8},{9,40... | collective-permute-start | bytes 442376 | tf_op jit(solution)/shard_map/weights/ppermute | solution.py:24
  69.4 23.6 %collective-permute-start = (bf16[4,128,384]{2,1,0:T(8,128)(2,1)S(1)}, bf16[4,128,384]{2,1,0:T(8,128)(2,1)S(1)}, u32[]{:S(2)}, u32[]{:S(2)}) collective-permute-start(bf16[4,128,384]{2,1,0:T(8,128)(2,1)S(1)} %all_to_all.19), channel_id=1, source_target_pairs={{0,0},{1,32},{2,64},{3,96},{4,4},{5,36},{6,68},{7,100},{8,8},{9,40... | collective-permute-start | bytes 1179656 | tf_op jit(solution)/shard_map/tokens/ppermute | solution.py:24
  93.1 71.3 %copy-start = (bf16[4,128,384]{2,1,0:T(8,128)(2,1)}, bf16[4,128,384]{2,1,0:T(8,128)(2,1)S(1)}, u32[]{:S(2)}) copy-start(bf16[4,128,384]{2,1,0:T(8,128)(2,1)S(1)} %collective-permute-done.t0) | copy-start | bytes 1179652
  93.1 57.9 %collective-permute-start.4 = (bf16[4,128,384]{2,1,0:T(8,128)(2,1)S(1)}, bf16[4,128,384]{2,1,0:T(8,128)(2,1)S(1)}, u32[]{:S(2)}, u32[]{:S(2)}) collective-permute-start(bf16[4,128,384]{2,1,0:T(8,128)(2,1)S(1)} %collective-permute-done.t0), channel_id=1, source_target_pairs={{0,4},{4,8},{8,12},{12,32},{32,36},{36,40},{40,44},{44,64},{64,68}... | collective-permute-start | bytes 1179656 | tf_op jit(solution)/shard_map/tokens/ppermute | solution.py:24
  96.4 57.1 %collective-permute-start.1 = (bf16[4,128,384]{2,1,0:T(8,128)(2,1)S(1)}, bf16[4,128,384]{2,1,0:T(8,128)(2,1)S(1)}, u32[]{:S(2)}, u32[]{:S(2)}) collective-permute-start(bf16[4,128,384]{2,1,0:T(8,128)(2,1)S(1)} %collective-permute-done.t0), channel_id=1, source_target_pairs={{0,108},{4,0},{8,4},{12,8},{32,12},{36,32},{40,36},{44,40},{64,44}... | collective-permute-start | bytes 1179656 | tf_op jit(solution)/shard_map/tokens/ppermute | solution.py:24
  133.2 29.7 %all-to-all-start.1 = ((f32[16,1,896]{2,1,0:T(1,128)}), f32[16,1,896]{2,1,0:T(1,128)S(1)}, u32[]{:S(2)}, u32[]{:S(2)}) async-start(f32[16,1,896]{2,1,0:T(1,128)} %broadcast_in_dim.9), calls=%async_computation.1 | async-start | bytes 114688 | tf_op jit(solution)/shard_map/gains/all_to_all | solution.py:44
  138.3 17.1 %collective-permute-start.3 = (bf16[4,64,384]{2,1,0:T(8,128)(2,1)S(1)}, bf16[4,64,384]{2,1,0:T(8,128)(2,1)S(1)}, u32[]{:S(2)}, u32[]{:S(2)}) collective-permute-start(bf16[4,64,384]{2,1,0:T(8,128)(2,1)S(1)} %get-tuple-element.9), channel_id=1, source_target_pairs={{0,104},{4,108},{8,0},{12,4},{32,8},{36,12},{40,32},{44,36},{64,40... | collective-permute-start | bytes 589832 | tf_op jit(solution)/shard_map/tokens/ppermute | solution.py:24
  147.2 13.8 %collective-permute-start.2 = (bf16[4,64,384]{2,1,0:T(8,128)(2,1)S(1)}, bf16[4,64,384]{2,1,0:T(8,128)(2,1)S(1)}, u32[]{:S(2)}, u32[]{:S(2)}) collective-permute-start(bf16[4,64,384]{2,1,0:T(8,128)(2,1)S(1)} %get-tuple-element.10), channel_id=1, source_target_pairs={{0,8},{4,12},{8,32},{12,36},{32,40},{36,44},{40,64},{44,68},{64,72... | collective-permute-start | bytes 589832 | tf_op jit(solution)/shard_map/tokens/ppermute | solution.py:24
  149.1 15.2 %collective-permute-start.5 = (bf16[4,128,384]{2,1,0:T(8,128)(2,1)S(1)}, bf16[4,128,384]{2,1,0:T(8,128)(2,1)S(1)}, u32[]{:S(2)}, u32[]{:S(2)}) collective-permute-start(bf16[4,128,384]{2,1,0:T(8,128)(2,1)S(1)} %collective-permute-done.t0), channel_id=1, source_target_pairs={{0,16},{16,0},{1,17},{17,1},{2,18},{18,2},{3,19},{19,3},{4,20},{20... | collective-permute-start | bytes 1179656 | tf_op jit(solution)/shard_map/tokens/ppermute | solution.py:24
  151.0 13.4 %copy-start.1 = (bf16[4,128,384]{2,1,0:T(8,128)(2,1)}, bf16[4,128,384]{2,1,0:T(8,128)(2,1)S(1)}, u32[]{:S(2)}) copy-start(bf16[4,128,384]{2,1,0:T(8,128)(2,1)S(1)} %collective-permute-done.4.t3) | copy-start | bytes 1179652
  151.0 13.3 %collective-permute-start.9 = (bf16[4,128,384]{2,1,0:T(8,128)(2,1)S(1)}, bf16[4,128,384]{2,1,0:T(8,128)(2,1)S(1)}, u32[]{:S(2)}, u32[]{:S(2)}) collective-permute-start(bf16[4,128,384]{2,1,0:T(8,128)(2,1)S(1)} %collective-permute-done.4.t3), channel_id=1, source_target_pairs={{0,16},{16,0},{1,17},{17,1},{2,18},{18,2},{3,19},{19,3},{4,20},{20... | collective-permute-start | bytes 1179656 | tf_op jit(solution)/shard_map/tokens/ppermute | solution.py:24
  153.5 10.9 %copy-start.2 = (bf16[4,128,384]{2,1,0:T(8,128)(2,1)}, bf16[4,128,384]{2,1,0:T(8,128)(2,1)S(1)}, u32[]{:S(2)}) copy-start(bf16[4,128,384]{2,1,0:T(8,128)(2,1)S(1)} %collective-permute-done.1.t1) | copy-start | bytes 1179652
  153.5 10.9 %collective-permute-start.6 = (bf16[4,128,384]{2,1,0:T(8,128)(2,1)S(1)}, bf16[4,128,384]{2,1,0:T(8,128)(2,1)S(1)}, u32[]{:S(2)}, u32[]{:S(2)}) collective-permute-start(bf16[4,128,384]{2,1,0:T(8,128)(2,1)S(1)} %collective-permute-done.1.t1), channel_id=1, source_target_pairs={{0,16},{16,0},{1,17},{17,1},{2,18},{18,2},{3,19},{19,3},{4,20},{20... | collective-permute-start | bytes 1179656 | tf_op jit(solution)/shard_map/tokens/ppermute | solution.py:24
  155.4 9.0 %copy-start.6 = (bf16[4,64,384]{2,1,0:T(8,128)(2,1)}, bf16[4,64,384]{2,1,0:T(8,128)(2,1)S(1)}, u32[]{:S(2)}) copy-start(bf16[4,64,384]{2,1,0:T(8,128)(2,1)S(1)} %collective-permute-done.3.t2b) | copy-start | bytes 589828
  155.4 8.7 %collective-permute-start.8 = (bf16[4,64,384]{2,1,0:T(8,128)(2,1)S(1)}, bf16[4,64,384]{2,1,0:T(8,128)(2,1)S(1)}, u32[]{:S(2)}, u32[]{:S(2)}) collective-permute-start(bf16[4,64,384]{2,1,0:T(8,128)(2,1)S(1)} %collective-permute-done.3.t2b), channel_id=1, source_target_pairs={{0,16},{16,0},{1,17},{17,1},{2,18},{18,2},{3,19},{19,3},{4,20},{20... | collective-permute-start | bytes 589832 | tf_op jit(solution)/shard_map/tokens/ppermute | solution.py:24
  161.0 3.4 %copy-start.7 = (bf16[4,64,384]{2,1,0:T(8,128)(2,1)}, bf16[4,64,384]{2,1,0:T(8,128)(2,1)S(1)}, u32[]{:S(2)}) copy-start(bf16[4,64,384]{2,1,0:T(8,128)(2,1)S(1)} %collective-permute-done.2.t2a) | copy-start | bytes 589828
  161.0 3.3 %collective-permute-start.7 = (bf16[4,64,384]{2,1,0:T(8,128)(2,1)S(1)}, bf16[4,64,384]{2,1,0:T(8,128)(2,1)S(1)}, u32[]{:S(2)}, u32[]{:S(2)}) collective-permute-start(bf16[4,64,384]{2,1,0:T(8,128)(2,1)S(1)} %collective-permute-done.2.t2a), channel_id=1, source_target_pairs={{0,16},{16,0},{1,17},{17,1},{2,18},{18,2},{3,19},{19,3},{4,20},{20... | collective-permute-start | bytes 589832 | tf_op jit(solution)/shard_map/tokens/ppermute | solution.py:24
  164.1 0.7 copy-start.8
  164.3 0.7 copy-start.9
  164.3 0.8 copy-start.3
  164.3 1.0 copy-start.4
  164.3 1.1 copy-start.5
  212.8 16.9 %collective-permute-start.12 = (bf16[128,128]{1,0:T(8,128)(2,1)S(1)}, bf16[128,128]{1,0:T(8,128)(2,1)S(1)}, u32[]{:S(2)}, u32[]{:S(2)}) collective-permute-start(bf16[128,128]{1,0:T(8,128)(2,1)S(1)} %get-tuple-element.13), channel_id=1, source_target_pairs={{0,0},{1,32},{2,64},{3,96},{4,4},{5,36},{6,68},{7,100},{8,8},{9,40... | collective-permute-start | bytes 98312 | tf_op jit(solution)/shard_map/home/ppermute | solution.py:24
  218.8 16.4 %collective-permute-start.13 = (bf16[128,128]{1,0:T(8,128)(2,1)S(1)}, bf16[128,128]{1,0:T(8,128)(2,1)S(1)}, u32[]{:S(2)}, u32[]{:S(2)}) collective-permute-start(bf16[128,128]{1,0:T(8,128)(2,1)S(1)} %get-tuple-element.14), channel_id=1, source_target_pairs={{0,16},{1,48},{2,80},{3,112},{4,20},{5,52},{6,84},{7,116},{8,24},{... | collective-permute-start | bytes 98312 | tf_op jit(solution)/shard_map/home/ppermute | solution.py:24
Sparse Core Ops, SparseCore 0:
  43.3 96.9 all-gather.1

commit v2 on v1

v2 whole, which is shorter than its diff:
```python
import numpy as np
import jax
import jax.numpy as jnp
from jax import lax
from jax.experimental import pallas as pl
from jax.experimental.pallas import tpu as pltpu
from jax.sharding import Mesh, PartitionSpec as P

DH = 128
EPSILON = 1e-06
NX = NZH = NZL = NY = 4
CORES = 2
AXES = ("x", "zh", "core", "zl", "y")
SIZES = (NX, NZH, CORES, NZL, NY)
VMEM_LIMIT = 56 * 1024 * 1024


def shift(values, axes, move):
    sizes = [SIZES[AXES.index(axis)] for axis in axes]
    pairs = [
        (int(np.ravel_multi_index(src, sizes)), int(np.ravel_multi_index(move(src), sizes)))
        for src in np.ndindex(*sizes)
    ]
    return lax.ppermute(values, axes, pairs)


def relabel(values):
    return shift(values, ("zh", "core", "zl", "y"), lambda i: (i[3], i[1], i[2], i[0]))


def relabel_cross(values):
    return shift(values, ("zh", "core", "zl", "y"), lambda i: (i[3], 1 - i[1], i[2], i[0]))


def rotate(values):
    return shift(values, ("x", "zh", "zl", "y"), lambda i: (i[2], i[3], i[0], i[1]))


def along_z(values, step):
    return shift(values, ("zh", "zl"), lambda i: divmod((i[0] * NZL + i[1] + step) % 16, NZL))


def swap_cores(values):
    return shift(values, ("core",), lambda i: (1 - i[0],))


def spread(values, axes, count):
    return lax.all_to_all(jnp.broadcast_to(values[None], (count,) + values.shape), axes, 0, 0)


def partial_kernel(
    where, t0, t1, t2a, t2b, t3, p0, p1, p2a, p2b, p3, w, out
):
    zl = where[0]
    pieces = (
        (t0, p0),
        (t1, p1),
        (t2a, t2b, p2a, p2b),
        (t3, p3),
    )
    for slot in range(4):
        acc = None
        for y in range(NY):
            x = jnp.concatenate([ref[y] for ref in pieces[slot]], axis=0)
            term = jnp.dot(x, w[y], preferred_element_type=jnp.float32)
            acc = term if acc is None else acc + term
        out[lax.rem(zl + slot, NZL)] = acc


def heads_kernel(part, head_gain, kv_out, q_out):
    acc = part[0] + part[1] + part[2] + part[3]

    def head_norm(values, row):
        mid = jnp.mean(values, axis=1, keepdims=True)
        var = jnp.mean(values * values, axis=1, keepdims=True) - mid * mid
        return ((values - mid) * lax.rsqrt(var + EPSILON) * row).astype(jnp.bfloat16)

    q_out[...] = head_norm(acc[:, :DH], head_gain[0])
    kv_out[:, :DH] = head_norm(acc[:, DH : 2 * DH], head_gain[1])
    kv_out[:, DH:] = acc[:, 2 * DH :].astype(jnp.bfloat16)


def attend_kernel(q, kv, out):
    keys = kv[:, :, :DH].reshape(-1, DH)
    values = kv[:, :, DH:].reshape(-1, DH)
    scores = lax.dot_general(
        q[...], keys, (((1,), (1,)), ((), ())), preferred_element_type=jnp.float32
    ) * (DH ** -0.5)
    top = jnp.max(scores, axis=1, keepdims=True)
    weights = jnp.exp(scores - top)
    total = jnp.sum(weights, axis=1, keepdims=True)
    mixed = jnp.dot(weights.astype(jnp.bfloat16), values, preferred_element_type=jnp.float32)
    out[...] = (mixed / total).astype(jnp.bfloat16)


def kernel_call(kernel, out_shape, args, scalars=0):
    vmem = pl.BlockSpec(memory_space=pltpu.VMEM)
    smem = pl.BlockSpec(memory_space=pltpu.SMEM)
    return pl.pallas_call(
        kernel,
        out_shape=out_shape,
        in_specs=[smem] * scalars + [vmem] * (len(args) - scalars),
        out_specs=jax.tree.map(lambda _: vmem, out_shape),
        compiler_params=pltpu.CompilerParams(vmem_limit_bytes=VMEM_LIMIT),
    )(*args)


def body(tokens, ln_gain, w_qkv, q_gain, k_gain):
    core = lax.axis_index("core")
    zl = lax.axis_index("zl")
    zh = lax.axis_index("zh")

    with jax.named_scope("weights"):
        w_mine = lax.dynamic_slice_in_dim(w_qkv, core * DH, DH, axis=2).reshape(192, 3 * DH)
        w_other = lax.dynamic_slice_in_dim(w_qkv, (1 - core) * DH, DH, axis=2).reshape(192, 3 * DH)
        w_same = relabel(w_mine)
        w_cross = relabel_cross(w_other)

    with jax.named_scope("norm"):
        x = tokens.astype(jnp.float32)
        sums = jnp.concatenate([jnp.sum(x, axis=1), jnp.sum(x * x, axis=1), q_gain, k_gain])
        shared = spread(sums[None], ("zl", "y"), NZL * NY)
        features = tokens.shape[1] * NZL * NY
        stats = jnp.sum(shared[:, 0, :256], axis=0) / features
        center = stats[:128, None]
        var = stats[128:, None] - center * center
        normed = ((x - center) * lax.rsqrt(var + EPSILON) * ln_gain.astype(jnp.float32)).astype(
            jnp.bfloat16
        )
        head = lax.dynamic_slice_in_dim(shared[:, 0, 256:], zl * NY + zh, 1, axis=0)
        head = lax.dynamic_slice_in_dim(head.reshape(2, 2, DH), core, 1, axis=1)

    with jax.named_scope("tokens"):
        line = spread(normed, "y", NY)
        t0 = rotate(line)
        t1 = along_z(t0, -1)
        t3 = along_z(t0, 1)
        t2a = along_z(t0[:, :64], 2)
        t2b = along_z(t0[:, 64:], -2)
        mine = (t0, t1, t2a, t2b, t3)
        theirs = tuple(swap_cores(t) for t in mine)

    with jax.named_scope("weights"):
        w_block = jnp.where(
            core == 0,
            jnp.concatenate([w_same, w_cross], axis=0),
            jnp.concatenate([w_cross, w_same], axis=0),
        )
        w_line = spread(w_block, "y", NY)

    with jax.named_scope("project"):
        part = kernel_call(
            partial_kernel,
            jax.ShapeDtypeStruct((NX, 256, 3 * DH), jnp.float32),
            (zl.reshape(1).astype(jnp.int32), *mine, *theirs, w_line),
            scalars=1,
        )
        part = lax.all_to_all(part, "x", 0, 0)
        kv, q = kernel_call(
            heads_kernel,
            (
                jax.ShapeDtypeStruct((256, 2 * DH), jnp.bfloat16),
                jax.ShapeDtypeStruct((256, DH), jnp.bfloat16),
            ),
            (part, head),
        )

    with jax.named_scope("keys"):
        kv_all = spread(kv, ("x", "y"), NX * NY)

    with jax.named_scope("attend"):
        out = kernel_call(
            attend_kernel, jax.ShapeDtypeStruct((256, DH), jnp.bfloat16), (q, kv_all)
        )

    with jax.named_scope("home"):
        same = relabel(out[:128])
        cross = relabel_cross(out[128:])
        return jnp.where(
            core == 0,
            jnp.concatenate([same, cross], axis=1),
            jnp.concatenate([cross, same], axis=1),
        )


def solution(mesh):
    fine = Mesh(mesh.devices.reshape(SIZES), AXES)
    rows = ("x", "zh", "core")
    cols = ("zl", "y")
    in_specs = (P(rows, cols), P(cols), P(rows, None, cols), P(cols), P(cols))
    return jax.shard_map(body, mesh=fine, in_specs=in_specs, out_specs=P(rows, cols), check_vma=False)
```

time: 243 us -> 283 us (1.16)
  starting transfers between devices: 113 us -> 170 us
  blocking collectives: 59.9 us -> 30.9 us
  waiting for transfers between devices: 36.6 us -> 56.9 us
  between operations: 13.8 us -> 0.34 us
    all_to_all x1 -> x3, starting transfers between devices: 5.05 us -> 70.8 us  [spread(): lax.all_to_all(jnp.broadcast_to(values[None], (count,) + values.shape), a...]
    all_to_all x2 -> x1, blocking collectives: 59.9 us -> 30.9 us  [spread(): lax.all_to_all(jnp.broadcast_to(values[None], (count,) + values.shape), a...]
    all_to_all x0 -> x1, waiting for transfers between devices: none -> 20.7 us  [body(): part = lax.all_to_all(part, 'x', 0, 0)]
    ppermute x14, starting transfers between devices: 108 us -> 95.1 us  [shift(): return lax.ppermute(values, axes, pairs)]
    ppermute x14, waiting for transfers between devices: 36.6 us -> 26.6 us  [shift(): return lax.ppermute(values, axes, pairs)]
    all_to_all x1 -> x3, waiting for transfers between devices: 0.01 us -> 9.66 us  [spread(): lax.all_to_all(jnp.broadcast_to(values[None], (count,) + values.shape), a...]
    all_to_all x0 -> x1, starting transfers between devices: none -> 3.69 us  [body(): part = lax.all_to_all(part, 'x', 0, 0)]
    pallas_call x2 -> x3, Pallas kernels: 11.7 us -> 12.1 us  [kernel_call(): pl.pallas_call(kernel, out_shape=out_shape, in_specs=[smem] * scalars + [...]
  transfers between devices with their start and end apart: 16 -> 18, of which waited for: 7 -> 10; matrix products, arithmetic and copies ran while one was open for 1% -> 1% of each run, Pallas kernels for 0% -> 0%
where the time goes in v2:
time: 283 us; the launch traced here: 282 us
  starting transfers between devices  170 us (60%)
  waiting for transfers between devices  56.9 us (20%)
  blocking collectives  30.9 us (11%)
  Pallas kernels  12.1 us (4%)
  local copies, waits for them, and re-layouts  7.4 us (3%)
  other arithmetic  4.22 us (1%)
    ppermute x14, starting transfers between devices, shift(): return lax.ppermute(values, axes, pairs)  95.1 us
    all_to_all x3, starting transfers between devices, spread(): lax.all_to_all(jnp.broadcast_to(values[None], (count,) + values.shape), a...  70.8 us
    all_to_all x1, blocking collectives, spread(): lax.all_to_all(jnp.broadcast_to(values[None], (count,) + values.shape), a...  30.9 us
    ppermute x14, waiting for transfers between devices, shift(): return lax.ppermute(values, axes, pairs)  26.6 us
    all_to_all x1, waiting for transfers between devices, body(): part = lax.all_to_all(part, 'x', 0, 0)  20.7 us
    pallas_call x3, Pallas kernels, kernel_call(): pl.pallas_call(kernel, out_shape=out_shape, in_specs=[smem] * scalars + [...  12.1 us
    all_to_all x3, waiting for transfers between devices, spread(): lax.all_to_all(jnp.broadcast_to(values[None], (count,) + values.shape), a...  9.66 us
  transfers between devices with their start and end apart: 18, of which 10 were waited for; matrix products, arithmetic and copies ran while one was open for 1% of the time, Pallas kernels for 0%

profile of v2, /device:TPU:16, one launch (start us, length us, event | category | flops | bytes accessed | tf_op | source)
XLA Modules:
  0.0 281.5 jit_solution(11875703097298513573)
XLA Ops:
  2.4 9.0 %all-to-all-start = ((f32[16,1,768]{2,1,0:T(1,128)}), f32[16,1,768]{2,1,0:T(1,128)S(1)}, u32[]{:S(2)}, u32[]{:S(2)}) async-start(f32[16,1,768]{2,1,0:T(1,128)} %broadcast_in_dim.8), calls=%async_computation | async-start | bytes 98304 | tf_op jit(solution)/shard_map/norm/all_to_all | solution.py:48
  12.1 5.2 %all-to-all-done = f32[16,1,768]{2,1,0:T(1,128)S(1)} async-done(((f32[16,1,768]{2,1,0:T(1,128)}), f32[16,1,768]{2,1,0:T(1,128)S(1)}, u32[]{:S(2)}, u32[]{:S(2)}) %all-to-all-start) | async-done | bytes 49184 | tf_op jit(solution)/shard_map/norm/all_to_all | solution.py:48
  19.2 5.9 %all-to-all-start.1 = ((bf16[4,128,384]{2,1,0:T(8,128)(2,1)}), bf16[4,128,384]{2,1,0:T(8,128)(2,1)S(1)}, u32[]{:S(2)}, u32[]{:S(2)}) async-start(bf16[4,128,384]{2,1,0:T(8,128)(2,1)} %broadcast_in_dim.9), calls=%async_computation.1 | async-start | bytes 786432 | tf_op jit(solution)/shard_map/tokens/all_to_all | solution.py:48
  25.1 4.4 %all-to-all-done.1 = bf16[4,128,384]{2,1,0:T(8,128)(2,1)S(1)} async-done(((bf16[4,128,384]{2,1,0:T(8,128)(2,1)}), bf16[4,128,384]{2,1,0:T(8,128)(2,1)S(1)}, u32[]{:S(2)}, u32[]{:S(2)}) %all-to-all-start.1) | async-done | bytes 393248 | tf_op jit(solution)/shard_map/tokens/all_to_all | solution.py:48
  29.6 15.2 %collective-permute-start = (bf16[4,128,384]{2,1,0:T(8,128)(2,1)S(1)}, bf16[4,128,384]{2,1,0:T(8,128)(2,1)S(1)}, u32[]{:S(2)}, u32[]{:S(2)}) collective-permute-start(bf16[4,128,384]{2,1,0:T(8,128)(2,1)S(1)} %all-to-all-done.1), channel_id=1, source_target_pairs={{0,0},{1,32},{2,64},{3,96},{4,128},{5,160},{6,192},{7,224},{8,256}... | collective-permute-start | bytes 1179656 | tf_op jit(solution)/shard_map/tokens/ppermute | solution.py:24
  44.9 1.9 collective-permute-start.11
  46.9 11.6 %collective-permute-start.10 = (bf16[192,384]{1,0:T(8,128)(2,1)S(1)}, bf16[192,384]{1,0:T(8,128)(2,1)S(1)}, u32[]{:S(2)}, u32[]{:S(2)}) collective-permute-start(bf16[192,384]{1,0:T(8,128)(2,1)S(1)} %bitcast.13), channel_id=1, source_target_pairs={{0,0},{1,32},{2,64},{3,96},{4,4},{5,36},{6,68},{7,100},{8,8},{9,40... | collective-permute-start | bytes 442376 | tf_op jit(solution)/shard_map/weights/ppermute | solution.py:24
  58.5 4.6 %collective-permute-done.11 = bf16[192,384]{1,0:T(8,128)(2,1)S(1)} collective-permute-done((bf16[192,384]{1,0:T(8,128)(2,1)S(1)}, bf16[192,384]{1,0:T(8,128)(2,1)S(1)}, u32[]{:S(2)}, u32[]{:S(2)}) %collective-permute-start.11) | collective-permute-done | bytes 147488 | tf_op jit(solution)/shard_map/weights/ppermute | solution.py:24
  63.1 3.5 %collective-permute-done.10 = bf16[192,384]{1,0:T(8,128)(2,1)S(1)} collective-permute-done((bf16[192,384]{1,0:T(8,128)(2,1)S(1)}, bf16[192,384]{1,0:T(8,128)(2,1)S(1)}, u32[]{:S(2)}, u32[]{:S(2)}) %collective-permute-start.10) | collective-permute-done | bytes 147488 | tf_op jit(solution)/shard_map/weights/ppermute | solution.py:24
  67.8 55.9 %all-to-all-start.2 = ((bf16[4,384,384]{2,1,0:T(8,128)(2,1)}), bf16[4,384,384]{2,1,0:T(8,128)(2,1)S(1)}, u32[]{:S(2)}, u32[]{:S(2)}) async-start(bf16[4,384,384]{2,1,0:T(8,128)(2,1)} %broadcast_in_dim.10), calls=%async_computation.2 | async-start | bytes 2359296 | tf_op jit(solution)/shard_map/weights/all_to_all | solution.py:48
  123.7 4.2 %collective-permute-start.4 = (bf16[4,128,384]{2,1,0:T(8,128)(2,1)S(1)}, bf16[4,128,384]{2,1,0:T(8,128)(2,1)S(1)}, u32[]{:S(2)}, u32[]{:S(2)}) collective-permute-start(bf16[4,128,384]{2,1,0:T(8,128)(2,1)S(1)} %collective-permute-done.t0), channel_id=1, source_target_pairs={{0,4},{4,8},{8,12},{12,32},{32,36},{36,40},{40,44},{44,64},{64,68}... | collective-permute-start | bytes 1179656 | tf_op jit(solution)/shard_map/tokens/ppermute | solution.py:24
  127.9 31.0 %collective-permute-start.1 = (bf16[4,128,384]{2,1,0:T(8,128)(2,1)S(1)}, bf16[4,128,384]{2,1,0:T(8,128)(2,1)S(1)}, u32[]{:S(2)}, u32[]{:S(2)}) collective-permute-start(bf16[4,128,384]{2,1,0:T(8,128)(2,1)S(1)} %collective-permute-done.t0), channel_id=1, source_target_pairs={{0,108},{4,0},{8,4},{12,8},{32,12},{36,32},{40,36},{44,40},{64,44}... | collective-permute-start | bytes 1179656 | tf_op jit(solution)/shard_map/tokens/ppermute | solution.py:24
  159.0 3.4 %collective-permute-start.3 = (bf16[4,64,384]{2,1,0:T(8,128)(2,1)S(1)}, bf16[4,64,384]{2,1,0:T(8,128)(2,1)}, u32[]{:S(2)}, u32[]{:S(2)}) collective-permute-start(bf16[4,64,384]{2,1,0:T(8,128)(2,1)S(1)} %get-tuple-element.11), channel_id=1, source_target_pairs={{0,104},{4,108},{8,0},{12,4},{32,8},{36,12},{40,32},{44,36},{64,40... | collective-permute-start | bytes 589832 | tf_op jit(solution)/shard_map/tokens/ppermute | solution.py:24
  162.4 3.4 %collective-permute-start.2 = (bf16[4,64,384]{2,1,0:T(8,128)(2,1)S(1)}, bf16[4,64,384]{2,1,0:T(8,128)(2,1)}, u32[]{:S(2)}, u32[]{:S(2)}) collective-permute-start(bf16[4,64,384]{2,1,0:T(8,128)(2,1)S(1)} %get-tuple-element.12), channel_id=1, source_target_pairs={{0,8},{4,12},{8,32},{12,36},{32,40},{36,44},{40,64},{44,68},{64,72... | collective-permute-start | bytes 589832 | tf_op jit(solution)/shard_map/tokens/ppermute | solution.py:24
  165.7 1.9 collective-permute-start.5
  167.7 2.4 collective-permute-start.9
  170.1 2.4 collective-permute-done.1.t1
  172.5 1.9 collective-permute-start.6
  174.6 2.2 collective-permute-start.8
  176.8 2.1 collective-permute-start.7
  179.0 1.5 collective-permute-done.7.p2a
  181.6 5.5 %project.2 = f32[4,256,384]{2,1,0:T(8,128)} custom-call(s32[1]{0:T(128)} %bitcast.where, bf16[4,128,384]{2,1,0:T(8,128)(2,1)} %copy-done.2, bf16[4,128,384]{2,1,0:T(8,128)(2,1)} %copy-done.4, bf16[4,64,384]{2,1,0:T(8,128)(2,1)} %collective-permute-done.2.t2a, bf16[4,64,384]{2,1,0:T(8,128)(2,1)} %collective-permute-done.3.t2b, ...), custom_call_target="tpu_custom_call" | custom-call | tf_op jit(solution)/shard_map/project/pallas_call | solution.py:99
  187.1 3.7 %all-to-all-start.3 = ((f32[4,256,384]{2,1,0:T(8,128)}), f32[4,256,384]{2,1,0:T(8,128)S(1)}, u32[]{:S(2)}, u32[]{:S(2)}) async-start(f32[4,256,384]{2,1,0:T(8,128)} %project.2), calls=%async_computation.3 | async-start | bytes 3145728 | tf_op jit(solution)/shard_map/project/all_to_all | solution.py:158
  191.4 20.7 %all-to-all-done.3.part = f32[4,256,384]{2,1,0:T(8,128)S(1)} async-done(((f32[4,256,384]{2,1,0:T(8,128)}), f32[4,256,384]{2,1,0:T(8,128)S(1)}, u32[]{:S(2)}, u32[]{:S(2)}) %all-to-all-start.3) | async-done | bytes 1572896 | tf_op jit(solution)/shard_map/project/all_to_all | solution.py:158
  212.1 1.2 copy-done
  213.3 2.3 project.3
  216.7 30.9 %all_to_all.25.kv = bf16[16,256,256]{2,1,0:T(8,128)(2,1)} all-to-all(bf16[16,256,256]{2,1,0:T(8,128)(2,1)S(1)} %broadcast_in_dim.11), channel_id=1, replica_groups=mesh['x'=4,'zh'=4,'core'=2,'zl'=4,'y'=4] {'x','y'}, dimensions={0} | all-to-all | bytes 4194304 | tf_op jit(solution)/shard_map/keys/all_to_all | solution.py:48
  247.6 4.3 %attend.1 = bf16[256,128]{1,0:T(8,128)(2,1)} custom-call(bf16[256,128]{1,0:T(8,128)(2,1)} %get-tuple-element.7.q, bf16[16,256,256]{2,1,0:T(8,128)(2,1)} %all_to_all.25.kv), custom_call_target="tpu_custom_call" | custom-call | tf_op jit(solution)/shard_map/attend/pallas_call | solution.py:99
  252.6 11.9 %collective-permute-start.12 = (bf16[128,128]{1,0:T(8,128)(2,1)S(1)}, bf16[128,128]{1,0:T(8,128)(2,1)S(1)}, u32[]{:S(2)}, u32[]{:S(2)}) collective-permute-start(bf16[128,128]{1,0:T(8,128)(2,1)S(1)} %get-tuple-element.15), channel_id=1, source_target_pairs={{0,0},{1,32},{2,64},{3,96},{4,4},{5,36},{6,68},{7,100},{8,8},{9,40... | collective-permute-start | bytes 98312 | tf_op jit(solution)/shard_map/home/ppermute | solution.py:24
  264.5 2.0 collective-permute-start.13
  266.5 3.0 %collective-permute-done.12 = bf16[128,128]{1,0:T(8,128)(2,1)S(1)} collective-permute-done((bf16[128,128]{1,0:T(8,128)(2,1)S(1)}, bf16[128,128]{1,0:T(8,128)(2,1)S(1)}, u32[]{:S(2)}, u32[]{:S(2)}) %collective-permute-start.12) | collective-permute-done | bytes 32800 | tf_op jit(solution)/shard_map/home/ppermute | solution.py:24
  269.6 11.3 %collective-permute-done.13 = bf16[128,128]{1,0:T(8,128)(2,1)S(1)} collective-permute-done((bf16[128,128]{1,0:T(8,128)(2,1)S(1)}, bf16[128,128]{1,0:T(8,128)(2,1)S(1)}, u32[]{:S(2)}, u32[]{:S(2)}) %collective-permute-start.13) | collective-permute-done | bytes 32800 | tf_op jit(solution)/shard_map/home/ppermute | solution.py:24
  (50 shorter events, 10.6 us)
Async XLA Ops:
  0.0 44.8 %copy-start.8 = (bf16[192,3,256]{2,0,1:T(8,128)(2,1)S(1)}, bf16[192,3,256]{2,0,1:T(8,128)(2,1)}, u32[]{:S(2)}) copy-start(bf16[192,3,256]{2,0,1:T(8,128)(2,1)} %param.7) | copy-start | bytes 884740
  2.4 14.9 %all-to-all-start = ((f32[16,1,768]{2,1,0:T(1,128)}), f32[16,1,768]{2,1,0:T(1,128)S(1)}, u32[]{:S(2)}, u32[]{:S(2)}) async-start(f32[16,1,768]{2,1,0:T(1,128)} %broadcast_in_dim.8), calls=%async_computation | async-start | bytes 98304 | tf_op jit(solution)/shard_map/norm/all_to_all | solution.py:48
  17.3 50.5 %copy-start.9 = (f32[16,1,768]{2,1,0:T(1,128)}, f32[16,1,768]{2,1,0:T(1,128)S(1)}, u32[]{:S(2)}) copy-start(f32[16,1,768]{2,1,0:T(1,128)S(1)} %all-to-all-done) | copy-start | bytes 147460
  19.2 10.4 %all-to-all-start.1 = ((bf16[4,128,384]{2,1,0:T(8,128)(2,1)}), bf16[4,128,384]{2,1,0:T(8,128)(2,1)S(1)}, u32[]{:S(2)}, u32[]{:S(2)}) async-start(bf16[4,128,384]{2,1,0:T(8,128)(2,1)} %broadcast_in_dim.9), calls=%async_computation.1 | async-start | bytes 786432 | tf_op jit(solution)/shard_map/tokens/all_to_all | solution.py:48
  29.6 94.2 %collective-permute-start = (bf16[4,128,384]{2,1,0:T(8,128)(2,1)S(1)}, bf16[4,128,384]{2,1,0:T(8,128)(2,1)S(1)}, u32[]{:S(2)}, u32[]{:S(2)}) collective-permute-start(bf16[4,128,384]{2,1,0:T(8,128)(2,1)S(1)} %all-to-all-done.1), channel_id=1, source_target_pairs={{0,0},{1,32},{2,64},{3,96},{4,128},{5,160},{6,192},{7,224},{8,256}... | collective-permute-start | bytes 1179656 | tf_op jit(solution)/shard_map/tokens/ppermute | solution.py:24
  44.9 18.2 %collective-permute-start.11 = (bf16[192,384]{1,0:T(8,128)(2,1)S(1)}, bf16[192,384]{1,0:T(8,128)(2,1)S(1)}, u32[]{:S(2)}, u32[]{:S(2)}) collective-permute-start(bf16[192,384]{1,0:T(8,128)(2,1)S(1)} %bitcast.12), channel_id=1, source_target_pairs={{0,16},{1,48},{2,80},{3,112},{4,20},{5,52},{6,84},{7,116},{8,24},{... | collective-permute-start | bytes 442376 | tf_op jit(solution)/shard_map/weights/ppermute | solution.py:24
  46.9 19.8 %collective-permute-start.10 = (bf16[192,384]{1,0:T(8,128)(2,1)S(1)}, bf16[192,384]{1,0:T(8,128)(2,1)S(1)}, u32[]{:S(2)}, u32[]{:S(2)}) collective-permute-start(bf16[192,384]{1,0:T(8,128)(2,1)S(1)} %bitcast.13), channel_id=1, source_target_pairs={{0,0},{1,32},{2,64},{3,96},{4,4},{5,36},{6,68},{7,100},{8,8},{9,40... | collective-permute-start | bytes 442376 | tf_op jit(solution)/shard_map/weights/ppermute | solution.py:24
  67.8 111.1 %all-to-all-start.2 = ((bf16[4,384,384]{2,1,0:T(8,128)(2,1)}), bf16[4,384,384]{2,1,0:T(8,128)(2,1)S(1)}, u32[]{:S(2)}, u32[]{:S(2)}) async-start(bf16[4,384,384]{2,1,0:T(8,128)(2,1)} %broadcast_in_dim.10), calls=%async_computation.2 | async-start | bytes 2359296 | tf_op jit(solution)/shard_map/weights/all_to_all | solution.py:48
  123.7 56.8 %copy-start.2 = (bf16[4,128,384]{2,1,0:T(8,128)(2,1)}, bf16[4,128,384]{2,1,0:T(8,128)(2,1)S(1)}, u32[]{:S(2)}) copy-start(bf16[4,128,384]{2,1,0:T(8,128)(2,1)S(1)} %collective-permute-done.t0) | copy-start | bytes 1179652
  123.7 43.9 %collective-permute-start.4 = (bf16[4,128,384]{2,1,0:T(8,128)(2,1)S(1)}, bf16[4,128,384]{2,1,0:T(8,128)(2,1)S(1)}, u32[]{:S(2)}, u32[]{:S(2)}) collective-permute-start(bf16[4,128,384]{2,1,0:T(8,128)(2,1)S(1)} %collective-permute-done.t0), channel_id=1, source_target_pairs={{0,4},{4,8},{8,12},{12,32},{32,36},{36,40},{40,44},{44,64},{64,68}... | collective-permute-start | bytes 1179656 | tf_op jit(solution)/shard_map/tokens/ppermute | solution.py:24
  127.9 44.6 %collective-permute-start.1 = (bf16[4,128,384]{2,1,0:T(8,128)(2,1)S(1)}, bf16[4,128,384]{2,1,0:T(8,128)(2,1)S(1)}, u32[]{:S(2)}, u32[]{:S(2)}) collective-permute-start(bf16[4,128,384]{2,1,0:T(8,128)(2,1)S(1)} %collective-permute-done.t0), channel_id=1, source_target_pairs={{0,108},{4,0},{8,4},{12,8},{32,12},{36,32},{40,36},{44,40},{64,44}... | collective-permute-start | bytes 1179656 | tf_op jit(solution)/shard_map/tokens/ppermute | solution.py:24
  159.0 15.6 %collective-permute-start.3 = (bf16[4,64,384]{2,1,0:T(8,128)(2,1)S(1)}, bf16[4,64,384]{2,1,0:T(8,128)(2,1)}, u32[]{:S(2)}, u32[]{:S(2)}) collective-permute-start(bf16[4,64,384]{2,1,0:T(8,128)(2,1)S(1)} %get-tuple-element.11), channel_id=1, source_target_pairs={{0,104},{4,108},{8,0},{12,4},{32,8},{36,12},{40,32},{44,36},{64,40... | collective-permute-start | bytes 589832 | tf_op jit(solution)/shard_map/tokens/ppermute | solution.py:24
  162.4 14.5 %collective-permute-start.2 = (bf16[4,64,384]{2,1,0:T(8,128)(2,1)S(1)}, bf16[4,64,384]{2,1,0:T(8,128)(2,1)}, u32[]{:S(2)}, u32[]{:S(2)}) collective-permute-start(bf16[4,64,384]{2,1,0:T(8,128)(2,1)S(1)} %get-tuple-element.12), channel_id=1, source_target_pairs={{0,8},{4,12},{8,32},{12,36},{32,40},{36,44},{40,64},{44,68},{64,72... | collective-permute-start | bytes 589832 | tf_op jit(solution)/shard_map/tokens/ppermute | solution.py:24
  165.7 14.8 %collective-permute-start.5 = (bf16[4,128,384]{2,1,0:T(8,128)(2,1)S(1)}, bf16[4,128,384]{2,1,0:T(8,128)(2,1)S(1)}, u32[]{:S(2)}, u32[]{:S(2)}) collective-permute-start(bf16[4,128,384]{2,1,0:T(8,128)(2,1)S(1)} %collective-permute-done.t0), channel_id=1, source_target_pairs={{0,16},{16,0},{1,17},{17,1},{2,18},{18,2},{3,19},{19,3},{4,20},{20... | collective-permute-start | bytes 1179656 | tf_op jit(solution)/shard_map/tokens/ppermute | solution.py:24
  167.7 12.9 %copy-start.3 = (bf16[4,128,384]{2,1,0:T(8,128)(2,1)}, bf16[4,128,384]{2,1,0:T(8,128)(2,1)S(1)}, u32[]{:S(2)}) copy-start(bf16[4,128,384]{2,1,0:T(8,128)(2,1)S(1)} %collective-permute-done.4.t3) | copy-start | bytes 1179652
  167.7 12.8 %collective-permute-start.9 = (bf16[4,128,384]{2,1,0:T(8,128)(2,1)S(1)}, bf16[4,128,384]{2,1,0:T(8,128)(2,1)S(1)}, u32[]{:S(2)}, u32[]{:S(2)}) collective-permute-start(bf16[4,128,384]{2,1,0:T(8,128)(2,1)S(1)} %collective-permute-done.4.t3), channel_id=1, source_target_pairs={{0,16},{16,0},{1,17},{17,1},{2,18},{18,2},{3,19},{19,3},{4,20},{20... | collective-permute-start | bytes 1179656 | tf_op jit(solution)/shard_map/tokens/ppermute | solution.py:24
  172.5 8.1 %copy-start.4 = (bf16[4,128,384]{2,1,0:T(8,128)(2,1)}, bf16[4,128,384]{2,1,0:T(8,128)(2,1)S(1)}, u32[]{:S(2)}) copy-start(bf16[4,128,384]{2,1,0:T(8,128)(2,1)S(1)} %collective-permute-done.1.t1) | copy-start | bytes 1179652
  172.5 8.1 %collective-permute-start.6 = (bf16[4,128,384]{2,1,0:T(8,128)(2,1)S(1)}, bf16[4,128,384]{2,1,0:T(8,128)(2,1)S(1)}, u32[]{:S(2)}, u32[]{:S(2)}) collective-permute-start(bf16[4,128,384]{2,1,0:T(8,128)(2,1)S(1)} %collective-permute-done.1.t1), channel_id=1, source_target_pairs={{0,16},{16,0},{1,17},{17,1},{2,18},{18,2},{3,19},{19,3},{4,20},{20... | collective-permute-start | bytes 1179656 | tf_op jit(solution)/shard_map/tokens/ppermute | solution.py:24
  174.6 4.4 %collective-permute-start.8 = (bf16[4,64,384]{2,1,0:T(8,128)(2,1)}, bf16[4,64,384]{2,1,0:T(8,128)(2,1)}, u32[]{:S(2)}, u32[]{:S(2)}) collective-permute-start(bf16[4,64,384]{2,1,0:T(8,128)(2,1)} %collective-permute-done.3.t2b), channel_id=1, source_target_pairs={{0,16},{16,0},{1,17},{17,1},{2,18},{18,2},{3,19},{19,3},{4,20},{20... | collective-permute-start | bytes 589832 | tf_op jit(solution)/shard_map/tokens/ppermute | solution.py:24
  176.8 3.7 %collective-permute-start.7 = (bf16[4,64,384]{2,1,0:T(8,128)(2,1)}, bf16[4,64,384]{2,1,0:T(8,128)(2,1)}, u32[]{:S(2)}, u32[]{:S(2)}) collective-permute-start(bf16[4,64,384]{2,1,0:T(8,128)(2,1)} %collective-permute-done.2.t2a), channel_id=1, source_target_pairs={{0,16},{16,0},{1,17},{17,1},{2,18},{18,2},{3,19},{19,3},{4,20},{20... | collective-permute-start | bytes 589832 | tf_op jit(solution)/shard_map/tokens/ppermute | solution.py:24
  179.0 1.6 copy-start.1
  180.5 0.8 copy-start.5
  180.5 0.9 copy-start.6
  180.6 1.0 copy-start.7
  187.1 3.7 %slice-start = ((f32[16,1,768]{2,1,0:T(1,128)}), f32[16,1,512]{2,1,0:T(1,128)S(1)}, s32[]{:S(2)}) async-start(f32[16,1,768]{2,1,0:T(1,128)} %copy-done.9), calls=%async_computation.5 | async-start | bytes 65536 | tf_op jit(solution)/shard_map/norm/slice | solution.py:130
  187.1 25.0 %all-to-all-start.3 = ((f32[4,256,384]{2,1,0:T(8,128)}), f32[4,256,384]{2,1,0:T(8,128)S(1)}, u32[]{:S(2)}, u32[]{:S(2)}) async-start(f32[4,256,384]{2,1,0:T(8,128)} %project.2), calls=%async_computation.3 | async-start | bytes 3145728 | tf_op jit(solution)/shard_map/project/all_to_all | solution.py:158
  212.1 1.2 copy-start
  252.6 16.9 %collective-permute-start.12 = (bf16[128,128]{1,0:T(8,128)(2,1)S(1)}, bf16[128,128]{1,0:T(8,128)(2,1)S(1)}, u32[]{:S(2)}, u32[]{:S(2)}) collective-permute-start(bf16[128,128]{1,0:T(8,128)(2,1)S(1)} %get-tuple-element.15), channel_id=1, source_target_pairs={{0,0},{1,32},{2,64},{3,96},{4,4},{5,36},{6,68},{7,100},{8,8},{9,40... | collective-permute-start | bytes 98312 | tf_op jit(solution)/shard_map/home/ppermute | solution.py:24
  264.5 16.4 %collective-permute-start.13 = (bf16[128,128]{1,0:T(8,128)(2,1)S(1)}, bf16[128,128]{1,0:T(8,128)(2,1)S(1)}, u32[]{:S(2)}, u32[]{:S(2)}) collective-permute-start(bf16[128,128]{1,0:T(8,128)(2,1)S(1)} %get-tuple-element.16), channel_id=1, source_target_pairs={{0,16},{1,48},{2,80},{3,112},{4,20},{5,52},{6,84},{7,116},{8,24},{... | collective-permute-start | bytes 98312 | tf_op jit(solution)/shard_map/home/ppermute | solution.py:24

commit v3 on v2

v3 whole, which is shorter than its diff:
```python
import numpy as np
import jax
import jax.numpy as jnp
from jax import lax
from jax.experimental import pallas as pl
from jax.experimental.pallas import tpu as pltpu
from jax.sharding import Mesh, PartitionSpec as P

DH = 128
EPSILON = 1e-06
NX = NZH = NZL = NY = 4
CORES = 2
AXES = ("x", "zh", "core", "zl", "y")
SIZES = (NX, NZH, CORES, NZL, NY)
VMEM_LIMIT = 56 * 1024 * 1024


def shift(values, axes, move):
    sizes = [SIZES[AXES.index(axis)] for axis in axes]
    pairs = [
        (int(np.ravel_multi_index(src, sizes)), int(np.ravel_multi_index(move(src), sizes)))
        for src in np.ndindex(*sizes)
    ]
    return lax.ppermute(values, axes, pairs)


def to_plane(values):
    return shift(values, ("zh", "zl", "y"), lambda i: ((i[2] + i[1]) % NZH, i[1], i[0]))


def to_home(values, cross):
    return shift(
        values,
        ("zh", "core", "zl", "y"),
        lambda i: ((i[0] + i[2] + i[3]) % NZH, i[1] ^ cross, i[2], (i[0] - i[2]) % NY),
    )


def along_z(values, step):
    return shift(values, ("zh", "zl"), lambda i: divmod((i[0] * NZL + i[1] + step) % 16, NZL))


def swap_cores(values):
    return shift(values, ("core",), lambda i: (1 - i[0],))


def spread(values, axes, count):
    return lax.all_to_all(jnp.broadcast_to(values[None], (count,) + values.shape), axes, 0, 0)


def partial_kernel(where, t0, t1, t2a, t2b, t3, stats, gain, w_mine, w_theirs, out, w, acc):
    zl, core, turn = where[0], where[1], where[2]
    half = w_mine.shape[1]
    for x in range(NX):
        w[x, pl.ds(pl.multiple_of(core * half, half), half)] = w_mine[x]
        w[x, pl.ds(pl.multiple_of((1 - core) * half, half), half)] = w_theirs[x]
    pieces = ((t0,), (t1,), (t2a, t2b), (t3,))
    for slot in range(NZL):
        part = lax.rem(zl + slot, NZL)
        row_gain = gain[part]
        normed = []
        for quarter in range(NZH):
            x = [ref[quarter].astype(jnp.float32) for ref in pieces[slot]]
            x = x[0] if len(x) == 1 else jnp.concatenate(x, axis=0)
            center = stats[quarter, :, 0:1]
            scale = stats[quarter, :, 1:2]
            normed.append(((x - center) * scale * row_gain).astype(jnp.bfloat16))
        term = jnp.dot(
            jnp.concatenate(normed, axis=0), w[part], preferred_element_type=jnp.float32
        )
        if slot == 0:
            acc[...] = term
        elif slot < NZL - 1:
            acc[...] += term
        else:
            for quarter in range(NZH):
                rows = slice(quarter * 128, quarter * 128 + 128)
                out[lax.rem(turn + quarter, NZH)] = acc[rows] + term[rows]


def heads_kernel(where, part, head_gain, out):
    core = where[1]
    acc = part[0] + part[1] + part[2] + part[3]

    def head_norm(values, row):
        mid = jnp.mean(values, axis=1, keepdims=True)
        var = jnp.mean(values * values, axis=1, keepdims=True) - mid * mid
        return ((values - mid) * lax.rsqrt(var + EPSILON) * row).astype(jnp.bfloat16)

    for head in range(2):
        slot = lax.rem(core + head, 2)
        cols = [slice(s * 256 + head * DH, s * 256 + head * DH + DH) for s in range(3)]
        out[slot, 0] = head_norm(acc[:, cols[0]], head_gain[0, :, head * DH : head * DH + DH])
        out[slot, 1] = head_norm(acc[:, cols[1]], head_gain[1, :, head * DH : head * DH + DH])
        out[slot, 2] = acc[:, cols[2]].astype(jnp.bfloat16)


def attend_kernel(q, kv, out):
    keys = kv[:, :, 0].reshape(-1, DH)
    values = kv[:, :, 1].reshape(-1, DH)
    queries = q[...].reshape(-1, DH)
    scores = lax.dot_general(
        queries, keys, (((1,), (1,)), ((), ())), preferred_element_type=jnp.float32
    ) * (DH ** -0.5)
    top = jnp.max(scores, axis=1, keepdims=True)
    weights = jnp.exp(scores - top)
    total = jnp.sum(weights, axis=1, keepdims=True)
    mixed = jnp.dot(weights.astype(jnp.bfloat16), values, preferred_element_type=jnp.float32)
    out[...] = (mixed / total).astype(jnp.bfloat16)


def kernel_call(kernel, out_shape, args, scalars=0, scratch=()):
    vmem = pl.BlockSpec(memory_space=pltpu.VMEM)
    smem = pl.BlockSpec(memory_space=pltpu.SMEM)
    return pl.pallas_call(
        kernel,
        out_shape=out_shape,
        in_specs=[smem] * scalars + [vmem] * (len(args) - scalars),
        out_specs=jax.tree.map(lambda _: vmem, out_shape),
        scratch_shapes=scratch,
        compiler_params=pltpu.CompilerParams(vmem_limit_bytes=VMEM_LIMIT),
    )(*args)


def body(tokens, ln_gain, w_qkv, q_gain, k_gain):
    core = lax.axis_index("core")
    zl = lax.axis_index("zl")
    zh = lax.axis_index("zh")
    y_here = lax.axis_index("y")
    turn = (2 * NZH - zh - zl) % NZH
    where = jnp.stack([zl, core, turn]).astype(jnp.int32)

    with jax.named_scope("weights"):
        w_moved = to_plane(w_qkv)

    with jax.named_scope("tokens"):
        t0, w_moved = lax.optimization_barrier((spread(tokens, "zh", NZH), w_moved))
        t1 = along_z(t0, -1)
        t3 = along_z(t0, 1)
        t2a = along_z(t0[:, :64], 2)
        t2b = along_z(t0[:, 64:], -2)

    with jax.named_scope("norm"):
        x = tokens.astype(jnp.float32)
        shared = spread(
            jnp.concatenate(
                [
                    jnp.sum(x, axis=1),
                    jnp.sum(x * x, axis=1),
                    ln_gain.astype(jnp.float32),
                    q_gain,
                    k_gain,
                ]
            )[None],
            ("zl", "y"),
            NZL * NY,
        )[:, 0]
        features = tokens.shape[1] * NZL * NY
        sums = spread(jnp.sum(shared[:, :256], axis=0)[None], "zh", NZH)[:, 0]
        center = sums[:, :128] / features
        var = sums[:, 128:] / features - center * center
        stats = jnp.stack([center, lax.rsqrt(var + EPSILON)], axis=2)
        gain = lax.dynamic_index_in_dim(
            shared[:, 256:640].reshape(NZL, NY, 1, 384), y_here, 1, keepdims=False
        )
        head_gain = lax.dynamic_index_in_dim(
            shared[:, 640:], zl * NY + (zh + NY - zl) % NY, 0, keepdims=False
        ).reshape(2, 1, 256)

    with jax.named_scope("weights"):
        w_mine = spread(w_moved.reshape(192, 768), "x", NX)
        w_theirs = swap_cores(w_mine)

    with jax.named_scope("project"):
        part = kernel_call(
            partial_kernel,
            jax.ShapeDtypeStruct((NZH, 128, 768), jnp.float32),
            (where, t0, t1, t2a, t2b, t3, stats, gain, w_mine, w_theirs),
            scalars=1,
            scratch=[
                pltpu.VMEM((NX, 384, 768), jnp.bfloat16),
                pltpu.VMEM((512, 768), jnp.float32),
            ],
        )
        part = lax.all_to_all(part, "y", 0, 0)
        heads = kernel_call(
            heads_kernel,
            jax.ShapeDtypeStruct((2, 3, 128, DH), jnp.bfloat16),
            (where, part, head_gain),
            scalars=1,
        )
        both = jnp.stack([heads[0], swap_cores(heads[1])])

    with jax.named_scope("keys"):
        kv_all = spread(both[:, 1:], ("x", "y"), NX * NY)

    with jax.named_scope("attend"):
        out = kernel_call(
            attend_kernel, jax.ShapeDtypeStruct((256, DH), jnp.bfloat16), (both[:, 0], kv_all)
        )

    with jax.named_scope("home"):
        same = to_home(out[:128], 0)
        cross = to_home(out[128:], 1)
        return jnp.where(
            core == 0,
            jnp.concatenate([same, cross], axis=1),
            jnp.concatenate([cross, same], axis=1),
        )


def solution(mesh):
    fine = Mesh(mesh.devices.reshape(SIZES), AXES)
    rows = ("x", "zh", "core")
    cols = ("zl", "y")
    in_specs = (P(rows, cols), P(cols), P(rows, None, cols), P(cols), P(cols))
    return jax.shard_map(body, mesh=fine, in_specs=in_specs, out_specs=P(rows, cols), check_vma=False)
```

time: 283 us -> 241 us (0.85)
  the two profiles are of different devices: /device:TPU:16 before, /device:TPU:64 now
where the time goes in v3:
time: 241 us; the launch traced here: 240 us
  waiting for transfers between devices  116 us (48%)
  starting transfers between devices  93.4 us (39%)
  local copies, waits for them, and re-layouts  16.4 us (7%)
  Pallas kernels  12.2 us (5%)
    all_to_all x5, waiting for transfers between devices, spread(): lax.all_to_all(jnp.broadcast_to(values[None], (count,) + values.shape), a...  63.2 us
    all_to_all x5, starting transfers between devices, spread(): lax.all_to_all(jnp.broadcast_to(values[None], (count,) + values.shape), a...  49 us
    ppermute x9, starting transfers between devices, shift(): return lax.ppermute(values, axes, pairs)  40.8 us
    ppermute x9, waiting for transfers between devices, shift(): return lax.ppermute(values, axes, pairs)  38 us
    all_to_all x1, waiting for transfers between devices, body(): part = lax.all_to_all(part, 'y', 0, 0)  14.3 us
    pallas_call x3, Pallas kernels, kernel_call(): pl.pallas_call(kernel, out_shape=out_shape, in_specs=[smem] * scalars + [...  12.2 us
    unnamed x30, local copies, waits for them, and re-layouts  6.03 us
    broadcast_in_dim x6, local copies, waits for them, and re-layouts, spread(): jnp.broadcast_to(values[None], (count,) + values.shape)  5.91 us
  transfers between devices with their start and end apart: 15, of which 10 were waited for; matrix products, arithmetic and copies ran while one was open for 3% of the time, Pallas kernels for 0%

profile of v3, /device:TPU:64, one launch (start us, length us, event | category | flops | bytes accessed | tf_op | source)
XLA Modules:
  0.0 239.8 jit_solution(11584561116891904375)
XLA Ops:
  0.0 1.7 broadcast_in_dim.12
  1.7 13.3 %all-to-all-start = ((bf16[4,128,384]{2,1,0:T(8,128)(2,1)}), bf16[4,128,384]{2,1,0:T(8,128)(2,1)S(1)}, u32[]{:S(2)}, u32[]{:S(2)}) async-start(bf16[4,128,384]{2,1,0:T(8,128)(2,1)} %broadcast_in_dim.12), calls=%async_computation | async-start | bytes 786432 | tf_op jit(solution)/shard_map/tokens/all_to_all | solution.py:48
  15.0 12.6 %collective-permute-start = (bf16[192,3,256]{2,0,1:T(8,128)(2,1)}, bf16[192,3,256]{2,0,1:T(8,128)(2,1)S(1)}, u32[]{:S(2)}, u32[]{:S(2)}) collective-permute-start(bf16[192,3,256]{2,0,1:T(8,128)(2,1)} %param.7), channel_id=1, source_target_pairs={{0,0},{1,32},{2,64},{3,96},{4,36},{5,68},{6,100},{7,4},{8,72},{9,1... | collective-permute-start | bytes 884744 | tf_op jit(solution)/shard_map/weights/ppermute | solution.py:24
  27.6 17.2 %collective-permute-done = bf16[192,3,256]{2,0,1:T(8,128)(2,1)S(1)} collective-permute-done((bf16[192,3,256]{2,0,1:T(8,128)(2,1)}, bf16[192,3,256]{2,0,1:T(8,128)(2,1)S(1)}, u32[]{:S(2)}, u32[]{:S(2)}) %collective-permute-start) | collective-permute-done | bytes 294944 | tf_op jit(solution)/shard_map/weights/ppermute | solution.py:24
  45.9 4.4 %all-to-all-start.3 = ((bf16[4,192,768]{2,1,0:T(8,128)(2,1)}), bf16[4,192,768]{2,1,0:T(8,128)(2,1)S(1)}, u32[]{:S(2)}, u32[]{:S(2)}) async-start(bf16[4,192,768]{2,1,0:T(8,128)(2,1)} %broadcast_in_dim.16), calls=%async_computation.3 | async-start | bytes 2359296 | tf_op jit(solution)/shard_map/weights/all_to_all | solution.py:48
  50.5 16.0 %all-to-all-done.3.w_mine = bf16[4,192,768]{2,1,0:T(8,128)(2,1)S(1)} async-done(((bf16[4,192,768]{2,1,0:T(8,128)(2,1)}), bf16[4,192,768]{2,1,0:T(8,128)(2,1)S(1)}, u32[]{:S(2)}, u32[]{:S(2)}) %all-to-all-start.3) | async-done | bytes 1179680 | tf_op jit(solution)/shard_map/weights/all_to_all | solution.py:48
  66.6 1.9 collective-permute-start.5
  69.2 22.3 %all-to-all-start.1 = ((f32[16,1,1152]{2,1,0:T(1,128)}), f32[16,1,1152]{2,1,0:T(1,128)S(1)}, u32[]{:S(2)}, u32[]{:S(2)}) async-start(f32[16,1,1152]{2,1,0:T(1,128)} %broadcast_in_dim.13), calls=%async_computation.1 | async-start | bytes 147456 | tf_op jit(solution)/shard_map/norm/all_to_all | solution.py:48
  92.1 5.3 %all-to-all-done.1 = f32[16,1,1152]{2,1,0:T(1,128)S(1)} async-done(((f32[16,1,1152]{2,1,0:T(1,128)}), f32[16,1,1152]{2,1,0:T(1,128)S(1)}, u32[]{:S(2)}, u32[]{:S(2)}) %all-to-all-start.1) | async-done | bytes 73760 | tf_op jit(solution)/shard_map/norm/all_to_all | solution.py:48
  98.6 5.3 %all-to-all-start.2 = ((f32[4,1,256]{2,1,0:T(1,128)}), f32[4,1,256]{2,1,0:T(1,128)S(1)}, u32[]{:S(2)}, u32[]{:S(2)}) async-start(f32[4,1,256]{2,1,0:T(1,128)} %broadcast_in_dim.14), calls=%async_computation.2 | async-start | bytes 8192 | tf_op jit(solution)/shard_map/norm/all_to_all | solution.py:48
  104.5 11.9 %all-to-all-done.2 = f32[4,1,256]{2,1,0:T(1,128)S(1)} async-done(((f32[4,1,256]{2,1,0:T(1,128)}), f32[4,1,256]{2,1,0:T(1,128)S(1)}, u32[]{:S(2)}, u32[]{:S(2)}) %all-to-all-start.2) | async-done | bytes 4128 | tf_op jit(solution)/shard_map/norm/all_to_all | solution.py:48
  116.4 2.6 %collective-permute-start.4 = (bf16[4,128,384]{2,1,0:T(8,128)(2,1)S(1)}, bf16[4,128,384]{2,1,0:T(8,128)(2,1)S(1)}, u32[]{:S(2)}, u32[]{:S(2)}) collective-permute-start(bf16[4,128,384]{2,1,0:T(8,128)(2,1)S(1)} %all-to-all-done.t0), channel_id=1, source_target_pairs={{0,4},{4,8},{8,12},{12,32},{32,36},{36,40},{40,44},{44,64},{64,68}... | collective-permute-start | bytes 1179656 | tf_op jit(solution)/shard_map/tokens/ppermute | solution.py:24
  119.0 3.2 %collective-permute-start.1 = (bf16[4,128,384]{2,1,0:T(8,128)(2,1)S(1)}, bf16[4,128,384]{2,1,0:T(8,128)(2,1)S(1)}, u32[]{:S(2)}, u32[]{:S(2)}) collective-permute-start(bf16[4,128,384]{2,1,0:T(8,128)(2,1)S(1)} %all-to-all-done.t0), channel_id=1, source_target_pairs={{0,108},{4,0},{8,4},{12,8},{32,12},{36,32},{40,36},{44,40},{64,44}... | collective-permute-start | bytes 1179656 | tf_op jit(solution)/shard_map/tokens/ppermute | solution.py:24
  123.1 5.9 %collective-permute-start.3 = (bf16[4,64,384]{2,1,0:T(8,128)(2,1)}, bf16[4,64,384]{2,1,0:T(8,128)(2,1)}, u32[]{:S(2)}, u32[]{:S(2)}) collective-permute-start(bf16[4,64,384]{2,1,0:T(8,128)(2,1)} %get-tuple-element.11), channel_id=1, source_target_pairs={{0,104},{4,108},{8,0},{12,4},{32,8},{36,12},{40,32},{44,36},{64,40... | collective-permute-start | bytes 589832 | tf_op jit(solution)/shard_map/tokens/ppermute | solution.py:24
  129.0 2.0 collective-permute-start.2
  131.9 7.6 %collective-permute-done.3.t2b = bf16[4,64,384]{2,1,0:T(8,128)(2,1)} collective-permute-done((bf16[4,64,384]{2,1,0:T(8,128)(2,1)}, bf16[4,64,384]{2,1,0:T(8,128)(2,1)}, u32[]{:S(2)}, u32[]{:S(2)}) %collective-permute-start.3) | collective-permute-done | bytes 196640 | tf_op jit(solution)/shard_map/tokens/ppermute | solution.py:24
  141.4 5.5 %project.2 = f32[4,128,768]{2,1,0:T(8,128)} custom-call(s32[3]{0:T(128)} %pad_add_fusion.where, bf16[4,128,384]{2,1,0:T(8,128)(2,1)} %copy-done.3, bf16[4,128,384]{2,1,0:T(8,128)(2,1)} %copy-done.6, bf16[4,64,384]{2,1,0:T(8,128)(2,1)} %collective-permute-done.2.t2a, bf16[4,64,384]{2,1,0:T(8,128)(2,1)} %collective-permute-done.3.t2b, ...), custom_call_target="tpu_custom_call" | custom-call | tf_op jit(solution)/shard_map/project/pallas_call | solution.py:115
  147.0 3.6 %all-to-all-start.4 = ((f32[4,128,768]{2,1,0:T(8,128)}), f32[4,128,768]{2,1,0:T(8,128)S(1)}, u32[]{:S(2)}, u32[]{:S(2)}) async-start(f32[4,128,768]{2,1,0:T(8,128)} %project.2), calls=%async_computation.4 | async-start | bytes 3145728 | tf_op jit(solution)/shard_map/project/all_to_all | solution.py:185
  151.9 14.3 %all-to-all-done.4.part = f32[4,128,768]{2,1,0:T(8,128)S(1)} async-done(((f32[4,128,768]{2,1,0:T(8,128)}), f32[4,128,768]{2,1,0:T(8,128)S(1)}, u32[]{:S(2)}, u32[]{:S(2)}) %all-to-all-start.4) | async-done | bytes 1572896 | tf_op jit(solution)/shard_map/project/all_to_all | solution.py:185
  166.2 1.2 copy-done.1
  167.4 2.3 project.3
  170.7 1.9 collective-permute-start.6
  172.6 1.3 collective-permute-done.6
  173.9 1.8 broadcast_in_dim.17
  175.8 3.7 %all-to-all-start.5 = ((bf16[16,2,2,128,128]{4,3,2,1,0:T(8,128)(2,1)}), bf16[16,2,2,128,128]{4,3,2,1,0:T(8,128)(2,1)S(1)}, u32[]{:S(2)}, u32[]{:S(2)}) async-start(bf16[16,2,2,128,128]{4,3,2,1,0:T(8,128)(2,1)} %broadcast_in_dim.17), calls=%async_computation.5 | async-start | bytes 4194304 | tf_op jit(solution)/shard_map/keys/all_to_all | solution.py:48
  180.2 30.0 %all-to-all-done.5.kv = bf16[16,2,2,128,128]{4,3,2,1,0:T(8,128)(2,1)S(1)} async-done(((bf16[16,2,2,128,128]{4,3,2,1,0:T(8,128)(2,1)}), bf16[16,2,2,128,128]{4,3,2,1,0:T(8,128)(2,1)S(1)}, u32[]{:S(2)}, u32[]{:S(2)}) %all-to-all-start.5) | async-done | bytes 2097184 | tf_op jit(solution)/shard_map/keys/all_to_all | solution.py:48
  210.1 1.3 copy-done
  211.5 4.3 %attend.1 = bf16[256,128]{1,0:T(8,128)(2,1)} custom-call(bf16[2,128,128]{2,1,0:T(8,128)(2,1)} %maximum_bitcast_fusion.q, bf16[16,2,2,128,128]{4,3,2,1,0:T(8,128)(2,1)} %copy-done), custom_call_target="tpu_custom_call" | custom-call | tf_op jit(solution)/shard_map/attend/pallas_call | solution.py:115
  216.6 8.6 %collective-permute-start.7 = (bf16[128,128]{1,0:T(8,128)(2,1)S(1)}, bf16[128,128]{1,0:T(8,128)(2,1)S(1)}, u32[]{:S(2)}, u32[]{:S(2)}) collective-permute-start(bf16[128,128]{1,0:T(8,128)(2,1)S(1)} %get-tuple-element.15), channel_id=1, source_target_pairs={{0,0},{1,32},{2,64},{3,96},{4,39},{5,71},{6,103},{7,7},{8,74},{9,1... | collective-permute-start | bytes 98312 | tf_op jit(solution)/shard_map/home/ppermute | solution.py:24
  225.2 1.9 collective-permute-start.8
  227.1 4.0 %collective-permute-done.7 = bf16[128,128]{1,0:T(8,128)(2,1)S(1)} collective-permute-done((bf16[128,128]{1,0:T(8,128)(2,1)S(1)}, bf16[128,128]{1,0:T(8,128)(2,1)S(1)}, u32[]{:S(2)}, u32[]{:S(2)}) %collective-permute-start.7) | collective-permute-done | bytes 32800 | tf_op jit(solution)/shard_map/home/ppermute | solution.py:24
  231.1 8.1 %collective-permute-done.8 = bf16[128,128]{1,0:T(8,128)(2,1)S(1)} collective-permute-done((bf16[128,128]{1,0:T(8,128)(2,1)S(1)}, bf16[128,128]{1,0:T(8,128)(2,1)S(1)}, u32[]{:S(2)}, u32[]{:S(2)}) %collective-permute-start.8) | collective-permute-done | bytes 32800 | tf_op jit(solution)/shard_map/home/ppermute | solution.py:24
  (57 shorter events, 12.4 us)
Async XLA Ops:
  1.7 43.1 %all-to-all-start = ((bf16[4,128,384]{2,1,0:T(8,128)(2,1)}), bf16[4,128,384]{2,1,0:T(8,128)(2,1)S(1)}, u32[]{:S(2)}, u32[]{:S(2)}) async-start(bf16[4,128,384]{2,1,0:T(8,128)(2,1)} %broadcast_in_dim.12), calls=%async_computation | async-start | bytes 786432 | tf_op jit(solution)/shard_map/tokens/all_to_all | solution.py:48
  15.0 29.8 %collective-permute-start = (bf16[192,3,256]{2,0,1:T(8,128)(2,1)}, bf16[192,3,256]{2,0,1:T(8,128)(2,1)S(1)}, u32[]{:S(2)}, u32[]{:S(2)}) collective-permute-start(bf16[192,3,256]{2,0,1:T(8,128)(2,1)} %param.7), channel_id=1, source_target_pairs={{0,0},{1,32},{2,64},{3,96},{4,36},{5,68},{6,100},{7,4},{8,72},{9,1... | collective-permute-start | bytes 884744 | tf_op jit(solution)/shard_map/weights/ppermute | solution.py:24
  44.8 77.5 %copy-start.3 = (bf16[4,128,384]{2,1,0:T(8,128)(2,1)}, bf16[4,128,384]{2,1,0:T(8,128)(2,1)S(1)}, u32[]{:S(2)}) copy-start(bf16[4,128,384]{2,1,0:T(8,128)(2,1)S(1)} %all-to-all-done.t0) | copy-start | bytes 1179652
  44.8 5.6 %copy-start.7 = (bf16[128,384]{1,0:T(8,128)(2,1)S(1)}, bf16[128,384]{1,0:T(8,128)(2,1)}, u32[]{:S(2)}) copy-start(bf16[128,384]{1,0:T(8,128)(2,1)} %param.5) | copy-start | bytes 294916
  45.9 4.6 %copy-start.9 = (bf16[384]{0:T(512)(128)(2,1)S(1)}, bf16[384]{0:T(512)(128)(2,1)}, u32[]{:S(2)}) copy-start(bf16[384]{0:T(512)(128)(2,1)} %param.6) | copy-start | bytes 2308
  45.9 4.6 %copy-start.10 = (f32[256]{0:T(256)S(1)}, f32[256]{0:T(256)}, u32[]{:S(2)}) copy-start(f32[256]{0:T(256)} %param.8) | copy-start | bytes 3076
  45.9 22.6 %copy-start.11 = (f32[256]{0:T(256)S(1)}, f32[256]{0:T(256)}, u32[]{:S(2)}) copy-start(f32[256]{0:T(256)} %param.9) | copy-start | bytes 3076
  45.9 20.6 %all-to-all-start.3 = ((bf16[4,192,768]{2,1,0:T(8,128)(2,1)}), bf16[4,192,768]{2,1,0:T(8,128)(2,1)S(1)}, u32[]{:S(2)}, u32[]{:S(2)}) async-start(bf16[4,192,768]{2,1,0:T(8,128)(2,1)} %broadcast_in_dim.16), calls=%async_computation.3 | async-start | bytes 2359296 | tf_op jit(solution)/shard_map/weights/all_to_all | solution.py:48
  66.6 73.0 %copy-start.2 = (bf16[4,192,768]{2,1,0:T(8,128)(2,1)}, bf16[4,192,768]{2,1,0:T(8,128)(2,1)S(1)}, u32[]{:S(2)}) copy-start(bf16[4,192,768]{2,1,0:T(8,128)(2,1)S(1)} %all-to-all-done.3.w_mine) | copy-start | bytes 3538948
  66.6 73.0 %collective-permute-start.5 = (bf16[4,192,768]{2,1,0:T(8,128)(2,1)S(1)}, bf16[4,192,768]{2,1,0:T(8,128)(2,1)S(1)}, u32[]{:S(2)}, u32[]{:S(2)}) collective-permute-start(bf16[4,192,768]{2,1,0:T(8,128)(2,1)S(1)} %all-to-all-done.3.w_mine), channel_id=1, source_target_pairs={{0,16},{16,0},{1,17},{17,1},{2,18},{18,2},{3,19},{19,3},{4,20},{20... | collective-permute-start | bytes 3538952 | tf_op jit(solution)/shard_map/weights/ppermute | solution.py:24
  69.2 28.2 %all-to-all-start.1 = ((f32[16,1,1152]{2,1,0:T(1,128)}), f32[16,1,1152]{2,1,0:T(1,128)S(1)}, u32[]{:S(2)}, u32[]{:S(2)}) async-start(f32[16,1,1152]{2,1,0:T(1,128)} %broadcast_in_dim.13), calls=%async_computation.1 | async-start | bytes 147456 | tf_op jit(solution)/shard_map/norm/all_to_all | solution.py:48
  97.4 0.6 copy-start.8
  98.6 17.8 %all-to-all-start.2 = ((f32[4,1,256]{2,1,0:T(1,128)}), f32[4,1,256]{2,1,0:T(1,128)S(1)}, u32[]{:S(2)}, u32[]{:S(2)}) async-start(f32[4,1,256]{2,1,0:T(1,128)} %broadcast_in_dim.14), calls=%async_computation.2 | async-start | bytes 8192 | tf_op jit(solution)/shard_map/norm/all_to_all | solution.py:48
  116.4 23.1 %collective-permute-start.4 = (bf16[4,128,384]{2,1,0:T(8,128)(2,1)S(1)}, bf16[4,128,384]{2,1,0:T(8,128)(2,1)S(1)}, u32[]{:S(2)}, u32[]{:S(2)}) collective-permute-start(bf16[4,128,384]{2,1,0:T(8,128)(2,1)S(1)} %all-to-all-done.t0), channel_id=1, source_target_pairs={{0,4},{4,8},{8,12},{12,32},{32,36},{36,40},{40,44},{44,64},{64,68}... | collective-permute-start | bytes 1179656 | tf_op jit(solution)/shard_map/tokens/ppermute | solution.py:24
  119.0 20.5 %collective-permute-start.1 = (bf16[4,128,384]{2,1,0:T(8,128)(2,1)S(1)}, bf16[4,128,384]{2,1,0:T(8,128)(2,1)S(1)}, u32[]{:S(2)}, u32[]{:S(2)}) collective-permute-start(bf16[4,128,384]{2,1,0:T(8,128)(2,1)S(1)} %all-to-all-done.t0), channel_id=1, source_target_pairs={{0,108},{4,0},{8,4},{12,8},{32,12},{36,32},{40,36},{44,40},{64,44}... | collective-permute-start | bytes 1179656 | tf_op jit(solution)/shard_map/tokens/ppermute | solution.py:24
  123.1 16.4 %collective-permute-start.3 = (bf16[4,64,384]{2,1,0:T(8,128)(2,1)}, bf16[4,64,384]{2,1,0:T(8,128)(2,1)}, u32[]{:S(2)}, u32[]{:S(2)}) collective-permute-start(bf16[4,64,384]{2,1,0:T(8,128)(2,1)} %get-tuple-element.11), channel_id=1, source_target_pairs={{0,104},{4,108},{8,0},{12,4},{32,8},{36,12},{40,32},{44,36},{64,40... | collective-permute-start | bytes 589832 | tf_op jit(solution)/shard_map/tokens/ppermute | solution.py:24
  129.0 10.5 %collective-permute-start.2 = (bf16[4,64,384]{2,1,0:T(8,128)(2,1)}, bf16[4,64,384]{2,1,0:T(8,128)(2,1)}, u32[]{:S(2)}, u32[]{:S(2)}) collective-permute-start(bf16[4,64,384]{2,1,0:T(8,128)(2,1)} %get-tuple-element.12), channel_id=1, source_target_pairs={{0,8},{4,12},{8,32},{12,36},{32,40},{36,44},{40,64},{44,68},{64,72... | collective-permute-start | bytes 589832 | tf_op jit(solution)/shard_map/tokens/ppermute | solution.py:24
  139.5 0.7 copy-start.5
  139.5 0.9 copy-start.6
  140.4 1.0 copy-start.4
  147.0 19.3 %all-to-all-start.4 = ((f32[4,128,768]{2,1,0:T(8,128)}), f32[4,128,768]{2,1,0:T(8,128)S(1)}, u32[]{:S(2)}, u32[]{:S(2)}) async-start(f32[4,128,768]{2,1,0:T(8,128)} %project.2), calls=%async_computation.4 | async-start | bytes 3145728 | tf_op jit(solution)/shard_map/project/all_to_all | solution.py:185
  166.2 1.2 copy-start.1
  170.7 3.2 %collective-permute-start.6 = (bf16[3,128,128]{2,1,0:T(8,128)(2,1)S(1)}, bf16[3,128,128]{2,1,0:T(8,128)(2,1)S(1)}, u32[]{:S(2)}, u32[]{:S(2)}) collective-permute-start(bf16[3,128,128]{2,1,0:T(8,128)(2,1)S(1)} %get-tuple-element.14), channel_id=1, source_target_pairs={{0,16},{16,0},{1,17},{17,1},{2,18},{18,2},{3,19},{19,3},{4,20},{20... | collective-permute-start | bytes 294920 | tf_op jit(solution)/shard_map/project/ppermute | solution.py:24
  175.8 34.3 %all-to-all-start.5 = ((bf16[16,2,2,128,128]{4,3,2,1,0:T(8,128)(2,1)}), bf16[16,2,2,128,128]{4,3,2,1,0:T(8,128)(2,1)S(1)}, u32[]{:S(2)}, u32[]{:S(2)}) async-start(bf16[16,2,2,128,128]{4,3,2,1,0:T(8,128)(2,1)} %broadcast_in_dim.17), calls=%async_computation.5 | async-start | bytes 4194304 | tf_op jit(solution)/shard_map/keys/all_to_all | solution.py:48
  210.1 1.3 copy-start
  216.6 14.5 %collective-permute-start.7 = (bf16[128,128]{1,0:T(8,128)(2,1)S(1)}, bf16[128,128]{1,0:T(8,128)(2,1)S(1)}, u32[]{:S(2)}, u32[]{:S(2)}) collective-permute-start(bf16[128,128]{1,0:T(8,128)(2,1)S(1)} %get-tuple-element.15), channel_id=1, source_target_pairs={{0,0},{1,32},{2,64},{3,96},{4,39},{5,71},{6,103},{7,7},{8,74},{9,1... | collective-permute-start | bytes 98312 | tf_op jit(solution)/shard_map/home/ppermute | solution.py:24
  225.2 13.9 %collective-permute-start.8 = (bf16[128,128]{1,0:T(8,128)(2,1)S(1)}, bf16[128,128]{1,0:T(8,128)(2,1)S(1)}, u32[]{:S(2)}, u32[]{:S(2)}) collective-permute-start(bf16[128,128]{1,0:T(8,128)(2,1)S(1)} %get-tuple-element.16), channel_id=1, source_target_pairs={{0,16},{1,48},{2,80},{3,112},{4,55},{5,87},{6,119},{7,23},{8,90},{... | collective-permute-start | bytes 98312 | tf_op jit(solution)/shard_map/home/ppermute | solution.py:24

commit v4 on v3

--- a/solution.py
+++ b/solution.py
@@ -12,7 +12,7 @@
 CORES = 2
 AXES = ("x", "zh", "core", "zl", "y")
 SIZES = (NX, NZH, CORES, NZL, NY)
-VMEM_LIMIT = 56 * 1024 * 1024
+VMEM_LIMIT = 28 * 1024 * 1024
 
 
 def shift(values, axes, move):
@@ -73,34 +73,36 @@
         elif slot < NZL - 1:
             acc[...] += term
         else:
+            total = acc[...] + term
             for quarter in range(NZH):
                 rows = slice(quarter * 128, quarter * 128 + 128)
-                out[lax.rem(turn + quarter, NZH)] = acc[rows] + term[rows]
-
-
-def heads_kernel(where, part, head_gain, out):
-    core = where[1]
-    acc = part[0] + part[1] + part[2] + part[3]
-
+                for head in range(2):
+                    for s in range(3):
+                        cols = slice(s * 256 + head * DH, s * 256 + head * DH + DH)
+                        out[head, lax.rem(turn + quarter, NZH), :, s * DH : s * DH + DH] = total[
+                            rows, cols
+                        ]
+
+
+def heads_kernel(part, head_gain, q_out, kv_out):
     def head_norm(values, row):
         mid = jnp.mean(values, axis=1, keepdims=True)
         var = jnp.mean(values * values, axis=1, keepdims=True) - mid * mid
         return ((values - mid) * lax.rsqrt(var + EPSILON) * row).astype(jnp.bfloat16)
 
-    for head in range(2):
-        slot = lax.rem(core + head, 2)
-        cols = [slice(s * 256 + head * DH, s * 256 + head * DH + DH) for s in range(3)]
-        out[slot, 0] = head_norm(acc[:, cols[0]], head_gain[0, :, head * DH : head * DH + DH])
-        out[slot, 1] = head_norm(acc[:, cols[1]], head_gain[1, :, head * DH : head * DH + DH])
-        out[slot, 2] = acc[:, cols[2]].astype(jnp.bfloat16)
+    for source in range(2):
+        rows = slice(source * 128, source * 128 + 128)
+        acc = part[source, 0] + part[source, 1] + part[source, 2] + part[source, 3]
+        q_out[rows] = head_norm(acc[:, :DH], head_gain[0])
+        kv_out[0, rows] = head_norm(acc[:, DH : 2 * DH], head_gain[1])
+        kv_out[1, rows] = acc[:, 2 * DH :].astype(jnp.bfloat16)
 
 
 def attend_kernel(q, kv, out):
-    keys = kv[:, :, 0].reshape(-1, DH)
-    values = kv[:, :, 1].reshape(-1, DH)
-    queries = q[...].reshape(-1, DH)
+    keys = kv[:, 0].reshape(-1, DH)
+    values = kv[:, 1].reshape(-1, DH)
     scores = lax.dot_general(
-        queries, keys, (((1,), (1,)), ((), ())), preferred_element_type=jnp.float32
+        q[...], keys, (((1,), (1,)), ((), ())), preferred_element_type=jnp.float32
     ) * (DH ** -0.5)
     top = jnp.max(scores, axis=1, keepdims=True)
     weights = jnp.exp(scores - top)
@@ -132,13 +134,6 @@
 
     with jax.named_scope("weights"):
         w_moved = to_plane(w_qkv)
-
-    with jax.named_scope("tokens"):
-        t0, w_moved = lax.optimization_barrier((spread(tokens, "zh", NZH), w_moved))
-        t1 = along_z(t0, -1)
-        t3 = along_z(t0, 1)
-        t2a = along_z(t0[:, :64], 2)
-        t2b = along_z(t0[:, 64:], -2)
 
     with jax.named_scope("norm"):
         x = tokens.astype(jnp.float32)
@@ -165,7 +160,17 @@
         )
         head_gain = lax.dynamic_index_in_dim(
             shared[:, 640:], zl * NY + (zh + NY - zl) % NY, 0, keepdims=False
-        ).reshape(2, 1, 256)
+        )
+        head_gain = lax.dynamic_index_in_dim(head_gain.reshape(2, 2, 1, DH), core, 1, keepdims=False)
+
+    with jax.named_scope("tokens"):
+        t0, w_moved, stats, gain, head_gain = lax.optimization_barrier(
+            (spread(tokens, "zh", NZH), w_moved, stats, gain, head_gain)
+        )
+        t1 = along_z(t0, -1)
+        t3 = along_z(t0, 1)
+        t2a = along_z(t0[:, :64], 2)
+        t2b = along_z(t0[:, 64:], -2)
 
     with jax.named_scope("weights"):
         w_mine = spread(w_moved.reshape(192, 768), "x", NX)
@@ -174,7 +179,7 @@
     with jax.named_scope("project"):
         part = kernel_call(
             partial_kernel,
-            jax.ShapeDtypeStruct((NZH, 128, 768), jnp.float32),
+            jax.ShapeDtypeStruct((CORES, NY, 128, 3 * DH), jnp.float32),
             (where, t0, t1, t2a, t2b, t3, stats, gain, w_mine, w_theirs),
             scalars=1,
             scratch=[
@@ -182,26 +187,28 @@
                 pltpu.VMEM((512, 768), jnp.float32),
             ],
         )
-        part = lax.all_to_all(part, "y", 0, 0)
-        heads = kernel_call(
+        part = part.reshape(CORES * NY, 128, 3 * DH)
+        part = lax.all_to_all(part, ("core", "y"), 0, 0).reshape(CORES, NY, 128, 3 * DH)
+        q, kv = kernel_call(
             heads_kernel,
-            jax.ShapeDtypeStruct((2, 3, 128, DH), jnp.bfloat16),
-            (where, part, head_gain),
-            scalars=1,
-        )
-        both = jnp.stack([heads[0], swap_cores(heads[1])])
+            (
+                jax.ShapeDtypeStruct((256, DH), jnp.bfloat16),
+                jax.ShapeDtypeStruct((2, 256, DH), jnp.bfloat16),
+            ),
+            (part, head_gain),
+        )
 
     with jax.named_scope("keys"):
-        kv_all = spread(both[:, 1:], ("x", "y"), NX * NY)
+        kv_all = spread(kv, ("x", "y"), NX * NY)
 
     with jax.named_scope("attend"):
         out = kernel_call(
-            attend_kernel, jax.ShapeDtypeStruct((256, DH), jnp.bfloat16), (both[:, 0], kv_all)
+            attend_kernel, jax.ShapeDtypeStruct((256, DH), jnp.bfloat16), (q, kv_all)
         )
 
     with jax.named_scope("home"):
-        same = to_home(out[:128], 0)
-        cross = to_home(out[128:], 1)
+        same = to_home(lax.dynamic_slice_in_dim(out, core * 128, 128), 0)
+        cross = to_home(lax.dynamic_slice_in_dim(out, (1 - core) * 128, 128), 1)
         return jnp.where(
             core == 0,
             jnp.concatenate([same, cross], axis=1),

time: 241 us -> 227 us (0.942)
  the two profiles are of different devices: /device:TPU:64 before, /device:TPU:40 now
where the time goes in v4:
time: 227 us; the launch traced here: 226 us
  blocking collectives  81.6 us (36%)
  waiting for transfers between devices  68.8 us (30%)
  starting transfers between devices  61.4 us (27%)
  local copies, waits for them, and re-layouts  6.04 us (3%)
  Pallas kernels  5.58 us (2%)
  other arithmetic  2.49 us (1%)
    all_to_all x3, blocking collectives, spread(): lax.all_to_all(jnp.broadcast_to(values[None], (count,) + values.shape), a...  58.8 us
    ppermute x8, starting transfers between devices, shift(): return lax.ppermute(values, axes, pairs)  53.1 us
    ppermute x8, waiting for transfers between devices, shift(): return lax.ppermute(values, axes, pairs)  39 us
    all_to_all x2, waiting for transfers between devices, spread(): lax.all_to_all(jnp.broadcast_to(values[None], (count,) + values.shape), a...  29.7 us
    all_to_all x1, blocking collectives, body(): lax.all_to_all(part, ('core', 'y'), 0, 0).reshape(CORES, NY, 128, 3 * DH)  22.9 us
    all_to_all x2, starting transfers between devices, spread(): lax.all_to_all(jnp.broadcast_to(values[None], (count,) + values.shape), a...  8.33 us
    pallas_call x3, Pallas kernels, kernel_call(): pl.pallas_call(kernel, out_shape=out_shape, in_specs=[smem] * scalars + [...  5.58 us
  transfers between devices with their start and end apart: 10, of which 5 were waited for; matrix products, arithmetic and copies ran while one was open for 0% of the time, Pallas kernels for 0%

profile of v4, /device:TPU:40, one launch (start us, length us, event | category | flops | bytes accessed | tf_op | source)
XLA Modules:
  0.0 226.2 jit_solution(15129400287885335993)
XLA Ops:
  0.0 1.1 fusion
  1.1 0.7 constant_dynamic-update-slice_fusion.2
  1.8 0.7 constant_dynamic-update-slice_fusion.1
  2.5 0.7 constant_dynamic-update-slice_fusion
  3.2 14.0 %all_to_all.30 = f32[16,1,1152]{2,1,0:T(1,128)S(1)} all-to-all(f32[16,1,1152]{2,1,0:T(1,128)S(1)} %broadcast_in_dim.13), channel_id=1, replica_groups=mesh['x'=4,'zh'=4,'core'=2,'zl'=4,'y'=4] {'zl','y'}, dimensions={0} | all-to-all | bytes 147456 | tf_op jit(solution)/shard_map/norm/all_to_all | solution.py:48
  17.3 24.7 %all_to_all.31 = f32[4,1,256]{2,1,0:T(1,128)S(1)} all-to-all(f32[4,1,256]{2,1,0:T(1,128)S(1)} %broadcast_in_dim.14), channel_id=1, replica_groups=mesh['x'=4,'zh'=4,'core'=2,'zl'=4,'y'=4] {'zh'}, dimensions={0} | all-to-all | bytes 8192 | tf_op jit(solution)/shard_map/norm/all_to_all | solution.py:48
  42.0 1.7 broadcast_in_dim.12
  43.6 3.5 %all-to-all-start = ((bf16[4,128,384]{2,1,0:T(8,128)(2,1)}), bf16[4,128,384]{2,1,0:T(8,128)(2,1)S(1)}, u32[]{:S(2)}, u32[]{:S(2)}) async-start(bf16[4,128,384]{2,1,0:T(8,128)(2,1)} %broadcast_in_dim.12), calls=%async_computation | async-start | bytes 786432 | tf_op jit(solution)/shard_map/tokens/all_to_all | solution.py:48
  47.1 13.5 %collective-permute-start = (bf16[192,3,256]{2,0,1:T(8,128)(2,1)S(1)}, bf16[192,3,256]{2,0,1:T(8,128)(2,1)S(1)}, u32[]{:S(2)}, u32[]{:S(2)}) collective-permute-start(bf16[192,3,256]{2,0,1:T(8,128)(2,1)S(1)} %copy-done), channel_id=1, source_target_pairs={{0,0},{1,32},{2,64},{3,96},{4,36},{5,68},{6,100},{7,4},{8,72},{9,1... | collective-permute-start | bytes 884744 | tf_op jit(solution)/shard_map/weights/ppermute | solution.py:24
  60.8 14.2 %collective-permute-done = bf16[192,3,256]{2,0,1:T(8,128)(2,1)S(1)} collective-permute-done((bf16[192,3,256]{2,0,1:T(8,128)(2,1)S(1)}, bf16[192,3,256]{2,0,1:T(8,128)(2,1)S(1)}, u32[]{:S(2)}, u32[]{:S(2)}) %collective-permute-start) | collective-permute-done | bytes 294944 | tf_op jit(solution)/shard_map/weights/ppermute | solution.py:24
  75.0 0.1 broadcast_in_dim.16
  75.1 20.0 %all_to_all.32.w_mine = bf16[4,192,768]{2,1,0:T(8,128)(2,1)S(1)} all-to-all(bf16[4,192,768]{2,1,0:T(8,128)(2,1)S(1)} %broadcast_in_dim.16), channel_id=1, replica_groups=mesh['x'=4,'zh'=4,'core'=2,'zl'=4,'y'=4] {'x'}, dimensions={0} | all-to-all | bytes 2359296 | tf_op jit(solution)/shard_map/weights/all_to_all | solution.py:48
  95.1 1.9 collective-permute-start.5
  97.0 6.7 %collective-permute-start.1 = (bf16[4,128,384]{2,1,0:T(8,128)(2,1)S(1)}, bf16[4,128,384]{2,1,0:T(8,128)(2,1)S(1)}, u32[]{:S(2)}, u32[]{:S(2)}) collective-permute-start(bf16[4,128,384]{2,1,0:T(8,128)(2,1)S(1)} %all-to-all-done.t0), channel_id=1, source_target_pairs={{0,108},{4,0},{8,4},{12,8},{32,12},{36,32},{40,36},{44,40},{64,44}... | collective-permute-start | bytes 1179656 | tf_op jit(solution)/shard_map/tokens/ppermute | solution.py:24
  103.8 1.9 collective-permute-start.4
  105.7 0.8 fusion.7
  106.5 8.8 %collective-permute-start.2 = (bf16[4,64,384]{2,1,0:T(8,128)(2,1)}, bf16[4,64,384]{2,1,0:T(8,128)(2,1)}, u32[]{:S(2)}, u32[]{:S(2)}) collective-permute-start(bf16[4,64,384]{2,1,0:T(8,128)(2,1)} %get-tuple-element.22), channel_id=1, source_target_pairs={{0,8},{4,12},{8,32},{12,36},{32,40},{36,44},{40,64},{44,68},{64,72... | collective-permute-start | bytes 589832 | tf_op jit(solution)/shard_map/tokens/ppermute | solution.py:24
  115.3 11.2 %collective-permute-start.3 = (bf16[4,64,384]{2,1,0:T(8,128)(2,1)}, bf16[4,64,384]{2,1,0:T(8,128)(2,1)}, u32[]{:S(2)}, u32[]{:S(2)}) collective-permute-start(bf16[4,64,384]{2,1,0:T(8,128)(2,1)} %get-tuple-element.21), channel_id=1, source_target_pairs={{0,104},{4,108},{8,0},{12,4},{32,8},{36,12},{40,32},{44,36},{64,40... | collective-permute-start | bytes 589832 | tf_op jit(solution)/shard_map/tokens/ppermute | solution.py:24
  126.6 0.1 copy.16.stats
  126.8 12.8 %collective-permute-done.2.t2a = bf16[4,64,384]{2,1,0:T(8,128)(2,1)} collective-permute-done((bf16[4,64,384]{2,1,0:T(8,128)(2,1)}, bf16[4,64,384]{2,1,0:T(8,128)(2,1)}, u32[]{:S(2)}, u32[]{:S(2)}) %collective-permute-start.2) | collective-permute-done | bytes 196640 | tf_op jit(solution)/shard_map/tokens/ppermute | solution.py:24
  139.6 3.3 %project.2 = f32[2,4,128,384]{3,2,1,0:T(8,128)S(1)} custom-call(s32[3]{0:T(128)S(1)} %pad_add_fusion.where, bf16[4,128,384]{2,1,0:T(8,128)(2,1)S(1)} %all-to-all-done.t0, bf16[4,128,384]{2,1,0:T(8,128)(2,1)S(1)} %collective-permute-done.1.t1, bf16[4,64,384]{2,1,0:T(8,128)(2,1)} %collective-permute-done.2.t2a, ...), custom_call_target="tpu_custom_call" | custom-call | tf_op jit(solution)/shard_map/project/pallas_call | solution.py:117
  142.9 22.9 %all_to_all.33 = f32[8,128,384]{2,1,0:T(8,128)S(1)} all-to-all(f32[8,128,384]{2,1,0:T(8,128)S(1)} %bitcast.24), channel_id=1, replica_groups=mesh['x'=4,'zh'=4,'core'=2,'zl'=4,'y'=4] {'core','y'}, dimensions={0} | all-to-all | bytes 3145728 | tf_op jit(solution)/shard_map/project/all_to_all | solution.py:191
  165.8 0.2 project.3
  166.0 1.8 broadcast_in_dim.17
  167.9 4.9 %all-to-all-start.5 = ((bf16[16,2,256,128]{3,2,1,0:T(8,128)(2,1)}), bf16[16,2,256,128]{3,2,1,0:T(8,128)(2,1)S(1)}, u32[]{:S(2)}, u32[]{:S(2)}) async-start(bf16[16,2,256,128]{3,2,1,0:T(8,128)(2,1)} %broadcast_in_dim.17), calls=%async_computation.5 | async-start | bytes 4194304 | tf_op jit(solution)/shard_map/keys/all_to_all | solution.py:48
  172.7 29.7 %all-to-all-done.5.kv = bf16[16,2,256,128]{3,2,1,0:T(8,128)(2,1)S(1)} async-done(((bf16[16,2,256,128]{3,2,1,0:T(8,128)(2,1)}), bf16[16,2,256,128]{3,2,1,0:T(8,128)(2,1)S(1)}, u32[]{:S(2)}, u32[]{:S(2)}) %all-to-all-start.5) | async-done | bytes 2097184 | tf_op jit(solution)/shard_map/keys/all_to_all | solution.py:48
  202.5 2.1 attend.1
  204.6 7.0 %collective-permute-start.6 = (bf16[128,128]{1,0:T(8,128)(2,1)S(1)}, bf16[128,128]{1,0:T(8,128)(2,1)S(1)}, u32[]{:S(2)}, u32[]{:S(2)}) collective-permute-start(bf16[128,128]{1,0:T(8,128)(2,1)S(1)} %get-tuple-element.23), channel_id=1, source_target_pairs={{0,0},{1,32},{2,64},{3,96},{4,39},{5,71},{6,103},{7,7},{8,74},{9,1... | collective-permute-start | bytes 98312 | tf_op jit(solution)/shard_map/home/ppermute | solution.py:24
  211.6 1.9 collective-permute-start.7
  213.6 5.5 %collective-permute-done.6 = bf16[128,128]{1,0:T(8,128)(2,1)S(1)} collective-permute-done((bf16[128,128]{1,0:T(8,128)(2,1)S(1)}, bf16[128,128]{1,0:T(8,128)(2,1)S(1)}, u32[]{:S(2)}, u32[]{:S(2)}) %collective-permute-start.6) | collective-permute-done | bytes 32800 | tf_op jit(solution)/shard_map/home/ppermute | solution.py:24
  219.1 6.5 %collective-permute-done.7 = bf16[128,128]{1,0:T(8,128)(2,1)S(1)} collective-permute-done((bf16[128,128]{1,0:T(8,128)(2,1)S(1)}, bf16[128,128]{1,0:T(8,128)(2,1)S(1)}, u32[]{:S(2)}, u32[]{:S(2)}) %collective-permute-start.7) | collective-permute-done | bytes 32800 | tf_op jit(solution)/shard_map/home/ppermute | solution.py:24
  225.6 0.6 maximum_select_fusion
  (26 shorter events, 0.3 us)
Async XLA Ops:
  0.0 47.1 %copy-start = (bf16[192,3,256]{2,0,1:T(8,128)(2,1)S(1)}, bf16[192,3,256]{2,0,1:T(8,128)(2,1)}, u32[]{:S(2)}) copy-start(bf16[192,3,256]{2,0,1:T(8,128)(2,1)} %param.7) | copy-start | bytes 884740
  43.6 31.3 %all-to-all-start = ((bf16[4,128,384]{2,1,0:T(8,128)(2,1)}), bf16[4,128,384]{2,1,0:T(8,128)(2,1)S(1)}, u32[]{:S(2)}, u32[]{:S(2)}) async-start(bf16[4,128,384]{2,1,0:T(8,128)(2,1)} %broadcast_in_dim.12), calls=%async_computation | async-start | bytes 786432 | tf_op jit(solution)/shard_map/tokens/all_to_all | solution.py:48
  47.1 27.9 %collective-permute-start = (bf16[192,3,256]{2,0,1:T(8,128)(2,1)S(1)}, bf16[192,3,256]{2,0,1:T(8,128)(2,1)S(1)}, u32[]{:S(2)}, u32[]{:S(2)}) collective-permute-start(bf16[192,3,256]{2,0,1:T(8,128)(2,1)S(1)} %copy-done), channel_id=1, source_target_pairs={{0,0},{1,32},{2,64},{3,96},{4,36},{5,68},{6,100},{7,4},{8,72},{9,1... | collective-permute-start | bytes 884744 | tf_op jit(solution)/shard_map/weights/ppermute | solution.py:24
  95.1 44.5 %collective-permute-start.5 = (bf16[4,192,768]{2,1,0:T(8,128)(2,1)S(1)}, bf16[4,192,768]{2,1,0:T(8,128)(2,1)S(1)}, u32[]{:S(2)}, u32[]{:S(2)}) collective-permute-start(bf16[4,192,768]{2,1,0:T(8,128)(2,1)S(1)} %all_to_all.32.w_mine), channel_id=1, source_target_pairs={{0,16},{16,0},{1,17},{17,1},{2,18},{18,2},{3,19},{19,3},{4,20},{20... | collective-permute-start | bytes 3538952 | tf_op jit(solution)/shard_map/weights/ppermute | solution.py:24
  97.0 42.6 %collective-permute-start.1 = (bf16[4,128,384]{2,1,0:T(8,128)(2,1)S(1)}, bf16[4,128,384]{2,1,0:T(8,128)(2,1)S(1)}, u32[]{:S(2)}, u32[]{:S(2)}) collective-permute-start(bf16[4,128,384]{2,1,0:T(8,128)(2,1)S(1)} %all-to-all-done.t0), channel_id=1, source_target_pairs={{0,108},{4,0},{8,4},{12,8},{32,12},{36,32},{40,36},{44,40},{64,44}... | collective-permute-start | bytes 1179656 | tf_op jit(solution)/shard_map/tokens/ppermute | solution.py:24
  103.8 35.9 %collective-permute-start.4 = (bf16[4,128,384]{2,1,0:T(8,128)(2,1)S(1)}, bf16[4,128,384]{2,1,0:T(8,128)(2,1)}, u32[]{:S(2)}, u32[]{:S(2)}) collective-permute-start(bf16[4,128,384]{2,1,0:T(8,128)(2,1)S(1)} %all-to-all-done.t0), channel_id=1, source_target_pairs={{0,4},{4,8},{8,12},{12,32},{32,36},{36,40},{40,44},{44,64},{64,68}... | collective-permute-start | bytes 1179656 | tf_op jit(solution)/shard_map/tokens/ppermute | solution.py:24
  106.5 33.1 %collective-permute-start.2 = (bf16[4,64,384]{2,1,0:T(8,128)(2,1)}, bf16[4,64,384]{2,1,0:T(8,128)(2,1)}, u32[]{:S(2)}, u32[]{:S(2)}) collective-permute-start(bf16[4,64,384]{2,1,0:T(8,128)(2,1)} %get-tuple-element.22), channel_id=1, source_target_pairs={{0,8},{4,12},{8,32},{12,36},{32,40},{36,44},{40,64},{44,68},{64,72... | collective-permute-start | bytes 589832 | tf_op jit(solution)/shard_map/tokens/ppermute | solution.py:24
  115.3 24.3 %collective-permute-start.3 = (bf16[4,64,384]{2,1,0:T(8,128)(2,1)}, bf16[4,64,384]{2,1,0:T(8,128)(2,1)}, u32[]{:S(2)}, u32[]{:S(2)}) collective-permute-start(bf16[4,64,384]{2,1,0:T(8,128)(2,1)} %get-tuple-element.21), channel_id=1, source_target_pairs={{0,104},{4,108},{8,0},{12,4},{32,8},{36,12},{40,32},{44,36},{64,40... | collective-permute-start | bytes 589832 | tf_op jit(solution)/shard_map/tokens/ppermute | solution.py:24
  167.9 34.6 %all-to-all-start.5 = ((bf16[16,2,256,128]{3,2,1,0:T(8,128)(2,1)}), bf16[16,2,256,128]{3,2,1,0:T(8,128)(2,1)S(1)}, u32[]{:S(2)}, u32[]{:S(2)}) async-start(bf16[16,2,256,128]{3,2,1,0:T(8,128)(2,1)} %broadcast_in_dim.17), calls=%async_computation.5 | async-start | bytes 4194304 | tf_op jit(solution)/shard_map/keys/all_to_all | solution.py:48
  204.6 14.5 %collective-permute-start.6 = (bf16[128,128]{1,0:T(8,128)(2,1)S(1)}, bf16[128,128]{1,0:T(8,128)(2,1)S(1)}, u32[]{:S(2)}, u32[]{:S(2)}) collective-permute-start(bf16[128,128]{1,0:T(8,128)(2,1)S(1)} %get-tuple-element.23), channel_id=1, source_target_pairs={{0,0},{1,32},{2,64},{3,96},{4,39},{5,71},{6,103},{7,7},{8,74},{9,1... | collective-permute-start | bytes 98312 | tf_op jit(solution)/shard_map/home/ppermute | solution.py:24
  211.6 14.0 %collective-permute-start.7 = (bf16[128,128]{1,0:T(8,128)(2,1)S(1)}, bf16[128,128]{1,0:T(8,128)(2,1)S(1)}, u32[]{:S(2)}, u32[]{:S(2)}) collective-permute-start(bf16[128,128]{1,0:T(8,128)(2,1)S(1)} %get-tuple-element.24), channel_id=1, source_target_pairs={{0,16},{1,48},{2,80},{3,112},{4,55},{5,87},{6,119},{7,23},{8,90},{... | collective-permute-start | bytes 98312 | tf_op jit(solution)/shard_map/home/ppermute | solution.py:24

commit v5 on v4

--- a/solution.py
+++ b/solution.py
@@ -8,6 +8,7 @@
 
 DH = 128
 EPSILON = 1e-06
+FEATURES = 6144
 NX = NZH = NZL = NY = 4
 CORES = 2
 AXES = ("x", "zh", "core", "zl", "y")
@@ -48,25 +49,56 @@
     return lax.all_to_all(jnp.broadcast_to(values[None], (count,) + values.shape), axes, 0, 0)
 
 
-def partial_kernel(where, t0, t1, t2a, t2b, t3, stats, gain, w_mine, w_theirs, out, w, acc):
-    zl, core, turn = where[0], where[1], where[2]
-    half = w_mine.shape[1]
-    for x in range(NX):
-        w[x, pl.ds(pl.multiple_of(core * half, half), half)] = w_mine[x]
-        w[x, pl.ds(pl.multiple_of((1 - core) * half, half), half)] = w_theirs[x]
-    pieces = ((t0,), (t1,), (t2a, t2b), (t3,))
+def pieces_of(values):
+    high = lax.reduce_precision(values, 8, 7)
+    rest = values - high
+    mid = lax.reduce_precision(rest, 8, 7)
+    return jnp.concatenate([high, mid, rest - mid]).astype(jnp.bfloat16)
+
+
+def partial_kernel(where, t0, t1, t2a, t2b, t3, w_mine, w_theirs, out, w, acc):
+    zl, core, turn, x_here = where[0], where[1], where[2], where[3]
+    half = w_mine.shape[2]
+    for step in range(NX):
+        x = lax.rem(x_here + step, NX)
+        for s in range(3):
+            cols = slice(s * 256, s * 256 + 256)
+            w[x, pl.ds(pl.multiple_of(core * half, half), half), cols] = w_mine[step, s]
+            w[x, pl.ds(pl.multiple_of((1 - core) * half, half), half), cols] = w_theirs[step, s]
+    tokens = (
+        ((t0, 128),),
+        ((t1, 128),),
+        ((t2a, 80), (t2b, 48)),
+        ((t3, 128),),
+    )
+    extras = ((t0, 128), (t1, 128), (t2b, 48), (t3, 128))
+
+    def extra(slot, quarter):
+        ref, row = extras[slot]
+        return ref[quarter, row : row + 16].astype(jnp.float32)
+
+    centers, scales = [], []
+    for quarter in range(NZH):
+        rows = sum(extra(slot, quarter)[:2] for slot in range(NZL))
+        sums = (rows[:, :128] + rows[:, 128:256] + rows[:, 256:]) / FEATURES
+        center = sums[0:1]
+        centers.append(center)
+        scales.append(lax.rsqrt(sums[1:2] - center * center + EPSILON))
+    stats = jnp.concatenate(centers + scales, axis=0).T
+
     for slot in range(NZL):
-        part = lax.rem(zl + slot, NZL)
-        row_gain = gain[part]
+        row_gain = extra(slot, 0)[2:3]
         normed = []
         for quarter in range(NZH):
-            x = [ref[quarter].astype(jnp.float32) for ref in pieces[slot]]
+            x = [ref[quarter, :count].astype(jnp.float32) for ref, count in tokens[slot]]
             x = x[0] if len(x) == 1 else jnp.concatenate(x, axis=0)
-            center = stats[quarter, :, 0:1]
-            scale = stats[quarter, :, 1:2]
+            center = stats[:, quarter : quarter + 1]
+            scale = stats[:, NZH + quarter : NZH + quarter + 1]
             normed.append(((x - center) * scale * row_gain).astype(jnp.bfloat16))
         term = jnp.dot(
-            jnp.concatenate(normed, axis=0), w[part], preferred_element_type=jnp.float32
+            jnp.concatenate(normed, axis=0),
+            w[lax.rem(zl + slot, NZL)],
+            preferred_element_type=jnp.float32,
         )
         if slot == 0:
             acc[...] = term
@@ -128,59 +160,54 @@
     core = lax.axis_index("core")
     zl = lax.axis_index("zl")
     zh = lax.axis_index("zh")
-    y_here = lax.axis_index("y")
     turn = (2 * NZH - zh - zl) % NZH
-    where = jnp.stack([zl, core, turn]).astype(jnp.int32)
+    where = jnp.stack([zl, core, turn, lax.axis_index("x")]).astype(jnp.int32)
 
     with jax.named_scope("weights"):
-        w_moved = to_plane(w_qkv)
+        w_moved = to_plane(jnp.transpose(w_qkv, (1, 0, 2)))
 
     with jax.named_scope("norm"):
         x = tokens.astype(jnp.float32)
         shared = spread(
-            jnp.concatenate(
-                [
-                    jnp.sum(x, axis=1),
-                    jnp.sum(x * x, axis=1),
-                    ln_gain.astype(jnp.float32),
-                    q_gain,
-                    k_gain,
-                ]
-            )[None],
-            ("zl", "y"),
-            NZL * NY,
+            jnp.concatenate([jnp.sum(x, axis=1), jnp.sum(x * x, axis=1), q_gain, k_gain])[None],
+            "y",
+            NY,
         )[:, 0]
-        features = tokens.shape[1] * NZL * NY
-        sums = spread(jnp.sum(shared[:, :256], axis=0)[None], "zh", NZH)[:, 0]
-        center = sums[:, :128] / features
-        var = sums[:, 128:] / features - center * center
-        stats = jnp.stack([center, lax.rsqrt(var + EPSILON)], axis=2)
-        gain = lax.dynamic_index_in_dim(
-            shared[:, 256:640].reshape(NZL, NY, 1, 384), y_here, 1, keepdims=False
-        )
+        sums = jnp.sum(shared[:, :256], axis=0)
         head_gain = lax.dynamic_index_in_dim(
-            shared[:, 640:], zl * NY + (zh + NY - zl) % NY, 0, keepdims=False
+            shared[:, 256:], (zh + NY - zl) % NY, 0, keepdims=False
         )
         head_gain = lax.dynamic_index_in_dim(head_gain.reshape(2, 2, 1, DH), core, 1, keepdims=False)
+        extended = jnp.concatenate(
+            [
+                tokens,
+                pieces_of(sums[:128])[None],
+                pieces_of(sums[128:])[None],
+                ln_gain[None],
+                jnp.zeros((13, 384), jnp.bfloat16),
+            ]
+        )
 
     with jax.named_scope("tokens"):
-        t0, w_moved, stats, gain, head_gain = lax.optimization_barrier(
-            (spread(tokens, "zh", NZH), w_moved, stats, gain, head_gain)
-        )
+        t0, w_moved = lax.optimization_barrier((spread(extended, "zh", NZH), w_moved))
         t1 = along_z(t0, -1)
         t3 = along_z(t0, 1)
-        t2a = along_z(t0[:, :64], 2)
-        t2b = along_z(t0[:, 64:], -2)
+        t2a = along_z(t0[:, :80], 2)
+        t2b = along_z(t0[:, 80:], -2)
 
     with jax.named_scope("weights"):
-        w_mine = spread(w_moved.reshape(192, 768), "x", NX)
+        along_x = [
+            shift(w_moved, ("x",), lambda i, step=step: ((i[0] - step) % NX,)) for step in (1, 2, 3)
+        ]
+        t2a, t2b, *along_x = lax.optimization_barrier((t2a, t2b, *along_x))
+        w_mine = jnp.stack([w_moved] + along_x)
         w_theirs = swap_cores(w_mine)
 
     with jax.named_scope("project"):
         part = kernel_call(
             partial_kernel,
             jax.ShapeDtypeStruct((CORES, NY, 128, 3 * DH), jnp.float32),
-            (where, t0, t1, t2a, t2b, t3, stats, gain, w_mine, w_theirs),
+            (where, t0, t1, t2a, t2b, t3, w_mine, w_theirs),
             scalars=1,
             scratch=[
                 pltpu.VMEM((NX, 384, 768), jnp.bfloat16),

time: 227 us -> 211 us (0.930)
  the two profiles are of different devices: /device:TPU:40 before, /device:TPU:16 now
where the time goes in v5:
time: 211 us; the launch traced here: 210 us
  waiting for transfers between devices  110 us (52%)
  starting transfers between devices  84 us (40%)
  local copies, waits for them, and re-layouts  6.72 us (3%)
  Pallas kernels  6.57 us (3%)
  other arithmetic  2.67 us (1%)
    ppermute x11, waiting for transfers between devices, shift(): return lax.ppermute(values, axes, pairs)  59.9 us
    ppermute x11, starting transfers between devices, shift(): return lax.ppermute(values, axes, pairs)  52.9 us
    all_to_all x3, waiting for transfers between devices, spread(): lax.all_to_all(jnp.broadcast_to(values[None], (count,) + values.shape), a...  31.8 us
    all_to_all x3, starting transfers between devices, spread(): lax.all_to_all(jnp.broadcast_to(values[None], (count,) + values.shape), a...  25.9 us
    all_to_all x1, waiting for transfers between devices, body(): lax.all_to_all(part, ('core', 'y'), 0, 0).reshape(CORES, NY, 128, 3 * DH)  18.4 us
    pallas_call x3, Pallas kernels, kernel_call(): pl.pallas_call(kernel, out_shape=out_shape, in_specs=[smem] * scalars + [...  6.57 us
    all_to_all x1, starting transfers between devices, body(): lax.all_to_all(part, ('core', 'y'), 0, 0).reshape(CORES, NY, 128, 3 * DH)  5.2 us
  transfers between devices with their start and end apart: 15, of which 9 were waited for; matrix products, arithmetic and copies ran while one was open for 0% of the time, Pallas kernels for 0%

profile of v5, /device:TPU:16, one launch (start us, length us, event | category | flops | bytes accessed | tf_op | source)
XLA Modules:
  0.0 210.3 jit_solution(16306413897069762379)
XLA Ops:
  0.0 1.1 convert_reduce_fusion
  1.1 0.7 pad_maximum_fusion.1
  2.4 8.9 %all-to-all-start = ((f32[4,1,768]{2,1,0:T(1,128)}), f32[4,1,768]{2,1,0:T(1,128)S(1)}, u32[]{:S(2)}, u32[]{:S(2)}) async-start(f32[4,1,768]{2,1,0:T(1,128)} %broadcast_in_dim.10), calls=%async_computation | async-start | bytes 24576 | tf_op jit(solution)/shard_map/norm/all_to_all | solution.py:49
  12.0 2.3 %all-to-all-done = f32[4,1,768]{2,1,0:T(1,128)S(1)} async-done(((f32[4,1,768]{2,1,0:T(1,128)}), f32[4,1,768]{2,1,0:T(1,128)S(1)}, u32[]{:S(2)}, u32[]{:S(2)}) %all-to-all-start) | async-done | bytes 12320 | tf_op jit(solution)/shard_map/norm/all_to_all | solution.py:49
  14.3 1.1 concatenate.55
  15.4 0.8 broadcast_in_dim.13
  16.2 10.9 %all-to-all-start.1 = ((bf16[4,144,384]{2,1,0:T(8,128)(2,1)}), bf16[4,144,384]{2,1,0:T(8,128)(2,1)S(1)}, u32[]{:S(2)}, u32[]{:S(2)}) async-start(bf16[4,144,384]{2,1,0:T(8,128)(2,1)} %broadcast_in_dim.13), calls=%async_computation.1 | async-start | bytes 884736 | tf_op jit(solution)/shard_map/tokens/all_to_all | solution.py:49
  27.2 14.5 %collective-permute-start = (bf16[3,192,256]{2,1,0:T(8,128)(2,1)S(1)}, bf16[3,192,256]{2,1,0:T(8,128)(2,1)S(1)}, u32[]{:S(2)}, u32[]{:S(2)}) collective-permute-start(bf16[3,192,256]{2,1,0:T(8,128)(2,1)S(1)} %bitcast.37), channel_id=1, source_target_pairs={{0,0},{1,32},{2,64},{3,96},{4,36},{5,68},{6,100},{7,4},{8,72},{9,1... | collective-permute-start | bytes 884744 | tf_op jit(solution)/shard_map/weights/ppermute | solution.py:25
  41.7 33.6 %collective-permute-done = bf16[3,192,256]{2,1,0:T(8,128)(2,1)S(1)} collective-permute-done((bf16[3,192,256]{2,1,0:T(8,128)(2,1)S(1)}, bf16[3,192,256]{2,1,0:T(8,128)(2,1)S(1)}, u32[]{:S(2)}, u32[]{:S(2)}) %collective-permute-start) | collective-permute-done | bytes 294944 | tf_op jit(solution)/shard_map/weights/ppermute | solution.py:25
  75.2 3.4 %collective-permute-start.6 = (bf16[3,192,256]{2,1,0:T(8,128)(2,1)S(1)}, bf16[3,192,256]{2,1,0:T(8,128)(2,1)S(1)}, u32[]{:S(2)}, u32[]{:S(2)}) collective-permute-start(bf16[3,192,256]{2,1,0:T(8,128)(2,1)S(1)} %collective-permute-done), channel_id=1, source_target_pairs={{0,128},{128,256},{256,384},{384,0},{1,129},{129,257},{257,385},{3... | collective-permute-start | bytes 884744 | tf_op jit(solution)/shard_map/weights/ppermute | solution.py:25
  78.7 4.7 %collective-permute-start.5 = (bf16[3,192,256]{2,1,0:T(8,128)(2,1)S(1)}, bf16[3,192,256]{2,1,0:T(8,128)(2,1)S(1)}, u32[]{:S(2)}, u32[]{:S(2)}) collective-permute-start(bf16[3,192,256]{2,1,0:T(8,128)(2,1)S(1)} %collective-permute-done), channel_id=1, source_target_pairs={{0,256},{128,384},{256,0},{384,128},{1,257},{129,385},{257,1},{385... | collective-permute-start | bytes 884744 | tf_op jit(solution)/shard_map/weights/ppermute | solution.py:25
  83.4 3.3 %collective-permute-start.4 = (bf16[3,192,256]{2,1,0:T(8,128)(2,1)S(1)}, bf16[3,192,256]{2,1,0:T(8,128)(2,1)S(1)}, u32[]{:S(2)}, u32[]{:S(2)}) collective-permute-start(bf16[3,192,256]{2,1,0:T(8,128)(2,1)S(1)} %collective-permute-done), channel_id=1, source_target_pairs={{0,384},{128,0},{256,128},{384,256},{1,385},{129,1},{257,129},{385... | collective-permute-start | bytes 884744 | tf_op jit(solution)/shard_map/weights/ppermute | solution.py:25
  86.8 1.9 collective-permute-start.2
  88.7 6.0 %collective-permute-start.3 = (bf16[4,64,384]{2,1,0:T(8,128)(2,1)S(1)}, bf16[4,64,384]{2,1,0:T(8,128)(2,1)S(1)}, u32[]{:S(2)}, u32[]{:S(2)}) collective-permute-start(bf16[4,64,384]{2,1,0:T(8,128)(2,1)S(1)} %slice.22), channel_id=1, source_target_pairs={{0,104},{4,108},{8,0},{12,4},{32,8},{36,12},{40,32},{44,36},{64,40... | collective-permute-start | bytes 589832 | tf_op jit(solution)/shard_map/tokens/ppermute | solution.py:25
  94.8 5.0 %collective-permute-done.3.t2b = bf16[4,64,384]{2,1,0:T(8,128)(2,1)S(1)} collective-permute-done((bf16[4,64,384]{2,1,0:T(8,128)(2,1)S(1)}, bf16[4,64,384]{2,1,0:T(8,128)(2,1)S(1)}, u32[]{:S(2)}, u32[]{:S(2)}) %collective-permute-start.3) | collective-permute-done | bytes 196640 | tf_op jit(solution)/shard_map/tokens/ppermute | solution.py:25
  100.6 1.9 collective-permute-start.8
  102.6 1.9 collective-permute-start.7
  104.5 5.1 %collective-permute-start.1 = (bf16[4,144,384]{2,1,0:T(8,128)(2,1)S(1)}, bf16[4,144,384]{2,1,0:T(8,128)(2,1)}, u32[]{:S(2)}, u32[]{:S(2)}) collective-permute-start(bf16[4,144,384]{2,1,0:T(8,128)(2,1)S(1)} %all-to-all-done.1.t0), channel_id=1, source_target_pairs={{0,108},{4,0},{8,4},{12,8},{32,12},{36,32},{40,36},{44,40},{64,44}... | collective-permute-start | bytes 1327112 | tf_op jit(solution)/shard_map/tokens/ppermute | solution.py:25
  109.7 8.5 %collective-permute-done.7.t3 = bf16[4,144,384]{2,1,0:T(8,128)(2,1)S(1)} collective-permute-done((bf16[4,144,384]{2,1,0:T(8,128)(2,1)S(1)}, bf16[4,144,384]{2,1,0:T(8,128)(2,1)S(1)}, u32[]{:S(2)}, u32[]{:S(2)}) %collective-permute-start.7) | collective-permute-done | bytes 442400 | tf_op jit(solution)/shard_map/tokens/ppermute | solution.py:25
  118.2 1.2 collective-permute-done.1.t1
  119.4 0.9 copy-done.1
  120.3 4.3 %project.2 = f32[2,4,128,384]{3,2,1,0:T(8,128)} custom-call(s32[4]{0:T(128)S(1)} %pad_add_fusion.where, bf16[4,144,384]{2,1,0:T(8,128)(2,1)S(1)} %all-to-all-done.1.t0, bf16[4,144,384]{2,1,0:T(8,128)(2,1)} %collective-permute-done.1.t1, bf16[4,80,384]{2,1,0:T(8,128)(2,1)S(1)} %collective-permute-done.2.t2a, bf16[4,64,384]{2,1,0:T(8,128)(2,1)S(1)} %copy-done.1, ...), custom_call_target="tpu_custom_call" | custom-call | tf_op jit(solution)/shard_map/project/pallas_call | solution.py:149
  124.6 5.2 %all-to-all-start.2 = ((f32[8,128,384]{2,1,0:T(8,128)}), f32[8,128,384]{2,1,0:T(8,128)S(1)}, u32[]{:S(2)}, u32[]{:S(2)}) async-start(f32[8,128,384]{2,1,0:T(8,128)} %bitcast.15), calls=%async_computation.2 | async-start | bytes 3145728 | tf_op jit(solution)/shard_map/project/all_to_all | solution.py:218
  129.9 18.4 %all-to-all-done.2 = f32[8,128,384]{2,1,0:T(8,128)S(1)} async-done(((f32[8,128,384]{2,1,0:T(8,128)}), f32[8,128,384]{2,1,0:T(8,128)S(1)}, u32[]{:S(2)}, u32[]{:S(2)}) %all-to-all-start.2) | async-done | bytes 1572896 | tf_op jit(solution)/shard_map/project/all_to_all | solution.py:218
  148.5 1.8 broadcast_in_dim.14
  150.3 6.1 %all-to-all-start.3 = ((bf16[16,2,256,128]{3,2,1,0:T(8,128)(2,1)}), bf16[16,2,256,128]{3,2,1,0:T(8,128)(2,1)S(1)}, u32[]{:S(2)}, u32[]{:S(2)}) async-start(bf16[16,2,256,128]{3,2,1,0:T(8,128)(2,1)} %broadcast_in_dim.14), calls=%async_computation.3 | async-start | bytes 4194304 | tf_op jit(solution)/shard_map/keys/all_to_all | solution.py:49
  156.4 29.6 %all-to-all-done.3.kv = bf16[16,2,256,128]{3,2,1,0:T(8,128)(2,1)S(1)} async-done(((bf16[16,2,256,128]{3,2,1,0:T(8,128)(2,1)}), bf16[16,2,256,128]{3,2,1,0:T(8,128)(2,1)S(1)}, u32[]{:S(2)}, u32[]{:S(2)}) %all-to-all-start.3) | async-done | bytes 2097184 | tf_op jit(solution)/shard_map/keys/all_to_all | solution.py:49
  185.9 2.1 attend.1
  188.0 7.5 %collective-permute-start.9 = (bf16[128,128]{1,0:T(8,128)(2,1)S(1)}, bf16[128,128]{1,0:T(8,128)(2,1)S(1)}, u32[]{:S(2)}, u32[]{:S(2)}) collective-permute-start(bf16[128,128]{1,0:T(8,128)(2,1)S(1)} %get-tuple-element.25), channel_id=1, source_target_pairs={{0,0},{1,32},{2,64},{3,96},{4,39},{5,71},{6,103},{7,7},{8,74},{9,1... | collective-permute-start | bytes 98312 | tf_op jit(solution)/shard_map/home/ppermute | solution.py:25
  195.5 2.5 %collective-permute-start.10 = (bf16[128,128]{1,0:T(8,128)(2,1)S(1)}, bf16[128,128]{1,0:T(8,128)(2,1)S(1)}, u32[]{:S(2)}, u32[]{:S(2)}) collective-permute-start(bf16[128,128]{1,0:T(8,128)(2,1)S(1)} %get-tuple-element.26), channel_id=1, source_target_pairs={{0,16},{1,48},{2,80},{3,112},{4,55},{5,87},{6,119},{7,23},{8,90},{... | collective-permute-start | bytes 98312 | tf_op jit(solution)/shard_map/home/ppermute | solution.py:25
  198.0 4.5 %collective-permute-done.9 = bf16[128,128]{1,0:T(8,128)(2,1)S(1)} collective-permute-done((bf16[128,128]{1,0:T(8,128)(2,1)S(1)}, bf16[128,128]{1,0:T(8,128)(2,1)S(1)}, u32[]{:S(2)}, u32[]{:S(2)}) %collective-permute-start.9) | collective-permute-done | bytes 32800 | tf_op jit(solution)/shard_map/home/ppermute | solution.py:25
  202.5 7.2 %collective-permute-done.10 = bf16[128,128]{1,0:T(8,128)(2,1)S(1)} collective-permute-done((bf16[128,128]{1,0:T(8,128)(2,1)S(1)}, bf16[128,128]{1,0:T(8,128)(2,1)S(1)}, u32[]{:S(2)}, u32[]{:S(2)}) %collective-permute-start.10) | collective-permute-done | bytes 32800 | tf_op jit(solution)/shard_map/home/ppermute | solution.py:25
  (28 shorter events, 3.2 us)
Async XLA Ops:
  0.0 27.2 %copy-start.2 = (bf16[192,3,256]{2,0,1:T(8,128)(2,1)S(1)}, bf16[192,3,256]{2,0,1:T(8,128)(2,1)}, u32[]{:S(2)}) copy-start(bf16[192,3,256]{2,0,1:T(8,128)(2,1)} %param.7) | copy-start | bytes 884740
  2.4 11.9 %all-to-all-start = ((f32[4,1,768]{2,1,0:T(1,128)}), f32[4,1,768]{2,1,0:T(1,128)S(1)}, u32[]{:S(2)}, u32[]{:S(2)}) async-start(f32[4,1,768]{2,1,0:T(1,128)} %broadcast_in_dim.10), calls=%async_computation | async-start | bytes 24576 | tf_op jit(solution)/shard_map/norm/all_to_all | solution.py:49
  16.2 59.0 %all-to-all-start.1 = ((bf16[4,144,384]{2,1,0:T(8,128)(2,1)}), bf16[4,144,384]{2,1,0:T(8,128)(2,1)S(1)}, u32[]{:S(2)}, u32[]{:S(2)}) async-start(bf16[4,144,384]{2,1,0:T(8,128)(2,1)} %broadcast_in_dim.13), calls=%async_computation.1 | async-start | bytes 884736 | tf_op jit(solution)/shard_map/tokens/all_to_all | solution.py:49
  27.2 48.1 %collective-permute-start = (bf16[3,192,256]{2,1,0:T(8,128)(2,1)S(1)}, bf16[3,192,256]{2,1,0:T(8,128)(2,1)S(1)}, u32[]{:S(2)}, u32[]{:S(2)}) collective-permute-start(bf16[3,192,256]{2,1,0:T(8,128)(2,1)S(1)} %bitcast.37), channel_id=1, source_target_pairs={{0,0},{1,32},{2,64},{3,96},{4,36},{5,68},{6,100},{7,4},{8,72},{9,1... | collective-permute-start | bytes 884744 | tf_op jit(solution)/shard_map/weights/ppermute | solution.py:25
  75.2 25.2 %collective-permute-start.6 = (bf16[3,192,256]{2,1,0:T(8,128)(2,1)S(1)}, bf16[3,192,256]{2,1,0:T(8,128)(2,1)S(1)}, u32[]{:S(2)}, u32[]{:S(2)}) collective-permute-start(bf16[3,192,256]{2,1,0:T(8,128)(2,1)S(1)} %collective-permute-done), channel_id=1, source_target_pairs={{0,128},{128,256},{256,384},{384,0},{1,129},{129,257},{257,385},{3... | collective-permute-start | bytes 884744 | tf_op jit(solution)/shard_map/weights/ppermute | solution.py:25
  78.7 21.8 %collective-permute-start.5 = (bf16[3,192,256]{2,1,0:T(8,128)(2,1)S(1)}, bf16[3,192,256]{2,1,0:T(8,128)(2,1)S(1)}, u32[]{:S(2)}, u32[]{:S(2)}) collective-permute-start(bf16[3,192,256]{2,1,0:T(8,128)(2,1)S(1)} %collective-permute-done), channel_id=1, source_target_pairs={{0,256},{128,384},{256,0},{384,128},{1,257},{129,385},{257,1},{385... | collective-permute-start | bytes 884744 | tf_op jit(solution)/shard_map/weights/ppermute | solution.py:25
  83.4 17.1 %collective-permute-start.4 = (bf16[3,192,256]{2,1,0:T(8,128)(2,1)S(1)}, bf16[3,192,256]{2,1,0:T(8,128)(2,1)S(1)}, u32[]{:S(2)}, u32[]{:S(2)}) collective-permute-start(bf16[3,192,256]{2,1,0:T(8,128)(2,1)S(1)} %collective-permute-done), channel_id=1, source_target_pairs={{0,384},{128,0},{256,128},{384,256},{1,385},{129,1},{257,129},{385... | collective-permute-start | bytes 884744 | tf_op jit(solution)/shard_map/weights/ppermute | solution.py:25
  86.8 13.7 %collective-permute-start.2 = (bf16[4,80,384]{2,1,0:T(8,128)(2,1)S(1)}, bf16[4,80,384]{2,1,0:T(8,128)(2,1)S(1)}, u32[]{:S(2)}, u32[]{:S(2)}) collective-permute-start(bf16[4,80,384]{2,1,0:T(8,128)(2,1)S(1)} %slice.21), channel_id=1, source_target_pairs={{0,8},{4,12},{8,32},{12,36},{32,40},{36,44},{40,64},{44,68},{64,72... | collective-permute-start | bytes 737288 | tf_op jit(solution)/shard_map/tokens/ppermute | solution.py:25
  88.7 11.0 %collective-permute-start.3 = (bf16[4,64,384]{2,1,0:T(8,128)(2,1)S(1)}, bf16[4,64,384]{2,1,0:T(8,128)(2,1)S(1)}, u32[]{:S(2)}, u32[]{:S(2)}) collective-permute-start(bf16[4,64,384]{2,1,0:T(8,128)(2,1)S(1)} %slice.22), channel_id=1, source_target_pairs={{0,104},{4,108},{8,0},{12,4},{32,8},{36,12},{40,32},{44,36},{64,40... | collective-permute-start | bytes 589832 | tf_op jit(solution)/shard_map/tokens/ppermute | solution.py:25
  99.8 0.7 copy-start
  100.6 18.8 %collective-permute-start.8 = (bf16[4,3,192,256]{3,2,1,0:T(8,128)(2,1)S(1)}, bf16[4,3,192,256]{3,2,1,0:T(8,128)(2,1)S(1)}, u32[]{:S(2)}, u32[]{:S(2)}) collective-permute-start(bf16[4,3,192,256]{3,2,1,0:T(8,128)(2,1)S(1)} %pad_maximum_fusion.w_mine), channel_id=1, source_target_pairs={{0,16},{16,0},{1,17},{17,1},{2,18},{18,2},{3,19},{19,3},{4,20},{20... | collective-permute-start | bytes 3538952 | tf_op jit(solution)/shard_map/weights/ppermute | solution.py:25
  102.6 15.7 %collective-permute-start.7 = (bf16[4,144,384]{2,1,0:T(8,128)(2,1)S(1)}, bf16[4,144,384]{2,1,0:T(8,128)(2,1)S(1)}, u32[]{:S(2)}, u32[]{:S(2)}) collective-permute-start(bf16[4,144,384]{2,1,0:T(8,128)(2,1)S(1)} %all-to-all-done.1.t0), channel_id=1, source_target_pairs={{0,4},{4,8},{8,12},{12,32},{32,36},{36,40},{40,44},{44,64},{64,68}... | collective-permute-start | bytes 1327112 | tf_op jit(solution)/shard_map/tokens/ppermute | solution.py:25
  104.5 14.9 %collective-permute-start.1 = (bf16[4,144,384]{2,1,0:T(8,128)(2,1)S(1)}, bf16[4,144,384]{2,1,0:T(8,128)(2,1)}, u32[]{:S(2)}, u32[]{:S(2)}) collective-permute-start(bf16[4,144,384]{2,1,0:T(8,128)(2,1)S(1)} %all-to-all-done.1.t0), channel_id=1, source_target_pairs={{0,108},{4,0},{8,4},{12,8},{32,12},{36,32},{40,36},{44,40},{64,44}... | collective-permute-start | bytes 1327112 | tf_op jit(solution)/shard_map/tokens/ppermute | solution.py:25
  119.4 0.9 copy-start.1
  124.6 23.6 %all-to-all-start.2 = ((f32[8,128,384]{2,1,0:T(8,128)}), f32[8,128,384]{2,1,0:T(8,128)S(1)}, u32[]{:S(2)}, u32[]{:S(2)}) async-start(f32[8,128,384]{2,1,0:T(8,128)} %bitcast.15), calls=%async_computation.2 | async-start | bytes 3145728 | tf_op jit(solution)/shard_map/project/all_to_all | solution.py:218
  150.3 35.6 %all-to-all-start.3 = ((bf16[16,2,256,128]{3,2,1,0:T(8,128)(2,1)}), bf16[16,2,256,128]{3,2,1,0:T(8,128)(2,1)S(1)}, u32[]{:S(2)}, u32[]{:S(2)}) async-start(bf16[16,2,256,128]{3,2,1,0:T(8,128)(2,1)} %broadcast_in_dim.14), calls=%async_computation.3 | async-start | bytes 4194304 | tf_op jit(solution)/shard_map/keys/all_to_all | solution.py:49
  188.0 14.5 %collective-permute-start.9 = (bf16[128,128]{1,0:T(8,128)(2,1)S(1)}, bf16[128,128]{1,0:T(8,128)(2,1)S(1)}, u32[]{:S(2)}, u32[]{:S(2)}) collective-permute-start(bf16[128,128]{1,0:T(8,128)(2,1)S(1)} %get-tuple-element.25), channel_id=1, source_target_pairs={{0,0},{1,32},{2,64},{3,96},{4,39},{5,71},{6,103},{7,7},{8,74},{9,1... | collective-permute-start | bytes 98312 | tf_op jit(solution)/shard_map/home/ppermute | solution.py:25
  195.5 14.2 %collective-permute-start.10 = (bf16[128,128]{1,0:T(8,128)(2,1)S(1)}, bf16[128,128]{1,0:T(8,128)(2,1)S(1)}, u32[]{:S(2)}, u32[]{:S(2)}) collective-permute-start(bf16[128,128]{1,0:T(8,128)(2,1)S(1)} %get-tuple-element.26), channel_id=1, source_target_pairs={{0,16},{1,48},{2,80},{3,112},{4,55},{5,87},{6,119},{7,23},{8,90},{... | collective-permute-start | bytes 98312 | tf_op jit(solution)/shard_map/home/ppermute | solution.py:25

commit v6 on v5

--- a/solution.py
+++ b/solution.py
@@ -189,19 +189,22 @@
         )
 
     with jax.named_scope("tokens"):
-        t0, w_moved = lax.optimization_barrier((spread(extended, "zh", NZH), w_moved))
+        extended, w_moved = lax.optimization_barrier((extended, w_moved))
+        t0 = spread(extended, "zh", NZH)
+
+    with jax.named_scope("weights"):
+        along_x = [
+            shift(w_moved, ("x",), lambda i, step=step: ((i[0] - step) % NX,)) for step in (1, 2, 3)
+        ]
+        t0, *along_x = lax.optimization_barrier((t0, *along_x))
+        w_mine = jnp.stack([w_moved] + along_x)
+        w_theirs = swap_cores(w_mine)
+
+    with jax.named_scope("tokens"):
         t1 = along_z(t0, -1)
         t3 = along_z(t0, 1)
         t2a = along_z(t0[:, :80], 2)
         t2b = along_z(t0[:, 80:], -2)
-
-    with jax.named_scope("weights"):
-        along_x = [
-            shift(w_moved, ("x",), lambda i, step=step: ((i[0] - step) % NX,)) for step in (1, 2, 3)
-        ]
-        t2a, t2b, *along_x = lax.optimization_barrier((t2a, t2b, *along_x))
-        w_mine = jnp.stack([w_moved] + along_x)
-        w_theirs = swap_cores(w_mine)
 
     with jax.named_scope("project"):
         part = kernel_call(

time: 211 us -> 197 us (0.934)
  waiting for transfers between devices: 110 us -> 98.8 us
  starting transfers between devices: 84 us -> 81.8 us
    ppermute x11, waiting for transfers between devices: 59.9 us -> 48.9 us  [shift(): return lax.ppermute(values, axes, pairs)]
    all_to_all x3, starting transfers between devices: 25.9 us -> 20.5 us  [spread(): lax.all_to_all(jnp.broadcast_to(values[None], (count,) + values.shape), a...]
    all_to_all x1, starting transfers between devices: 5.2 us -> 9.65 us  [body(): lax.all_to_all(part, ('core', 'y'), 0, 0).reshape(CORES, NY, 128, 3 * DH)]
  transfers between devices with their start and end apart: 15 -> 15, of which waited for: 9 -> 10; matrix products, arithmetic and copies ran while one was open for 0% -> 2% of each run, Pallas kernels for 0% -> 0%
where the time goes in v6:
time: 197 us; the launch traced here: 196 us
  waiting for transfers between devices  98.8 us (50%)
  starting transfers between devices  81.8 us (42%)
  Pallas kernels  6.61 us (3%)
  local copies, waits for them, and re-layouts  6.48 us (3%)
  other arithmetic  2.62 us (1%)
    ppermute x11, starting transfers between devices, shift(): return lax.ppermute(values, axes, pairs)  51.6 us
    ppermute x11, waiting for transfers between devices, shift(): return lax.ppermute(values, axes, pairs)  48.9 us
    all_to_all x3, waiting for transfers between devices, spread(): lax.all_to_all(jnp.broadcast_to(values[None], (count,) + values.shape), a...  31.5 us
    all_to_all x3, starting transfers between devices, spread(): lax.all_to_all(jnp.broadcast_to(values[None], (count,) + values.shape), a...  20.5 us
    all_to_all x1, waiting for transfers between devices, body(): lax.all_to_all(part, ('core', 'y'), 0, 0).reshape(CORES, NY, 128, 3 * DH)  18.4 us
    all_to_all x1, starting transfers between devices, body(): lax.all_to_all(part, ('core', 'y'), 0, 0).reshape(CORES, NY, 128, 3 * DH)  9.65 us
    pallas_call x3, Pallas kernels, kernel_call(): pl.pallas_call(kernel, out_shape=out_shape, in_specs=[smem] * scalars + [...  6.61 us
  transfers between devices with their start and end apart: 15, of which 10 were waited for; matrix products, arithmetic and copies ran while one was open for 2% of the time, Pallas kernels for 0%

profile of v6, /device:TPU:16, one launch (start us, length us, event | category | flops | bytes accessed | tf_op | source)
XLA Modules:
  0.0 196.5 jit_solution(16480926236276172084)
XLA Ops:
  0.0 1.0 convert_reduce_fusion
  1.0 0.7 pad_maximum_fusion.1
  2.3 8.9 %all-to-all-start = ((f32[4,1,768]{2,1,0:T(1,128)}), f32[4,1,768]{2,1,0:T(1,128)S(1)}, u32[]{:S(2)}, u32[]{:S(2)}) async-start(f32[4,1,768]{2,1,0:T(1,128)} %broadcast_in_dim.10), calls=%async_computation | async-start | bytes 24576 | tf_op jit(solution)/shard_map/norm/all_to_all | solution.py:49
  11.3 11.0 %collective-permute-start = (bf16[3,192,256]{2,1,0:T(8,128)(2,1)}, bf16[3,192,256]{2,1,0:T(8,128)(2,1)S(1)}, u32[]{:S(2)}, u32[]{:S(2)}) collective-permute-start(bf16[3,192,256]{2,1,0:T(8,128)(2,1)} %bitcast.37), channel_id=1, source_target_pairs={{0,0},{1,32},{2,64},{3,96},{4,36},{5,68},{6,100},{7,4},{8,72},{9,1... | collective-permute-start | bytes 884744 | tf_op jit(solution)/shard_map/weights/ppermute | solution.py:25
  23.0 1.1 concatenate.55
  24.1 19.7 %collective-permute-done = bf16[3,192,256]{2,1,0:T(8,128)(2,1)S(1)} collective-permute-done((bf16[3,192,256]{2,1,0:T(8,128)(2,1)}, bf16[3,192,256]{2,1,0:T(8,128)(2,1)S(1)}, u32[]{:S(2)}, u32[]{:S(2)}) %collective-permute-start) | collective-permute-done | bytes 294944 | tf_op jit(solution)/shard_map/weights/ppermute | solution.py:25
  43.8 0.8 broadcast_in_dim.13
  44.6 3.5 %all-to-all-start.1 = ((bf16[4,144,384]{2,1,0:T(8,128)(2,1)}), bf16[4,144,384]{2,1,0:T(8,128)(2,1)S(1)}, u32[]{:S(2)}, u32[]{:S(2)}) async-start(bf16[4,144,384]{2,1,0:T(8,128)(2,1)} %broadcast_in_dim.13), calls=%async_computation.1 | async-start | bytes 884736 | tf_op jit(solution)/shard_map/tokens/all_to_all | solution.py:49
  48.1 1.9 collective-permute-start.3
  50.0 4.1 %collective-permute-start.2 = (bf16[3,192,256]{2,1,0:T(8,128)(2,1)S(1)}, bf16[3,192,256]{2,1,0:T(8,128)(2,1)S(1)}, u32[]{:S(2)}, u32[]{:S(2)}) collective-permute-start(bf16[3,192,256]{2,1,0:T(8,128)(2,1)S(1)} %collective-permute-done), channel_id=1, source_target_pairs={{0,256},{128,384},{256,0},{384,128},{1,257},{129,385},{257,1},{385... | collective-permute-start | bytes 884744 | tf_op jit(solution)/shard_map/weights/ppermute | solution.py:25
  54.2 3.3 %collective-permute-start.1 = (bf16[3,192,256]{2,1,0:T(8,128)(2,1)S(1)}, bf16[3,192,256]{2,1,0:T(8,128)(2,1)S(1)}, u32[]{:S(2)}, u32[]{:S(2)}) collective-permute-start(bf16[3,192,256]{2,1,0:T(8,128)(2,1)S(1)} %collective-permute-done), channel_id=1, source_target_pairs={{0,384},{128,0},{256,128},{384,256},{1,385},{129,1},{257,129},{385... | collective-permute-start | bytes 884744 | tf_op jit(solution)/shard_map/weights/ppermute | solution.py:25
  57.5 4.2 %collective-permute-done.3 = bf16[3,192,256]{2,1,0:T(8,128)(2,1)S(1)} collective-permute-done((bf16[3,192,256]{2,1,0:T(8,128)(2,1)S(1)}, bf16[3,192,256]{2,1,0:T(8,128)(2,1)S(1)}, u32[]{:S(2)}, u32[]{:S(2)}) %collective-permute-start.3) | collective-permute-done | bytes 294944 | tf_op jit(solution)/shard_map/weights/ppermute | solution.py:25
  61.7 2.2 %collective-permute-done.1 = bf16[3,192,256]{2,1,0:T(8,128)(2,1)S(1)} collective-permute-done((bf16[3,192,256]{2,1,0:T(8,128)(2,1)S(1)}, bf16[3,192,256]{2,1,0:T(8,128)(2,1)S(1)}, u32[]{:S(2)}, u32[]{:S(2)}) %collective-permute-start.1) | collective-permute-done | bytes 294944 | tf_op jit(solution)/shard_map/weights/ppermute | solution.py:25
  63.9 4.4 %all-to-all-done.1.t0 = bf16[4,144,384]{2,1,0:T(8,128)(2,1)S(1)} async-done(((bf16[4,144,384]{2,1,0:T(8,128)(2,1)}), bf16[4,144,384]{2,1,0:T(8,128)(2,1)S(1)}, u32[]{:S(2)}, u32[]{:S(2)}) %all-to-all-start.1) | async-done | bytes 442400 | tf_op jit(solution)/shard_map/tokens/all_to_all | solution.py:49
  68.4 1.9 collective-permute-start.8
  70.4 1.9 collective-permute-start.7
  72.3 5.1 %collective-permute-start.4 = (bf16[4,144,384]{2,1,0:T(8,128)(2,1)S(1)}, bf16[4,144,384]{2,1,0:T(8,128)(2,1)}, u32[]{:S(2)}, u32[]{:S(2)}) collective-permute-start(bf16[4,144,384]{2,1,0:T(8,128)(2,1)S(1)} %all-to-all-done.1.t0), channel_id=1, source_target_pairs={{0,108},{4,0},{8,4},{12,8},{32,12},{36,32},{40,36},{44,40},{64,44}... | collective-permute-start | bytes 1327112 | tf_op jit(solution)/shard_map/tokens/ppermute | solution.py:25
  77.4 0.7 slice.21
  78.2 3.1 %collective-permute-start.5 = (bf16[4,80,384]{2,1,0:T(8,128)(2,1)}, bf16[4,80,384]{2,1,0:T(8,128)(2,1)S(1)}, u32[]{:S(2)}, u32[]{:S(2)}) collective-permute-start(bf16[4,80,384]{2,1,0:T(8,128)(2,1)} %slice.21), channel_id=1, source_target_pairs={{0,8},{4,12},{8,32},{12,36},{32,40},{36,44},{40,64},{44,68},{64,72... | collective-permute-start | bytes 737288 | tf_op jit(solution)/shard_map/tokens/ppermute | solution.py:25
  81.3 0.7 slice.22
  82.0 4.8 %collective-permute-start.6 = (bf16[4,64,384]{2,1,0:T(8,128)(2,1)}, bf16[4,64,384]{2,1,0:T(8,128)(2,1)}, u32[]{:S(2)}, u32[]{:S(2)}) collective-permute-start(bf16[4,64,384]{2,1,0:T(8,128)(2,1)} %slice.22), channel_id=1, source_target_pairs={{0,104},{4,108},{8,0},{12,4},{32,8},{36,12},{40,32},{44,36},{64,40... | collective-permute-start | bytes 589832 | tf_op jit(solution)/shard_map/tokens/ppermute | solution.py:25
  86.9 10.5 %collective-permute-done.6.t2b = bf16[4,64,384]{2,1,0:T(8,128)(2,1)} collective-permute-done((bf16[4,64,384]{2,1,0:T(8,128)(2,1)}, bf16[4,64,384]{2,1,0:T(8,128)(2,1)}, u32[]{:S(2)}, u32[]{:S(2)}) %collective-permute-start.6) | collective-permute-done | bytes 196640 | tf_op jit(solution)/shard_map/tokens/ppermute | solution.py:25
  97.7 4.3 %project.2 = f32[2,4,128,384]{3,2,1,0:T(8,128)} custom-call(s32[4]{0:T(128)S(1)} %pad_add_fusion.where, bf16[4,144,384]{2,1,0:T(8,128)(2,1)S(1)} %all-to-all-done.1.t0, bf16[4,144,384]{2,1,0:T(8,128)(2,1)} %collective-permute-done.4.t1, bf16[4,80,384]{2,1,0:T(8,128)(2,1)S(1)} %collective-permute-done.5.t2a, bf16[4,64,384]{2,1,0:T(8,128)(2,1)} %collective-permute-done.6.t2b, ...), custom_call_target="tpu_custom_call" | custom-call | tf_op jit(solution)/shard_map/project/pallas_call | solution.py:149
  102.1 9.7 %all-to-all-start.2 = ((f32[8,128,384]{2,1,0:T(8,128)}), f32[8,128,384]{2,1,0:T(8,128)S(1)}, u32[]{:S(2)}, u32[]{:S(2)}) async-start(f32[8,128,384]{2,1,0:T(8,128)} %bitcast.15), calls=%async_computation.2 | async-start | bytes 3145728 | tf_op jit(solution)/shard_map/project/all_to_all | solution.py:221
  111.7 18.4 %all-to-all-done.2 = f32[8,128,384]{2,1,0:T(8,128)S(1)} async-done(((f32[8,128,384]{2,1,0:T(8,128)}), f32[8,128,384]{2,1,0:T(8,128)S(1)}, u32[]{:S(2)}, u32[]{:S(2)}) %all-to-all-start.2) | async-done | bytes 1572896 | tf_op jit(solution)/shard_map/project/all_to_all | solution.py:221
  130.4 1.8 broadcast_in_dim.14
  132.2 8.1 %all-to-all-start.3 = ((bf16[16,2,256,128]{3,2,1,0:T(8,128)(2,1)}), bf16[16,2,256,128]{3,2,1,0:T(8,128)(2,1)S(1)}, u32[]{:S(2)}, u32[]{:S(2)}) async-start(bf16[16,2,256,128]{3,2,1,0:T(8,128)(2,1)} %broadcast_in_dim.14), calls=%async_computation.3 | async-start | bytes 4194304 | tf_op jit(solution)/shard_map/keys/all_to_all | solution.py:49
  140.3 27.1 %all-to-all-done.3.kv = bf16[16,2,256,128]{3,2,1,0:T(8,128)(2,1)S(1)} async-done(((bf16[16,2,256,128]{3,2,1,0:T(8,128)(2,1)}), bf16[16,2,256,128]{3,2,1,0:T(8,128)(2,1)S(1)}, u32[]{:S(2)}, u32[]{:S(2)}) %all-to-all-start.3) | async-done | bytes 2097184 | tf_op jit(solution)/shard_map/keys/all_to_all | solution.py:49
  167.4 2.1 %attend.1 = bf16[256,128]{1,0:T(8,128)(2,1)S(1)} custom-call(bf16[256,128]{1,0:T(8,128)(2,1)S(1)} %get-tuple-element.19.q, bf16[16,2,256,128]{3,2,1,0:T(8,128)(2,1)S(1)} %all-to-all-done.3.kv), custom_call_target="tpu_custom_call" | custom-call | tf_op jit(solution)/shard_map/attend/pallas_call | solution.py:149
  169.5 12.4 %collective-permute-start.9 = (bf16[128,128]{1,0:T(8,128)(2,1)S(1)}, bf16[128,128]{1,0:T(8,128)(2,1)S(1)}, u32[]{:S(2)}, u32[]{:S(2)}) collective-permute-start(bf16[128,128]{1,0:T(8,128)(2,1)S(1)} %get-tuple-element.23), channel_id=1, source_target_pairs={{0,0},{1,32},{2,64},{3,96},{4,39},{5,71},{6,103},{7,7},{8,74},{9,1... | collective-permute-start | bytes 98312 | tf_op jit(solution)/shard_map/home/ppermute | solution.py:25
  181.9 1.9 collective-permute-start.10
  184.0 11.8 %collective-permute-done.10 = bf16[128,128]{1,0:T(8,128)(2,1)S(1)} collective-permute-done((bf16[128,128]{1,0:T(8,128)(2,1)S(1)}, bf16[128,128]{1,0:T(8,128)(2,1)S(1)}, u32[]{:S(2)}, u32[]{:S(2)}) %collective-permute-start.10) | collective-permute-done | bytes 32800 | tf_op jit(solution)/shard_map/home/ppermute | solution.py:25
  (22 shorter events, 3.0 us)
Async XLA Ops:
  2.3 20.6 %all-to-all-start = ((f32[4,1,768]{2,1,0:T(1,128)}), f32[4,1,768]{2,1,0:T(1,128)S(1)}, u32[]{:S(2)}, u32[]{:S(2)}) async-start(f32[4,1,768]{2,1,0:T(1,128)} %broadcast_in_dim.10), calls=%async_computation | async-start | bytes 24576 | tf_op jit(solution)/shard_map/norm/all_to_all | solution.py:49
  11.3 32.6 %collective-permute-start = (bf16[3,192,256]{2,1,0:T(8,128)(2,1)}, bf16[3,192,256]{2,1,0:T(8,128)(2,1)S(1)}, u32[]{:S(2)}, u32[]{:S(2)}) collective-permute-start(bf16[3,192,256]{2,1,0:T(8,128)(2,1)} %bitcast.37), channel_id=1, source_target_pairs={{0,0},{1,32},{2,64},{3,96},{4,36},{5,68},{6,100},{7,4},{8,72},{9,1... | collective-permute-start | bytes 884744 | tf_op jit(solution)/shard_map/weights/ppermute | solution.py:25
  44.6 23.6 %all-to-all-start.1 = ((bf16[4,144,384]{2,1,0:T(8,128)(2,1)}), bf16[4,144,384]{2,1,0:T(8,128)(2,1)S(1)}, u32[]{:S(2)}, u32[]{:S(2)}) async-start(bf16[4,144,384]{2,1,0:T(8,128)(2,1)} %broadcast_in_dim.13), calls=%async_computation.1 | async-start | bytes 884736 | tf_op jit(solution)/shard_map/tokens/all_to_all | solution.py:49
  48.1 13.6 %collective-permute-start.3 = (bf16[3,192,256]{2,1,0:T(8,128)(2,1)S(1)}, bf16[3,192,256]{2,1,0:T(8,128)(2,1)S(1)}, u32[]{:S(2)}, u32[]{:S(2)}) collective-permute-start(bf16[3,192,256]{2,1,0:T(8,128)(2,1)S(1)} %collective-permute-done), channel_id=1, source_target_pairs={{0,128},{128,256},{256,384},{384,0},{1,129},{129,257},{257,385},{3... | collective-permute-start | bytes 884744 | tf_op jit(solution)/shard_map/weights/ppermute | solution.py:25
  50.0 11.6 %collective-permute-start.2 = (bf16[3,192,256]{2,1,0:T(8,128)(2,1)S(1)}, bf16[3,192,256]{2,1,0:T(8,128)(2,1)S(1)}, u32[]{:S(2)}, u32[]{:S(2)}) collective-permute-start(bf16[3,192,256]{2,1,0:T(8,128)(2,1)S(1)} %collective-permute-done), channel_id=1, source_target_pairs={{0,256},{128,384},{256,0},{384,128},{1,257},{129,385},{257,1},{385... | collective-permute-start | bytes 884744 | tf_op jit(solution)/shard_map/weights/ppermute | solution.py:25
  54.2 9.7 %collective-permute-start.1 = (bf16[3,192,256]{2,1,0:T(8,128)(2,1)S(1)}, bf16[3,192,256]{2,1,0:T(8,128)(2,1)S(1)}, u32[]{:S(2)}, u32[]{:S(2)}) collective-permute-start(bf16[3,192,256]{2,1,0:T(8,128)(2,1)S(1)} %collective-permute-done), channel_id=1, source_target_pairs={{0,384},{128,0},{256,128},{384,256},{1,385},{129,1},{257,129},{385... | collective-permute-start | bytes 884744 | tf_op jit(solution)/shard_map/weights/ppermute | solution.py:25
  68.4 29.3 %collective-permute-start.8 = (bf16[4,3,192,256]{3,2,1,0:T(8,128)(2,1)S(1)}, bf16[4,3,192,256]{3,2,1,0:T(8,128)(2,1)S(1)}, u32[]{:S(2)}, u32[]{:S(2)}) collective-permute-start(bf16[4,3,192,256]{3,2,1,0:T(8,128)(2,1)S(1)} %pad_maximum_fusion.w_mine), channel_id=1, source_target_pairs={{0,16},{16,0},{1,17},{17,1},{2,18},{18,2},{3,19},{19,3},{4,20},{20... | collective-permute-start | bytes 3538952 | tf_op jit(solution)/shard_map/weights/ppermute | solution.py:25
  70.4 27.4 %collective-permute-start.7 = (bf16[4,144,384]{2,1,0:T(8,128)(2,1)S(1)}, bf16[4,144,384]{2,1,0:T(8,128)(2,1)S(1)}, u32[]{:S(2)}, u32[]{:S(2)}) collective-permute-start(bf16[4,144,384]{2,1,0:T(8,128)(2,1)S(1)} %all-to-all-done.1.t0), channel_id=1, source_target_pairs={{0,4},{4,8},{8,12},{12,32},{32,36},{36,40},{40,44},{44,64},{64,68}... | collective-permute-start | bytes 1327112 | tf_op jit(solution)/shard_map/tokens/ppermute | solution.py:25
  72.3 25.4 %collective-permute-start.4 = (bf16[4,144,384]{2,1,0:T(8,128)(2,1)S(1)}, bf16[4,144,384]{2,1,0:T(8,128)(2,1)}, u32[]{:S(2)}, u32[]{:S(2)}) collective-permute-start(bf16[4,144,384]{2,1,0:T(8,128)(2,1)S(1)} %all-to-all-done.1.t0), channel_id=1, source_target_pairs={{0,108},{4,0},{8,4},{12,8},{32,12},{36,32},{40,36},{44,40},{64,44}... | collective-permute-start | bytes 1327112 | tf_op jit(solution)/shard_map/tokens/ppermute | solution.py:25
  78.2 19.6 %collective-permute-start.5 = (bf16[4,80,384]{2,1,0:T(8,128)(2,1)}, bf16[4,80,384]{2,1,0:T(8,128)(2,1)S(1)}, u32[]{:S(2)}, u32[]{:S(2)}) collective-permute-start(bf16[4,80,384]{2,1,0:T(8,128)(2,1)} %slice.21), channel_id=1, source_target_pairs={{0,8},{4,12},{8,32},{12,36},{32,40},{36,44},{40,64},{44,68},{64,72... | collective-permute-start | bytes 737288 | tf_op jit(solution)/shard_map/tokens/ppermute | solution.py:25
  82.0 15.4 %collective-permute-start.6 = (bf16[4,64,384]{2,1,0:T(8,128)(2,1)}, bf16[4,64,384]{2,1,0:T(8,128)(2,1)}, u32[]{:S(2)}, u32[]{:S(2)}) collective-permute-start(bf16[4,64,384]{2,1,0:T(8,128)(2,1)} %slice.22), channel_id=1, source_target_pairs={{0,104},{4,108},{8,0},{12,4},{32,8},{36,12},{40,32},{44,36},{64,40... | collective-permute-start | bytes 589832 | tf_op jit(solution)/shard_map/tokens/ppermute | solution.py:25
  102.1 28.1 %all-to-all-start.2 = ((f32[8,128,384]{2,1,0:T(8,128)}), f32[8,128,384]{2,1,0:T(8,128)S(1)}, u32[]{:S(2)}, u32[]{:S(2)}) async-start(f32[8,128,384]{2,1,0:T(8,128)} %bitcast.15), calls=%async_computation.2 | async-start | bytes 3145728 | tf_op jit(solution)/shard_map/project/all_to_all | solution.py:221
  132.2 35.2 %all-to-all-start.3 = ((bf16[16,2,256,128]{3,2,1,0:T(8,128)(2,1)}), bf16[16,2,256,128]{3,2,1,0:T(8,128)(2,1)S(1)}, u32[]{:S(2)}, u32[]{:S(2)}) async-start(bf16[16,2,256,128]{3,2,1,0:T(8,128)(2,1)} %broadcast_in_dim.14), calls=%async_computation.3 | async-start | bytes 4194304 | tf_op jit(solution)/shard_map/keys/all_to_all | solution.py:49
  169.5 14.6 %collective-permute-start.9 = (bf16[128,128]{1,0:T(8,128)(2,1)S(1)}, bf16[128,128]{1,0:T(8,128)(2,1)S(1)}, u32[]{:S(2)}, u32[]{:S(2)}) collective-permute-start(bf16[128,128]{1,0:T(8,128)(2,1)S(1)} %get-tuple-element.23), channel_id=1, source_target_pairs={{0,0},{1,32},{2,64},{3,96},{4,39},{5,71},{6,103},{7,7},{8,74},{9,1... | collective-permute-start | bytes 98312 | tf_op jit(solution)/shard_map/home/ppermute | solution.py:25
  181.9 13.9 %collective-permute-start.10 = (bf16[128,128]{1,0:T(8,128)(2,1)S(1)}, bf16[128,128]{1,0:T(8,128)(2,1)S(1)}, u32[]{:S(2)}, u32[]{:S(2)}) collective-permute-start(bf16[128,128]{1,0:T(8,128)(2,1)S(1)} %get-tuple-element.24), channel_id=1, source_target_pairs={{0,16},{1,48},{2,80},{3,112},{4,55},{5,87},{6,119},{7,23},{8,90},{... | collective-permute-start | bytes 98312 | tf_op jit(solution)/shard_map/home/ppermute | solution.py:25

commit v7 on v6

--- a/solution.py
+++ b/solution.py
@@ -41,6 +41,14 @@
     return shift(values, ("zh", "zl"), lambda i: divmod((i[0] * NZL + i[1] + step) % 16, NZL))
 
 
+def along_z_two(values):
+    def move(i):
+        step = 2 if i[1] % 2 == 0 else -2
+        return divmod((i[0] * NZL + i[1] + step) % 16, NZL)
+
+    return shift(values, ("zh", "zl"), move)
+
+
 def swap_cores(values):
     return shift(values, ("core",), lambda i: (1 - i[0],))
 
@@ -56,7 +64,7 @@
     return jnp.concatenate([high, mid, rest - mid]).astype(jnp.bfloat16)
 
 
-def partial_kernel(where, t0, t1, t2a, t2b, t3, w_mine, w_theirs, out, w, acc):
+def partial_kernel(where, t0, t1, t2, t3, w_mine, w_theirs, out, w, acc):
     zl, core, turn, x_here = where[0], where[1], where[2], where[3]
     half = w_mine.shape[2]
     for step in range(NX):
@@ -65,17 +73,10 @@
             cols = slice(s * 256, s * 256 + 256)
             w[x, pl.ds(pl.multiple_of(core * half, half), half), cols] = w_mine[step, s]
             w[x, pl.ds(pl.multiple_of((1 - core) * half, half), half), cols] = w_theirs[step, s]
-    tokens = (
-        ((t0, 128),),
-        ((t1, 128),),
-        ((t2a, 80), (t2b, 48)),
-        ((t3, 128),),
-    )
-    extras = ((t0, 128), (t1, 128), (t2b, 48), (t3, 128))
+    tokens = (t0, t1, t2, t3)
 
     def extra(slot, quarter):
-        ref, row = extras[slot]
-        return ref[quarter, row : row + 16].astype(jnp.float32)
+        return tokens[slot][quarter, 128:144].astype(jnp.float32)
 
     centers, scales = [], []
     for quarter in range(NZH):
@@ -90,8 +91,7 @@
         row_gain = extra(slot, 0)[2:3]
         normed = []
         for quarter in range(NZH):
-            x = [ref[quarter, :count].astype(jnp.float32) for ref, count in tokens[slot]]
-            x = x[0] if len(x) == 1 else jnp.concatenate(x, axis=0)
+            x = tokens[slot][quarter, :128].astype(jnp.float32)
             center = stats[:, quarter : quarter + 1]
             scale = stats[:, NZH + quarter : NZH + quarter + 1]
             normed.append(((x - center) * scale * row_gain).astype(jnp.bfloat16))
@@ -113,7 +113,7 @@
                         cols = slice(s * 256 + head * DH, s * 256 + head * DH + DH)
                         out[head, lax.rem(turn + quarter, NZH), :, s * DH : s * DH + DH] = total[
                             rows, cols
-                        ]
+                        ].astype(jnp.bfloat16)
 
 
 def heads_kernel(part, head_gain, q_out, kv_out):
@@ -124,10 +124,13 @@
 
     for source in range(2):
         rows = slice(source * 128, source * 128 + 128)
-        acc = part[source, 0] + part[source, 1] + part[source, 2] + part[source, 3]
+        acc = sum(part[source, y].astype(jnp.float32) for y in range(NY))
         q_out[rows] = head_norm(acc[:, :DH], head_gain[0])
-        kv_out[0, rows] = head_norm(acc[:, DH : 2 * DH], head_gain[1])
-        kv_out[1, rows] = acc[:, 2 * DH :].astype(jnp.bfloat16)
+        key = head_norm(acc[:, DH : 2 * DH], head_gain[1])
+        value = acc[:, 2 * DH :].astype(jnp.bfloat16)
+        for target in range(NX * NY):
+            kv_out[target, 0, rows] = key
+            kv_out[target, 1, rows] = value
 
 
 def attend_kernel(q, kv, out):
@@ -203,14 +206,13 @@
     with jax.named_scope("tokens"):
         t1 = along_z(t0, -1)
         t3 = along_z(t0, 1)
-        t2a = along_z(t0[:, :80], 2)
-        t2b = along_z(t0[:, 80:], -2)
+        t2 = along_z_two(t0)
 
     with jax.named_scope("project"):
         part = kernel_call(
             partial_kernel,
-            jax.ShapeDtypeStruct((CORES, NY, 128, 3 * DH), jnp.float32),
-            (where, t0, t1, t2a, t2b, t3, w_mine, w_theirs),
+            jax.ShapeDtypeStruct((CORES, NY, 128, 3 * DH), jnp.bfloat16),
+            (where, t0, t1, t2, t3, w_mine, w_theirs),
             scalars=1,
             scratch=[
                 pltpu.VMEM((NX, 384, 768), jnp.bfloat16),
@@ -223,13 +225,13 @@
             heads_kernel,
             (
                 jax.ShapeDtypeStruct((256, DH), jnp.bfloat16),
-                jax.ShapeDtypeStruct((2, 256, DH), jnp.bfloat16),
+                jax.ShapeDtypeStruct((NX * NY, 2, 256, DH), jnp.bfloat16),
             ),
             (part, head_gain),
         )
 
     with jax.named_scope("keys"):
-        kv_all = spread(kv, ("x", "y"), NX * NY)
+        kv_all = lax.all_to_all(kv, ("x", "y"), 0, 0)
 
     with jax.named_scope("attend"):
         out = kernel_call(

time: 197 us -> 191 us (0.970)
  starting transfers between devices: 81.8 us -> 77.7 us
    all_to_all x3 -> x2, waiting for transfers between devices: 31.5 us -> 4.41 us  [spread(): lax.all_to_all(jnp.broadcast_to(values[None], (count,) + values.shape), a...]
    all_to_all x0 -> x1, waiting for transfers between devices: none -> 27.1 us  [body(): kv_all = lax.all_to_all(kv, ('x', 'y'), 0, 0)]
    ppermute x11 -> x10, waiting for transfers between devices: 48.9 us -> 57.3 us  [shift(): return lax.ppermute(values, axes, pairs)]
    all_to_all x1, waiting for transfers between devices: 18.4 us -> 9.98 us  [body(): lax.all_to_all(part, ('core', 'y'), 0, 0).reshape(CORES, NY, 128, 3 * DH)]
    all_to_all x0 -> x1, starting transfers between devices: none -> 8.12 us  [body(): kv_all = lax.all_to_all(kv, ('x', 'y'), 0, 0)]
    all_to_all x3 -> x2, starting transfers between devices: 20.5 us -> 12.4 us  [spread(): lax.all_to_all(jnp.broadcast_to(values[None], (count,) + values.shape), a...]
    ppermute x11 -> x10, starting transfers between devices: 51.6 us -> 48 us  [shift(): return lax.ppermute(values, axes, pairs)]
  transfers between devices with their start and end apart: 15 -> 14, of which waited for: 10 -> 10; matrix products, arithmetic and copies ran while one was open for 2% -> 1% of each run, Pallas kernels for 0% -> 0%
where the time goes in v7:
time: 191 us
  waiting for transfers between devices  98.8 us (52%)
  starting transfers between devices  77.7 us (41%)
  Pallas kernels  6.57 us (3%)
  local copies, waits for them, and re-layouts  4.57 us (2%)
  other arithmetic  2.62 us (1%)
    ppermute x10, waiting for transfers between devices, shift(): return lax.ppermute(values, axes, pairs)  57.3 us
    ppermute x10, starting transfers between devices, shift(): return lax.ppermute(values, axes, pairs)  48 us
    all_to_all x1, waiting for transfers between devices, body(): kv_all = lax.all_to_all(kv, ('x', 'y'), 0, 0)  27.1 us
    all_to_all x2, starting transfers between devices, spread(): lax.all_to_all(jnp.broadcast_to(values[None], (count,) + values.shape), a...  12.4 us
    all_to_all x1, waiting for transfers between devices, body(): lax.all_to_all(part, ('core', 'y'), 0, 0).reshape(CORES, NY, 128, 3 * DH)  9.98 us
    all_to_all x1, starting transfers between devices, body(): lax.all_to_all(part, ('core', 'y'), 0, 0).reshape(CORES, NY, 128, 3 * DH)  9.2 us
    all_to_all x1, starting transfers between devices, body(): kv_all = lax.all_to_all(kv, ('x', 'y'), 0, 0)  8.12 us
    pallas_call x3, Pallas kernels, kernel_call(): pl.pallas_call(kernel, out_shape=out_shape, in_specs=[smem] * scalars + [...  6.57 us
  transfers between devices with their start and end apart: 14, of which 10 were waited for; matrix products, arithmetic and copies ran while one was open for 1% of the time, Pallas kernels for 0%

profile of v7, /device:TPU:16, one launch (start us, length us, event | category | flops | bytes accessed | tf_op | source)
XLA Modules:
  0.0 190.5 jit_solution(4684420434808637074)
XLA Ops:
  0.0 1.0 convert_reduce_fusion
  1.0 0.7 pad_maximum_fusion.1
  2.3 8.9 %all-to-all-start = ((f32[4,1,768]{2,1,0:T(1,128)}), f32[4,1,768]{2,1,0:T(1,128)S(1)}, u32[]{:S(2)}, u32[]{:S(2)}) async-start(f32[4,1,768]{2,1,0:T(1,128)} %broadcast_in_dim.8), calls=%async_computation | async-start | bytes 24576 | tf_op jit(solution)/shard_map/norm/all_to_all | solution.py:57
  11.3 11.0 %collective-permute-start = (bf16[3,192,256]{2,1,0:T(8,128)(2,1)}, bf16[3,192,256]{2,1,0:T(8,128)(2,1)S(1)}, u32[]{:S(2)}, u32[]{:S(2)}) collective-permute-start(bf16[3,192,256]{2,1,0:T(8,128)(2,1)} %bitcast.37), channel_id=1, source_target_pairs={{0,0},{1,32},{2,64},{3,96},{4,36},{5,68},{6,100},{7,4},{8,72},{9,1... | collective-permute-start | bytes 884744 | tf_op jit(solution)/shard_map/weights/ppermute | solution.py:25
  22.3 0.7 broadcast_in_dim.9
  23.0 1.1 concatenate.55
  24.1 19.7 %collective-permute-done = bf16[3,192,256]{2,1,0:T(8,128)(2,1)S(1)} collective-permute-done((bf16[3,192,256]{2,1,0:T(8,128)(2,1)}, bf16[3,192,256]{2,1,0:T(8,128)(2,1)S(1)}, u32[]{:S(2)}, u32[]{:S(2)}) %collective-permute-start) | collective-permute-done | bytes 294944 | tf_op jit(solution)/shard_map/weights/ppermute | solution.py:25
  43.8 0.8 broadcast_in_dim.11
  44.6 3.5 %all-to-all-start.1 = ((bf16[4,144,384]{2,1,0:T(8,128)(2,1)}), bf16[4,144,384]{2,1,0:T(8,128)(2,1)S(1)}, u32[]{:S(2)}, u32[]{:S(2)}) async-start(bf16[4,144,384]{2,1,0:T(8,128)(2,1)} %broadcast_in_dim.11), calls=%async_computation.1 | async-start | bytes 884736 | tf_op jit(solution)/shard_map/tokens/all_to_all | solution.py:57
  48.1 1.9 %collective-permute-start.3 = (bf16[3,192,256]{2,1,0:T(8,128)(2,1)S(1)}, bf16[3,192,256]{2,1,0:T(8,128)(2,1)S(1)}, u32[]{:S(2)}, u32[]{:S(2)}) collective-permute-start(bf16[3,192,256]{2,1,0:T(8,128)(2,1)S(1)} %collective-permute-done), channel_id=1, source_target_pairs={{0,128},{128,256},{256,384},{384,0},{1,129},{129,257},{257,385},{3... | collective-permute-start | bytes 884744 | tf_op jit(solution)/shard_map/weights/ppermute | solution.py:25
  50.0 4.1 %collective-permute-start.2 = (bf16[3,192,256]{2,1,0:T(8,128)(2,1)S(1)}, bf16[3,192,256]{2,1,0:T(8,128)(2,1)S(1)}, u32[]{:S(2)}, u32[]{:S(2)}) collective-permute-start(bf16[3,192,256]{2,1,0:T(8,128)(2,1)S(1)} %collective-permute-done), channel_id=1, source_target_pairs={{0,256},{128,384},{256,0},{384,128},{1,257},{129,385},{257,1},{385... | collective-permute-start | bytes 884744 | tf_op jit(solution)/shard_map/weights/ppermute | solution.py:25
  54.2 3.3 %collective-permute-start.1 = (bf16[3,192,256]{2,1,0:T(8,128)(2,1)S(1)}, bf16[3,192,256]{2,1,0:T(8,128)(2,1)S(1)}, u32[]{:S(2)}, u32[]{:S(2)}) collective-permute-start(bf16[3,192,256]{2,1,0:T(8,128)(2,1)S(1)} %collective-permute-done), channel_id=1, source_target_pairs={{0,384},{128,0},{256,128},{384,256},{1,385},{129,1},{257,129},{385... | collective-permute-start | bytes 884744 | tf_op jit(solution)/shard_map/weights/ppermute | solution.py:25
  57.5 4.2 %collective-permute-done.3 = bf16[3,192,256]{2,1,0:T(8,128)(2,1)S(1)} collective-permute-done((bf16[3,192,256]{2,1,0:T(8,128)(2,1)S(1)}, bf16[3,192,256]{2,1,0:T(8,128)(2,1)S(1)}, u32[]{:S(2)}, u32[]{:S(2)}) %collective-permute-start.3) | collective-permute-done | bytes 294944 | tf_op jit(solution)/shard_map/weights/ppermute | solution.py:25
  61.7 2.2 %collective-permute-done.1 = bf16[3,192,256]{2,1,0:T(8,128)(2,1)S(1)} collective-permute-done((bf16[3,192,256]{2,1,0:T(8,128)(2,1)S(1)}, bf16[3,192,256]{2,1,0:T(8,128)(2,1)S(1)}, u32[]{:S(2)}, u32[]{:S(2)}) %collective-permute-start.1) | collective-permute-done | bytes 294944 | tf_op jit(solution)/shard_map/weights/ppermute | solution.py:25
  63.9 4.4 %all-to-all-done.1.t0 = bf16[4,144,384]{2,1,0:T(8,128)(2,1)S(1)} async-done(((bf16[4,144,384]{2,1,0:T(8,128)(2,1)}), bf16[4,144,384]{2,1,0:T(8,128)(2,1)S(1)}, u32[]{:S(2)}, u32[]{:S(2)}) %all-to-all-start.1) | async-done | bytes 442400 | tf_op jit(solution)/shard_map/tokens/all_to_all | solution.py:57
  68.4 1.9 %collective-permute-start.7 = (bf16[4,3,192,256]{3,2,1,0:T(8,128)(2,1)S(1)}, bf16[4,3,192,256]{3,2,1,0:T(8,128)(2,1)S(1)}, u32[]{:S(2)}, u32[]{:S(2)}) collective-permute-start(bf16[4,3,192,256]{3,2,1,0:T(8,128)(2,1)S(1)} %pad_maximum_fusion.w_mine), channel_id=1, source_target_pairs={{0,16},{16,0},{1,17},{17,1},{2,18},{18,2},{3,19},{19,3},{4,20},{20... | collective-permute-start | bytes 3538952 | tf_op jit(solution)/shard_map/weights/ppermute | solution.py:25
  70.4 1.9 %collective-permute-start.6 = (bf16[4,144,384]{2,1,0:T(8,128)(2,1)S(1)}, bf16[4,144,384]{2,1,0:T(8,128)(2,1)S(1)}, u32[]{:S(2)}, u32[]{:S(2)}) collective-permute-start(bf16[4,144,384]{2,1,0:T(8,128)(2,1)S(1)} %all-to-all-done.1.t0), channel_id=1, source_target_pairs={{0,4},{4,8},{8,12},{12,32},{32,36},{36,40},{40,44},{44,64},{64,68}... | collective-permute-start | bytes 1327112 | tf_op jit(solution)/shard_map/tokens/ppermute | solution.py:25
  72.3 4.9 %collective-permute-start.5 = (bf16[4,144,384]{2,1,0:T(8,128)(2,1)S(1)}, bf16[4,144,384]{2,1,0:T(8,128)(2,1)}, u32[]{:S(2)}, u32[]{:S(2)}) collective-permute-start(bf16[4,144,384]{2,1,0:T(8,128)(2,1)S(1)} %all-to-all-done.1.t0), channel_id=1, source_target_pairs={{0,8},{4,108},{8,32},{12,4},{32,40},{36,12},{40,64},{44,36},{64,72... | collective-permute-start | bytes 1327112 | tf_op jit(solution)/shard_map/tokens/ppermute | solution.py:25
  77.1 2.2 %collective-permute-start.4 = (bf16[4,144,384]{2,1,0:T(8,128)(2,1)S(1)}, bf16[4,144,384]{2,1,0:T(8,128)(2,1)}, u32[]{:S(2)}, u32[]{:S(2)}) collective-permute-start(bf16[4,144,384]{2,1,0:T(8,128)(2,1)S(1)} %all-to-all-done.1.t0), channel_id=1, source_target_pairs={{0,108},{4,0},{8,4},{12,8},{32,12},{36,32},{40,36},{44,40},{64,44}... | collective-permute-start | bytes 1327112 | tf_op jit(solution)/shard_map/tokens/ppermute | solution.py:25
  79.5 6.6 %collective-permute-done.6.t3 = bf16[4,144,384]{2,1,0:T(8,128)(2,1)S(1)} collective-permute-done((bf16[4,144,384]{2,1,0:T(8,128)(2,1)S(1)}, bf16[4,144,384]{2,1,0:T(8,128)(2,1)S(1)}, u32[]{:S(2)}, u32[]{:S(2)}) %collective-permute-start.6) | collective-permute-done | bytes 442400 | tf_op jit(solution)/shard_map/tokens/ppermute | solution.py:25
  86.0 10.7 %collective-permute-done.5.t2 = bf16[4,144,384]{2,1,0:T(8,128)(2,1)} collective-permute-done((bf16[4,144,384]{2,1,0:T(8,128)(2,1)S(1)}, bf16[4,144,384]{2,1,0:T(8,128)(2,1)}, u32[]{:S(2)}, u32[]{:S(2)}) %collective-permute-start.5) | collective-permute-done | bytes 442400 | tf_op jit(solution)/shard_map/tokens/ppermute | solution.py:25
  96.7 2.0 %collective-permute-done.4.t1 = bf16[4,144,384]{2,1,0:T(8,128)(2,1)} collective-permute-done((bf16[4,144,384]{2,1,0:T(8,128)(2,1)S(1)}, bf16[4,144,384]{2,1,0:T(8,128)(2,1)}, u32[]{:S(2)}, u32[]{:S(2)}) %collective-permute-start.4) | collective-permute-done | bytes 442400 | tf_op jit(solution)/shard_map/tokens/ppermute | solution.py:25
  98.8 4.2 %project.2 = bf16[2,4,128,384]{3,2,1,0:T(8,128)(2,1)} custom-call(s32[4]{0:T(128)S(1)} %pad_add_fusion.where, bf16[4,144,384]{2,1,0:T(8,128)(2,1)S(1)} %all-to-all-done.1.t0, bf16[4,144,384]{2,1,0:T(8,128)(2,1)} %collective-permute-done.4.t1, bf16[4,144,384]{2,1,0:T(8,128)(2,1)} %collective-permute-done.5.t2, ...), custom_call_target="tpu_custom_call" | custom-call | tf_op jit(solution)/shard_map/project/pallas_call | solution.py:152
  102.9 9.2 %all-to-all-start.2 = ((bf16[8,128,384]{2,1,0:T(8,128)(2,1)}), bf16[8,128,384]{2,1,0:T(8,128)(2,1)S(1)}, u32[]{:S(2)}, u32[]{:S(2)}) async-start(bf16[8,128,384]{2,1,0:T(8,128)(2,1)} %bitcast.15), calls=%async_computation.2 | async-start | bytes 1572864 | tf_op jit(solution)/shard_map/project/all_to_all | solution.py:223
  112.1 10.0 %all-to-all-done.2 = bf16[8,128,384]{2,1,0:T(8,128)(2,1)S(1)} async-done(((bf16[8,128,384]{2,1,0:T(8,128)(2,1)}), bf16[8,128,384]{2,1,0:T(8,128)(2,1)S(1)}, u32[]{:S(2)}, u32[]{:S(2)}) %all-to-all-start.2) | async-done | bytes 786464 | tf_op jit(solution)/shard_map/project/all_to_all | solution.py:223
  122.5 1.3 copy-done
  123.8 8.1 %all-to-all-start.3 = ((bf16[16,2,256,128]{3,2,1,0:T(8,128)(2,1)}), bf16[16,2,256,128]{3,2,1,0:T(8,128)(2,1)S(1)}, u32[]{:S(2)}, u32[]{:S(2)}) async-start(bf16[16,2,256,128]{3,2,1,0:T(8,128)(2,1)} %copy-done), calls=%async_computation.3 | async-start | bytes 4194304 | tf_op jit(solution)/shard_map/keys/all_to_all | solution.py:234
  131.9 27.1 %all-to-all-done.3.kv = bf16[16,2,256,128]{3,2,1,0:T(8,128)(2,1)S(1)} async-done(((bf16[16,2,256,128]{3,2,1,0:T(8,128)(2,1)}), bf16[16,2,256,128]{3,2,1,0:T(8,128)(2,1)S(1)}, u32[]{:S(2)}, u32[]{:S(2)}) %all-to-all-start.3) | async-done | bytes 2097184 | tf_op jit(solution)/shard_map/keys/all_to_all | solution.py:234
  159.0 2.1 %attend.1 = bf16[256,128]{1,0:T(8,128)(2,1)S(1)} custom-call(bf16[256,128]{1,0:T(8,128)(2,1)S(1)} %get-tuple-element.19.q, bf16[16,2,256,128]{3,2,1,0:T(8,128)(2,1)S(1)} %all-to-all-done.3.kv), custom_call_target="tpu_custom_call" | custom-call | tf_op jit(solution)/shard_map/attend/pallas_call | solution.py:152
  161.1 14.8 %collective-permute-start.8 = (bf16[128,128]{1,0:T(8,128)(2,1)S(1)}, bf16[128,128]{1,0:T(8,128)(2,1)S(1)}, u32[]{:S(2)}, u32[]{:S(2)}) collective-permute-start(bf16[128,128]{1,0:T(8,128)(2,1)S(1)} %get-tuple-element.23), channel_id=1, source_target_pairs={{0,0},{1,32},{2,64},{3,96},{4,39},{5,71},{6,103},{7,7},{8,74},{9,1... | collective-permute-start | bytes 98312 | tf_op jit(solution)/shard_map/home/ppermute | solution.py:25
  175.9 1.9 %collective-permute-start.9 = (bf16[128,128]{1,0:T(8,128)(2,1)S(1)}, bf16[128,128]{1,0:T(8,128)(2,1)S(1)}, u32[]{:S(2)}, u32[]{:S(2)}) collective-permute-start(bf16[128,128]{1,0:T(8,128)(2,1)S(1)} %get-tuple-element.24), channel_id=1, source_target_pairs={{0,16},{1,48},{2,80},{3,112},{4,55},{5,87},{6,119},{7,23},{8,90},{... | collective-permute-start | bytes 98312 | tf_op jit(solution)/shard_map/home/ppermute | solution.py:25
  177.9 12.0 %collective-permute-done.9 = bf16[128,128]{1,0:T(8,128)(2,1)S(1)} collective-permute-done((bf16[128,128]{1,0:T(8,128)(2,1)S(1)}, bf16[128,128]{1,0:T(8,128)(2,1)S(1)}, u32[]{:S(2)}, u32[]{:S(2)}) %collective-permute-start.9) | collective-permute-done | bytes 32800 | tf_op jit(solution)/shard_map/home/ppermute | solution.py:25
  (19 shorter events, 1.9 us)
Async XLA Ops:
  2.3 20.6 %all-to-all-start = ((f32[4,1,768]{2,1,0:T(1,128)}), f32[4,1,768]{2,1,0:T(1,128)S(1)}, u32[]{:S(2)}, u32[]{:S(2)}) async-start(f32[4,1,768]{2,1,0:T(1,128)} %broadcast_in_dim.8), calls=%async_computation | async-start | bytes 24576 | tf_op jit(solution)/shard_map/norm/all_to_all | solution.py:57
  11.3 32.6 %collective-permute-start = (bf16[3,192,256]{2,1,0:T(8,128)(2,1)}, bf16[3,192,256]{2,1,0:T(8,128)(2,1)S(1)}, u32[]{:S(2)}, u32[]{:S(2)}) collective-permute-start(bf16[3,192,256]{2,1,0:T(8,128)(2,1)} %bitcast.37), channel_id=1, source_target_pairs={{0,0},{1,32},{2,64},{3,96},{4,36},{5,68},{6,100},{7,4},{8,72},{9,1... | collective-permute-start | bytes 884744 | tf_op jit(solution)/shard_map/weights/ppermute | solution.py:25
  44.6 23.6 %all-to-all-start.1 = ((bf16[4,144,384]{2,1,0:T(8,128)(2,1)}), bf16[4,144,384]{2,1,0:T(8,128)(2,1)S(1)}, u32[]{:S(2)}, u32[]{:S(2)}) async-start(bf16[4,144,384]{2,1,0:T(8,128)(2,1)} %broadcast_in_dim.11), calls=%async_computation.1 | async-start | bytes 884736 | tf_op jit(solution)/shard_map/tokens/all_to_all | solution.py:57
  48.1 13.6 %collective-permute-start.3 = (bf16[3,192,256]{2,1,0:T(8,128)(2,1)S(1)}, bf16[3,192,256]{2,1,0:T(8,128)(2,1)S(1)}, u32[]{:S(2)}, u32[]{:S(2)}) collective-permute-start(bf16[3,192,256]{2,1,0:T(8,128)(2,1)S(1)} %collective-permute-done), channel_id=1, source_target_pairs={{0,128},{128,256},{256,384},{384,0},{1,129},{129,257},{257,385},{3... | collective-permute-start | bytes 884744 | tf_op jit(solution)/shard_map/weights/ppermute | solution.py:25
  50.0 11.6 %collective-permute-start.2 = (bf16[3,192,256]{2,1,0:T(8,128)(2,1)S(1)}, bf16[3,192,256]{2,1,0:T(8,128)(2,1)S(1)}, u32[]{:S(2)}, u32[]{:S(2)}) collective-permute-start(bf16[3,192,256]{2,1,0:T(8,128)(2,1)S(1)} %collective-permute-done), channel_id=1, source_target_pairs={{0,256},{128,384},{256,0},{384,128},{1,257},{129,385},{257,1},{385... | collective-permute-start | bytes 884744 | tf_op jit(solution)/shard_map/weights/ppermute | solution.py:25
  54.2 9.7 %collective-permute-start.1 = (bf16[3,192,256]{2,1,0:T(8,128)(2,1)S(1)}, bf16[3,192,256]{2,1,0:T(8,128)(2,1)S(1)}, u32[]{:S(2)}, u32[]{:S(2)}) collective-permute-start(bf16[3,192,256]{2,1,0:T(8,128)(2,1)S(1)} %collective-permute-done), channel_id=1, source_target_pairs={{0,384},{128,0},{256,128},{384,256},{1,385},{129,1},{257,129},{385... | collective-permute-start | bytes 884744 | tf_op jit(solution)/shard_map/weights/ppermute | solution.py:25
  68.4 30.3 %collective-permute-start.7 = (bf16[4,3,192,256]{3,2,1,0:T(8,128)(2,1)S(1)}, bf16[4,3,192,256]{3,2,1,0:T(8,128)(2,1)S(1)}, u32[]{:S(2)}, u32[]{:S(2)}) collective-permute-start(bf16[4,3,192,256]{3,2,1,0:T(8,128)(2,1)S(1)} %pad_maximum_fusion.w_mine), channel_id=1, source_target_pairs={{0,16},{16,0},{1,17},{17,1},{2,18},{18,2},{3,19},{19,3},{4,20},{20... | collective-permute-start | bytes 3538952 | tf_op jit(solution)/shard_map/weights/ppermute | solution.py:25
  70.4 15.7 %collective-permute-start.6 = (bf16[4,144,384]{2,1,0:T(8,128)(2,1)S(1)}, bf16[4,144,384]{2,1,0:T(8,128)(2,1)S(1)}, u32[]{:S(2)}, u32[]{:S(2)}) collective-permute-start(bf16[4,144,384]{2,1,0:T(8,128)(2,1)S(1)} %all-to-all-done.1.t0), channel_id=1, source_target_pairs={{0,4},{4,8},{8,12},{12,32},{32,36},{36,40},{40,44},{44,64},{64,68}... | collective-permute-start | bytes 1327112 | tf_op jit(solution)/shard_map/tokens/ppermute | solution.py:25
  72.3 24.4 %collective-permute-start.5 = (bf16[4,144,384]{2,1,0:T(8,128)(2,1)S(1)}, bf16[4,144,384]{2,1,0:T(8,128)(2,1)}, u32[]{:S(2)}, u32[]{:S(2)}) collective-permute-start(bf16[4,144,384]{2,1,0:T(8,128)(2,1)S(1)} %all-to-all-done.1.t0), channel_id=1, source_target_pairs={{0,8},{4,108},{8,32},{12,4},{32,40},{36,12},{40,64},{44,36},{64,72... | collective-permute-start | bytes 1327112 | tf_op jit(solution)/shard_map/tokens/ppermute | solution.py:25
  77.1 21.6 %collective-permute-start.4 = (bf16[4,144,384]{2,1,0:T(8,128)(2,1)S(1)}, bf16[4,144,384]{2,1,0:T(8,128)(2,1)}, u32[]{:S(2)}, u32[]{:S(2)}) collective-permute-start(bf16[4,144,384]{2,1,0:T(8,128)(2,1)S(1)} %all-to-all-done.1.t0), channel_id=1, source_target_pairs={{0,108},{4,0},{8,4},{12,8},{32,12},{36,32},{40,36},{44,40},{64,44}... | collective-permute-start | bytes 1327112 | tf_op jit(solution)/shard_map/tokens/ppermute | solution.py:25
  102.9 19.2 %all-to-all-start.2 = ((bf16[8,128,384]{2,1,0:T(8,128)(2,1)}), bf16[8,128,384]{2,1,0:T(8,128)(2,1)S(1)}, u32[]{:S(2)}, u32[]{:S(2)}) async-start(bf16[8,128,384]{2,1,0:T(8,128)(2,1)} %bitcast.15), calls=%async_computation.2 | async-start | bytes 1572864 | tf_op jit(solution)/shard_map/project/all_to_all | solution.py:223
  122.5 1.3 copy-start
  123.8 35.2 %all-to-all-start.3 = ((bf16[16,2,256,128]{3,2,1,0:T(8,128)(2,1)}), bf16[16,2,256,128]{3,2,1,0:T(8,128)(2,1)S(1)}, u32[]{:S(2)}, u32[]{:S(2)}) async-start(bf16[16,2,256,128]{3,2,1,0:T(8,128)(2,1)} %copy-done), calls=%async_computation.3 | async-start | bytes 4194304 | tf_op jit(solution)/shard_map/keys/all_to_all | solution.py:234
  161.1 16.7 %collective-permute-start.8 = (bf16[128,128]{1,0:T(8,128)(2,1)S(1)}, bf16[128,128]{1,0:T(8,128)(2,1)S(1)}, u32[]{:S(2)}, u32[]{:S(2)}) collective-permute-start(bf16[128,128]{1,0:T(8,128)(2,1)S(1)} %get-tuple-element.23), channel_id=1, source_target_pairs={{0,0},{1,32},{2,64},{3,96},{4,39},{5,71},{6,103},{7,7},{8,74},{9,1... | collective-permute-start | bytes 98312 | tf_op jit(solution)/shard_map/home/ppermute | solution.py:25
  175.9 13.9 %collective-permute-start.9 = (bf16[128,128]{1,0:T(8,128)(2,1)S(1)}, bf16[128,128]{1,0:T(8,128)(2,1)S(1)}, u32[]{:S(2)}, u32[]{:S(2)}) collective-permute-start(bf16[128,128]{1,0:T(8,128)(2,1)S(1)} %get-tuple-element.24), channel_id=1, source_target_pairs={{0,16},{1,48},{2,80},{3,112},{4,55},{5,87},{6,119},{7,23},{8,90},{... | collective-permute-start | bytes 98312 | tf_op jit(solution)/shard_map/home/ppermute | solution.py:25

commit v8 on v7

--- a/solution.py
+++ b/solution.py
@@ -25,16 +25,25 @@
     return lax.ppermute(values, axes, pairs)
 
 
+def plane_offset(zl):
+    return (0, 1, 0, 2)[zl]
+
+
 def to_plane(values):
-    return shift(values, ("zh", "zl", "y"), lambda i: ((i[2] + i[1]) % NZH, i[1], i[0]))
-
-
-def to_home(values, cross):
     return shift(
         values,
-        ("zh", "core", "zl", "y"),
-        lambda i: ((i[0] + i[2] + i[3]) % NZH, i[1] ^ cross, i[2], (i[0] - i[2]) % NY),
+        ("zh", "zl", "y"),
+        lambda i: ((i[2] + plane_offset(i[1])) % NZH, (i[1] + 2) % NZL, i[0]),
     )
+
+
+def to_home(values, cross):
+    def move(i):
+        zh, core, zl, y = i
+        zh_home, zl_home = divmod((zh * NZL + zl + 4 * ((y + zl) % 4) + 2) % 16, NZL)
+        return zh_home, core ^ cross, zl_home, (zh - plane_offset(zl_home)) % NY
+
+    return shift(values, ("zh", "core", "zl", "y"), move)
 
 
 def along_z(values, step):
@@ -64,7 +73,7 @@
     return jnp.concatenate([high, mid, rest - mid]).astype(jnp.bfloat16)
 
 
-def partial_kernel(where, t0, t1, t2, t3, w_mine, w_theirs, out, w, acc):
+def partial_kernel(where, t0, t1, t2, t3, gain, w_mine, w_theirs, out, w, acc):
     zl, core, turn, x_here = where[0], where[1], where[2], where[3]
     half = w_mine.shape[2]
     for step in range(NX):
@@ -75,12 +84,9 @@
             w[x, pl.ds(pl.multiple_of((1 - core) * half, half), half), cols] = w_theirs[step, s]
     tokens = (t0, t1, t2, t3)
 
-    def extra(slot, quarter):
-        return tokens[slot][quarter, 128:144].astype(jnp.float32)
-
     centers, scales = [], []
     for quarter in range(NZH):
-        rows = sum(extra(slot, quarter)[:2] for slot in range(NZL))
+        rows = t0[quarter, 128:144].astype(jnp.float32)
         sums = (rows[:, :128] + rows[:, 128:256] + rows[:, 256:]) / FEATURES
         center = sums[0:1]
         centers.append(center)
@@ -88,7 +94,8 @@
     stats = jnp.concatenate(centers + scales, axis=0).T
 
     for slot in range(NZL):
-        row_gain = extra(slot, 0)[2:3]
+        part = lax.rem(zl + slot, NZL)
+        row_gain = gain[part]
         normed = []
         for quarter in range(NZH):
             x = tokens[slot][quarter, :128].astype(jnp.float32)
@@ -97,7 +104,7 @@
             normed.append(((x - center) * scale * row_gain).astype(jnp.bfloat16))
         term = jnp.dot(
             jnp.concatenate(normed, axis=0),
-            w[lax.rem(zl + slot, NZL)],
+            w[part],
             preferred_element_type=jnp.float32,
         )
         if slot == 0:
@@ -163,7 +170,10 @@
     core = lax.axis_index("core")
     zl = lax.axis_index("zl")
     zh = lax.axis_index("zh")
-    turn = (2 * NZH - zh - zl) % NZH
+    y_here = lax.axis_index("y")
+    head_zl = (zl + 2) % NZL
+    head_y = (zh + NY - jnp.where(head_zl == 1, 1, jnp.where(head_zl == 3, 2, 0))) % NY
+    turn = (3 * NZH - zh - zl - (zl >= 2)) % NZH
     where = jnp.stack([zl, core, turn, lax.axis_index("x")]).astype(jnp.int32)
 
     with jax.named_scope("weights"):
@@ -172,24 +182,34 @@
     with jax.named_scope("norm"):
         x = tokens.astype(jnp.float32)
         shared = spread(
-            jnp.concatenate([jnp.sum(x, axis=1), jnp.sum(x * x, axis=1), q_gain, k_gain])[None],
-            "y",
-            NY,
+            jnp.concatenate(
+                [
+                    jnp.sum(x, axis=1),
+                    jnp.sum(x * x, axis=1),
+                    ln_gain.astype(jnp.float32),
+                    q_gain,
+                    k_gain,
+                ]
+            )[None],
+            ("zl", "y"),
+            NZL * NY,
         )[:, 0]
         sums = jnp.sum(shared[:, :256], axis=0)
-        head_gain = lax.dynamic_index_in_dim(
-            shared[:, 256:], (zh + NY - zl) % NY, 0, keepdims=False
-        )
-        head_gain = lax.dynamic_index_in_dim(head_gain.reshape(2, 2, 1, DH), core, 1, keepdims=False)
         extended = jnp.concatenate(
             [
                 tokens,
                 pieces_of(sums[:128])[None],
                 pieces_of(sums[128:])[None],
-                ln_gain[None],
-                jnp.zeros((13, 384), jnp.bfloat16),
+                jnp.zeros((14, 384), jnp.bfloat16),
             ]
         )
+        gain = lax.dynamic_index_in_dim(
+            shared[:, 256:640].reshape(NZL, NY, 1, 384), y_here, 1, keepdims=False
+        )
+        head_gain = lax.dynamic_index_in_dim(
+            shared[:, 640:], head_zl * NY + head_y, 0, keepdims=False
+        )
+        head_gain = lax.dynamic_index_in_dim(head_gain.reshape(2, 2, 1, DH), core, 1, keepdims=False)
 
     with jax.named_scope("tokens"):
         extended, w_moved = lax.optimization_barrier((extended, w_moved))
@@ -200,19 +220,23 @@
             shift(w_moved, ("x",), lambda i, step=step: ((i[0] - step) % NX,)) for step in (1, 2, 3)
         ]
         t0, *along_x = lax.optimization_barrier((t0, *along_x))
+
+    with jax.named_scope("tokens"):
+        block = t0[:, :128]
+        t1 = along_z(block, -1)
+        t3 = along_z(block, 1)
+        t2 = along_z_two(block)
+
+    with jax.named_scope("weights"):
+        t3, *along_x = lax.optimization_barrier((t3, *along_x))
         w_mine = jnp.stack([w_moved] + along_x)
         w_theirs = swap_cores(w_mine)
-
-    with jax.named_scope("tokens"):
-        t1 = along_z(t0, -1)
-        t3 = along_z(t0, 1)
-        t2 = along_z_two(t0)
 
     with jax.named_scope("project"):
         part = kernel_call(
             partial_kernel,
             jax.ShapeDtypeStruct((CORES, NY, 128, 3 * DH), jnp.bfloat16),
-            (where, t0, t1, t2, t3, w_mine, w_theirs),
+            (where, t0, t1, t2, t3, gain, w_mine, w_theirs),
             scalars=1,
             scratch=[
                 pltpu.VMEM((NX, 384, 768), jnp.bfloat16),

time: 191 us -> 202 us (1.058)
  the two profiles are of different devices: /device:TPU:16 before, /device:TPU:40 now
where the time goes in v8:
time: 202 us; the launch traced here: 201 us
  waiting for transfers between devices  96.2 us (48%)
  starting transfers between devices  89.4 us (44%)
  Pallas kernels  6.53 us (3%)
  local copies, waits for them, and re-layouts  5.11 us (3%)
  other arithmetic  3.57 us (2%)
    ppermute x10, starting transfers between devices, shift(): return lax.ppermute(values, axes, pairs)  56.8 us
    ppermute x10, waiting for transfers between devices, shift(): return lax.ppermute(values, axes, pairs)  55.5 us
    all_to_all x1, waiting for transfers between devices, body(): kv_all = lax.all_to_all(kv, ('x', 'y'), 0, 0)  29.6 us
    all_to_all x2, starting transfers between devices, spread(): lax.all_to_all(jnp.broadcast_to(values[None], (count,) + values.shape), a...  20.7 us
    all_to_all x1, waiting for transfers between devices, body(): lax.all_to_all(part, ('core', 'y'), 0, 0).reshape(CORES, NY, 128, 3 * DH)  11.2 us
    all_to_all x1, starting transfers between devices, body(): lax.all_to_all(part, ('core', 'y'), 0, 0).reshape(CORES, NY, 128, 3 * DH)  7.1 us
    pallas_call x3, Pallas kernels, kernel_call(): pl.pallas_call(kernel, out_shape=out_shape, in_specs=[smem] * scalars + [...  6.53 us
    all_to_all x1, starting transfers between devices, body(): kv_all = lax.all_to_all(kv, ('x', 'y'), 0, 0)  4.82 us
  transfers between devices with their start and end apart: 14, of which 10 were waited for; matrix products, arithmetic and copies ran while one was open for 1% of the time, Pallas kernels for 0%

profile of v8, /device:TPU:40, one launch (start us, length us, event | category | flops | bytes accessed | tf_op | source)
XLA Modules:
  0.0 201.1 jit_solution(3976959484959193129)
XLA Ops:
  0.0 1.0 fusion
  1.0 0.7 constant_dynamic-update-slice_fusion.2
  3.8 8.7 %all-to-all-start = ((f32[16,1,1152]{2,1,0:T(1,128)}), f32[16,1,1152]{2,1,0:T(1,128)S(1)}, u32[]{:S(2)}, u32[]{:S(2)}) async-start(f32[16,1,1152]{2,1,0:T(1,128)} %broadcast_in_dim.6), calls=%async_computation | async-start | bytes 147456 | tf_op jit(solution)/shard_map/norm/all_to_all | solution.py:66
  12.4 12.9 %collective-permute-start = (bf16[3,192,256]{2,1,0:T(8,128)(2,1)}, bf16[3,192,256]{2,1,0:T(8,128)(2,1)S(1)}, u32[]{:S(2)}, u32[]{:S(2)}) collective-permute-start(bf16[3,192,256]{2,1,0:T(8,128)(2,1)} %bitcast.42), channel_id=1, source_target_pairs={{0,8},{1,40},{2,72},{3,104},{4,44},{5,76},{6,108},{7,12},{8,0},{9,... | collective-permute-start | bytes 884744 | tf_op jit(solution)/shard_map/weights/ppermute | solution.py:25
  25.5 1.0 maximum_maximum_fusion
  26.4 10.0 %collective-permute-done = bf16[3,192,256]{2,1,0:T(8,128)(2,1)S(1)} collective-permute-done((bf16[3,192,256]{2,1,0:T(8,128)(2,1)}, bf16[3,192,256]{2,1,0:T(8,128)(2,1)S(1)}, u32[]{:S(2)}, u32[]{:S(2)}) %collective-permute-start) | collective-permute-done | bytes 294944 | tf_op jit(solution)/shard_map/weights/ppermute | solution.py:25
  36.4 0.8 broadcast_in_dim.8
  37.3 12.0 %all-to-all-start.1 = ((bf16[4,144,384]{2,1,0:T(8,128)(2,1)}), bf16[4,144,384]{2,1,0:T(8,128)(2,1)S(1)}, u32[]{:S(2)}, u32[]{:S(2)}) async-start(bf16[4,144,384]{2,1,0:T(8,128)(2,1)} %broadcast_in_dim.8), calls=%async_computation.1 | async-start | bytes 884736 | tf_op jit(solution)/shard_map/tokens/all_to_all | solution.py:66
  49.3 4.7 %collective-permute-start.1 = (bf16[3,192,256]{2,1,0:T(8,128)(2,1)S(1)}, bf16[3,192,256]{2,1,0:T(8,128)(2,1)S(1)}, u32[]{:S(2)}, u32[]{:S(2)}) collective-permute-start(bf16[3,192,256]{2,1,0:T(8,128)(2,1)S(1)} %collective-permute-done), channel_id=1, source_target_pairs={{0,384},{128,0},{256,128},{384,256},{1,385},{129,1},{257,129},{385... | collective-permute-start | bytes 884744 | tf_op jit(solution)/shard_map/weights/ppermute | solution.py:25
  54.0 2.7 %collective-permute-start.2 = (bf16[3,192,256]{2,1,0:T(8,128)(2,1)S(1)}, bf16[3,192,256]{2,1,0:T(8,128)(2,1)S(1)}, u32[]{:S(2)}, u32[]{:S(2)}) collective-permute-start(bf16[3,192,256]{2,1,0:T(8,128)(2,1)S(1)} %collective-permute-done), channel_id=1, source_target_pairs={{0,256},{128,384},{256,0},{384,128},{1,257},{129,385},{257,1},{385... | collective-permute-start | bytes 884744 | tf_op jit(solution)/shard_map/weights/ppermute | solution.py:25
  56.7 2.8 %collective-permute-start.3 = (bf16[3,192,256]{2,1,0:T(8,128)(2,1)S(1)}, bf16[3,192,256]{2,1,0:T(8,128)(2,1)S(1)}, u32[]{:S(2)}, u32[]{:S(2)}) collective-permute-start(bf16[3,192,256]{2,1,0:T(8,128)(2,1)S(1)} %collective-permute-done), channel_id=1, source_target_pairs={{0,128},{128,256},{256,384},{384,0},{1,129},{129,257},{257,385},{3... | collective-permute-start | bytes 884744 | tf_op jit(solution)/shard_map/weights/ppermute | solution.py:25
  59.5 4.4 %collective-permute-done.1 = bf16[3,192,256]{2,1,0:T(8,128)(2,1)S(1)} collective-permute-done((bf16[3,192,256]{2,1,0:T(8,128)(2,1)S(1)}, bf16[3,192,256]{2,1,0:T(8,128)(2,1)S(1)}, u32[]{:S(2)}, u32[]{:S(2)}) %collective-permute-start.1) | collective-permute-done | bytes 294944 | tf_op jit(solution)/shard_map/weights/ppermute | solution.py:25
  63.9 2.3 %collective-permute-done.2 = bf16[3,192,256]{2,1,0:T(8,128)(2,1)S(1)} collective-permute-done((bf16[3,192,256]{2,1,0:T(8,128)(2,1)S(1)}, bf16[3,192,256]{2,1,0:T(8,128)(2,1)S(1)}, u32[]{:S(2)}, u32[]{:S(2)}) %collective-permute-start.2) | collective-permute-done | bytes 294944 | tf_op jit(solution)/shard_map/weights/ppermute | solution.py:25
  66.2 3.1 %collective-permute-done.3 = bf16[3,192,256]{2,1,0:T(8,128)(2,1)S(1)} collective-permute-done((bf16[3,192,256]{2,1,0:T(8,128)(2,1)S(1)}, bf16[3,192,256]{2,1,0:T(8,128)(2,1)S(1)}, u32[]{:S(2)}, u32[]{:S(2)}) %collective-permute-start.3) | collective-permute-done | bytes 294944 | tf_op jit(solution)/shard_map/weights/ppermute | solution.py:25
  69.3 0.8 slice.21
  70.1 9.4 %collective-permute-start.6 = (bf16[4,128,384]{2,1,0:T(8,128)(2,1)}, bf16[4,128,384]{2,1,0:T(8,128)(2,1)S(1)}, u32[]{:S(2)}, u32[]{:S(2)}) collective-permute-start(bf16[4,128,384]{2,1,0:T(8,128)(2,1)} %slice.21), channel_id=1, source_target_pairs={{0,4},{4,8},{8,12},{12,32},{32,36},{36,40},{40,44},{44,64},{64,68}... | collective-permute-start | bytes 1179656 | tf_op jit(solution)/shard_map/tokens/ppermute | solution.py:25
  79.5 8.8 %collective-permute-done.6.t3 = bf16[4,128,384]{2,1,0:T(8,128)(2,1)S(1)} collective-permute-done((bf16[4,128,384]{2,1,0:T(8,128)(2,1)}, bf16[4,128,384]{2,1,0:T(8,128)(2,1)S(1)}, u32[]{:S(2)}, u32[]{:S(2)}) %collective-permute-start.6) | collective-permute-done | bytes 393248 | tf_op jit(solution)/shard_map/tokens/ppermute | solution.py:25
  88.5 1.9 collective-permute-start.7
  90.4 3.8 %collective-permute-start.4 = (bf16[4,128,384]{2,1,0:T(8,128)(2,1)}, bf16[4,128,384]{2,1,0:T(8,128)(2,1)}, u32[]{:S(2)}, u32[]{:S(2)}) collective-permute-start(bf16[4,128,384]{2,1,0:T(8,128)(2,1)} %slice.21), channel_id=1, source_target_pairs={{0,108},{4,0},{8,4},{12,8},{32,12},{36,32},{40,36},{44,40},{64,44}... | collective-permute-start | bytes 1179656 | tf_op jit(solution)/shard_map/tokens/ppermute | solution.py:25
  94.1 4.4 %collective-permute-start.5 = (bf16[4,128,384]{2,1,0:T(8,128)(2,1)}, bf16[4,128,384]{2,1,0:T(8,128)(2,1)}, u32[]{:S(2)}, u32[]{:S(2)}) collective-permute-start(bf16[4,128,384]{2,1,0:T(8,128)(2,1)} %slice.21), channel_id=1, source_target_pairs={{0,8},{4,108},{8,32},{12,4},{32,40},{36,12},{40,64},{44,36},{64,72... | collective-permute-start | bytes 1179656 | tf_op jit(solution)/shard_map/tokens/ppermute | solution.py:25
  98.7 6.1 %collective-permute-done.4.t1 = bf16[4,128,384]{2,1,0:T(8,128)(2,1)} collective-permute-done((bf16[4,128,384]{2,1,0:T(8,128)(2,1)}, bf16[4,128,384]{2,1,0:T(8,128)(2,1)}, u32[]{:S(2)}, u32[]{:S(2)}) %collective-permute-start.4) | collective-permute-done | bytes 393248 | tf_op jit(solution)/shard_map/tokens/ppermute | solution.py:25
  104.8 9.6 %collective-permute-done.5.t2 = bf16[4,128,384]{2,1,0:T(8,128)(2,1)} collective-permute-done((bf16[4,128,384]{2,1,0:T(8,128)(2,1)}, bf16[4,128,384]{2,1,0:T(8,128)(2,1)}, u32[]{:S(2)}, u32[]{:S(2)}) %collective-permute-start.5) | collective-permute-done | bytes 393248 | tf_op jit(solution)/shard_map/tokens/ppermute | solution.py:25
  114.4 4.1 %project.2 = bf16[2,4,128,384]{3,2,1,0:T(8,128)(2,1)} custom-call(s32[4]{0:T(128)S(1)} %pad_add_fusion.where, bf16[4,144,384]{2,1,0:T(8,128)(2,1)S(1)} %all-to-all-done.1.t0, bf16[4,128,384]{2,1,0:T(8,128)(2,1)} %collective-permute-done.4.t1, bf16[4,128,384]{2,1,0:T(8,128)(2,1)} %collective-permute-done.5.t2, ...), custom_call_target="tpu_custom_call" | custom-call | tf_op jit(solution)/shard_map/project/pallas_call | solution.py:159
  118.5 7.1 %all-to-all-start.2 = ((bf16[8,128,384]{2,1,0:T(8,128)(2,1)}), bf16[8,128,384]{2,1,0:T(8,128)(2,1)S(1)}, u32[]{:S(2)}, u32[]{:S(2)}) async-start(bf16[8,128,384]{2,1,0:T(8,128)(2,1)} %bitcast.17), calls=%async_computation.2 | async-start | bytes 1572864 | tf_op jit(solution)/shard_map/project/all_to_all | solution.py:247
  125.6 11.2 %all-to-all-done.2 = bf16[8,128,384]{2,1,0:T(8,128)(2,1)S(1)} async-done(((bf16[8,128,384]{2,1,0:T(8,128)(2,1)}), bf16[8,128,384]{2,1,0:T(8,128)(2,1)S(1)}, u32[]{:S(2)}, u32[]{:S(2)}) %all-to-all-start.2) | async-done | bytes 786464 | tf_op jit(solution)/shard_map/project/all_to_all | solution.py:247
  137.2 1.3 copy-done
  138.5 4.8 %all-to-all-start.3 = ((bf16[16,2,256,128]{3,2,1,0:T(8,128)(2,1)}), bf16[16,2,256,128]{3,2,1,0:T(8,128)(2,1)S(1)}, u32[]{:S(2)}, u32[]{:S(2)}) async-start(bf16[16,2,256,128]{3,2,1,0:T(8,128)(2,1)} %copy-done), calls=%async_computation.3 | async-start | bytes 4194304 | tf_op jit(solution)/shard_map/keys/all_to_all | solution.py:258
  143.4 29.6 %all-to-all-done.3.kv = bf16[16,2,256,128]{3,2,1,0:T(8,128)(2,1)S(1)} async-done(((bf16[16,2,256,128]{3,2,1,0:T(8,128)(2,1)}), bf16[16,2,256,128]{3,2,1,0:T(8,128)(2,1)S(1)}, u32[]{:S(2)}, u32[]{:S(2)}) %all-to-all-start.3) | async-done | bytes 2097184 | tf_op jit(solution)/shard_map/keys/all_to_all | solution.py:258
  172.9 2.1 %attend.1 = bf16[256,128]{1,0:T(8,128)(2,1)S(1)} custom-call(bf16[256,128]{1,0:T(8,128)(2,1)S(1)} %get-tuple-element.27.q, bf16[16,2,256,128]{3,2,1,0:T(8,128)(2,1)S(1)} %all-to-all-done.3.kv), custom_call_target="tpu_custom_call" | custom-call | tf_op jit(solution)/shard_map/attend/pallas_call | solution.py:159
  175.0 12.4 %collective-permute-start.8 = (bf16[128,128]{1,0:T(8,128)(2,1)S(1)}, bf16[128,128]{1,0:T(8,128)(2,1)S(1)}, u32[]{:S(2)}, u32[]{:S(2)}) collective-permute-start(bf16[128,128]{1,0:T(8,128)(2,1)S(1)} %get-tuple-element.31), channel_id=1, source_target_pairs={{0,8},{1,40},{2,72},{3,104},{4,46},{5,78},{6,110},{7,14},{8,96},{9... | collective-permute-start | bytes 98312 | tf_op jit(solution)/shard_map/home/ppermute | solution.py:25
  187.4 1.9 collective-permute-start.9
  189.4 11.1 %collective-permute-done.9 = bf16[128,128]{1,0:T(8,128)(2,1)S(1)} collective-permute-done((bf16[128,128]{1,0:T(8,128)(2,1)S(1)}, bf16[128,128]{1,0:T(8,128)(2,1)S(1)}, u32[]{:S(2)}, u32[]{:S(2)}) %collective-permute-start.9) | collective-permute-done | bytes 32800 | tf_op jit(solution)/shard_map/home/ppermute | solution.py:25
  (27 shorter events, 3.5 us)
Async XLA Ops:
  3.8 21.7 %all-to-all-start = ((f32[16,1,1152]{2,1,0:T(1,128)}), f32[16,1,1152]{2,1,0:T(1,128)S(1)}, u32[]{:S(2)}, u32[]{:S(2)}) async-start(f32[16,1,1152]{2,1,0:T(1,128)} %broadcast_in_dim.6), calls=%async_computation | async-start | bytes 147456 | tf_op jit(solution)/shard_map/norm/all_to_all | solution.py:66
  12.4 24.0 %collective-permute-start = (bf16[3,192,256]{2,1,0:T(8,128)(2,1)}, bf16[3,192,256]{2,1,0:T(8,128)(2,1)S(1)}, u32[]{:S(2)}, u32[]{:S(2)}) collective-permute-start(bf16[3,192,256]{2,1,0:T(8,128)(2,1)} %bitcast.42), channel_id=1, source_target_pairs={{0,8},{1,40},{2,72},{3,104},{4,44},{5,76},{6,108},{7,12},{8,0},{9,... | collective-permute-start | bytes 884744 | tf_op jit(solution)/shard_map/weights/ppermute | solution.py:25
  37.3 32.0 %all-to-all-start.1 = ((bf16[4,144,384]{2,1,0:T(8,128)(2,1)}), bf16[4,144,384]{2,1,0:T(8,128)(2,1)S(1)}, u32[]{:S(2)}, u32[]{:S(2)}) async-start(bf16[4,144,384]{2,1,0:T(8,128)(2,1)} %broadcast_in_dim.8), calls=%async_computation.1 | async-start | bytes 884736 | tf_op jit(solution)/shard_map/tokens/all_to_all | solution.py:66
  49.3 14.6 %collective-permute-start.1 = (bf16[3,192,256]{2,1,0:T(8,128)(2,1)S(1)}, bf16[3,192,256]{2,1,0:T(8,128)(2,1)S(1)}, u32[]{:S(2)}, u32[]{:S(2)}) collective-permute-start(bf16[3,192,256]{2,1,0:T(8,128)(2,1)S(1)} %collective-permute-done), channel_id=1, source_target_pairs={{0,384},{128,0},{256,128},{384,256},{1,385},{129,1},{257,129},{385... | collective-permute-start | bytes 884744 | tf_op jit(solution)/shard_map/weights/ppermute | solution.py:25
  54.0 12.3 %collective-permute-start.2 = (bf16[3,192,256]{2,1,0:T(8,128)(2,1)S(1)}, bf16[3,192,256]{2,1,0:T(8,128)(2,1)S(1)}, u32[]{:S(2)}, u32[]{:S(2)}) collective-permute-start(bf16[3,192,256]{2,1,0:T(8,128)(2,1)S(1)} %collective-permute-done), channel_id=1, source_target_pairs={{0,256},{128,384},{256,0},{384,128},{1,257},{129,385},{257,1},{385... | collective-permute-start | bytes 884744 | tf_op jit(solution)/shard_map/weights/ppermute | solution.py:25
  56.7 12.6 %collective-permute-start.3 = (bf16[3,192,256]{2,1,0:T(8,128)(2,1)S(1)}, bf16[3,192,256]{2,1,0:T(8,128)(2,1)S(1)}, u32[]{:S(2)}, u32[]{:S(2)}) collective-permute-start(bf16[3,192,256]{2,1,0:T(8,128)(2,1)S(1)} %collective-permute-done), channel_id=1, source_target_pairs={{0,128},{128,256},{256,384},{384,0},{1,129},{129,257},{257,385},{3... | collective-permute-start | bytes 884744 | tf_op jit(solution)/shard_map/weights/ppermute | solution.py:25
  70.1 18.2 %collective-permute-start.6 = (bf16[4,128,384]{2,1,0:T(8,128)(2,1)}, bf16[4,128,384]{2,1,0:T(8,128)(2,1)S(1)}, u32[]{:S(2)}, u32[]{:S(2)}) collective-permute-start(bf16[4,128,384]{2,1,0:T(8,128)(2,1)} %slice.21), channel_id=1, source_target_pairs={{0,4},{4,8},{8,12},{12,32},{32,36},{36,40},{40,44},{44,64},{64,68}... | collective-permute-start | bytes 1179656 | tf_op jit(solution)/shard_map/tokens/ppermute | solution.py:25
  88.5 25.9 %collective-permute-start.7 = (bf16[4,3,192,256]{3,2,1,0:T(8,128)(2,1)S(1)}, bf16[4,3,192,256]{3,2,1,0:T(8,128)(2,1)S(1)}, u32[]{:S(2)}, u32[]{:S(2)}) collective-permute-start(bf16[4,3,192,256]{3,2,1,0:T(8,128)(2,1)S(1)} %pad_maximum_fusion.w_mine), channel_id=1, source_target_pairs={{0,16},{16,0},{1,17},{17,1},{2,18},{18,2},{3,19},{19,3},{4,20},{20... | collective-permute-start | bytes 3538952 | tf_op jit(solution)/shard_map/weights/ppermute | solution.py:25
  90.4 14.4 %collective-permute-start.4 = (bf16[4,128,384]{2,1,0:T(8,128)(2,1)}, bf16[4,128,384]{2,1,0:T(8,128)(2,1)}, u32[]{:S(2)}, u32[]{:S(2)}) collective-permute-start(bf16[4,128,384]{2,1,0:T(8,128)(2,1)} %slice.21), channel_id=1, source_target_pairs={{0,108},{4,0},{8,4},{12,8},{32,12},{36,32},{40,36},{44,40},{64,44}... | collective-permute-start | bytes 1179656 | tf_op jit(solution)/shard_map/tokens/ppermute | solution.py:25
  94.1 20.2 %collective-permute-start.5 = (bf16[4,128,384]{2,1,0:T(8,128)(2,1)}, bf16[4,128,384]{2,1,0:T(8,128)(2,1)}, u32[]{:S(2)}, u32[]{:S(2)}) collective-permute-start(bf16[4,128,384]{2,1,0:T(8,128)(2,1)} %slice.21), channel_id=1, source_target_pairs={{0,8},{4,108},{8,32},{12,4},{32,40},{36,12},{40,64},{44,36},{64,72... | collective-permute-start | bytes 1179656 | tf_op jit(solution)/shard_map/tokens/ppermute | solution.py:25
  118.5 18.3 %all-to-all-start.2 = ((bf16[8,128,384]{2,1,0:T(8,128)(2,1)}), bf16[8,128,384]{2,1,0:T(8,128)(2,1)S(1)}, u32[]{:S(2)}, u32[]{:S(2)}) async-start(bf16[8,128,384]{2,1,0:T(8,128)(2,1)} %bitcast.17), calls=%async_computation.2 | async-start | bytes 1572864 | tf_op jit(solution)/shard_map/project/all_to_all | solution.py:247
  137.2 1.3 copy-start
  138.5 34.4 %all-to-all-start.3 = ((bf16[16,2,256,128]{3,2,1,0:T(8,128)(2,1)}), bf16[16,2,256,128]{3,2,1,0:T(8,128)(2,1)S(1)}, u32[]{:S(2)}, u32[]{:S(2)}) async-start(bf16[16,2,256,128]{3,2,1,0:T(8,128)(2,1)} %copy-done), calls=%async_computation.3 | async-start | bytes 4194304 | tf_op jit(solution)/shard_map/keys/all_to_all | solution.py:258
  175.0 14.4 %collective-permute-start.8 = (bf16[128,128]{1,0:T(8,128)(2,1)S(1)}, bf16[128,128]{1,0:T(8,128)(2,1)S(1)}, u32[]{:S(2)}, u32[]{:S(2)}) collective-permute-start(bf16[128,128]{1,0:T(8,128)(2,1)S(1)} %get-tuple-element.31), channel_id=1, source_target_pairs={{0,8},{1,40},{2,72},{3,104},{4,46},{5,78},{6,110},{7,14},{8,96},{9... | collective-permute-start | bytes 98312 | tf_op jit(solution)/shard_map/home/ppermute | solution.py:25
  187.4 13.0 %collective-permute-start.9 = (bf16[128,128]{1,0:T(8,128)(2,1)S(1)}, bf16[128,128]{1,0:T(8,128)(2,1)S(1)}, u32[]{:S(2)}, u32[]{:S(2)}) collective-permute-start(bf16[128,128]{1,0:T(8,128)(2,1)S(1)} %get-tuple-element.32), channel_id=1, source_target_pairs={{0,24},{1,56},{2,88},{3,120},{4,62},{5,94},{6,126},{7,30},{8,112},... | collective-permute-start | bytes 98312 | tf_op jit(solution)/shard_map/home/ppermute | solution.py:25

commit v9 on v7

--- a/solution.py
+++ b/solution.py
@@ -11,8 +11,9 @@
 FEATURES = 6144
 NX = NZH = NZL = NY = 4
 CORES = 2
-AXES = ("x", "zh", "core", "zl", "y")
-SIZES = (NX, NZH, CORES, NZL, NY)
+AXES = ("x", "zh", "core", "zl", "yh", "yl")
+SIZES = (NX, NZH, CORES, NZL, 2, 2)
+Y = ("yh", "yl")
 VMEM_LIMIT = 28 * 1024 * 1024
 
 
@@ -26,15 +27,20 @@
 
 
 def to_plane(values):
-    return shift(values, ("zh", "zl", "y"), lambda i: ((i[2] + i[1]) % NZH, i[1], i[0]))
+    def move(i):
+        zh, zl, yh, yl = i
+        return ((yh * 2 + yl + zl) % NZH, zl) + divmod(zh, 2)
+
+    return shift(values, ("zh", "zl") + Y, move)
 
 
 def to_home(values, cross):
-    return shift(
-        values,
-        ("zh", "core", "zl", "y"),
-        lambda i: ((i[0] + i[2] + i[3]) % NZH, i[1] ^ cross, i[2], (i[0] - i[2]) % NY),
-    )
+    def move(i):
+        zh, core, zl, yh, yl = i
+        zh_home = (zh + zl + yh * 2 + yl + 2 * core) % NZH
+        return (zh_home, core ^ cross, zl) + divmod((zh - zl) % NY, 2)
+
+    return shift(values, ("zh", "core", "zl") + Y, move)
 
 
 def along_z(values, step):
@@ -102,18 +108,16 @@
         )
         if slot == 0:
             acc[...] = term
-        elif slot < NZL - 1:
+        else:
             acc[...] += term
-        else:
-            total = acc[...] + term
-            for quarter in range(NZH):
-                rows = slice(quarter * 128, quarter * 128 + 128)
-                for head in range(2):
-                    for s in range(3):
-                        cols = slice(s * 256 + head * DH, s * 256 + head * DH + DH)
-                        out[head, lax.rem(turn + quarter, NZH), :, s * DH : s * DH + DH] = total[
-                            rows, cols
-                        ].astype(jnp.bfloat16)
+    for core_to in range(CORES):
+        for y_to in range(NY):
+            quarter = lax.rem(turn + y_to + 2 * core_to, NZH)
+            rows = pl.ds(pl.multiple_of(quarter * 128, 128), 128)
+            head = y_to // 2
+            for s in range(3):
+                cols = slice(s * 256 + head * DH, s * 256 + head * DH + DH)
+                out[core_to, y_to, :, s * DH : s * DH + DH] = acc[rows, cols].astype(jnp.bfloat16)
 
 
 def heads_kernel(part, head_gain, q_out, kv_out):
@@ -128,21 +132,31 @@
         q_out[rows] = head_norm(acc[:, :DH], head_gain[0])
         key = head_norm(acc[:, DH : 2 * DH], head_gain[1])
         value = acc[:, 2 * DH :].astype(jnp.bfloat16)
-        for target in range(NX * NY):
+        for target in range(NX * 2):
             kv_out[target, 0, rows] = key
             kv_out[target, 1, rows] = value
 
 
-def attend_kernel(q, kv, out):
-    keys = kv[:, 0].reshape(-1, DH)
-    values = kv[:, 1].reshape(-1, DH)
-    scores = lax.dot_general(
-        q[...], keys, (((1,), (1,)), ((), ())), preferred_element_type=jnp.float32
-    ) * (DH ** -0.5)
-    top = jnp.max(scores, axis=1, keepdims=True)
-    weights = jnp.exp(scores - top)
-    total = jnp.sum(weights, axis=1, keepdims=True)
-    mixed = jnp.dot(weights.astype(jnp.bfloat16), values, preferred_element_type=jnp.float32)
+def attend_kernel(q, kv_mine, kv_theirs, out):
+    scores = [
+        lax.dot_general(
+            q[...],
+            kv[:, 0].reshape(-1, DH),
+            (((1,), (1,)), ((), ())),
+            preferred_element_type=jnp.float32,
+        )
+        * (DH ** -0.5)
+        for kv in (kv_mine, kv_theirs)
+    ]
+    top = jnp.maximum(*[jnp.max(part, axis=1, keepdims=True) for part in scores])
+    weights = [jnp.exp(part - top) for part in scores]
+    total = sum(jnp.sum(part, axis=1, keepdims=True) for part in weights)
+    mixed = sum(
+        jnp.dot(
+            part.astype(jnp.bfloat16), kv[:, 1].reshape(-1, DH), preferred_element_type=jnp.float32
+        )
+        for part, kv in zip(weights, (kv_mine, kv_theirs))
+    )
     out[...] = (mixed / total).astype(jnp.bfloat16)
 
 
@@ -163,7 +177,9 @@
     core = lax.axis_index("core")
     zl = lax.axis_index("zl")
     zh = lax.axis_index("zh")
-    turn = (2 * NZH - zh - zl) % NZH
+    y_high = lax.axis_index("yh")
+    y_here = y_high * 2 + lax.axis_index("yl")
+    turn = (zh + zl) % NZH
     where = jnp.stack([zl, core, turn, lax.axis_index("x")]).astype(jnp.int32)
 
     with jax.named_scope("weights"):
@@ -173,14 +189,16 @@
         x = tokens.astype(jnp.float32)
         shared = spread(
             jnp.concatenate([jnp.sum(x, axis=1), jnp.sum(x * x, axis=1), q_gain, k_gain])[None],
-            "y",
+            Y,
             NY,
         )[:, 0]
         sums = jnp.sum(shared[:, :256], axis=0)
         head_gain = lax.dynamic_index_in_dim(
             shared[:, 256:], (zh + NY - zl) % NY, 0, keepdims=False
         )
-        head_gain = lax.dynamic_index_in_dim(head_gain.reshape(2, 2, 1, DH), core, 1, keepdims=False)
+        head_gain = lax.dynamic_index_in_dim(
+            head_gain.reshape(2, 2, 1, DH), y_high, 1, keepdims=False
+        )
         extended = jnp.concatenate(
             [
                 tokens,
@@ -199,9 +217,9 @@
         along_x = [
             shift(w_moved, ("x",), lambda i, step=step: ((i[0] - step) % NX,)) for step in (1, 2, 3)
         ]
-        t0, *along_x = lax.optimization_barrier((t0, *along_x))
         w_mine = jnp.stack([w_moved] + along_x)
         w_theirs = swap_cores(w_mine)
+        t0, w_mine, w_theirs = lax.optimization_barrier((t0, w_mine, w_theirs))
 
     with jax.named_scope("tokens"):
         t1 = along_z(t0, -1)
@@ -220,29 +238,31 @@
             ],
         )
         part = part.reshape(CORES * NY, 128, 3 * DH)
-        part = lax.all_to_all(part, ("core", "y"), 0, 0).reshape(CORES, NY, 128, 3 * DH)
+        part = lax.all_to_all(part, ("core",) + Y, 0, 0).reshape(CORES, NY, 128, 3 * DH)
         q, kv = kernel_call(
             heads_kernel,
             (
                 jax.ShapeDtypeStruct((256, DH), jnp.bfloat16),
-                jax.ShapeDtypeStruct((NX * NY, 2, 256, DH), jnp.bfloat16),
+                jax.ShapeDtypeStruct((NX * 2, 2, 256, DH), jnp.bfloat16),
             ),
             (part, head_gain),
         )
 
     with jax.named_scope("keys"):
-        kv_all = lax.all_to_all(kv, ("x", "y"), 0, 0)
+        kv_mine = lax.all_to_all(kv, ("x", "yl"), 0, 0)
+        kv_theirs = swap_cores(kv_mine)
 
     with jax.named_scope("attend"):
         out = kernel_call(
-            attend_kernel, jax.ShapeDtypeStruct((256, DH), jnp.bfloat16), (q, kv_all)
+            attend_kernel, jax.ShapeDtypeStruct((256, DH), jnp.bfloat16), (q, kv_mine, kv_theirs)
         )
 
     with jax.named_scope("home"):
         same = to_home(lax.dynamic_slice_in_dim(out, core * 128, 128), 0)
         cross = to_home(lax.dynamic_slice_in_dim(out, (1 - core) * 128, 128), 1)
+        first = (zh + 3 * NY - y_here - 2 * zl - 2 * core) % NY < 2
         return jnp.where(
-            core == 0,
+            first,
             jnp.concatenate([same, cross], axis=1),
             jnp.concatenate([cross, same], axis=1),
         )
@@ -251,6 +271,6 @@
 def solution(mesh):
     fine = Mesh(mesh.devices.reshape(SIZES), AXES)
     rows = ("x", "zh", "core")
-    cols = ("zl", "y")
+    cols = ("zl",) + Y
     in_specs = (P(rows, cols), P(cols), P(rows, None, cols), P(cols), P(cols))
     return jax.shard_map(body, mesh=fine, in_specs=in_specs, out_specs=P(rows, cols), check_vma=False)

time: 191 us -> 179 us (0.937)
  waiting for transfers between devices: 98.8 us -> 76.9 us
  blocking collectives: 0 us -> 18.5 us
  starting transfers between devices: 77.7 us -> 69.5 us
    all_to_all x2 -> x1, waiting for transfers between devices: 37.1 us -> 9.97 us  [body(): lax.all_to_all(part, ('core',) + Y, 0, 0).reshape(CORES, NY, 128, 3 * DH)]
    all_to_all x0 -> x1, blocking collectives: none -> 18.5 us  [body(): kv_mine = lax.all_to_all(kv, ('x', 'yl'), 0, 0)]
    all_to_all x2, waiting for transfers between devices: 4.41 us -> 17.3 us  [spread(): lax.all_to_all(jnp.broadcast_to(values[None], (count,) + values.shape), a...]
    all_to_all x2 -> x1, starting transfers between devices: 17.3 us -> 7.49 us  [body(): lax.all_to_all(part, ('core',) + Y, 0, 0).reshape(CORES, NY, 128, 3 * DH)]
    ppermute x10 -> x11, waiting for transfers between devices: 57.3 us -> 49.7 us  [shift(): return lax.ppermute(values, axes, pairs)]
    ppermute x10 -> x11, starting transfers between devices: 48 us -> 49.6 us  [shift(): return lax.ppermute(values, axes, pairs)]
  transfers between devices with their start and end apart: 14 -> 14, of which waited for: 10 -> 9; matrix products, arithmetic and copies ran while one was open for 1% -> 2% of each run, Pallas kernels for 0% -> 0%
where the time goes in v9:
time: 179 us; the launch traced here: 178 us
  waiting for transfers between devices  76.9 us (43%)
  starting transfers between devices  69.5 us (39%)
  blocking collectives  18.5 us (10%)
  Pallas kernels  6.83 us (4%)
  local copies, waits for them, and re-layouts  3.25 us (2%)
  other arithmetic  2.62 us (1%)
    ppermute x11, waiting for transfers between devices, shift(): return lax.ppermute(values, axes, pairs)  49.7 us
    ppermute x11, starting transfers between devices, shift(): return lax.ppermute(values, axes, pairs)  49.6 us
    all_to_all x1, blocking collectives, body(): kv_mine = lax.all_to_all(kv, ('x', 'yl'), 0, 0)  18.5 us
    all_to_all x2, waiting for transfers between devices, spread(): lax.all_to_all(jnp.broadcast_to(values[None], (count,) + values.shape), a...  17.3 us
    all_to_all x2, starting transfers between devices, spread(): lax.all_to_all(jnp.broadcast_to(values[None], (count,) + values.shape), a...  12.4 us
    all_to_all x1, waiting for transfers between devices, body(): lax.all_to_all(part, ('core',) + Y, 0, 0).reshape(CORES, NY, 128, 3 * DH)  9.97 us
    all_to_all x1, starting transfers between devices, body(): lax.all_to_all(part, ('core',) + Y, 0, 0).reshape(CORES, NY, 128, 3 * DH)  7.49 us
    pallas_call x3, Pallas kernels, kernel_call(): pl.pallas_call(kernel, out_shape=out_shape, in_specs=[smem] * scalars + [...  6.83 us
  transfers between devices with their start and end apart: 14, of which 9 were waited for; matrix products, arithmetic and copies ran while one was open for 2% of the time, Pallas kernels for 0%

profile of v9, /device:TPU:16, one launch (start us, length us, event | category | flops | bytes accessed | tf_op | source)
XLA Modules:
  0.0 177.9 jit_solution(7442615339883858166)
XLA Ops:
  0.0 1.0 convert_reduce_fusion
  1.0 0.7 pad_maximum_fusion.1
  2.3 8.9 %all-to-all-start = ((f32[4,1,768]{2,1,0:T(1,128)}), f32[4,1,768]{2,1,0:T(1,128)S(1)}, u32[]{:S(2)}, u32[]{:S(2)}) async-start(f32[4,1,768]{2,1,0:T(1,128)} %broadcast_in_dim.8), calls=%async_computation | async-start | bytes 24576 | tf_op jit(solution)/shard_map/norm/all_to_all | solution.py:63
  11.3 11.0 %collective-permute-start = (bf16[3,192,256]{2,1,0:T(8,128)(2,1)}, bf16[3,192,256]{2,1,0:T(8,128)(2,1)S(1)}, u32[]{:S(2)}, u32[]{:S(2)}) collective-permute-start(bf16[3,192,256]{2,1,0:T(8,128)(2,1)} %bitcast.37), channel_id=1, source_target_pairs={{0,0},{1,32},{2,64},{3,96},{4,36},{5,68},{6,100},{7,4},{8,72},{9,1... | collective-permute-start | bytes 884744 | tf_op jit(solution)/shard_map/weights/ppermute | solution.py:26
  22.3 0.7 broadcast_in_dim.9
  23.0 1.1 concatenate.55
  24.1 19.7 %collective-permute-done = bf16[3,192,256]{2,1,0:T(8,128)(2,1)S(1)} collective-permute-done((bf16[3,192,256]{2,1,0:T(8,128)(2,1)}, bf16[3,192,256]{2,1,0:T(8,128)(2,1)S(1)}, u32[]{:S(2)}, u32[]{:S(2)}) %collective-permute-start) | collective-permute-done | bytes 294944 | tf_op jit(solution)/shard_map/weights/ppermute | solution.py:26
  43.8 1.9 %collective-permute-start.3 = (bf16[3,192,256]{2,1,0:T(8,128)(2,1)S(1)}, bf16[3,192,256]{2,1,0:T(8,128)(2,1)S(1)}, u32[]{:S(2)}, u32[]{:S(2)}) collective-permute-start(bf16[3,192,256]{2,1,0:T(8,128)(2,1)S(1)} %collective-permute-done), channel_id=1, source_target_pairs={{0,128},{128,256},{256,384},{384,0},{1,129},{129,257},{257,385},{3... | collective-permute-start | bytes 884744 | tf_op jit(solution)/shard_map/weights/ppermute | solution.py:26
  45.7 4.1 %collective-permute-start.2 = (bf16[3,192,256]{2,1,0:T(8,128)(2,1)S(1)}, bf16[3,192,256]{2,1,0:T(8,128)(2,1)S(1)}, u32[]{:S(2)}, u32[]{:S(2)}) collective-permute-start(bf16[3,192,256]{2,1,0:T(8,128)(2,1)S(1)} %collective-permute-done), channel_id=1, source_target_pairs={{0,256},{128,384},{256,0},{384,128},{1,257},{129,385},{257,1},{385... | collective-permute-start | bytes 884744 | tf_op jit(solution)/shard_map/weights/ppermute | solution.py:26
  49.9 3.3 %collective-permute-start.1 = (bf16[3,192,256]{2,1,0:T(8,128)(2,1)S(1)}, bf16[3,192,256]{2,1,0:T(8,128)(2,1)S(1)}, u32[]{:S(2)}, u32[]{:S(2)}) collective-permute-start(bf16[3,192,256]{2,1,0:T(8,128)(2,1)S(1)} %collective-permute-done), channel_id=1, source_target_pairs={{0,384},{128,0},{256,128},{384,256},{1,385},{129,1},{257,129},{385... | collective-permute-start | bytes 884744 | tf_op jit(solution)/shard_map/weights/ppermute | solution.py:26
  53.2 0.8 broadcast_in_dim.11
  54.1 3.5 %all-to-all-start.1 = ((bf16[4,144,384]{2,1,0:T(8,128)(2,1)}), bf16[4,144,384]{2,1,0:T(8,128)(2,1)S(1)}, u32[]{:S(2)}, u32[]{:S(2)}) async-start(bf16[4,144,384]{2,1,0:T(8,128)(2,1)} %broadcast_in_dim.11), calls=%async_computation.1 | async-start | bytes 884736 | tf_op jit(solution)/shard_map/tokens/all_to_all | solution.py:63
  57.5 2.0 %collective-permute-done.1 = bf16[3,192,256]{2,1,0:T(8,128)(2,1)S(1)} collective-permute-done((bf16[3,192,256]{2,1,0:T(8,128)(2,1)S(1)}, bf16[3,192,256]{2,1,0:T(8,128)(2,1)S(1)}, u32[]{:S(2)}, u32[]{:S(2)}) %collective-permute-start.1) | collective-permute-done | bytes 294944 | tf_op jit(solution)/shard_map/weights/ppermute | solution.py:26
  59.7 1.9 %collective-permute-start.4 = (bf16[4,3,192,256]{3,2,1,0:T(8,128)(2,1)S(1)}, bf16[4,3,192,256]{3,2,1,0:T(8,128)(2,1)S(1)}, u32[]{:S(2)}, u32[]{:S(2)}) collective-permute-start(bf16[4,3,192,256]{3,2,1,0:T(8,128)(2,1)S(1)} %pad_maximum_fusion.w_mine), channel_id=1, source_target_pairs={{0,16},{16,0},{1,17},{17,1},{2,18},{18,2},{3,19},{19,3},{4,20},{20... | collective-permute-start | bytes 3538952 | tf_op jit(solution)/shard_map/weights/ppermute | solution.py:26
  61.7 17.3 %all-to-all-done.1.t0 = bf16[4,144,384]{2,1,0:T(8,128)(2,1)S(1)} async-done(((bf16[4,144,384]{2,1,0:T(8,128)(2,1)}), bf16[4,144,384]{2,1,0:T(8,128)(2,1)S(1)}, u32[]{:S(2)}, u32[]{:S(2)}) %all-to-all-start.1) | async-done | bytes 442400 | tf_op jit(solution)/shard_map/tokens/all_to_all | solution.py:63
  78.9 1.9 %collective-permute-start.7 = (bf16[4,144,384]{2,1,0:T(8,128)(2,1)S(1)}, bf16[4,144,384]{2,1,0:T(8,128)(2,1)S(1)}, u32[]{:S(2)}, u32[]{:S(2)}) collective-permute-start(bf16[4,144,384]{2,1,0:T(8,128)(2,1)S(1)} %all-to-all-done.1.t0), channel_id=1, source_target_pairs={{0,4},{4,8},{8,12},{12,32},{32,36},{36,40},{40,44},{44,64},{64,68}... | collective-permute-start | bytes 1327112 | tf_op jit(solution)/shard_map/tokens/ppermute | solution.py:26
  80.9 4.7 %collective-permute-start.6 = (bf16[4,144,384]{2,1,0:T(8,128)(2,1)S(1)}, bf16[4,144,384]{2,1,0:T(8,128)(2,1)}, u32[]{:S(2)}, u32[]{:S(2)}) collective-permute-start(bf16[4,144,384]{2,1,0:T(8,128)(2,1)S(1)} %all-to-all-done.1.t0), channel_id=1, source_target_pairs={{0,8},{4,108},{8,32},{12,4},{32,40},{36,12},{40,64},{44,36},{64,72... | collective-permute-start | bytes 1327112 | tf_op jit(solution)/shard_map/tokens/ppermute | solution.py:26
  85.6 2.3 %collective-permute-start.5 = (bf16[4,144,384]{2,1,0:T(8,128)(2,1)S(1)}, bf16[4,144,384]{2,1,0:T(8,128)(2,1)}, u32[]{:S(2)}, u32[]{:S(2)}) collective-permute-start(bf16[4,144,384]{2,1,0:T(8,128)(2,1)S(1)} %all-to-all-done.1.t0), channel_id=1, source_target_pairs={{0,108},{4,0},{8,4},{12,8},{32,12},{36,32},{40,36},{44,40},{64,44}... | collective-permute-start | bytes 1327112 | tf_op jit(solution)/shard_map/tokens/ppermute | solution.py:26
  88.0 5.2 %collective-permute-done.7.t3 = bf16[4,144,384]{2,1,0:T(8,128)(2,1)S(1)} collective-permute-done((bf16[4,144,384]{2,1,0:T(8,128)(2,1)S(1)}, bf16[4,144,384]{2,1,0:T(8,128)(2,1)S(1)}, u32[]{:S(2)}, u32[]{:S(2)}) %collective-permute-start.7) | collective-permute-done | bytes 442400 | tf_op jit(solution)/shard_map/tokens/ppermute | solution.py:26
  93.2 10.8 %collective-permute-done.6.t2 = bf16[4,144,384]{2,1,0:T(8,128)(2,1)} collective-permute-done((bf16[4,144,384]{2,1,0:T(8,128)(2,1)S(1)}, bf16[4,144,384]{2,1,0:T(8,128)(2,1)}, u32[]{:S(2)}, u32[]{:S(2)}) %collective-permute-start.6) | collective-permute-done | bytes 442400 | tf_op jit(solution)/shard_map/tokens/ppermute | solution.py:26
  104.0 2.0 %collective-permute-done.5.t1 = bf16[4,144,384]{2,1,0:T(8,128)(2,1)} collective-permute-done((bf16[4,144,384]{2,1,0:T(8,128)(2,1)S(1)}, bf16[4,144,384]{2,1,0:T(8,128)(2,1)}, u32[]{:S(2)}, u32[]{:S(2)}) %collective-permute-start.5) | collective-permute-done | bytes 442400 | tf_op jit(solution)/shard_map/tokens/ppermute | solution.py:26
  106.0 4.4 %project.2 = bf16[2,4,128,384]{3,2,1,0:T(8,128)(2,1)} custom-call(s32[4]{0:T(128)S(1)} %pad_add_fusion.where, bf16[4,144,384]{2,1,0:T(8,128)(2,1)S(1)} %all-to-all-done.1.t0, bf16[4,144,384]{2,1,0:T(8,128)(2,1)} %collective-permute-done.5.t1, bf16[4,144,384]{2,1,0:T(8,128)(2,1)} %collective-permute-done.6.t2, ...), custom_call_target="tpu_custom_call" | custom-call | tf_op jit(solution)/shard_map/project/pallas_call | solution.py:166
  110.3 7.5 %all-to-all-start.2 = ((bf16[8,128,384]{2,1,0:T(8,128)(2,1)}), bf16[8,128,384]{2,1,0:T(8,128)(2,1)S(1)}, u32[]{:S(2)}, u32[]{:S(2)}) async-start(bf16[8,128,384]{2,1,0:T(8,128)(2,1)} %bitcast.15), calls=%async_computation.2 | async-start | bytes 1572864 | tf_op jit(solution)/shard_map/project/all_to_all | solution.py:241
  117.8 10.0 %all-to-all-done.2 = bf16[8,128,384]{2,1,0:T(8,128)(2,1)S(1)} async-done(((bf16[8,128,384]{2,1,0:T(8,128)(2,1)}), bf16[8,128,384]{2,1,0:T(8,128)(2,1)S(1)}, u32[]{:S(2)}, u32[]{:S(2)}) %all-to-all-start.2) | async-done | bytes 786464 | tf_op jit(solution)/shard_map/project/all_to_all | solution.py:241
  128.1 18.5 %all_to_all.20.kv_mine = bf16[8,2,256,128]{3,2,1,0:T(8,128)(2,1)S(1)} all-to-all(bf16[8,2,256,128]{3,2,1,0:T(8,128)(2,1)S(1)} %get-tuple-element.18), channel_id=1, replica_groups=mesh['x'=4,'zh'=4,'core'=2,'zl'=4,'yh'=2,'yl'=2] {'x','yl'}, dimensions={0} | all-to-all | bytes 2097152 | tf_op jit(solution)/shard_map/keys/all_to_all | solution.py:252
  146.6 1.9 %collective-permute-start.8 = (bf16[8,2,256,128]{3,2,1,0:T(8,128)(2,1)S(1)}, bf16[8,2,256,128]{3,2,1,0:T(8,128)(2,1)S(1)}, u32[]{:S(2)}, u32[]{:S(2)}) collective-permute-start(bf16[8,2,256,128]{3,2,1,0:T(8,128)(2,1)S(1)} %all_to_all.20.kv_mine), channel_id=1, source_target_pairs={{0,16},{16,0},{1,17},{17,1},{2,18},{18,2},{3,19},{19,3},{4,20},{20... | collective-permute-start | bytes 3145736 | tf_op jit(solution)/shard_map/keys/ppermute | solution.py:26
  148.5 2.6 %collective-permute-done.8.kv_theirs = bf16[8,2,256,128]{3,2,1,0:T(8,128)(2,1)S(1)} collective-permute-done((bf16[8,2,256,128]{3,2,1,0:T(8,128)(2,1)S(1)}, bf16[8,2,256,128]{3,2,1,0:T(8,128)(2,1)S(1)}, u32[]{:S(2)}, u32[]{:S(2)}) %collective-permute-start.8) | collective-permute-done | bytes 1048608 | tf_op jit(solution)/shard_map/keys/ppermute | solution.py:26
  151.1 2.2 %attend.1 = bf16[256,128]{1,0:T(8,128)(2,1)S(1)} custom-call(bf16[256,128]{1,0:T(8,128)(2,1)S(1)} %get-tuple-element.17.q, bf16[8,2,256,128]{3,2,1,0:T(8,128)(2,1)S(1)} %all_to_all.20.kv_mine, bf16[8,2,256,128]{3,2,1,0:T(8,128)(2,1)S(1)} %collective-permute-done.8.kv_theirs), custom_call_target="tpu_custom_call" | custom-call | tf_op jit(solution)/shard_map/attend/pallas_call | solution.py:166
  153.4 7.2 %collective-permute-start.9 = (bf16[128,128]{1,0:T(8,128)(2,1)S(1)}, bf16[128,128]{1,0:T(8,128)(2,1)S(1)}, u32[]{:S(2)}, u32[]{:S(2)}) collective-permute-start(bf16[128,128]{1,0:T(8,128)(2,1)S(1)} %get-tuple-element.21), channel_id=1, source_target_pairs={{0,0},{1,32},{2,64},{3,96},{4,39},{5,71},{6,103},{7,7},{8,74},{9,1... | collective-permute-start | bytes 98312 | tf_op jit(solution)/shard_map/home/ppermute | solution.py:26
  160.6 9.2 %collective-permute-start.10 = (bf16[128,128]{1,0:T(8,128)(2,1)S(1)}, bf16[128,128]{1,0:T(8,128)(2,1)S(1)}, u32[]{:S(2)}, u32[]{:S(2)}) collective-permute-start(bf16[128,128]{1,0:T(8,128)(2,1)S(1)} %get-tuple-element.22), channel_id=1, source_target_pairs={{0,16},{1,48},{2,80},{3,112},{4,55},{5,87},{6,119},{7,23},{8,90},{... | collective-permute-start | bytes 98312 | tf_op jit(solution)/shard_map/home/ppermute | solution.py:26
  169.8 7.4 %collective-permute-done.10 = bf16[128,128]{1,0:T(8,128)(2,1)S(1)} collective-permute-done((bf16[128,128]{1,0:T(8,128)(2,1)S(1)}, bf16[128,128]{1,0:T(8,128)(2,1)S(1)}, u32[]{:S(2)}, u32[]{:S(2)}) %collective-permute-start.10) | collective-permute-done | bytes 32800 | tf_op jit(solution)/shard_map/home/ppermute | solution.py:26
  177.3 0.6 maximum_select_fusion
  (18 shorter events, 1.2 us)
Async XLA Ops:
  2.3 20.6 %all-to-all-start = ((f32[4,1,768]{2,1,0:T(1,128)}), f32[4,1,768]{2,1,0:T(1,128)S(1)}, u32[]{:S(2)}, u32[]{:S(2)}) async-start(f32[4,1,768]{2,1,0:T(1,128)} %broadcast_in_dim.8), calls=%async_computation | async-start | bytes 24576 | tf_op jit(solution)/shard_map/norm/all_to_all | solution.py:63
  11.3 32.6 %collective-permute-start = (bf16[3,192,256]{2,1,0:T(8,128)(2,1)}, bf16[3,192,256]{2,1,0:T(8,128)(2,1)S(1)}, u32[]{:S(2)}, u32[]{:S(2)}) collective-permute-start(bf16[3,192,256]{2,1,0:T(8,128)(2,1)} %bitcast.37), channel_id=1, source_target_pairs={{0,0},{1,32},{2,64},{3,96},{4,36},{5,68},{6,100},{7,4},{8,72},{9,1... | collective-permute-start | bytes 884744 | tf_op jit(solution)/shard_map/weights/ppermute | solution.py:26
  43.8 13.7 %collective-permute-start.3 = (bf16[3,192,256]{2,1,0:T(8,128)(2,1)S(1)}, bf16[3,192,256]{2,1,0:T(8,128)(2,1)S(1)}, u32[]{:S(2)}, u32[]{:S(2)}) collective-permute-start(bf16[3,192,256]{2,1,0:T(8,128)(2,1)S(1)} %collective-permute-done), channel_id=1, source_target_pairs={{0,128},{128,256},{256,384},{384,0},{1,129},{129,257},{257,385},{3... | collective-permute-start | bytes 884744 | tf_op jit(solution)/shard_map/weights/ppermute | solution.py:26
  45.7 11.8 %collective-permute-start.2 = (bf16[3,192,256]{2,1,0:T(8,128)(2,1)S(1)}, bf16[3,192,256]{2,1,0:T(8,128)(2,1)S(1)}, u32[]{:S(2)}, u32[]{:S(2)}) collective-permute-start(bf16[3,192,256]{2,1,0:T(8,128)(2,1)S(1)} %collective-permute-done), channel_id=1, source_target_pairs={{0,256},{128,384},{256,0},{384,128},{1,257},{129,385},{257,1},{385... | collective-permute-start | bytes 884744 | tf_op jit(solution)/shard_map/weights/ppermute | solution.py:26
  49.9 9.7 %collective-permute-start.1 = (bf16[3,192,256]{2,1,0:T(8,128)(2,1)S(1)}, bf16[3,192,256]{2,1,0:T(8,128)(2,1)S(1)}, u32[]{:S(2)}, u32[]{:S(2)}) collective-permute-start(bf16[3,192,256]{2,1,0:T(8,128)(2,1)S(1)} %collective-permute-done), channel_id=1, source_target_pairs={{0,384},{128,0},{256,128},{384,256},{1,385},{129,1},{257,129},{385... | collective-permute-start | bytes 884744 | tf_op jit(solution)/shard_map/weights/ppermute | solution.py:26
  54.1 24.9 %all-to-all-start.1 = ((bf16[4,144,384]{2,1,0:T(8,128)(2,1)}), bf16[4,144,384]{2,1,0:T(8,128)(2,1)S(1)}, u32[]{:S(2)}, u32[]{:S(2)}) async-start(bf16[4,144,384]{2,1,0:T(8,128)(2,1)} %broadcast_in_dim.11), calls=%async_computation.1 | async-start | bytes 884736 | tf_op jit(solution)/shard_map/tokens/all_to_all | solution.py:63
  59.7 19.2 %collective-permute-start.4 = (bf16[4,3,192,256]{3,2,1,0:T(8,128)(2,1)S(1)}, bf16[4,3,192,256]{3,2,1,0:T(8,128)(2,1)S(1)}, u32[]{:S(2)}, u32[]{:S(2)}) collective-permute-start(bf16[4,3,192,256]{3,2,1,0:T(8,128)(2,1)S(1)} %pad_maximum_fusion.w_mine), channel_id=1, source_target_pairs={{0,16},{16,0},{1,17},{17,1},{2,18},{18,2},{3,19},{19,3},{4,20},{20... | collective-permute-start | bytes 3538952 | tf_op jit(solution)/shard_map/weights/ppermute | solution.py:26
  78.9 14.3 %collective-permute-start.7 = (bf16[4,144,384]{2,1,0:T(8,128)(2,1)S(1)}, bf16[4,144,384]{2,1,0:T(8,128)(2,1)S(1)}, u32[]{:S(2)}, u32[]{:S(2)}) collective-permute-start(bf16[4,144,384]{2,1,0:T(8,128)(2,1)S(1)} %all-to-all-done.1.t0), channel_id=1, source_target_pairs={{0,4},{4,8},{8,12},{12,32},{32,36},{36,40},{40,44},{44,64},{64,68}... | collective-permute-start | bytes 1327112 | tf_op jit(solution)/shard_map/tokens/ppermute | solution.py:26
  80.9 23.1 %collective-permute-start.6 = (bf16[4,144,384]{2,1,0:T(8,128)(2,1)S(1)}, bf16[4,144,384]{2,1,0:T(8,128)(2,1)}, u32[]{:S(2)}, u32[]{:S(2)}) collective-permute-start(bf16[4,144,384]{2,1,0:T(8,128)(2,1)S(1)} %all-to-all-done.1.t0), channel_id=1, source_target_pairs={{0,8},{4,108},{8,32},{12,4},{32,40},{36,12},{40,64},{44,36},{64,72... | collective-permute-start | bytes 1327112 | tf_op jit(solution)/shard_map/tokens/ppermute | solution.py:26
  85.6 20.3 %collective-permute-start.5 = (bf16[4,144,384]{2,1,0:T(8,128)(2,1)S(1)}, bf16[4,144,384]{2,1,0:T(8,128)(2,1)}, u32[]{:S(2)}, u32[]{:S(2)}) collective-permute-start(bf16[4,144,384]{2,1,0:T(8,128)(2,1)S(1)} %all-to-all-done.1.t0), channel_id=1, source_target_pairs={{0,108},{4,0},{8,4},{12,8},{32,12},{36,32},{40,36},{44,40},{64,44}... | collective-permute-start | bytes 1327112 | tf_op jit(solution)/shard_map/tokens/ppermute | solution.py:26
  110.3 17.5 %all-to-all-start.2 = ((bf16[8,128,384]{2,1,0:T(8,128)(2,1)}), bf16[8,128,384]{2,1,0:T(8,128)(2,1)S(1)}, u32[]{:S(2)}, u32[]{:S(2)}) async-start(bf16[8,128,384]{2,1,0:T(8,128)(2,1)} %bitcast.15), calls=%async_computation.2 | async-start | bytes 1572864 | tf_op jit(solution)/shard_map/project/all_to_all | solution.py:241
  146.6 4.5 %collective-permute-start.8 = (bf16[8,2,256,128]{3,2,1,0:T(8,128)(2,1)S(1)}, bf16[8,2,256,128]{3,2,1,0:T(8,128)(2,1)S(1)}, u32[]{:S(2)}, u32[]{:S(2)}) collective-permute-start(bf16[8,2,256,128]{3,2,1,0:T(8,128)(2,1)S(1)} %all_to_all.20.kv_mine), channel_id=1, source_target_pairs={{0,16},{16,0},{1,17},{17,1},{2,18},{18,2},{3,19},{19,3},{4,20},{20... | collective-permute-start | bytes 3145736 | tf_op jit(solution)/shard_map/keys/ppermute | solution.py:26
  153.4 16.5 %collective-permute-start.9 = (bf16[128,128]{1,0:T(8,128)(2,1)S(1)}, bf16[128,128]{1,0:T(8,128)(2,1)S(1)}, u32[]{:S(2)}, u32[]{:S(2)}) collective-permute-start(bf16[128,128]{1,0:T(8,128)(2,1)S(1)} %get-tuple-element.21), channel_id=1, source_target_pairs={{0,0},{1,32},{2,64},{3,96},{4,39},{5,71},{6,103},{7,7},{8,74},{9,1... | collective-permute-start | bytes 98312 | tf_op jit(solution)/shard_map/home/ppermute | solution.py:26
  160.6 16.7 %collective-permute-start.10 = (bf16[128,128]{1,0:T(8,128)(2,1)S(1)}, bf16[128,128]{1,0:T(8,128)(2,1)S(1)}, u32[]{:S(2)}, u32[]{:S(2)}) collective-permute-start(bf16[128,128]{1,0:T(8,128)(2,1)S(1)} %get-tuple-element.22), channel_id=1, source_target_pairs={{0,16},{1,48},{2,80},{3,112},{4,55},{5,87},{6,119},{7,23},{8,90},{... | collective-permute-start | bytes 98312 | tf_op jit(solution)/shard_map/home/ppermute | solution.py:26

commit v10 on v9

--- a/solution.py
+++ b/solution.py
@@ -34,11 +34,11 @@
     return shift(values, ("zh", "zl") + Y, move)
 
 
-def to_home(values, cross):
+def to_home(values):
     def move(i):
         zh, core, zl, yh, yl = i
         zh_home = (zh + zl + yh * 2 + yl + 2 * core) % NZH
-        return (zh_home, core ^ cross, zl) + divmod((zh - zl) % NY, 2)
+        return (zh_home, core, zl) + divmod((zh - zl) % NY, 2)
 
     return shift(values, ("zh", "core", "zl") + Y, move)
 
@@ -217,9 +217,9 @@
         along_x = [
             shift(w_moved, ("x",), lambda i, step=step: ((i[0] - step) % NX,)) for step in (1, 2, 3)
         ]
+        t0, *along_x = lax.optimization_barrier((t0, *along_x))
         w_mine = jnp.stack([w_moved] + along_x)
         w_theirs = swap_cores(w_mine)
-        t0, w_mine, w_theirs = lax.optimization_barrier((t0, w_mine, w_theirs))
 
     with jax.named_scope("tokens"):
         t1 = along_z(t0, -1)
@@ -258,8 +258,9 @@
         )
 
     with jax.named_scope("home"):
-        same = to_home(lax.dynamic_slice_in_dim(out, core * 128, 128), 0)
-        cross = to_home(lax.dynamic_slice_in_dim(out, (1 - core) * 128, 128), 1)
+        arrived = to_home(out)
+        same = lax.dynamic_slice_in_dim(arrived, core * 128, 128)
+        cross = swap_cores(lax.dynamic_slice_in_dim(arrived, (1 - core) * 128, 128))
         first = (zh + 3 * NY - y_here - 2 * zl - 2 * core) % NY < 2
         return jnp.where(
             first,

time: 179 us -> 173 us (0.966)
  the two profiles are of different devices: /device:TPU:16 before, /device:TPU:121 now
where the time goes in v10:
time: 173 us; the launch traced here: 172 us
  starting transfers between devices  78.2 us (45%)
  waiting for transfers between devices  62.3 us (36%)
  blocking collectives  18.7 us (11%)
  Pallas kernels  6.83 us (4%)
  local copies, waits for them, and re-layouts  3.24 us (2%)
  other arithmetic  2.62 us (2%)
    ppermute x11, waiting for transfers between devices, shift(): return lax.ppermute(values, axes, pairs)  50.9 us
    ppermute x11, starting transfers between devices, shift(): return lax.ppermute(values, axes, pairs)  43 us
    all_to_all x2, starting transfers between devices, spread(): lax.all_to_all(jnp.broadcast_to(values[None], (count,) + values.shape), a...  25 us
    all_to_all x1, blocking collectives, body(): kv_mine = lax.all_to_all(kv, ('x', 'yl'), 0, 0)  18.7 us
    all_to_all x1, waiting for transfers between devices, body(): lax.all_to_all(part, ('core',) + Y, 0, 0).reshape(CORES, NY, 128, 3 * DH)  10.5 us
    all_to_all x1, starting transfers between devices, body(): lax.all_to_all(part, ('core',) + Y, 0, 0).reshape(CORES, NY, 128, 3 * DH)  10.2 us
    pallas_call x3, Pallas kernels, kernel_call(): pl.pallas_call(kernel, out_shape=out_shape, in_specs=[smem] * scalars + [...  6.83 us
  transfers between devices with their start and end apart: 14, of which 12 were waited for; matrix products, arithmetic and copies ran while one was open for 1% of the time, Pallas kernels for 0%

profile of v10, /device:TPU:121, one launch (start us, length us, event | category | flops | bytes accessed | tf_op | source)
XLA Modules:
  0.0 172.1 jit_solution(12780798077165703028)
XLA Ops:
  0.0 1.0 convert_reduce_fusion
  1.0 0.7 pad_maximum_fusion.1
  2.3 4.1 %all-to-all-start = ((f32[4,1,768]{2,1,0:T(1,128)}), f32[4,1,768]{2,1,0:T(1,128)S(1)}, u32[]{:S(2)}, u32[]{:S(2)}) async-start(f32[4,1,768]{2,1,0:T(1,128)} %broadcast_in_dim.8), calls=%async_computation | async-start | bytes 24576 | tf_op jit(solution)/shard_map/norm/all_to_all | solution.py:63
  6.4 12.5 %collective-permute-start = (bf16[3,192,256]{2,1,0:T(8,128)(2,1)}, bf16[3,192,256]{2,1,0:T(8,128)(2,1)S(1)}, u32[]{:S(2)}, u32[]{:S(2)}) collective-permute-start(bf16[3,192,256]{2,1,0:T(8,128)(2,1)} %bitcast.37), channel_id=1, source_target_pairs={{0,0},{1,32},{2,64},{3,96},{4,36},{5,68},{6,100},{7,4},{8,72},{9,1... | collective-permute-start | bytes 884744 | tf_op jit(solution)/shard_map/weights/ppermute | solution.py:26
  19.7 1.1 concatenate.55
  20.8 5.4 %collective-permute-done = bf16[3,192,256]{2,1,0:T(8,128)(2,1)S(1)} collective-permute-done((bf16[3,192,256]{2,1,0:T(8,128)(2,1)}, bf16[3,192,256]{2,1,0:T(8,128)(2,1)S(1)}, u32[]{:S(2)}, u32[]{:S(2)}) %collective-permute-start) | collective-permute-done | bytes 294944 | tf_op jit(solution)/shard_map/weights/ppermute | solution.py:26
  26.1 0.8 broadcast_in_dim.11
  27.0 20.9 %all-to-all-start.1 = ((bf16[4,144,384]{2,1,0:T(8,128)(2,1)}), bf16[4,144,384]{2,1,0:T(8,128)(2,1)S(1)}, u32[]{:S(2)}, u32[]{:S(2)}) async-start(bf16[4,144,384]{2,1,0:T(8,128)(2,1)} %broadcast_in_dim.11), calls=%async_computation.1 | async-start | bytes 884736 | tf_op jit(solution)/shard_map/tokens/all_to_all | solution.py:63
  47.9 3.1 %collective-permute-start.3 = (bf16[3,192,256]{2,1,0:T(8,128)(2,1)S(1)}, bf16[3,192,256]{2,1,0:T(8,128)(2,1)S(1)}, u32[]{:S(2)}, u32[]{:S(2)}) collective-permute-start(bf16[3,192,256]{2,1,0:T(8,128)(2,1)S(1)} %collective-permute-done), channel_id=1, source_target_pairs={{0,128},{128,256},{256,384},{384,0},{1,129},{129,257},{257,385},{3... | collective-permute-start | bytes 884744 | tf_op jit(solution)/shard_map/weights/ppermute | solution.py:26
  51.0 4.4 %collective-permute-start.2 = (bf16[3,192,256]{2,1,0:T(8,128)(2,1)S(1)}, bf16[3,192,256]{2,1,0:T(8,128)(2,1)S(1)}, u32[]{:S(2)}, u32[]{:S(2)}) collective-permute-start(bf16[3,192,256]{2,1,0:T(8,128)(2,1)S(1)} %collective-permute-done), channel_id=1, source_target_pairs={{0,256},{128,384},{256,0},{384,128},{1,257},{129,385},{257,1},{385... | collective-permute-start | bytes 884744 | tf_op jit(solution)/shard_map/weights/ppermute | solution.py:26
  55.3 3.1 %collective-permute-start.1 = (bf16[3,192,256]{2,1,0:T(8,128)(2,1)S(1)}, bf16[3,192,256]{2,1,0:T(8,128)(2,1)S(1)}, u32[]{:S(2)}, u32[]{:S(2)}) collective-permute-start(bf16[3,192,256]{2,1,0:T(8,128)(2,1)S(1)} %collective-permute-done), channel_id=1, source_target_pairs={{0,384},{128,0},{256,128},{384,256},{1,385},{129,1},{257,129},{385... | collective-permute-start | bytes 884744 | tf_op jit(solution)/shard_map/weights/ppermute | solution.py:26
  58.7 7.3 %collective-permute-done.2 = bf16[3,192,256]{2,1,0:T(8,128)(2,1)S(1)} collective-permute-done((bf16[3,192,256]{2,1,0:T(8,128)(2,1)S(1)}, bf16[3,192,256]{2,1,0:T(8,128)(2,1)S(1)}, u32[]{:S(2)}, u32[]{:S(2)}) %collective-permute-start.2) | collective-permute-done | bytes 294944 | tf_op jit(solution)/shard_map/weights/ppermute | solution.py:26
  66.0 1.3 collective-permute-done.1
  67.3 0.8 all-to-all-done.1.t0
  68.2 3.0 %collective-permute-start.7 = (bf16[4,3,192,256]{3,2,1,0:T(8,128)(2,1)S(1)}, bf16[4,3,192,256]{3,2,1,0:T(8,128)(2,1)S(1)}, u32[]{:S(2)}, u32[]{:S(2)}) collective-permute-start(bf16[4,3,192,256]{3,2,1,0:T(8,128)(2,1)S(1)} %pad_maximum_fusion.w_mine), channel_id=1, source_target_pairs={{0,16},{16,0},{1,17},{17,1},{2,18},{18,2},{3,19},{19,3},{4,20},{20... | collective-permute-start | bytes 3538952 | tf_op jit(solution)/shard_map/weights/ppermute | solution.py:26
  71.3 2.0 %collective-permute-start.6 = (bf16[4,144,384]{2,1,0:T(8,128)(2,1)S(1)}, bf16[4,144,384]{2,1,0:T(8,128)(2,1)S(1)}, u32[]{:S(2)}, u32[]{:S(2)}) collective-permute-start(bf16[4,144,384]{2,1,0:T(8,128)(2,1)S(1)} %all-to-all-done.1.t0), channel_id=1, source_target_pairs={{0,4},{4,8},{8,12},{12,32},{32,36},{36,40},{40,44},{44,64},{64,68}... | collective-permute-start | bytes 1327112 | tf_op jit(solution)/shard_map/tokens/ppermute | solution.py:26
  73.2 1.9 %collective-permute-start.5 = (bf16[4,144,384]{2,1,0:T(8,128)(2,1)S(1)}, bf16[4,144,384]{2,1,0:T(8,128)(2,1)}, u32[]{:S(2)}, u32[]{:S(2)}) collective-permute-start(bf16[4,144,384]{2,1,0:T(8,128)(2,1)S(1)} %all-to-all-done.1.t0), channel_id=1, source_target_pairs={{0,8},{4,108},{8,32},{12,4},{32,40},{36,12},{40,64},{44,36},{64,72... | collective-permute-start | bytes 1327112 | tf_op jit(solution)/shard_map/tokens/ppermute | solution.py:26
  75.2 3.3 %collective-permute-start.4 = (bf16[4,144,384]{2,1,0:T(8,128)(2,1)S(1)}, bf16[4,144,384]{2,1,0:T(8,128)(2,1)}, u32[]{:S(2)}, u32[]{:S(2)}) collective-permute-start(bf16[4,144,384]{2,1,0:T(8,128)(2,1)S(1)} %all-to-all-done.1.t0), channel_id=1, source_target_pairs={{0,108},{4,0},{8,4},{12,8},{32,12},{36,32},{40,36},{44,40},{64,44}... | collective-permute-start | bytes 1327112 | tf_op jit(solution)/shard_map/tokens/ppermute | solution.py:26
  78.6 6.5 %collective-permute-done.6.t3 = bf16[4,144,384]{2,1,0:T(8,128)(2,1)S(1)} collective-permute-done((bf16[4,144,384]{2,1,0:T(8,128)(2,1)S(1)}, bf16[4,144,384]{2,1,0:T(8,128)(2,1)S(1)}, u32[]{:S(2)}, u32[]{:S(2)}) %collective-permute-start.6) | collective-permute-done | bytes 442400 | tf_op jit(solution)/shard_map/tokens/ppermute | solution.py:26
  85.1 3.8 %collective-permute-done.5.t2 = bf16[4,144,384]{2,1,0:T(8,128)(2,1)} collective-permute-done((bf16[4,144,384]{2,1,0:T(8,128)(2,1)S(1)}, bf16[4,144,384]{2,1,0:T(8,128)(2,1)}, u32[]{:S(2)}, u32[]{:S(2)}) %collective-permute-start.5) | collective-permute-done | bytes 442400 | tf_op jit(solution)/shard_map/tokens/ppermute | solution.py:26
  88.9 10.1 %collective-permute-done.4.t1 = bf16[4,144,384]{2,1,0:T(8,128)(2,1)} collective-permute-done((bf16[4,144,384]{2,1,0:T(8,128)(2,1)S(1)}, bf16[4,144,384]{2,1,0:T(8,128)(2,1)}, u32[]{:S(2)}, u32[]{:S(2)}) %collective-permute-start.4) | collective-permute-done | bytes 442400 | tf_op jit(solution)/shard_map/tokens/ppermute | solution.py:26
  98.9 4.4 %project.2 = bf16[2,4,128,384]{3,2,1,0:T(8,128)(2,1)} custom-call(s32[4]{0:T(128)S(1)} %pad_add_fusion.where, bf16[4,144,384]{2,1,0:T(8,128)(2,1)S(1)} %all-to-all-done.1.t0, bf16[4,144,384]{2,1,0:T(8,128)(2,1)} %collective-permute-done.4.t1, bf16[4,144,384]{2,1,0:T(8,128)(2,1)} %collective-permute-done.5.t2, ...), custom_call_target="tpu_custom_call" | custom-call | tf_op jit(solution)/shard_map/project/pallas_call | solution.py:166
  103.3 10.2 %all-to-all-start.2 = ((bf16[8,128,384]{2,1,0:T(8,128)(2,1)}), bf16[8,128,384]{2,1,0:T(8,128)(2,1)S(1)}, u32[]{:S(2)}, u32[]{:S(2)}) async-start(bf16[8,128,384]{2,1,0:T(8,128)(2,1)} %bitcast.15), calls=%async_computation.2 | async-start | bytes 1572864 | tf_op jit(solution)/shard_map/project/all_to_all | solution.py:241
  113.6 10.5 %all-to-all-done.2 = bf16[8,128,384]{2,1,0:T(8,128)(2,1)S(1)} async-done(((bf16[8,128,384]{2,1,0:T(8,128)(2,1)}), bf16[8,128,384]{2,1,0:T(8,128)(2,1)S(1)}, u32[]{:S(2)}, u32[]{:S(2)}) %all-to-all-start.2) | async-done | bytes 786464 | tf_op jit(solution)/shard_map/project/all_to_all | solution.py:241
  124.4 18.7 %all_to_all.20.kv_mine = bf16[8,2,256,128]{3,2,1,0:T(8,128)(2,1)S(1)} all-to-all(bf16[8,2,256,128]{3,2,1,0:T(8,128)(2,1)S(1)} %get-tuple-element.20), channel_id=1, replica_groups=mesh['x'=4,'zh'=4,'core'=2,'zl'=4,'yh'=2,'yl'=2] {'x','yl'}, dimensions={0} | all-to-all | bytes 2097152 | tf_op jit(solution)/shard_map/keys/all_to_all | solution.py:252
  143.1 4.0 %collective-permute-start.8 = (bf16[8,2,256,128]{3,2,1,0:T(8,128)(2,1)S(1)}, bf16[8,2,256,128]{3,2,1,0:T(8,128)(2,1)S(1)}, u32[]{:S(2)}, u32[]{:S(2)}) collective-permute-start(bf16[8,2,256,128]{3,2,1,0:T(8,128)(2,1)S(1)} %all_to_all.20.kv_mine), channel_id=1, source_target_pairs={{0,16},{16,0},{1,17},{17,1},{2,18},{18,2},{3,19},{19,3},{4,20},{20... | collective-permute-start | bytes 3145736 | tf_op jit(solution)/shard_map/keys/ppermute | solution.py:26
  147.1 2.3 %collective-permute-done.8.kv_theirs = bf16[8,2,256,128]{3,2,1,0:T(8,128)(2,1)S(1)} collective-permute-done((bf16[8,2,256,128]{3,2,1,0:T(8,128)(2,1)S(1)}, bf16[8,2,256,128]{3,2,1,0:T(8,128)(2,1)S(1)}, u32[]{:S(2)}, u32[]{:S(2)}) %collective-permute-start.8) | collective-permute-done | bytes 1048608 | tf_op jit(solution)/shard_map/keys/ppermute | solution.py:26
  149.4 2.2 %attend.1 = bf16[256,128]{1,0:T(8,128)(2,1)S(1)} custom-call(bf16[256,128]{1,0:T(8,128)(2,1)S(1)} %get-tuple-element.19.q, bf16[8,2,256,128]{3,2,1,0:T(8,128)(2,1)S(1)} %all_to_all.20.kv_mine, bf16[8,2,256,128]{3,2,1,0:T(8,128)(2,1)S(1)} %collective-permute-done.8.kv_theirs), custom_call_target="tpu_custom_call" | custom-call | tf_op jit(solution)/shard_map/attend/pallas_call | solution.py:166
  151.6 3.9 %collective-permute-start.9 = (bf16[256,128]{1,0:T(8,128)(2,1)S(1)}, bf16[256,128]{1,0:T(8,128)(2,1)S(1)}, u32[]{:S(2)}, u32[]{:S(2)}) collective-permute-start(bf16[256,128]{1,0:T(8,128)(2,1)S(1)} %attend.1), channel_id=1, source_target_pairs={{0,0},{1,32},{2,64},{3,96},{4,39},{5,71},{6,103},{7,7},{8,74},{9,1... | collective-permute-start | bytes 196616 | tf_op jit(solution)/shard_map/home/ppermute | solution.py:26
  155.5 12.9 %collective-permute-done.9 = bf16[256,128]{1,0:T(8,128)(2,1)S(1)} collective-permute-done((bf16[256,128]{1,0:T(8,128)(2,1)S(1)}, bf16[256,128]{1,0:T(8,128)(2,1)S(1)}, u32[]{:S(2)}, u32[]{:S(2)}) %collective-permute-start.9) | collective-permute-done | bytes 65568 | tf_op jit(solution)/shard_map/home/ppermute | solution.py:26
  168.4 1.9 %collective-permute-start.10 = (bf16[128,128]{1,0:T(8,128)(2,1)S(1)}, bf16[128,128]{1,0:T(8,128)(2,1)S(1)}, u32[]{:S(2)}, u32[]{:S(2)}) collective-permute-start(bf16[128,128]{1,0:T(8,128)(2,1)S(1)} %get-tuple-element.24), channel_id=1, source_target_pairs={{0,16},{16,0},{1,17},{17,1},{2,18},{18,2},{3,19},{19,3},{4,20},{20... | collective-permute-start | bytes 98312 | tf_op jit(solution)/shard_map/home/ppermute | solution.py:26
  170.4 1.1 collective-permute-done.10
  (18 shorter events, 2.8 us)
Async XLA Ops:
  2.3 17.3 %all-to-all-start = ((f32[4,1,768]{2,1,0:T(1,128)}), f32[4,1,768]{2,1,0:T(1,128)S(1)}, u32[]{:S(2)}, u32[]{:S(2)}) async-start(f32[4,1,768]{2,1,0:T(1,128)} %broadcast_in_dim.8), calls=%async_computation | async-start | bytes 24576 | tf_op jit(solution)/shard_map/norm/all_to_all | solution.py:63
  6.4 19.7 %collective-permute-start = (bf16[3,192,256]{2,1,0:T(8,128)(2,1)}, bf16[3,192,256]{2,1,0:T(8,128)(2,1)S(1)}, u32[]{:S(2)}, u32[]{:S(2)}) collective-permute-start(bf16[3,192,256]{2,1,0:T(8,128)(2,1)} %bitcast.37), channel_id=1, source_target_pairs={{0,0},{1,32},{2,64},{3,96},{4,36},{5,68},{6,100},{7,4},{8,72},{9,1... | collective-permute-start | bytes 884744 | tf_op jit(solution)/shard_map/weights/ppermute | solution.py:26
  27.0 41.1 %all-to-all-start.1 = ((bf16[4,144,384]{2,1,0:T(8,128)(2,1)}), bf16[4,144,384]{2,1,0:T(8,128)(2,1)S(1)}, u32[]{:S(2)}, u32[]{:S(2)}) async-start(bf16[4,144,384]{2,1,0:T(8,128)(2,1)} %broadcast_in_dim.11), calls=%async_computation.1 | async-start | bytes 884736 | tf_op jit(solution)/shard_map/tokens/all_to_all | solution.py:63
  47.9 10.8 %collective-permute-start.3 = (bf16[3,192,256]{2,1,0:T(8,128)(2,1)S(1)}, bf16[3,192,256]{2,1,0:T(8,128)(2,1)S(1)}, u32[]{:S(2)}, u32[]{:S(2)}) collective-permute-start(bf16[3,192,256]{2,1,0:T(8,128)(2,1)S(1)} %collective-permute-done), channel_id=1, source_target_pairs={{0,128},{128,256},{256,384},{384,0},{1,129},{129,257},{257,385},{3... | collective-permute-start | bytes 884744 | tf_op jit(solution)/shard_map/weights/ppermute | solution.py:26
  51.0 15.0 %collective-permute-start.2 = (bf16[3,192,256]{2,1,0:T(8,128)(2,1)S(1)}, bf16[3,192,256]{2,1,0:T(8,128)(2,1)S(1)}, u32[]{:S(2)}, u32[]{:S(2)}) collective-permute-start(bf16[3,192,256]{2,1,0:T(8,128)(2,1)S(1)} %collective-permute-done), channel_id=1, source_target_pairs={{0,256},{128,384},{256,0},{384,128},{1,257},{129,385},{257,1},{385... | collective-permute-start | bytes 884744 | tf_op jit(solution)/shard_map/weights/ppermute | solution.py:26
  55.3 11.9 %collective-permute-start.1 = (bf16[3,192,256]{2,1,0:T(8,128)(2,1)S(1)}, bf16[3,192,256]{2,1,0:T(8,128)(2,1)S(1)}, u32[]{:S(2)}, u32[]{:S(2)}) collective-permute-start(bf16[3,192,256]{2,1,0:T(8,128)(2,1)S(1)} %collective-permute-done), channel_id=1, source_target_pairs={{0,384},{128,0},{256,128},{384,256},{1,385},{129,1},{257,129},{385... | collective-permute-start | bytes 884744 | tf_op jit(solution)/shard_map/weights/ppermute | solution.py:26
  68.2 30.7 %collective-permute-start.7 = (bf16[4,3,192,256]{3,2,1,0:T(8,128)(2,1)S(1)}, bf16[4,3,192,256]{3,2,1,0:T(8,128)(2,1)S(1)}, u32[]{:S(2)}, u32[]{:S(2)}) collective-permute-start(bf16[4,3,192,256]{3,2,1,0:T(8,128)(2,1)S(1)} %pad_maximum_fusion.w_mine), channel_id=1, source_target_pairs={{0,16},{16,0},{1,17},{17,1},{2,18},{18,2},{3,19},{19,3},{4,20},{20... | collective-permute-start | bytes 3538952 | tf_op jit(solution)/shard_map/weights/ppermute | solution.py:26
  71.3 13.8 %collective-permute-start.6 = (bf16[4,144,384]{2,1,0:T(8,128)(2,1)S(1)}, bf16[4,144,384]{2,1,0:T(8,128)(2,1)S(1)}, u32[]{:S(2)}, u32[]{:S(2)}) collective-permute-start(bf16[4,144,384]{2,1,0:T(8,128)(2,1)S(1)} %all-to-all-done.1.t0), channel_id=1, source_target_pairs={{0,4},{4,8},{8,12},{12,32},{32,36},{36,40},{40,44},{44,64},{64,68}... | collective-permute-start | bytes 1327112 | tf_op jit(solution)/shard_map/tokens/ppermute | solution.py:26
  73.2 15.6 %collective-permute-start.5 = (bf16[4,144,384]{2,1,0:T(8,128)(2,1)S(1)}, bf16[4,144,384]{2,1,0:T(8,128)(2,1)}, u32[]{:S(2)}, u32[]{:S(2)}) collective-permute-start(bf16[4,144,384]{2,1,0:T(8,128)(2,1)S(1)} %all-to-all-done.1.t0), channel_id=1, source_target_pairs={{0,8},{4,108},{8,32},{12,4},{32,40},{36,12},{40,64},{44,36},{64,72... | collective-permute-start | bytes 1327112 | tf_op jit(solution)/shard_map/tokens/ppermute | solution.py:26
  75.2 23.8 %collective-permute-start.4 = (bf16[4,144,384]{2,1,0:T(8,128)(2,1)S(1)}, bf16[4,144,384]{2,1,0:T(8,128)(2,1)}, u32[]{:S(2)}, u32[]{:S(2)}) collective-permute-start(bf16[4,144,384]{2,1,0:T(8,128)(2,1)S(1)} %all-to-all-done.1.t0), channel_id=1, source_target_pairs={{0,108},{4,0},{8,4},{12,8},{32,12},{36,32},{40,36},{44,40},{64,44}... | collective-permute-start | bytes 1327112 | tf_op jit(solution)/shard_map/tokens/ppermute | solution.py:26
  103.3 20.8 %all-to-all-start.2 = ((bf16[8,128,384]{2,1,0:T(8,128)(2,1)}), bf16[8,128,384]{2,1,0:T(8,128)(2,1)S(1)}, u32[]{:S(2)}, u32[]{:S(2)}) async-start(bf16[8,128,384]{2,1,0:T(8,128)(2,1)} %bitcast.15), calls=%async_computation.2 | async-start | bytes 1572864 | tf_op jit(solution)/shard_map/project/all_to_all | solution.py:241
  143.1 6.2 %collective-permute-start.8 = (bf16[8,2,256,128]{3,2,1,0:T(8,128)(2,1)S(1)}, bf16[8,2,256,128]{3,2,1,0:T(8,128)(2,1)S(1)}, u32[]{:S(2)}, u32[]{:S(2)}) collective-permute-start(bf16[8,2,256,128]{3,2,1,0:T(8,128)(2,1)S(1)} %all_to_all.20.kv_mine), channel_id=1, source_target_pairs={{0,16},{16,0},{1,17},{17,1},{2,18},{18,2},{3,19},{19,3},{4,20},{20... | collective-permute-start | bytes 3145736 | tf_op jit(solution)/shard_map/keys/ppermute | solution.py:26
  151.6 16.8 %collective-permute-start.9 = (bf16[256,128]{1,0:T(8,128)(2,1)S(1)}, bf16[256,128]{1,0:T(8,128)(2,1)S(1)}, u32[]{:S(2)}, u32[]{:S(2)}) collective-permute-start(bf16[256,128]{1,0:T(8,128)(2,1)S(1)} %attend.1), channel_id=1, source_target_pairs={{0,0},{1,32},{2,64},{3,96},{4,39},{5,71},{6,103},{7,7},{8,74},{9,1... | collective-permute-start | bytes 196616 | tf_op jit(solution)/shard_map/home/ppermute | solution.py:26
  168.4 3.1 %collective-permute-start.10 = (bf16[128,128]{1,0:T(8,128)(2,1)S(1)}, bf16[128,128]{1,0:T(8,128)(2,1)S(1)}, u32[]{:S(2)}, u32[]{:S(2)}) collective-permute-start(bf16[128,128]{1,0:T(8,128)(2,1)S(1)} %get-tuple-element.24), channel_id=1, source_target_pairs={{0,16},{16,0},{1,17},{17,1},{2,18},{18,2},{3,19},{19,3},{4,20},{20... | collective-permute-start | bytes 98312 | tf_op jit(solution)/shard_map/home/ppermute | solution.py:26

commit v11 on v10

--- a/solution.py
+++ b/solution.py
@@ -26,10 +26,14 @@
     return lax.ppermute(values, axes, pairs)
 
 
+def plane_turn(zl):
+    return (0, 1, 0, 2)[zl]
+
+
 def to_plane(values):
     def move(i):
         zh, zl, yh, yl = i
-        return ((yh * 2 + yl + zl) % NZH, zl) + divmod(zh, 2)
+        return ((yh * 2 + yl + plane_turn(zl)) % NZH, (zl + 2) % NZL) + divmod(zh, 2)
 
     return shift(values, ("zh", "zl") + Y, move)
 
@@ -37,8 +41,9 @@
 def to_home(values):
     def move(i):
         zh, core, zl, yh, yl = i
-        zh_home = (zh + zl + yh * 2 + yl + 2 * core) % NZH
-        return (zh_home, core, zl) + divmod((zh - zl) % NY, 2)
+        step = 4 * ((yh * 2 + yl + 2 * core + zl) % 4) + 2
+        zh_home, zl_home = divmod((zh * NZL + zl + step) % 16, NZL)
+        return (zh_home, core, zl_home) + divmod((zh - plane_turn(zl_home)) % NY, 2)
 
     return shift(values, ("zh", "core", "zl") + Y, move)
 
@@ -179,26 +184,20 @@
     zh = lax.axis_index("zh")
     y_high = lax.axis_index("yh")
     y_here = y_high * 2 + lax.axis_index("yl")
-    turn = (zh + zl) % NZH
+    turn = (zh + zl + (zl >= 2)) % NZH
     where = jnp.stack([zl, core, turn, lax.axis_index("x")]).astype(jnp.int32)
 
     with jax.named_scope("weights"):
         w_moved = to_plane(jnp.transpose(w_qkv, (1, 0, 2)))
+        head_gain = to_plane(jnp.concatenate([q_gain, k_gain]).reshape(2, 2, 1, DH))
+        head_gain = lax.dynamic_index_in_dim(head_gain, y_high, 1, keepdims=False)
 
     with jax.named_scope("norm"):
         x = tokens.astype(jnp.float32)
         shared = spread(
-            jnp.concatenate([jnp.sum(x, axis=1), jnp.sum(x * x, axis=1), q_gain, k_gain])[None],
-            Y,
-            NY,
-        )[:, 0]
-        sums = jnp.sum(shared[:, :256], axis=0)
-        head_gain = lax.dynamic_index_in_dim(
-            shared[:, 256:], (zh + NY - zl) % NY, 0, keepdims=False
-        )
-        head_gain = lax.dynamic_index_in_dim(
-            head_gain.reshape(2, 2, 1, DH), y_high, 1, keepdims=False
-        )
+            jnp.concatenate([jnp.sum(x, axis=1), jnp.sum(x * x, axis=1)])[None], Y, NY
+        )
+        sums = jnp.sum(shared[:, 0], axis=0)
         extended = jnp.concatenate(
             [
                 tokens,
@@ -261,7 +260,10 @@
         arrived = to_home(out)
         same = lax.dynamic_slice_in_dim(arrived, core * 128, 128)
         cross = swap_cores(lax.dynamic_slice_in_dim(arrived, (1 - core) * 128, 128))
-        first = (zh + 3 * NY - y_here - 2 * zl - 2 * core) % NY < 2
+        zl_from = (zl + 2) % NZL
+        zh_from = y_here + jnp.where(zl == 1, 1, jnp.where(zl == 3, 2, 0))
+        y_from = zh + 4 * NY - zh_from - zl_from - (zl_from >= 2) - 2 * core
+        first = y_from % NY < 2
         return jnp.where(
             first,
             jnp.concatenate([same, cross], axis=1),

time: 173 us -> 173 us (level)
  the two profiles are of different devices: /device:TPU:121 before, /device:TPU:16 now
where the time goes in v11:
time: 173 us; the launch traced here: 171 us
  starting transfers between devices  81.7 us (47%)
  waiting for transfers between devices  59.8 us (35%)
  blocking collectives  17.7 us (10%)
  Pallas kernels  6.84 us (4%)
  local copies, waits for them, and re-layouts  3.2 us (2%)
  other arithmetic  1.94 us (1%)
    ppermute x12, waiting for transfers between devices, shift(): return lax.ppermute(values, axes, pairs)  59.8 us
    ppermute x12, starting transfers between devices, shift(): return lax.ppermute(values, axes, pairs)  58.5 us
    all_to_all x1, blocking collectives, body(): kv_mine = lax.all_to_all(kv, ('x', 'yl'), 0, 0)  17.7 us
    all_to_all x2, starting transfers between devices, spread(): lax.all_to_all(jnp.broadcast_to(values[None], (count,) + values.shape), a...  16.9 us
    pallas_call x3, Pallas kernels, kernel_call(): pl.pallas_call(kernel, out_shape=out_shape, in_specs=[smem] * scalars + [...  6.84 us
    all_to_all x1, starting transfers between devices, body(): lax.all_to_all(part, ('core',) + Y, 0, 0).reshape(CORES, NY, 128, 3 * DH)  6.31 us
  transfers between devices with their start and end apart: 15, of which 10 were waited for; matrix products, arithmetic and copies ran while one was open for 1% of the time, Pallas kernels for 0%

profile of v11, /device:TPU:16, one launch (start us, length us, event | category | flops | bytes accessed | tf_op | source)
XLA Modules:
  0.0 171.4 jit_solution(5422598662558594952)
XLA Ops:
  0.0 1.0 convert_reduce_fusion
  1.6 8.9 %all-to-all-start = ((f32[4,1,256]{2,1,0:T(1,128)}), f32[4,1,256]{2,1,0:T(1,128)S(1)}, u32[]{:S(2)}, u32[]{:S(2)}) async-start(f32[4,1,256]{2,1,0:T(1,128)} %broadcast_in_dim.8), calls=%async_computation | async-start | bytes 8192 | tf_op jit(solution)/shard_map/norm/all_to_all | solution.py:68
  10.5 10.1 %collective-permute-start = (bf16[3,192,256]{2,1,0:T(8,128)(2,1)}, bf16[3,192,256]{2,1,0:T(8,128)(2,1)S(1)}, u32[]{:S(2)}, u32[]{:S(2)}) collective-permute-start(bf16[3,192,256]{2,1,0:T(8,128)(2,1)} %bitcast.34), channel_id=1, source_target_pairs={{0,8},{1,40},{2,72},{3,104},{4,44},{5,76},{6,108},{7,12},{8,0},{9,... | collective-permute-start | bytes 884744 | tf_op jit(solution)/shard_map/weights/ppermute | solution.py:26
  20.7 0.7 broadcast_in_dim.9
  21.4 1.1 concatenate.63
  22.6 14.6 %collective-permute-done = bf16[3,192,256]{2,1,0:T(8,128)(2,1)S(1)} collective-permute-done((bf16[3,192,256]{2,1,0:T(8,128)(2,1)}, bf16[3,192,256]{2,1,0:T(8,128)(2,1)S(1)}, u32[]{:S(2)}, u32[]{:S(2)}) %collective-permute-start) | collective-permute-done | bytes 294944 | tf_op jit(solution)/shard_map/weights/ppermute | solution.py:26
  37.1 0.8 broadcast_in_dim.11
  37.9 8.0 %all-to-all-start.1 = ((bf16[4,144,384]{2,1,0:T(8,128)(2,1)}), bf16[4,144,384]{2,1,0:T(8,128)(2,1)S(1)}, u32[]{:S(2)}, u32[]{:S(2)}) async-start(bf16[4,144,384]{2,1,0:T(8,128)(2,1)} %broadcast_in_dim.11), calls=%async_computation.1 | async-start | bytes 884736 | tf_op jit(solution)/shard_map/tokens/all_to_all | solution.py:68
  45.9 4.7 %collective-permute-start.1 = (bf16[3,192,256]{2,1,0:T(8,128)(2,1)S(1)}, bf16[3,192,256]{2,1,0:T(8,128)(2,1)S(1)}, u32[]{:S(2)}, u32[]{:S(2)}) collective-permute-start(bf16[3,192,256]{2,1,0:T(8,128)(2,1)S(1)} %collective-permute-done), channel_id=1, source_target_pairs={{0,384},{128,0},{256,128},{384,256},{1,385},{129,1},{257,129},{385... | collective-permute-start | bytes 884744 | tf_op jit(solution)/shard_map/weights/ppermute | solution.py:26
  50.5 2.7 %collective-permute-start.2 = (bf16[3,192,256]{2,1,0:T(8,128)(2,1)S(1)}, bf16[3,192,256]{2,1,0:T(8,128)(2,1)S(1)}, u32[]{:S(2)}, u32[]{:S(2)}) collective-permute-start(bf16[3,192,256]{2,1,0:T(8,128)(2,1)S(1)} %collective-permute-done), channel_id=1, source_target_pairs={{0,256},{128,384},{256,0},{384,128},{1,257},{129,385},{257,1},{385... | collective-permute-start | bytes 884744 | tf_op jit(solution)/shard_map/weights/ppermute | solution.py:26
  53.3 2.8 %collective-permute-start.3 = (bf16[3,192,256]{2,1,0:T(8,128)(2,1)S(1)}, bf16[3,192,256]{2,1,0:T(8,128)(2,1)S(1)}, u32[]{:S(2)}, u32[]{:S(2)}) collective-permute-start(bf16[3,192,256]{2,1,0:T(8,128)(2,1)S(1)} %collective-permute-done), channel_id=1, source_target_pairs={{0,128},{128,256},{256,384},{384,0},{1,129},{129,257},{257,385},{3... | collective-permute-start | bytes 884744 | tf_op jit(solution)/shard_map/weights/ppermute | solution.py:26
  56.1 4.7 %collective-permute-done.1 = bf16[3,192,256]{2,1,0:T(8,128)(2,1)S(1)} collective-permute-done((bf16[3,192,256]{2,1,0:T(8,128)(2,1)S(1)}, bf16[3,192,256]{2,1,0:T(8,128)(2,1)S(1)}, u32[]{:S(2)}, u32[]{:S(2)}) %collective-permute-start.1) | collective-permute-done | bytes 294944 | tf_op jit(solution)/shard_map/weights/ppermute | solution.py:26
  60.7 2.5 %collective-permute-done.2 = bf16[3,192,256]{2,1,0:T(8,128)(2,1)S(1)} collective-permute-done((bf16[3,192,256]{2,1,0:T(8,128)(2,1)S(1)}, bf16[3,192,256]{2,1,0:T(8,128)(2,1)S(1)}, u32[]{:S(2)}, u32[]{:S(2)}) %collective-permute-start.2) | collective-permute-done | bytes 294944 | tf_op jit(solution)/shard_map/weights/ppermute | solution.py:26
  63.2 3.1 %collective-permute-done.3 = bf16[3,192,256]{2,1,0:T(8,128)(2,1)S(1)} collective-permute-done((bf16[3,192,256]{2,1,0:T(8,128)(2,1)S(1)}, bf16[3,192,256]{2,1,0:T(8,128)(2,1)S(1)}, u32[]{:S(2)}, u32[]{:S(2)}) %collective-permute-start.3) | collective-permute-done | bytes 294944 | tf_op jit(solution)/shard_map/weights/ppermute | solution.py:26
  66.5 1.9 %collective-permute-start.7 = (bf16[4,3,192,256]{3,2,1,0:T(8,128)(2,1)S(1)}, bf16[4,3,192,256]{3,2,1,0:T(8,128)(2,1)S(1)}, u32[]{:S(2)}, u32[]{:S(2)}) collective-permute-start(bf16[4,3,192,256]{3,2,1,0:T(8,128)(2,1)S(1)} %pad_maximum_fusion.w_mine), channel_id=1, source_target_pairs={{0,16},{16,0},{1,17},{17,1},{2,18},{18,2},{3,19},{19,3},{4,20},{20... | collective-permute-start | bytes 3538952 | tf_op jit(solution)/shard_map/weights/ppermute | solution.py:26
  68.4 9.2 %collective-permute-start.4 = (bf16[4,144,384]{2,1,0:T(8,128)(2,1)S(1)}, bf16[4,144,384]{2,1,0:T(8,128)(2,1)S(1)}, u32[]{:S(2)}, u32[]{:S(2)}) collective-permute-start(bf16[4,144,384]{2,1,0:T(8,128)(2,1)S(1)} %all-to-all-done.1.t0), channel_id=1, source_target_pairs={{0,108},{4,0},{8,4},{12,8},{32,12},{36,32},{40,36},{44,40},{64,44}... | collective-permute-start | bytes 1327112 | tf_op jit(solution)/shard_map/tokens/ppermute | solution.py:26
  77.6 2.0 %collective-permute-start.5 = (bf16[4,144,384]{2,1,0:T(8,128)(2,1)S(1)}, bf16[4,144,384]{2,1,0:T(8,128)(2,1)}, u32[]{:S(2)}, u32[]{:S(2)}) collective-permute-start(bf16[4,144,384]{2,1,0:T(8,128)(2,1)S(1)} %all-to-all-done.1.t0), channel_id=1, source_target_pairs={{0,8},{4,108},{8,32},{12,4},{32,40},{36,12},{40,64},{44,36},{64,72... | collective-permute-start | bytes 1327112 | tf_op jit(solution)/shard_map/tokens/ppermute | solution.py:26
  79.6 3.8 %collective-permute-start.6 = (bf16[4,144,384]{2,1,0:T(8,128)(2,1)S(1)}, bf16[4,144,384]{2,1,0:T(8,128)(2,1)}, u32[]{:S(2)}, u32[]{:S(2)}) collective-permute-start(bf16[4,144,384]{2,1,0:T(8,128)(2,1)S(1)} %all-to-all-done.1.t0), channel_id=1, source_target_pairs={{0,4},{4,8},{8,12},{12,32},{32,36},{36,40},{40,44},{44,64},{64,68}... | collective-permute-start | bytes 1327112 | tf_op jit(solution)/shard_map/tokens/ppermute | solution.py:26
  83.5 13.6 %collective-permute-done.4.t1 = bf16[4,144,384]{2,1,0:T(8,128)(2,1)S(1)} collective-permute-done((bf16[4,144,384]{2,1,0:T(8,128)(2,1)S(1)}, bf16[4,144,384]{2,1,0:T(8,128)(2,1)S(1)}, u32[]{:S(2)}, u32[]{:S(2)}) %collective-permute-start.4) | collective-permute-done | bytes 442400 | tf_op jit(solution)/shard_map/tokens/ppermute | solution.py:26
  97.1 6.3 %collective-permute-done.6.t3 = bf16[4,144,384]{2,1,0:T(8,128)(2,1)} collective-permute-done((bf16[4,144,384]{2,1,0:T(8,128)(2,1)S(1)}, bf16[4,144,384]{2,1,0:T(8,128)(2,1)}, u32[]{:S(2)}, u32[]{:S(2)}) %collective-permute-start.6) | collective-permute-done | bytes 442400 | tf_op jit(solution)/shard_map/tokens/ppermute | solution.py:26
  103.5 4.4 %project.2 = bf16[2,4,128,384]{3,2,1,0:T(8,128)(2,1)} custom-call(s32[4]{0:T(128)S(1)} %pad_add_fusion.where, bf16[4,144,384]{2,1,0:T(8,128)(2,1)S(1)} %all-to-all-done.1.t0, bf16[4,144,384]{2,1,0:T(8,128)(2,1)S(1)} %collective-permute-done.4.t1, bf16[4,144,384]{2,1,0:T(8,128)(2,1)} %collective-permute-done.5.t2, ...), custom_call_target="tpu_custom_call" | custom-call | tf_op jit(solution)/shard_map/project/pallas_call | solution.py:171
  107.8 6.3 %all-to-all-start.2 = ((bf16[8,128,384]{2,1,0:T(8,128)(2,1)}), bf16[8,128,384]{2,1,0:T(8,128)(2,1)S(1)}, u32[]{:S(2)}, u32[]{:S(2)}) async-start(bf16[8,128,384]{2,1,0:T(8,128)(2,1)} %bitcast.15), calls=%async_computation.2 | async-start | bytes 1572864 | tf_op jit(solution)/shard_map/project/all_to_all | solution.py:240
  114.2 8.9 %collective-permute-start.8 = (f32[2,2,1,128]{3,0,2,1:T(2,128)S(1)}, f32[2,2,1,128]{3,0,2,1:T(2,128)S(1)}, u32[]{:S(2)}, u32[]{:S(2)}) collective-permute-start(f32[2,2,1,128]{3,0,2,1:T(2,128)S(1)} %pad_maximum_fusion.1), channel_id=1, source_target_pairs={{0,8},{1,40},{2,72},{3,104},{4,44},{5,76},{6,108},{7,12},{8,0},{9,... | collective-permute-start | bytes 6152 | tf_op jit(solution)/shard_map/weights/ppermute | solution.py:26
  123.1 5.9 %collective-permute-done.8 = f32[2,2,1,128]{3,0,2,1:T(2,128)S(1)} collective-permute-done((f32[2,2,1,128]{3,0,2,1:T(2,128)S(1)}, f32[2,2,1,128]{3,0,2,1:T(2,128)S(1)}, u32[]{:S(2)}, u32[]{:S(2)}) %collective-permute-start.8) | collective-permute-done | bytes 2080 | tf_op jit(solution)/shard_map/weights/ppermute | solution.py:26
  129.2 17.7 %all_to_all.20.kv_mine = bf16[8,2,256,128]{3,2,1,0:T(8,128)(2,1)S(1)} all-to-all(bf16[8,2,256,128]{3,2,1,0:T(8,128)(2,1)S(1)} %get-tuple-element.20), channel_id=1, replica_groups=mesh['x'=4,'zh'=4,'core'=2,'zl'=4,'yh'=2,'yl'=2] {'x','yl'}, dimensions={0} | all-to-all | bytes 2097152 | tf_op jit(solution)/shard_map/keys/all_to_all | solution.py:251
  147.0 1.9 %collective-permute-start.9 = (bf16[8,2,256,128]{3,2,1,0:T(8,128)(2,1)S(1)}, bf16[8,2,256,128]{3,2,1,0:T(8,128)(2,1)S(1)}, u32[]{:S(2)}, u32[]{:S(2)}) collective-permute-start(bf16[8,2,256,128]{3,2,1,0:T(8,128)(2,1)S(1)} %all_to_all.20.kv_mine), channel_id=1, source_target_pairs={{0,16},{16,0},{1,17},{17,1},{2,18},{18,2},{3,19},{19,3},{4,20},{20... | collective-permute-start | bytes 3145736 | tf_op jit(solution)/shard_map/keys/ppermute | solution.py:26
  148.9 2.6 %collective-permute-done.9.kv_theirs = bf16[8,2,256,128]{3,2,1,0:T(8,128)(2,1)S(1)} collective-permute-done((bf16[8,2,256,128]{3,2,1,0:T(8,128)(2,1)S(1)}, bf16[8,2,256,128]{3,2,1,0:T(8,128)(2,1)S(1)}, u32[]{:S(2)}, u32[]{:S(2)}) %collective-permute-start.9) | collective-permute-done | bytes 1048608 | tf_op jit(solution)/shard_map/keys/ppermute | solution.py:26
  151.5 2.2 %attend.1 = bf16[256,128]{1,0:T(8,128)(2,1)S(1)} custom-call(bf16[256,128]{1,0:T(8,128)(2,1)S(1)} %get-tuple-element.19.q, bf16[8,2,256,128]{3,2,1,0:T(8,128)(2,1)S(1)} %all_to_all.20.kv_mine, bf16[8,2,256,128]{3,2,1,0:T(8,128)(2,1)S(1)} %collective-permute-done.9.kv_theirs), custom_call_target="tpu_custom_call" | custom-call | tf_op jit(solution)/shard_map/attend/pallas_call | solution.py:171
  153.7 8.7 %collective-permute-start.10 = (bf16[256,128]{1,0:T(8,128)(2,1)S(1)}, bf16[256,128]{1,0:T(8,128)(2,1)S(1)}, u32[]{:S(2)}, u32[]{:S(2)}) collective-permute-start(bf16[256,128]{1,0:T(8,128)(2,1)S(1)} %attend.1), channel_id=1, source_target_pairs={{0,8},{1,40},{2,72},{3,104},{4,46},{5,78},{6,110},{7,14},{8,96},{9... | collective-permute-start | bytes 196616 | tf_op jit(solution)/shard_map/home/ppermute | solution.py:26
  162.4 5.3 %collective-permute-done.10 = bf16[256,128]{1,0:T(8,128)(2,1)S(1)} collective-permute-done((bf16[256,128]{1,0:T(8,128)(2,1)S(1)}, bf16[256,128]{1,0:T(8,128)(2,1)S(1)}, u32[]{:S(2)}, u32[]{:S(2)}) %collective-permute-start.10) | collective-permute-done | bytes 65568 | tf_op jit(solution)/shard_map/home/ppermute | solution.py:26
  167.7 1.9 %collective-permute-start.11 = (bf16[128,128]{1,0:T(8,128)(2,1)S(1)}, bf16[128,128]{1,0:T(8,128)(2,1)S(1)}, u32[]{:S(2)}, u32[]{:S(2)}) collective-permute-start(bf16[128,128]{1,0:T(8,128)(2,1)S(1)} %get-tuple-element.24), channel_id=1, source_target_pairs={{0,16},{16,0},{1,17},{17,1},{2,18},{18,2},{3,19},{19,3},{4,20},{20... | collective-permute-start | bytes 98312 | tf_op jit(solution)/shard_map/home/ppermute | solution.py:26
  169.7 1.1 collective-permute-done.11
  (22 shorter events, 1.8 us)
Async XLA Ops:
  1.6 19.8 %all-to-all-start = ((f32[4,1,256]{2,1,0:T(1,128)}), f32[4,1,256]{2,1,0:T(1,128)S(1)}, u32[]{:S(2)}, u32[]{:S(2)}) async-start(f32[4,1,256]{2,1,0:T(1,128)} %broadcast_in_dim.8), calls=%async_computation | async-start | bytes 8192 | tf_op jit(solution)/shard_map/norm/all_to_all | solution.py:68
  10.5 26.6 %collective-permute-start = (bf16[3,192,256]{2,1,0:T(8,128)(2,1)}, bf16[3,192,256]{2,1,0:T(8,128)(2,1)S(1)}, u32[]{:S(2)}, u32[]{:S(2)}) collective-permute-start(bf16[3,192,256]{2,1,0:T(8,128)(2,1)} %bitcast.34), channel_id=1, source_target_pairs={{0,8},{1,40},{2,72},{3,104},{4,44},{5,76},{6,108},{7,12},{8,0},{9,... | collective-permute-start | bytes 884744 | tf_op jit(solution)/shard_map/weights/ppermute | solution.py:26
  37.9 28.4 %all-to-all-start.1 = ((bf16[4,144,384]{2,1,0:T(8,128)(2,1)}), bf16[4,144,384]{2,1,0:T(8,128)(2,1)S(1)}, u32[]{:S(2)}, u32[]{:S(2)}) async-start(bf16[4,144,384]{2,1,0:T(8,128)(2,1)} %broadcast_in_dim.11), calls=%async_computation.1 | async-start | bytes 884736 | tf_op jit(solution)/shard_map/tokens/all_to_all | solution.py:68
  45.9 14.9 %collective-permute-start.1 = (bf16[3,192,256]{2,1,0:T(8,128)(2,1)S(1)}, bf16[3,192,256]{2,1,0:T(8,128)(2,1)S(1)}, u32[]{:S(2)}, u32[]{:S(2)}) collective-permute-start(bf16[3,192,256]{2,1,0:T(8,128)(2,1)S(1)} %collective-permute-done), channel_id=1, source_target_pairs={{0,384},{128,0},{256,128},{384,256},{1,385},{129,1},{257,129},{385... | collective-permute-start | bytes 884744 | tf_op jit(solution)/shard_map/weights/ppermute | solution.py:26
  50.5 12.7 %collective-permute-start.2 = (bf16[3,192,256]{2,1,0:T(8,128)(2,1)S(1)}, bf16[3,192,256]{2,1,0:T(8,128)(2,1)S(1)}, u32[]{:S(2)}, u32[]{:S(2)}) collective-permute-start(bf16[3,192,256]{2,1,0:T(8,128)(2,1)S(1)} %collective-permute-done), channel_id=1, source_target_pairs={{0,256},{128,384},{256,0},{384,128},{1,257},{129,385},{257,1},{385... | collective-permute-start | bytes 884744 | tf_op jit(solution)/shard_map/weights/ppermute | solution.py:26
  53.3 13.1 %collective-permute-start.3 = (bf16[3,192,256]{2,1,0:T(8,128)(2,1)S(1)}, bf16[3,192,256]{2,1,0:T(8,128)(2,1)S(1)}, u32[]{:S(2)}, u32[]{:S(2)}) collective-permute-start(bf16[3,192,256]{2,1,0:T(8,128)(2,1)S(1)} %collective-permute-done), channel_id=1, source_target_pairs={{0,128},{128,256},{256,384},{384,0},{1,129},{129,257},{257,385},{3... | collective-permute-start | bytes 884744 | tf_op jit(solution)/shard_map/weights/ppermute | solution.py:26
  66.5 37.0 %collective-permute-start.7 = (bf16[4,3,192,256]{3,2,1,0:T(8,128)(2,1)S(1)}, bf16[4,3,192,256]{3,2,1,0:T(8,128)(2,1)S(1)}, u32[]{:S(2)}, u32[]{:S(2)}) collective-permute-start(bf16[4,3,192,256]{3,2,1,0:T(8,128)(2,1)S(1)} %pad_maximum_fusion.w_mine), channel_id=1, source_target_pairs={{0,16},{16,0},{1,17},{17,1},{2,18},{18,2},{3,19},{19,3},{4,20},{20... | collective-permute-start | bytes 3538952 | tf_op jit(solution)/shard_map/weights/ppermute | solution.py:26
  68.4 28.7 %collective-permute-start.4 = (bf16[4,144,384]{2,1,0:T(8,128)(2,1)S(1)}, bf16[4,144,384]{2,1,0:T(8,128)(2,1)S(1)}, u32[]{:S(2)}, u32[]{:S(2)}) collective-permute-start(bf16[4,144,384]{2,1,0:T(8,128)(2,1)S(1)} %all-to-all-done.1.t0), channel_id=1, source_target_pairs={{0,108},{4,0},{8,4},{12,8},{32,12},{36,32},{40,36},{44,40},{64,44}... | collective-permute-start | bytes 1327112 | tf_op jit(solution)/shard_map/tokens/ppermute | solution.py:26
  77.6 19.6 %collective-permute-start.5 = (bf16[4,144,384]{2,1,0:T(8,128)(2,1)S(1)}, bf16[4,144,384]{2,1,0:T(8,128)(2,1)}, u32[]{:S(2)}, u32[]{:S(2)}) collective-permute-start(bf16[4,144,384]{2,1,0:T(8,128)(2,1)S(1)} %all-to-all-done.1.t0), channel_id=1, source_target_pairs={{0,8},{4,108},{8,32},{12,4},{32,40},{36,12},{40,64},{44,36},{64,72... | collective-permute-start | bytes 1327112 | tf_op jit(solution)/shard_map/tokens/ppermute | solution.py:26
  79.6 23.8 %collective-permute-start.6 = (bf16[4,144,384]{2,1,0:T(8,128)(2,1)S(1)}, bf16[4,144,384]{2,1,0:T(8,128)(2,1)}, u32[]{:S(2)}, u32[]{:S(2)}) collective-permute-start(bf16[4,144,384]{2,1,0:T(8,128)(2,1)S(1)} %all-to-all-done.1.t0), channel_id=1, source_target_pairs={{0,4},{4,8},{8,12},{12,32},{32,36},{36,40},{40,44},{44,64},{64,68}... | collective-permute-start | bytes 1327112 | tf_op jit(solution)/shard_map/tokens/ppermute | solution.py:26
  107.8 6.3 %copy-start = (f32[256]{0:T(256)S(1)}, f32[256]{0:T(256)}, u32[]{:S(2)}) copy-start(f32[256]{0:T(256)} %param.9) | copy-start | bytes 3076
  107.8 6.3 %copy-start.1 = (f32[256]{0:T(256)S(1)}, f32[256]{0:T(256)}, u32[]{:S(2)}) copy-start(f32[256]{0:T(256)} %param.8) | copy-start | bytes 3076
  107.8 21.1 %all-to-all-start.2 = ((bf16[8,128,384]{2,1,0:T(8,128)(2,1)}), bf16[8,128,384]{2,1,0:T(8,128)(2,1)S(1)}, u32[]{:S(2)}, u32[]{:S(2)}) async-start(bf16[8,128,384]{2,1,0:T(8,128)(2,1)} %bitcast.15), calls=%async_computation.2 | async-start | bytes 1572864 | tf_op jit(solution)/shard_map/project/all_to_all | solution.py:240
  114.2 14.8 %collective-permute-start.8 = (f32[2,2,1,128]{3,0,2,1:T(2,128)S(1)}, f32[2,2,1,128]{3,0,2,1:T(2,128)S(1)}, u32[]{:S(2)}, u32[]{:S(2)}) collective-permute-start(f32[2,2,1,128]{3,0,2,1:T(2,128)S(1)} %pad_maximum_fusion.1), channel_id=1, source_target_pairs={{0,8},{1,40},{2,72},{3,104},{4,44},{5,76},{6,108},{7,12},{8,0},{9,... | collective-permute-start | bytes 6152 | tf_op jit(solution)/shard_map/weights/ppermute | solution.py:26
  147.0 4.5 %collective-permute-start.9 = (bf16[8,2,256,128]{3,2,1,0:T(8,128)(2,1)S(1)}, bf16[8,2,256,128]{3,2,1,0:T(8,128)(2,1)S(1)}, u32[]{:S(2)}, u32[]{:S(2)}) collective-permute-start(bf16[8,2,256,128]{3,2,1,0:T(8,128)(2,1)S(1)} %all_to_all.20.kv_mine), channel_id=1, source_target_pairs={{0,16},{16,0},{1,17},{17,1},{2,18},{18,2},{3,19},{19,3},{4,20},{20... | collective-permute-start | bytes 3145736 | tf_op jit(solution)/shard_map/keys/ppermute | solution.py:26
  153.7 14.0 %collective-permute-start.10 = (bf16[256,128]{1,0:T(8,128)(2,1)S(1)}, bf16[256,128]{1,0:T(8,128)(2,1)S(1)}, u32[]{:S(2)}, u32[]{:S(2)}) collective-permute-start(bf16[256,128]{1,0:T(8,128)(2,1)S(1)} %attend.1), channel_id=1, source_target_pairs={{0,8},{1,40},{2,72},{3,104},{4,46},{5,78},{6,110},{7,14},{8,96},{9... | collective-permute-start | bytes 196616 | tf_op jit(solution)/shard_map/home/ppermute | solution.py:26
  167.7 3.1 %collective-permute-start.11 = (bf16[128,128]{1,0:T(8,128)(2,1)S(1)}, bf16[128,128]{1,0:T(8,128)(2,1)S(1)}, u32[]{:S(2)}, u32[]{:S(2)}) collective-permute-start(bf16[128,128]{1,0:T(8,128)(2,1)S(1)} %get-tuple-element.24), channel_id=1, source_target_pairs={{0,16},{16,0},{1,17},{17,1},{2,18},{18,2},{3,19},{19,3},{4,20},{20... | collective-permute-start | bytes 98312 | tf_op jit(solution)/shard_map/home/ppermute | solution.py:26

commit v12 on v10

--- a/solution.py
+++ b/solution.py
@@ -9,6 +9,7 @@
 DH = 128
 EPSILON = 1e-06
 FEATURES = 6144
+SUMS_FLOPS = 20_000_000_000
 NX = NZH = NZL = NY = 4
 CORES = 2
 AXES = ("x", "zh", "core", "zl", "yh", "yl")
@@ -68,6 +69,14 @@
     rest = values - high
     mid = lax.reduce_precision(rest, 8, 7)
     return jnp.concatenate([high, mid, rest - mid]).astype(jnp.bfloat16)
+
+
+def sums_kernel(tokens, out):
+    x = tokens[...].astype(jnp.float32)
+    first = jnp.sum(x, axis=1, keepdims=True)
+    second = jnp.sum(x * x, axis=1, keepdims=True)
+    lane = lax.broadcasted_iota(jnp.int32, (128, 128), 1)
+    out[...] = jnp.where(lane == 0, first, second).T[:8]
 
 
 def partial_kernel(where, t0, t1, t2, t3, w_mine, w_theirs, out, w, acc):
@@ -160,7 +169,7 @@
     out[...] = (mixed / total).astype(jnp.bfloat16)
 
 
-def kernel_call(kernel, out_shape, args, scalars=0, scratch=()):
+def kernel_call(kernel, out_shape, args, scalars=0, scratch=(), flops=None):
     vmem = pl.BlockSpec(memory_space=pltpu.VMEM)
     smem = pl.BlockSpec(memory_space=pltpu.SMEM)
     return pl.pallas_call(
@@ -169,6 +178,7 @@
         in_specs=[smem] * scalars + [vmem] * (len(args) - scalars),
         out_specs=jax.tree.map(lambda _: vmem, out_shape),
         scratch_shapes=scratch,
+        cost_estimate=flops and pl.CostEstimate(flops=flops, bytes_accessed=0, transcendentals=0),
         compiler_params=pltpu.CompilerParams(vmem_limit_bytes=VMEM_LIMIT),
     )(*args)
 
@@ -186,9 +196,11 @@
         w_moved = to_plane(jnp.transpose(w_qkv, (1, 0, 2)))
 
     with jax.named_scope("norm"):
-        x = tokens.astype(jnp.float32)
+        own = kernel_call(
+            sums_kernel, jax.ShapeDtypeStruct((8, 128), jnp.float32), (tokens,), flops=SUMS_FLOPS
+        )
         shared = spread(
-            jnp.concatenate([jnp.sum(x, axis=1), jnp.sum(x * x, axis=1), q_gain, k_gain])[None],
+            jnp.concatenate([own[:2].reshape(-1), q_gain, k_gain])[None],
             Y,
             NY,
         )[:, 0]

time: 173 us -> 172 us (level)
    pallas_call x3 -> x4, Pallas kernels: 6.83 us -> 6.96 us  [kernel_call(): pl.pallas_call(kernel, out_shape=out_shape, in_specs=[smem] * scalars + [...]
  transfers between devices with their start and end apart: 14 -> 14, of which waited for: 12 -> 12; matrix products, arithmetic and copies ran while one was open for 1% -> 0% of each run, Pallas kernels for 0% -> 0%
where the time goes in v12:
time: 172 us
  starting transfers between devices  78.5 us (46%)
  waiting for transfers between devices  63.3 us (37%)
  blocking collectives  18.7 us (11%)
  Pallas kernels  6.96 us (4%)
  local copies, waits for them, and re-layouts  3.11 us (2%)
    ppermute x11, waiting for transfers between devices, shift(): return lax.ppermute(values, axes, pairs)  52.1 us
    ppermute x11, starting transfers between devices, shift(): return lax.ppermute(values, axes, pairs)  43.1 us
    all_to_all x2, starting transfers between devices, spread(): lax.all_to_all(jnp.broadcast_to(values[None], (count,) + values.shape), a...  25.1 us
    all_to_all x1, blocking collectives, body(): kv_mine = lax.all_to_all(kv, ('x', 'yl'), 0, 0)  18.7 us
    all_to_all x1, waiting for transfers between devices, body(): lax.all_to_all(part, ('core',) + Y, 0, 0).reshape(CORES, NY, 128, 3 * DH)  10.5 us
    all_to_all x1, starting transfers between devices, body(): lax.all_to_all(part, ('core',) + Y, 0, 0).reshape(CORES, NY, 128, 3 * DH)  10.2 us
    pallas_call x4, Pallas kernels, kernel_call(): pl.pallas_call(kernel, out_shape=out_shape, in_specs=[smem] * scalars + [...  6.96 us
  transfers between devices with their start and end apart: 14, of which 12 were waited for; matrix products, arithmetic and copies ran while one was open for 0% of the time, Pallas kernels for 0%

profile of v12, /device:TPU:121, one launch (start us, length us, event | category | flops | bytes accessed | tf_op | source)
XLA Modules:
  0.0 171.8 jit_solution(6413787858661632453)
XLA Ops:
  0.0 0.9 copy-done
  1.6 0.6 broadcast_in_dim.8
  2.2 4.1 %all-to-all-start = ((f32[4,1,768]{2,1,0:T(1,128)}), f32[4,1,768]{2,1,0:T(1,128)S(1)}, u32[]{:S(2)}, u32[]{:S(2)}) async-start(f32[4,1,768]{2,1,0:T(1,128)} %broadcast_in_dim.8), calls=%async_computation | async-start | bytes 24576 | tf_op jit(solution)/shard_map/norm/all_to_all | solution.py:64
  6.3 12.5 %collective-permute-start = (bf16[3,192,256]{2,1,0:T(8,128)(2,1)S(1)}, bf16[3,192,256]{2,1,0:T(8,128)(2,1)S(1)}, u32[]{:S(2)}, u32[]{:S(2)}) collective-permute-start(bf16[3,192,256]{2,1,0:T(8,128)(2,1)S(1)} %bitcast.39), channel_id=1, source_target_pairs={{0,0},{1,32},{2,64},{3,96},{4,36},{5,68},{6,100},{7,4},{8,72},{9,1... | collective-permute-start | bytes 884744 | tf_op jit(solution)/shard_map/weights/ppermute | solution.py:27
  19.1 6.6 %collective-permute-done = bf16[3,192,256]{2,1,0:T(8,128)(2,1)S(1)} collective-permute-done((bf16[3,192,256]{2,1,0:T(8,128)(2,1)S(1)}, bf16[3,192,256]{2,1,0:T(8,128)(2,1)S(1)}, u32[]{:S(2)}, u32[]{:S(2)}) %collective-permute-start) | collective-permute-done | bytes 294944 | tf_op jit(solution)/shard_map/weights/ppermute | solution.py:27
  25.7 0.8 broadcast_in_dim.11
  26.5 21.0 %all-to-all-start.1 = ((bf16[4,144,384]{2,1,0:T(8,128)(2,1)}), bf16[4,144,384]{2,1,0:T(8,128)(2,1)S(1)}, u32[]{:S(2)}, u32[]{:S(2)}) async-start(bf16[4,144,384]{2,1,0:T(8,128)(2,1)} %broadcast_in_dim.11), calls=%async_computation.1 | async-start | bytes 884736 | tf_op jit(solution)/shard_map/tokens/all_to_all | solution.py:64
  47.5 3.1 %collective-permute-start.3 = (bf16[3,192,256]{2,1,0:T(8,128)(2,1)S(1)}, bf16[3,192,256]{2,1,0:T(8,128)(2,1)S(1)}, u32[]{:S(2)}, u32[]{:S(2)}) collective-permute-start(bf16[3,192,256]{2,1,0:T(8,128)(2,1)S(1)} %collective-permute-done), channel_id=1, source_target_pairs={{0,128},{128,256},{256,384},{384,0},{1,129},{129,257},{257,385},{3... | collective-permute-start | bytes 884744 | tf_op jit(solution)/shard_map/weights/ppermute | solution.py:27
  50.6 4.4 %collective-permute-start.2 = (bf16[3,192,256]{2,1,0:T(8,128)(2,1)S(1)}, bf16[3,192,256]{2,1,0:T(8,128)(2,1)S(1)}, u32[]{:S(2)}, u32[]{:S(2)}) collective-permute-start(bf16[3,192,256]{2,1,0:T(8,128)(2,1)S(1)} %collective-permute-done), channel_id=1, source_target_pairs={{0,256},{128,384},{256,0},{384,128},{1,257},{129,385},{257,1},{385... | collective-permute-start | bytes 884744 | tf_op jit(solution)/shard_map/weights/ppermute | solution.py:27
  55.0 3.1 %collective-permute-start.1 = (bf16[3,192,256]{2,1,0:T(8,128)(2,1)S(1)}, bf16[3,192,256]{2,1,0:T(8,128)(2,1)S(1)}, u32[]{:S(2)}, u32[]{:S(2)}) collective-permute-start(bf16[3,192,256]{2,1,0:T(8,128)(2,1)S(1)} %collective-permute-done), channel_id=1, source_target_pairs={{0,384},{128,0},{256,128},{384,256},{1,385},{129,1},{257,129},{385... | collective-permute-start | bytes 884744 | tf_op jit(solution)/shard_map/weights/ppermute | solution.py:27
  58.3 7.3 %collective-permute-done.2 = bf16[3,192,256]{2,1,0:T(8,128)(2,1)S(1)} collective-permute-done((bf16[3,192,256]{2,1,0:T(8,128)(2,1)S(1)}, bf16[3,192,256]{2,1,0:T(8,128)(2,1)S(1)}, u32[]{:S(2)}, u32[]{:S(2)}) %collective-permute-start.2) | collective-permute-done | bytes 294944 | tf_op jit(solution)/shard_map/weights/ppermute | solution.py:27
  65.6 1.3 collective-permute-done.1
  66.9 0.7 all-to-all-done.1.t0
  67.8 3.1 %collective-permute-start.7 = (bf16[4,3,192,256]{3,2,1,0:T(8,128)(2,1)S(1)}, bf16[4,3,192,256]{3,2,1,0:T(8,128)(2,1)S(1)}, u32[]{:S(2)}, u32[]{:S(2)}) collective-permute-start(bf16[4,3,192,256]{3,2,1,0:T(8,128)(2,1)S(1)} %pad_maximum_fusion.w_mine), channel_id=1, source_target_pairs={{0,16},{16,0},{1,17},{17,1},{2,18},{18,2},{3,19},{19,3},{4,20},{20... | collective-permute-start | bytes 3538952 | tf_op jit(solution)/shard_map/weights/ppermute | solution.py:27
  70.9 2.0 %collective-permute-start.6 = (bf16[4,144,384]{2,1,0:T(8,128)(2,1)S(1)}, bf16[4,144,384]{2,1,0:T(8,128)(2,1)S(1)}, u32[]{:S(2)}, u32[]{:S(2)}) collective-permute-start(bf16[4,144,384]{2,1,0:T(8,128)(2,1)S(1)} %all-to-all-done.1.t0), channel_id=1, source_target_pairs={{0,4},{4,8},{8,12},{12,32},{32,36},{36,40},{40,44},{44,64},{64,68}... | collective-permute-start | bytes 1327112 | tf_op jit(solution)/shard_map/tokens/ppermute | solution.py:27
  72.9 1.9 %collective-permute-start.5 = (bf16[4,144,384]{2,1,0:T(8,128)(2,1)S(1)}, bf16[4,144,384]{2,1,0:T(8,128)(2,1)}, u32[]{:S(2)}, u32[]{:S(2)}) collective-permute-start(bf16[4,144,384]{2,1,0:T(8,128)(2,1)S(1)} %all-to-all-done.1.t0), channel_id=1, source_target_pairs={{0,8},{4,108},{8,32},{12,4},{32,40},{36,12},{40,64},{44,36},{64,72... | collective-permute-start | bytes 1327112 | tf_op jit(solution)/shard_map/tokens/ppermute | solution.py:27
  74.8 3.3 %collective-permute-start.4 = (bf16[4,144,384]{2,1,0:T(8,128)(2,1)S(1)}, bf16[4,144,384]{2,1,0:T(8,128)(2,1)}, u32[]{:S(2)}, u32[]{:S(2)}) collective-permute-start(bf16[4,144,384]{2,1,0:T(8,128)(2,1)S(1)} %all-to-all-done.1.t0), channel_id=1, source_target_pairs={{0,108},{4,0},{8,4},{12,8},{32,12},{36,32},{40,36},{44,40},{64,44}... | collective-permute-start | bytes 1327112 | tf_op jit(solution)/shard_map/tokens/ppermute | solution.py:27
  78.3 6.5 %collective-permute-done.6.t3 = bf16[4,144,384]{2,1,0:T(8,128)(2,1)S(1)} collective-permute-done((bf16[4,144,384]{2,1,0:T(8,128)(2,1)S(1)}, bf16[4,144,384]{2,1,0:T(8,128)(2,1)S(1)}, u32[]{:S(2)}, u32[]{:S(2)}) %collective-permute-start.6) | collective-permute-done | bytes 442400 | tf_op jit(solution)/shard_map/tokens/ppermute | solution.py:27
  84.7 3.8 %collective-permute-done.5.t2 = bf16[4,144,384]{2,1,0:T(8,128)(2,1)} collective-permute-done((bf16[4,144,384]{2,1,0:T(8,128)(2,1)S(1)}, bf16[4,144,384]{2,1,0:T(8,128)(2,1)}, u32[]{:S(2)}, u32[]{:S(2)}) %collective-permute-start.5) | collective-permute-done | bytes 442400 | tf_op jit(solution)/shard_map/tokens/ppermute | solution.py:27
  88.5 10.1 %collective-permute-done.4.t1 = bf16[4,144,384]{2,1,0:T(8,128)(2,1)} collective-permute-done((bf16[4,144,384]{2,1,0:T(8,128)(2,1)S(1)}, bf16[4,144,384]{2,1,0:T(8,128)(2,1)}, u32[]{:S(2)}, u32[]{:S(2)}) %collective-permute-start.4) | collective-permute-done | bytes 442400 | tf_op jit(solution)/shard_map/tokens/ppermute | solution.py:27
  98.6 4.3 %project.2 = bf16[2,4,128,384]{3,2,1,0:T(8,128)(2,1)} custom-call(s32[4]{0:T(128)S(1)} %pad_add_fusion.where, bf16[4,144,384]{2,1,0:T(8,128)(2,1)S(1)} %all-to-all-done.1.t0, bf16[4,144,384]{2,1,0:T(8,128)(2,1)} %collective-permute-done.4.t1, bf16[4,144,384]{2,1,0:T(8,128)(2,1)} %collective-permute-done.5.t2, ...), custom_call_target="tpu_custom_call" | custom-call | tf_op jit(solution)/shard_map/project/pallas_call | solution.py:175
  102.9 10.2 %all-to-all-start.2 = ((bf16[8,128,384]{2,1,0:T(8,128)(2,1)}), bf16[8,128,384]{2,1,0:T(8,128)(2,1)S(1)}, u32[]{:S(2)}, u32[]{:S(2)}) async-start(bf16[8,128,384]{2,1,0:T(8,128)(2,1)} %bitcast.16), calls=%async_computation.2 | async-start | bytes 1572864 | tf_op jit(solution)/shard_map/project/all_to_all | solution.py:253
  113.2 10.5 %all-to-all-done.2 = bf16[8,128,384]{2,1,0:T(8,128)(2,1)S(1)} async-done(((bf16[8,128,384]{2,1,0:T(8,128)(2,1)}), bf16[8,128,384]{2,1,0:T(8,128)(2,1)S(1)}, u32[]{:S(2)}, u32[]{:S(2)}) %all-to-all-start.2) | async-done | bytes 786464 | tf_op jit(solution)/shard_map/project/all_to_all | solution.py:253
  124.0 18.7 %all_to_all.20.kv_mine = bf16[8,2,256,128]{3,2,1,0:T(8,128)(2,1)S(1)} all-to-all(bf16[8,2,256,128]{3,2,1,0:T(8,128)(2,1)S(1)} %get-tuple-element.20), channel_id=1, replica_groups=mesh['x'=4,'zh'=4,'core'=2,'zl'=4,'yh'=2,'yl'=2] {'x','yl'}, dimensions={0} | all-to-all | bytes 2097152 | tf_op jit(solution)/shard_map/keys/all_to_all | solution.py:264
  142.8 4.0 %collective-permute-start.8 = (bf16[8,2,256,128]{3,2,1,0:T(8,128)(2,1)S(1)}, bf16[8,2,256,128]{3,2,1,0:T(8,128)(2,1)S(1)}, u32[]{:S(2)}, u32[]{:S(2)}) collective-permute-start(bf16[8,2,256,128]{3,2,1,0:T(8,128)(2,1)S(1)} %all_to_all.20.kv_mine), channel_id=1, source_target_pairs={{0,16},{16,0},{1,17},{17,1},{2,18},{18,2},{3,19},{19,3},{4,20},{20... | collective-permute-start | bytes 3145736 | tf_op jit(solution)/shard_map/keys/ppermute | solution.py:27
  146.7 2.3 %collective-permute-done.8.kv_theirs = bf16[8,2,256,128]{3,2,1,0:T(8,128)(2,1)S(1)} collective-permute-done((bf16[8,2,256,128]{3,2,1,0:T(8,128)(2,1)S(1)}, bf16[8,2,256,128]{3,2,1,0:T(8,128)(2,1)S(1)}, u32[]{:S(2)}, u32[]{:S(2)}) %collective-permute-start.8) | collective-permute-done | bytes 1048608 | tf_op jit(solution)/shard_map/keys/ppermute | solution.py:27
  149.0 2.2 %attend.1 = bf16[256,128]{1,0:T(8,128)(2,1)S(1)} custom-call(bf16[256,128]{1,0:T(8,128)(2,1)S(1)} %get-tuple-element.19.q, bf16[8,2,256,128]{3,2,1,0:T(8,128)(2,1)S(1)} %all_to_all.20.kv_mine, bf16[8,2,256,128]{3,2,1,0:T(8,128)(2,1)S(1)} %collective-permute-done.8.kv_theirs), custom_call_target="tpu_custom_call" | custom-call | tf_op jit(solution)/shard_map/attend/pallas_call | solution.py:175
  151.2 3.9 %collective-permute-start.9 = (bf16[256,128]{1,0:T(8,128)(2,1)S(1)}, bf16[256,128]{1,0:T(8,128)(2,1)S(1)}, u32[]{:S(2)}, u32[]{:S(2)}) collective-permute-start(bf16[256,128]{1,0:T(8,128)(2,1)S(1)} %attend.1), channel_id=1, source_target_pairs={{0,0},{1,32},{2,64},{3,96},{4,39},{5,71},{6,103},{7,7},{8,74},{9,1... | collective-permute-start | bytes 196616 | tf_op jit(solution)/shard_map/home/ppermute | solution.py:27
  155.1 12.9 %collective-permute-done.9 = bf16[256,128]{1,0:T(8,128)(2,1)S(1)} collective-permute-done((bf16[256,128]{1,0:T(8,128)(2,1)S(1)}, bf16[256,128]{1,0:T(8,128)(2,1)S(1)}, u32[]{:S(2)}, u32[]{:S(2)}) %collective-permute-start.9) | collective-permute-done | bytes 65568 | tf_op jit(solution)/shard_map/home/ppermute | solution.py:27
  168.1 1.9 %collective-permute-start.10 = (bf16[128,128]{1,0:T(8,128)(2,1)S(1)}, bf16[128,128]{1,0:T(8,128)(2,1)S(1)}, u32[]{:S(2)}, u32[]{:S(2)}) collective-permute-start(bf16[128,128]{1,0:T(8,128)(2,1)S(1)} %get-tuple-element.22), channel_id=1, source_target_pairs={{0,16},{16,0},{1,17},{17,1},{2,18},{18,2},{3,19},{19,3},{4,20},{20... | collective-permute-start | bytes 98312 | tf_op jit(solution)/shard_map/home/ppermute | solution.py:27
  170.0 1.1 collective-permute-done.10
  171.1 0.6 maximum_select_fusion
  (31 shorter events, 1.8 us)
Async XLA Ops:
  0.0 0.9 copy-start
  0.9 0.7 copy-start.2
  0.9 0.7 copy-start.3
  0.9 5.4 %copy-start.5 = (bf16[192,3,256]{2,0,1:T(8,128)(2,1)S(1)}, bf16[192,3,256]{2,0,1:T(8,128)(2,1)}, u32[]{:S(2)}) copy-start(bf16[192,3,256]{2,0,1:T(8,128)(2,1)} %param.7) | copy-start | bytes 884740
  0.9 17.9 %copy-start.4 = (bf16[384]{0:T(512)(128)(2,1)S(1)}, bf16[384]{0:T(512)(128)(2,1)}, u32[]{:S(2)}) copy-start(bf16[384]{0:T(512)(128)(2,1)} %param.6) | copy-start | bytes 2308
  0.9 18.0 %copy-start.1 = (bf16[128,384]{1,0:T(8,128)(2,1)S(1)}, bf16[128,384]{1,0:T(8,128)(2,1)}, u32[]{:S(2)}) copy-start(bf16[128,384]{1,0:T(8,128)(2,1)} %tokens.1) | copy-start | bytes 294916
  2.2 16.6 %all-to-all-start = ((f32[4,1,768]{2,1,0:T(1,128)}), f32[4,1,768]{2,1,0:T(1,128)S(1)}, u32[]{:S(2)}, u32[]{:S(2)}) async-start(f32[4,1,768]{2,1,0:T(1,128)} %broadcast_in_dim.8), calls=%async_computation | async-start | bytes 24576 | tf_op jit(solution)/shard_map/norm/all_to_all | solution.py:64
  6.3 19.4 %collective-permute-start = (bf16[3,192,256]{2,1,0:T(8,128)(2,1)S(1)}, bf16[3,192,256]{2,1,0:T(8,128)(2,1)S(1)}, u32[]{:S(2)}, u32[]{:S(2)}) collective-permute-start(bf16[3,192,256]{2,1,0:T(8,128)(2,1)S(1)} %bitcast.39), channel_id=1, source_target_pairs={{0,0},{1,32},{2,64},{3,96},{4,36},{5,68},{6,100},{7,4},{8,72},{9,1... | collective-permute-start | bytes 884744 | tf_op jit(solution)/shard_map/weights/ppermute | solution.py:27
  26.5 41.1 %all-to-all-start.1 = ((bf16[4,144,384]{2,1,0:T(8,128)(2,1)}), bf16[4,144,384]{2,1,0:T(8,128)(2,1)S(1)}, u32[]{:S(2)}, u32[]{:S(2)}) async-start(bf16[4,144,384]{2,1,0:T(8,128)(2,1)} %broadcast_in_dim.11), calls=%async_computation.1 | async-start | bytes 884736 | tf_op jit(solution)/shard_map/tokens/all_to_all | solution.py:64
  47.5 10.8 %collective-permute-start.3 = (bf16[3,192,256]{2,1,0:T(8,128)(2,1)S(1)}, bf16[3,192,256]{2,1,0:T(8,128)(2,1)S(1)}, u32[]{:S(2)}, u32[]{:S(2)}) collective-permute-start(bf16[3,192,256]{2,1,0:T(8,128)(2,1)S(1)} %collective-permute-done), channel_id=1, source_target_pairs={{0,128},{128,256},{256,384},{384,0},{1,129},{129,257},{257,385},{3... | collective-permute-start | bytes 884744 | tf_op jit(solution)/shard_map/weights/ppermute | solution.py:27
  50.6 15.0 %collective-permute-start.2 = (bf16[3,192,256]{2,1,0:T(8,128)(2,1)S(1)}, bf16[3,192,256]{2,1,0:T(8,128)(2,1)S(1)}, u32[]{:S(2)}, u32[]{:S(2)}) collective-permute-start(bf16[3,192,256]{2,1,0:T(8,128)(2,1)S(1)} %collective-permute-done), channel_id=1, source_target_pairs={{0,256},{128,384},{256,0},{384,128},{1,257},{129,385},{257,1},{385... | collective-permute-start | bytes 884744 | tf_op jit(solution)/shard_map/weights/ppermute | solution.py:27
  55.0 11.9 %collective-permute-start.1 = (bf16[3,192,256]{2,1,0:T(8,128)(2,1)S(1)}, bf16[3,192,256]{2,1,0:T(8,128)(2,1)S(1)}, u32[]{:S(2)}, u32[]{:S(2)}) collective-permute-start(bf16[3,192,256]{2,1,0:T(8,128)(2,1)S(1)} %collective-permute-done), channel_id=1, source_target_pairs={{0,384},{128,0},{256,128},{384,256},{1,385},{129,1},{257,129},{385... | collective-permute-start | bytes 884744 | tf_op jit(solution)/shard_map/weights/ppermute | solution.py:27
  67.8 30.8 %collective-permute-start.7 = (bf16[4,3,192,256]{3,2,1,0:T(8,128)(2,1)S(1)}, bf16[4,3,192,256]{3,2,1,0:T(8,128)(2,1)S(1)}, u32[]{:S(2)}, u32[]{:S(2)}) collective-permute-start(bf16[4,3,192,256]{3,2,1,0:T(8,128)(2,1)S(1)} %pad_maximum_fusion.w_mine), channel_id=1, source_target_pairs={{0,16},{16,0},{1,17},{17,1},{2,18},{18,2},{3,19},{19,3},{4,20},{20... | collective-permute-start | bytes 3538952 | tf_op jit(solution)/shard_map/weights/ppermute | solution.py:27
  70.9 13.8 %collective-permute-start.6 = (bf16[4,144,384]{2,1,0:T(8,128)(2,1)S(1)}, bf16[4,144,384]{2,1,0:T(8,128)(2,1)S(1)}, u32[]{:S(2)}, u32[]{:S(2)}) collective-permute-start(bf16[4,144,384]{2,1,0:T(8,128)(2,1)S(1)} %all-to-all-done.1.t0), channel_id=1, source_target_pairs={{0,4},{4,8},{8,12},{12,32},{32,36},{36,40},{40,44},{44,64},{64,68}... | collective-permute-start | bytes 1327112 | tf_op jit(solution)/shard_map/tokens/ppermute | solution.py:27
  72.9 15.6 %collective-permute-start.5 = (bf16[4,144,384]{2,1,0:T(8,128)(2,1)S(1)}, bf16[4,144,384]{2,1,0:T(8,128)(2,1)}, u32[]{:S(2)}, u32[]{:S(2)}) collective-permute-start(bf16[4,144,384]{2,1,0:T(8,128)(2,1)S(1)} %all-to-all-done.1.t0), channel_id=1, source_target_pairs={{0,8},{4,108},{8,32},{12,4},{32,40},{36,12},{40,64},{44,36},{64,72... | collective-permute-start | bytes 1327112 | tf_op jit(solution)/shard_map/tokens/ppermute | solution.py:27
  74.8 23.8 %collective-permute-start.4 = (bf16[4,144,384]{2,1,0:T(8,128)(2,1)S(1)}, bf16[4,144,384]{2,1,0:T(8,128)(2,1)}, u32[]{:S(2)}, u32[]{:S(2)}) collective-permute-start(bf16[4,144,384]{2,1,0:T(8,128)(2,1)S(1)} %all-to-all-done.1.t0), channel_id=1, source_target_pairs={{0,108},{4,0},{8,4},{12,8},{32,12},{36,32},{40,36},{44,40},{64,44}... | collective-permute-start | bytes 1327112 | tf_op jit(solution)/shard_map/tokens/ppermute | solution.py:27
  102.9 20.8 %all-to-all-start.2 = ((bf16[8,128,384]{2,1,0:T(8,128)(2,1)}), bf16[8,128,384]{2,1,0:T(8,128)(2,1)S(1)}, u32[]{:S(2)}, u32[]{:S(2)}) async-start(bf16[8,128,384]{2,1,0:T(8,128)(2,1)} %bitcast.16), calls=%async_computation.2 | async-start | bytes 1572864 | tf_op jit(solution)/shard_map/project/all_to_all | solution.py:253
  142.8 6.2 %collective-permute-start.8 = (bf16[8,2,256,128]{3,2,1,0:T(8,128)(2,1)S(1)}, bf16[8,2,256,128]{3,2,1,0:T(8,128)(2,1)S(1)}, u32[]{:S(2)}, u32[]{:S(2)}) collective-permute-start(bf16[8,2,256,128]{3,2,1,0:T(8,128)(2,1)S(1)} %all_to_all.20.kv_mine), channel_id=1, source_target_pairs={{0,16},{16,0},{1,17},{17,1},{2,18},{18,2},{3,19},{19,3},{4,20},{20... | collective-permute-start | bytes 3145736 | tf_op jit(solution)/shard_map/keys/ppermute | solution.py:27
  151.2 16.8 %collective-permute-start.9 = (bf16[256,128]{1,0:T(8,128)(2,1)S(1)}, bf16[256,128]{1,0:T(8,128)(2,1)S(1)}, u32[]{:S(2)}, u32[]{:S(2)}) collective-permute-start(bf16[256,128]{1,0:T(8,128)(2,1)S(1)} %attend.1), channel_id=1, source_target_pairs={{0,0},{1,32},{2,64},{3,96},{4,39},{5,71},{6,103},{7,7},{8,74},{9,1... | collective-permute-start | bytes 196616 | tf_op jit(solution)/shard_map/home/ppermute | solution.py:27
  168.1 3.1 %collective-permute-start.10 = (bf16[128,128]{1,0:T(8,128)(2,1)S(1)}, bf16[128,128]{1,0:T(8,128)(2,1)S(1)}, u32[]{:S(2)}, u32[]{:S(2)}) collective-permute-start(bf16[128,128]{1,0:T(8,128)(2,1)S(1)} %get-tuple-element.22), channel_id=1, source_target_pairs={{0,16},{16,0},{1,17},{17,1},{2,18},{18,2},{3,19},{19,3},{4,20},{20... | collective-permute-start | bytes 98312 | tf_op jit(solution)/shard_map/home/ppermute | solution.py:27

commit v13 on v11

--- a/solution.py
+++ b/solution.py
@@ -68,14 +68,17 @@
     return lax.all_to_all(jnp.broadcast_to(values[None], (count,) + values.shape), axes, 0, 0)
 
 
-def pieces_of(values):
-    high = lax.reduce_precision(values, 8, 7)
-    rest = values - high
-    mid = lax.reduce_precision(rest, 8, 7)
-    return jnp.concatenate([high, mid, rest - mid]).astype(jnp.bfloat16)
-
-
-def partial_kernel(where, t0, t1, t2, t3, w_mine, w_theirs, out, w, acc):
+def sums_kernel(tokens, out):
+    lane = lax.broadcasted_iota(jnp.int32, (128, 128), 1)
+    columns = jnp.zeros((128, 128), jnp.float32)
+    for quarter in range(NZH):
+        x = tokens[quarter].astype(jnp.float32)
+        columns = jnp.where(lane == quarter, jnp.sum(x, axis=1, keepdims=True), columns)
+        columns = jnp.where(lane == quarter + NZH, jnp.sum(x * x, axis=1, keepdims=True), columns)
+    out[...] = columns.T[: 2 * NZH]
+
+
+def partial_kernel(where, t0, t1, t2, t3, sums, gain, w_mine, w_theirs, out, w, acc):
     zl, core, turn, x_here = where[0], where[1], where[2], where[3]
     half = w_mine.shape[2]
     for step in range(NX):
@@ -86,29 +89,22 @@
             w[x, pl.ds(pl.multiple_of((1 - core) * half, half), half), cols] = w_theirs[step, s]
     tokens = (t0, t1, t2, t3)
 
-    def extra(slot, quarter):
-        return tokens[slot][quarter, 128:144].astype(jnp.float32)
-
-    centers, scales = [], []
-    for quarter in range(NZH):
-        rows = sum(extra(slot, quarter)[:2] for slot in range(NZL))
-        sums = (rows[:, :128] + rows[:, 128:256] + rows[:, 256:]) / FEATURES
-        center = sums[0:1]
-        centers.append(center)
-        scales.append(lax.rsqrt(sums[1:2] - center * center + EPSILON))
-    stats = jnp.concatenate(centers + scales, axis=0).T
+    center = sums[:NZH] / FEATURES
+    scale = lax.rsqrt(sums[NZH:] / FEATURES - center * center + EPSILON)
+    stats = jnp.concatenate([center, scale], axis=0).T
 
     for slot in range(NZL):
-        row_gain = extra(slot, 0)[2:3]
+        part = lax.rem(zl + slot, NZL)
+        row_gain = gain[part]
         normed = []
         for quarter in range(NZH):
-            x = tokens[slot][quarter, :128].astype(jnp.float32)
+            x = tokens[slot][quarter].astype(jnp.float32)
             center = stats[:, quarter : quarter + 1]
             scale = stats[:, NZH + quarter : NZH + quarter + 1]
             normed.append(((x - center) * scale * row_gain).astype(jnp.bfloat16))
         term = jnp.dot(
             jnp.concatenate(normed, axis=0),
-            w[lax.rem(zl + slot, NZL)],
+            w[part],
             preferred_element_type=jnp.float32,
         )
         if slot == 0:
@@ -185,32 +181,16 @@
     y_high = lax.axis_index("yh")
     y_here = y_high * 2 + lax.axis_index("yl")
     turn = (zh + zl + (zl >= 2)) % NZH
+    head_zl = (zl + 2) % NZL
+    head_y = (zh + NY - jnp.where(head_zl == 1, 1, jnp.where(head_zl == 3, 2, 0))) % NY
     where = jnp.stack([zl, core, turn, lax.axis_index("x")]).astype(jnp.int32)
 
     with jax.named_scope("weights"):
         w_moved = to_plane(jnp.transpose(w_qkv, (1, 0, 2)))
-        head_gain = to_plane(jnp.concatenate([q_gain, k_gain]).reshape(2, 2, 1, DH))
-        head_gain = lax.dynamic_index_in_dim(head_gain, y_high, 1, keepdims=False)
-
-    with jax.named_scope("norm"):
-        x = tokens.astype(jnp.float32)
-        shared = spread(
-            jnp.concatenate([jnp.sum(x, axis=1), jnp.sum(x * x, axis=1)])[None], Y, NY
-        )
-        sums = jnp.sum(shared[:, 0], axis=0)
-        extended = jnp.concatenate(
-            [
-                tokens,
-                pieces_of(sums[:128])[None],
-                pieces_of(sums[128:])[None],
-                ln_gain[None],
-                jnp.zeros((13, 384), jnp.bfloat16),
-            ]
-        )
 
     with jax.named_scope("tokens"):
-        extended, w_moved = lax.optimization_barrier((extended, w_moved))
-        t0 = spread(extended, "zh", NZH)
+        tokens, w_moved = lax.optimization_barrier((tokens, w_moved))
+        t0 = spread(tokens, "zh", NZH)
 
     with jax.named_scope("weights"):
         along_x = [
@@ -225,11 +205,29 @@
         t3 = along_z(t0, 1)
         t2 = along_z_two(t0)
 
+    with jax.named_scope("norm"):
+        own = kernel_call(sums_kernel, jax.ShapeDtypeStruct((2 * NZH, 128), jnp.float32), (t0,))
+        shared = spread(
+            jnp.concatenate([own.reshape(-1), ln_gain.astype(jnp.float32), q_gain, k_gain])[None],
+            ("zl",) + Y,
+            NZL * NY,
+        )[:, 0]
+        sums = jnp.sum(shared[:, :1024], axis=0).reshape(2 * NZH, 128)
+        gain = lax.dynamic_index_in_dim(
+            shared[:, 1024:1408].reshape(NZL, NY, 1, 384), y_here, 1, keepdims=False
+        )
+        head_gain = lax.dynamic_index_in_dim(
+            shared[:, 1408:], head_zl * NY + head_y, 0, keepdims=False
+        )
+        head_gain = lax.dynamic_index_in_dim(
+            head_gain.reshape(2, 2, 1, DH), y_high, 1, keepdims=False
+        )
+
     with jax.named_scope("project"):
         part = kernel_call(
             partial_kernel,
             jax.ShapeDtypeStruct((CORES, NY, 128, 3 * DH), jnp.bfloat16),
-            (where, t0, t1, t2, t3, w_mine, w_theirs),
+            (where, t0, t1, t2, t3, sums, gain, w_mine, w_theirs),
             scalars=1,
             scratch=[
                 pltpu.VMEM((NX, 384, 768), jnp.bfloat16),

time: 173 us -> 169 us (0.977)
  the two profiles are of different devices: /device:TPU:16 before, /device:TPU:9 now
where the time goes in v13:
time: 169 us; the launch traced here: 168 us
  starting transfers between devices  76.8 us (45%)
  waiting for transfers between devices  55.9 us (33%)
  blocking collectives  19.2 us (11%)
  local copies, waits for them, and re-layouts  7.46 us (4%)
  Pallas kernels  6.88 us (4%)
  other arithmetic  1.73 us (1%)
    ppermute x11, starting transfers between devices, shift(): return lax.ppermute(values, axes, pairs)  47 us
    ppermute x11, waiting for transfers between devices, shift(): return lax.ppermute(values, axes, pairs)  42.2 us
    all_to_all x2, starting transfers between devices, spread(): lax.all_to_all(jnp.broadcast_to(values[None], (count,) + values.shape), a...  23.9 us
    all_to_all x1, blocking collectives, body(): kv_mine = lax.all_to_all(kv, ('x', 'yl'), 0, 0)  19.2 us
    all_to_all x1, waiting for transfers between devices, body(): lax.all_to_all(part, ('core',) + Y, 0, 0).reshape(CORES, NY, 128, 3 * DH)  10.6 us
    pallas_call x4, Pallas kernels, kernel_call(): pl.pallas_call(kernel, out_shape=out_shape, in_specs=[smem] * scalars + [...  6.88 us
    all_to_all x1, starting transfers between devices, body(): lax.all_to_all(part, ('core',) + Y, 0, 0).reshape(CORES, NY, 128, 3 * DH)  5.87 us
  transfers between devices with their start and end apart: 14, of which 10 were waited for; matrix products, arithmetic and copies ran while one was open for 4% of the time, Pallas kernels for 0%

profile of v13, /device:TPU:9, one launch (start us, length us, event | category | flops | bytes accessed | tf_op | source)
XLA Modules:
  0.0 168.2 jit_solution(12690710979425252667)
XLA Ops:
  0.0 11.4 %collective-permute-start = (bf16[3,192,256]{2,1,0:T(8,128)(2,1)}, bf16[3,192,256]{2,1,0:T(8,128)(2,1)S(1)}, u32[]{:S(2)}, u32[]{:S(2)}) collective-permute-start(bf16[3,192,256]{2,1,0:T(8,128)(2,1)} %bitcast.34), channel_id=1, source_target_pairs={{0,8},{1,40},{2,72},{3,104},{4,44},{5,76},{6,108},{7,12},{8,0},{9,... | collective-permute-start | bytes 884744 | tf_op jit(solution)/shard_map/weights/ppermute | solution.py:26
  11.4 12.4 %collective-permute-done = bf16[3,192,256]{2,1,0:T(8,128)(2,1)S(1)} collective-permute-done((bf16[3,192,256]{2,1,0:T(8,128)(2,1)}, bf16[3,192,256]{2,1,0:T(8,128)(2,1)S(1)}, u32[]{:S(2)}, u32[]{:S(2)}) %collective-permute-start) | collective-permute-done | bytes 294944 | tf_op jit(solution)/shard_map/weights/ppermute | solution.py:26
  23.8 1.7 broadcast_in_dim.4
  25.4 19.9 %all-to-all-start = ((bf16[4,128,384]{2,1,0:T(8,128)(2,1)}), bf16[4,128,384]{2,1,0:T(8,128)(2,1)S(1)}, u32[]{:S(2)}, u32[]{:S(2)}) async-start(bf16[4,128,384]{2,1,0:T(8,128)(2,1)} %broadcast_in_dim.4), calls=%async_computation | async-start | bytes 786432 | tf_op jit(solution)/shard_map/tokens/all_to_all | solution.py:68
  45.3 3.1 %collective-permute-start.3 = (bf16[3,192,256]{2,1,0:T(8,128)(2,1)S(1)}, bf16[3,192,256]{2,1,0:T(8,128)(2,1)S(1)}, u32[]{:S(2)}, u32[]{:S(2)}) collective-permute-start(bf16[3,192,256]{2,1,0:T(8,128)(2,1)S(1)} %collective-permute-done), channel_id=1, source_target_pairs={{0,128},{128,256},{256,384},{384,0},{1,129},{129,257},{257,385},{3... | collective-permute-start | bytes 884744 | tf_op jit(solution)/shard_map/weights/ppermute | solution.py:26
  48.4 4.4 %collective-permute-start.2 = (bf16[3,192,256]{2,1,0:T(8,128)(2,1)S(1)}, bf16[3,192,256]{2,1,0:T(8,128)(2,1)S(1)}, u32[]{:S(2)}, u32[]{:S(2)}) collective-permute-start(bf16[3,192,256]{2,1,0:T(8,128)(2,1)S(1)} %collective-permute-done), channel_id=1, source_target_pairs={{0,256},{128,384},{256,0},{384,128},{1,257},{129,385},{257,1},{385... | collective-permute-start | bytes 884744 | tf_op jit(solution)/shard_map/weights/ppermute | solution.py:26
  52.8 3.1 %collective-permute-start.1 = (bf16[3,192,256]{2,1,0:T(8,128)(2,1)S(1)}, bf16[3,192,256]{2,1,0:T(8,128)(2,1)S(1)}, u32[]{:S(2)}, u32[]{:S(2)}) collective-permute-start(bf16[3,192,256]{2,1,0:T(8,128)(2,1)S(1)} %collective-permute-done), channel_id=1, source_target_pairs={{0,384},{128,0},{256,128},{384,256},{1,385},{129,1},{257,129},{385... | collective-permute-start | bytes 884744 | tf_op jit(solution)/shard_map/weights/ppermute | solution.py:26
  55.9 6.4 %collective-permute-done.2 = bf16[3,192,256]{2,1,0:T(8,128)(2,1)S(1)} collective-permute-done((bf16[3,192,256]{2,1,0:T(8,128)(2,1)S(1)}, bf16[3,192,256]{2,1,0:T(8,128)(2,1)S(1)}, u32[]{:S(2)}, u32[]{:S(2)}) %collective-permute-start.2) | collective-permute-done | bytes 294944 | tf_op jit(solution)/shard_map/weights/ppermute | solution.py:26
  62.3 1.4 collective-permute-done.1
  63.8 3.1 %all-to-all-done.tokens.t0 = bf16[4,128,384]{2,1,0:T(8,128)(2,1)S(1)} async-done(((bf16[4,128,384]{2,1,0:T(8,128)(2,1)}), bf16[4,128,384]{2,1,0:T(8,128)(2,1)S(1)}, u32[]{:S(2)}, u32[]{:S(2)}) %all-to-all-start) | async-done | bytes 393248 | tf_op jit(solution)/shard_map/tokens/all_to_all | solution.py:68
  67.0 2.9 %collective-permute-start.7 = (bf16[4,3,192,256]{3,2,1,0:T(8,128)(2,1)S(1)}, bf16[4,3,192,256]{3,2,1,0:T(8,128)(2,1)S(1)}, u32[]{:S(2)}, u32[]{:S(2)}) collective-permute-start(bf16[4,3,192,256]{3,2,1,0:T(8,128)(2,1)S(1)} %pad_maximum_fusion.w_mine), channel_id=1, source_target_pairs={{0,16},{16,0},{1,17},{17,1},{2,18},{18,2},{3,19},{19,3},{4,20},{20... | collective-permute-start | bytes 3538952 | tf_op jit(solution)/shard_map/weights/ppermute | solution.py:26
  71.0 4.0 %all-to-all-start.1 = ((f32[16,1,1920]{2,1,0:T(1,128)}), f32[16,1,1920]{2,1,0:T(1,128)}, u32[]{:S(2)}, u32[]{:S(2)}) async-start(f32[16,1,1920]{2,1,0:T(1,128)} %broadcast_in_dim.5), calls=%async_computation.1 | async-start | bytes 245760 | tf_op jit(solution)/shard_map/norm/all_to_all | solution.py:68
  75.0 2.6 %collective-permute-start.6 = (bf16[4,128,384]{2,1,0:T(8,128)(2,1)S(1)}, bf16[4,128,384]{2,1,0:T(8,128)(2,1)S(1)}, u32[]{:S(2)}, u32[]{:S(2)}) collective-permute-start(bf16[4,128,384]{2,1,0:T(8,128)(2,1)S(1)} %all-to-all-done.tokens.t0), channel_id=1, source_target_pairs={{0,4},{4,8},{8,12},{12,32},{32,36},{36,40},{40,44},{44,64},{64,68}... | collective-permute-start | bytes 1179656 | tf_op jit(solution)/shard_map/tokens/ppermute | solution.py:26
  77.6 4.0 %collective-permute-start.5 = (bf16[4,128,384]{2,1,0:T(8,128)(2,1)S(1)}, bf16[4,128,384]{2,1,0:T(8,128)(2,1)S(1)}, u32[]{:S(2)}, u32[]{:S(2)}) collective-permute-start(bf16[4,128,384]{2,1,0:T(8,128)(2,1)S(1)} %all-to-all-done.tokens.t0), channel_id=1, source_target_pairs={{0,8},{4,108},{8,32},{12,4},{32,40},{36,12},{40,64},{44,36},{64,72... | collective-permute-start | bytes 1179656 | tf_op jit(solution)/shard_map/tokens/ppermute | solution.py:26
  81.6 5.4 %collective-permute-start.4 = (bf16[4,128,384]{2,1,0:T(8,128)(2,1)S(1)}, bf16[4,128,384]{2,1,0:T(8,128)(2,1)}, u32[]{:S(2)}, u32[]{:S(2)}) collective-permute-start(bf16[4,128,384]{2,1,0:T(8,128)(2,1)S(1)} %all-to-all-done.tokens.t0), channel_id=1, source_target_pairs={{0,108},{4,0},{8,4},{12,8},{32,12},{36,32},{40,36},{44,40},{64,44}... | collective-permute-start | bytes 1179656 | tf_op jit(solution)/shard_map/tokens/ppermute | solution.py:26
  87.1 0.9 copy.10
  89.3 1.4 reshape.25
  91.4 0.9 slice_reduce_fusion
  92.3 7.7 %collective-permute-done.5.t2 = bf16[4,128,384]{2,1,0:T(8,128)(2,1)S(1)} collective-permute-done((bf16[4,128,384]{2,1,0:T(8,128)(2,1)S(1)}, bf16[4,128,384]{2,1,0:T(8,128)(2,1)S(1)}, u32[]{:S(2)}, u32[]{:S(2)}) %collective-permute-start.5) | collective-permute-done | bytes 393248 | tf_op jit(solution)/shard_map/tokens/ppermute | solution.py:26
  99.9 2.1 %collective-permute-done.4.t1 = bf16[4,128,384]{2,1,0:T(8,128)(2,1)} collective-permute-done((bf16[4,128,384]{2,1,0:T(8,128)(2,1)S(1)}, bf16[4,128,384]{2,1,0:T(8,128)(2,1)}, u32[]{:S(2)}, u32[]{:S(2)}) %collective-permute-start.4) | collective-permute-done | bytes 393248 | tf_op jit(solution)/shard_map/tokens/ppermute | solution.py:26
  102.0 4.2 %project.2 = bf16[2,4,128,384]{3,2,1,0:T(8,128)(2,1)} custom-call(s32[4]{0:T(128)S(1)} %pad_add_fusion.where, bf16[4,128,384]{2,1,0:T(8,128)(2,1)S(1)} %all-to-all-done.tokens.t0, bf16[4,128,384]{2,1,0:T(8,128)(2,1)} %collective-permute-done.4.t1, bf16[4,128,384]{2,1,0:T(8,128)(2,1)S(1)} %collective-permute-done.5.t2, ...), custom_call_target="tpu_custom_call" | custom-call | tf_op jit(solution)/shard_map/project/pallas_call | solution.py:167
  106.2 5.9 %all-to-all-start.2 = ((bf16[8,128,384]{2,1,0:T(8,128)(2,1)}), bf16[8,128,384]{2,1,0:T(8,128)(2,1)S(1)}, u32[]{:S(2)}, u32[]{:S(2)}) async-start(bf16[8,128,384]{2,1,0:T(8,128)(2,1)} %bitcast.13), calls=%async_computation.2 | async-start | bytes 1572864 | tf_op jit(solution)/shard_map/project/all_to_all | solution.py:238
  112.1 0.8 slice.14
  112.8 10.6 %all-to-all-done.2 = bf16[8,128,384]{2,1,0:T(8,128)(2,1)S(1)} async-done(((bf16[8,128,384]{2,1,0:T(8,128)(2,1)}), bf16[8,128,384]{2,1,0:T(8,128)(2,1)S(1)}, u32[]{:S(2)}, u32[]{:S(2)}) %all-to-all-start.2) | async-done | bytes 786464 | tf_op jit(solution)/shard_map/project/all_to_all | solution.py:238
  123.7 19.2 %all_to_all.20.kv_mine = bf16[8,2,256,128]{3,2,1,0:T(8,128)(2,1)S(1)} all-to-all(bf16[8,2,256,128]{3,2,1,0:T(8,128)(2,1)S(1)} %get-tuple-element.20), channel_id=1, replica_groups=mesh['x'=4,'zh'=4,'core'=2,'zl'=4,'yh'=2,'yl'=2] {'x','yl'}, dimensions={0} | all-to-all | bytes 2097152 | tf_op jit(solution)/shard_map/keys/all_to_all | solution.py:249
  142.9 3.5 %collective-permute-start.8 = (bf16[8,2,256,128]{3,2,1,0:T(8,128)(2,1)S(1)}, bf16[8,2,256,128]{3,2,1,0:T(8,128)(2,1)S(1)}, u32[]{:S(2)}, u32[]{:S(2)}) collective-permute-start(bf16[8,2,256,128]{3,2,1,0:T(8,128)(2,1)S(1)} %all_to_all.20.kv_mine), channel_id=1, source_target_pairs={{0,16},{16,0},{1,17},{17,1},{2,18},{18,2},{3,19},{19,3},{4,20},{20... | collective-permute-start | bytes 3145736 | tf_op jit(solution)/shard_map/keys/ppermute | solution.py:26
  146.4 2.3 %collective-permute-done.8.kv_theirs = bf16[8,2,256,128]{3,2,1,0:T(8,128)(2,1)S(1)} collective-permute-done((bf16[8,2,256,128]{3,2,1,0:T(8,128)(2,1)S(1)}, bf16[8,2,256,128]{3,2,1,0:T(8,128)(2,1)S(1)}, u32[]{:S(2)}, u32[]{:S(2)}) %collective-permute-start.8) | collective-permute-done | bytes 1048608 | tf_op jit(solution)/shard_map/keys/ppermute | solution.py:26
  148.7 2.2 %attend.1 = bf16[256,128]{1,0:T(8,128)(2,1)S(1)} custom-call(bf16[256,128]{1,0:T(8,128)(2,1)S(1)} %get-tuple-element.19.q, bf16[8,2,256,128]{3,2,1,0:T(8,128)(2,1)S(1)} %all_to_all.20.kv_mine, bf16[8,2,256,128]{3,2,1,0:T(8,128)(2,1)S(1)} %collective-permute-done.8.kv_theirs), custom_call_target="tpu_custom_call" | custom-call | tf_op jit(solution)/shard_map/attend/pallas_call | solution.py:167
  150.9 3.6 %collective-permute-start.9 = (bf16[256,128]{1,0:T(8,128)(2,1)S(1)}, bf16[256,128]{1,0:T(8,128)(2,1)S(1)}, u32[]{:S(2)}, u32[]{:S(2)}) collective-permute-start(bf16[256,128]{1,0:T(8,128)(2,1)S(1)} %attend.1), channel_id=1, source_target_pairs={{0,8},{1,40},{2,72},{3,104},{4,46},{5,78},{6,110},{7,14},{8,96},{9... | collective-permute-start | bytes 196616 | tf_op jit(solution)/shard_map/home/ppermute | solution.py:26
  154.5 9.1 %collective-permute-done.9 = bf16[256,128]{1,0:T(8,128)(2,1)S(1)} collective-permute-done((bf16[256,128]{1,0:T(8,128)(2,1)S(1)}, bf16[256,128]{1,0:T(8,128)(2,1)S(1)}, u32[]{:S(2)}, u32[]{:S(2)}) %collective-permute-start.9) | collective-permute-done | bytes 65568 | tf_op jit(solution)/shard_map/home/ppermute | solution.py:26
  163.7 3.0 %collective-permute-start.10 = (bf16[128,128]{1,0:T(8,128)(2,1)S(1)}, bf16[128,128]{1,0:T(8,128)(2,1)S(1)}, u32[]{:S(2)}, u32[]{:S(2)}) collective-permute-start(bf16[128,128]{1,0:T(8,128)(2,1)S(1)} %get-tuple-element.22), channel_id=1, source_target_pairs={{0,16},{16,0},{1,17},{17,1},{2,18},{18,2},{3,19},{19,3},{4,20},{20... | collective-permute-start | bytes 98312 | tf_op jit(solution)/shard_map/home/ppermute | solution.py:26
  166.7 0.8 collective-permute-done.10
  (25 shorter events, 4.2 us)
Async XLA Ops:
  0.0 23.8 %collective-permute-start = (bf16[3,192,256]{2,1,0:T(8,128)(2,1)}, bf16[3,192,256]{2,1,0:T(8,128)(2,1)S(1)}, u32[]{:S(2)}, u32[]{:S(2)}) collective-permute-start(bf16[3,192,256]{2,1,0:T(8,128)(2,1)} %bitcast.34), channel_id=1, source_target_pairs={{0,8},{1,40},{2,72},{3,104},{4,44},{5,76},{6,108},{7,12},{8,0},{9,... | collective-permute-start | bytes 884744 | tf_op jit(solution)/shard_map/weights/ppermute | solution.py:26
  25.4 41.4 %all-to-all-start = ((bf16[4,128,384]{2,1,0:T(8,128)(2,1)}), bf16[4,128,384]{2,1,0:T(8,128)(2,1)S(1)}, u32[]{:S(2)}, u32[]{:S(2)}) async-start(bf16[4,128,384]{2,1,0:T(8,128)(2,1)} %broadcast_in_dim.4), calls=%async_computation | async-start | bytes 786432 | tf_op jit(solution)/shard_map/tokens/all_to_all | solution.py:68
  45.3 10.6 %collective-permute-start.3 = (bf16[3,192,256]{2,1,0:T(8,128)(2,1)S(1)}, bf16[3,192,256]{2,1,0:T(8,128)(2,1)S(1)}, u32[]{:S(2)}, u32[]{:S(2)}) collective-permute-start(bf16[3,192,256]{2,1,0:T(8,128)(2,1)S(1)} %collective-permute-done), channel_id=1, source_target_pairs={{0,128},{128,256},{256,384},{384,0},{1,129},{129,257},{257,385},{3... | collective-permute-start | bytes 884744 | tf_op jit(solution)/shard_map/weights/ppermute | solution.py:26
  48.4 13.9 %collective-permute-start.2 = (bf16[3,192,256]{2,1,0:T(8,128)(2,1)S(1)}, bf16[3,192,256]{2,1,0:T(8,128)(2,1)S(1)}, u32[]{:S(2)}, u32[]{:S(2)}) collective-permute-start(bf16[3,192,256]{2,1,0:T(8,128)(2,1)S(1)} %collective-permute-done), channel_id=1, source_target_pairs={{0,256},{128,384},{256,0},{384,128},{1,257},{129,385},{257,1},{385... | collective-permute-start | bytes 884744 | tf_op jit(solution)/shard_map/weights/ppermute | solution.py:26
  52.8 10.9 %collective-permute-start.1 = (bf16[3,192,256]{2,1,0:T(8,128)(2,1)S(1)}, bf16[3,192,256]{2,1,0:T(8,128)(2,1)S(1)}, u32[]{:S(2)}, u32[]{:S(2)}) collective-permute-start(bf16[3,192,256]{2,1,0:T(8,128)(2,1)S(1)} %collective-permute-done), channel_id=1, source_target_pairs={{0,384},{128,0},{256,128},{384,256},{1,385},{129,1},{257,129},{385... | collective-permute-start | bytes 884744 | tf_op jit(solution)/shard_map/weights/ppermute | solution.py:26
  66.9 3.1 %copy-start.1 = (bf16[384]{0:T(512)(128)(2,1)S(1)}, bf16[384]{0:T(512)(128)(2,1)}, u32[]{:S(2)}) copy-start(bf16[384]{0:T(512)(128)(2,1)} %param.6) | copy-start | bytes 2308
  66.9 3.3 %copy-start.2 = (f32[256]{0:T(256)S(1)}, f32[256]{0:T(256)}, u32[]{:S(2)}) copy-start(f32[256]{0:T(256)} %param.9) | copy-start | bytes 3076
  66.9 3.3 %copy-start.3 = (f32[256]{0:T(256)S(1)}, f32[256]{0:T(256)}, u32[]{:S(2)}) copy-start(f32[256]{0:T(256)} %param.8) | copy-start | bytes 3076
  67.0 35.0 %collective-permute-start.7 = (bf16[4,3,192,256]{3,2,1,0:T(8,128)(2,1)S(1)}, bf16[4,3,192,256]{3,2,1,0:T(8,128)(2,1)S(1)}, u32[]{:S(2)}, u32[]{:S(2)}) collective-permute-start(bf16[4,3,192,256]{3,2,1,0:T(8,128)(2,1)S(1)} %pad_maximum_fusion.w_mine), channel_id=1, source_target_pairs={{0,16},{16,0},{1,17},{17,1},{2,18},{18,2},{3,19},{19,3},{4,20},{20... | collective-permute-start | bytes 3538952 | tf_op jit(solution)/shard_map/weights/ppermute | solution.py:26
  71.0 16.2 %all-to-all-start.1 = ((f32[16,1,1920]{2,1,0:T(1,128)}), f32[16,1,1920]{2,1,0:T(1,128)}, u32[]{:S(2)}, u32[]{:S(2)}) async-start(f32[16,1,1920]{2,1,0:T(1,128)} %broadcast_in_dim.5), calls=%async_computation.1 | async-start | bytes 245760 | tf_op jit(solution)/shard_map/norm/all_to_all | solution.py:68
  75.0 17.2 %collective-permute-start.6 = (bf16[4,128,384]{2,1,0:T(8,128)(2,1)S(1)}, bf16[4,128,384]{2,1,0:T(8,128)(2,1)S(1)}, u32[]{:S(2)}, u32[]{:S(2)}) collective-permute-start(bf16[4,128,384]{2,1,0:T(8,128)(2,1)S(1)} %all-to-all-done.tokens.t0), channel_id=1, source_target_pairs={{0,4},{4,8},{8,12},{12,32},{32,36},{36,40},{40,44},{44,64},{64,68}... | collective-permute-start | bytes 1179656 | tf_op jit(solution)/shard_map/tokens/ppermute | solution.py:26
  77.6 22.3 %collective-permute-start.5 = (bf16[4,128,384]{2,1,0:T(8,128)(2,1)S(1)}, bf16[4,128,384]{2,1,0:T(8,128)(2,1)S(1)}, u32[]{:S(2)}, u32[]{:S(2)}) collective-permute-start(bf16[4,128,384]{2,1,0:T(8,128)(2,1)S(1)} %all-to-all-done.tokens.t0), channel_id=1, source_target_pairs={{0,8},{4,108},{8,32},{12,4},{32,40},{36,12},{40,64},{44,36},{64,72... | collective-permute-start | bytes 1179656 | tf_op jit(solution)/shard_map/tokens/ppermute | solution.py:26
  81.6 20.4 %collective-permute-start.4 = (bf16[4,128,384]{2,1,0:T(8,128)(2,1)S(1)}, bf16[4,128,384]{2,1,0:T(8,128)(2,1)}, u32[]{:S(2)}, u32[]{:S(2)}) collective-permute-start(bf16[4,128,384]{2,1,0:T(8,128)(2,1)S(1)} %all-to-all-done.tokens.t0), channel_id=1, source_target_pairs={{0,108},{4,0},{8,4},{12,8},{32,12},{36,32},{40,36},{44,40},{64,44}... | collective-permute-start | bytes 1179656 | tf_op jit(solution)/shard_map/tokens/ppermute | solution.py:26
  88.0 0.6 copy-start
  106.2 17.2 %all-to-all-start.2 = ((bf16[8,128,384]{2,1,0:T(8,128)(2,1)}), bf16[8,128,384]{2,1,0:T(8,128)(2,1)S(1)}, u32[]{:S(2)}, u32[]{:S(2)}) async-start(bf16[8,128,384]{2,1,0:T(8,128)(2,1)} %bitcast.13), calls=%async_computation.2 | async-start | bytes 1572864 | tf_op jit(solution)/shard_map/project/all_to_all | solution.py:238
  142.9 5.8 %collective-permute-start.8 = (bf16[8,2,256,128]{3,2,1,0:T(8,128)(2,1)S(1)}, bf16[8,2,256,128]{3,2,1,0:T(8,128)(2,1)S(1)}, u32[]{:S(2)}, u32[]{:S(2)}) collective-permute-start(bf16[8,2,256,128]{3,2,1,0:T(8,128)(2,1)S(1)} %all_to_all.20.kv_mine), channel_id=1, source_target_pairs={{0,16},{16,0},{1,17},{17,1},{2,18},{18,2},{3,19},{19,3},{4,20},{20... | collective-permute-start | bytes 3145736 | tf_op jit(solution)/shard_map/keys/ppermute | solution.py:26
  150.9 12.8 %collective-permute-start.9 = (bf16[256,128]{1,0:T(8,128)(2,1)S(1)}, bf16[256,128]{1,0:T(8,128)(2,1)S(1)}, u32[]{:S(2)}, u32[]{:S(2)}) collective-permute-start(bf16[256,128]{1,0:T(8,128)(2,1)S(1)} %attend.1), channel_id=1, source_target_pairs={{0,8},{1,40},{2,72},{3,104},{4,46},{5,78},{6,110},{7,14},{8,96},{9... | collective-permute-start | bytes 196616 | tf_op jit(solution)/shard_map/home/ppermute | solution.py:26
  163.7 3.9 %collective-permute-start.10 = (bf16[128,128]{1,0:T(8,128)(2,1)S(1)}, bf16[128,128]{1,0:T(8,128)(2,1)S(1)}, u32[]{:S(2)}, u32[]{:S(2)}) collective-permute-start(bf16[128,128]{1,0:T(8,128)(2,1)S(1)} %get-tuple-element.22), channel_id=1, source_target_pairs={{0,16},{16,0},{1,17},{17,1},{2,18},{18,2},{3,19},{19,3},{4,20},{20... | collective-permute-start | bytes 98312 | tf_op jit(solution)/shard_map/home/ppermute | solution.py:26

commit v14 on v13

--- a/solution.py
+++ b/solution.py
@@ -68,18 +68,24 @@
     return lax.all_to_all(jnp.broadcast_to(values[None], (count,) + values.shape), axes, 0, 0)
 
 
-def sums_kernel(tokens, out):
+def share_kernel(tokens, ln_gain, q_gain, k_gain, out):
     lane = lax.broadcasted_iota(jnp.int32, (128, 128), 1)
     columns = jnp.zeros((128, 128), jnp.float32)
     for quarter in range(NZH):
         x = tokens[quarter].astype(jnp.float32)
         columns = jnp.where(lane == quarter, jnp.sum(x, axis=1, keepdims=True), columns)
         columns = jnp.where(lane == quarter + NZH, jnp.sum(x * x, axis=1, keepdims=True), columns)
-    out[...] = columns.T[: 2 * NZH]
-
-
-def partial_kernel(where, t0, t1, t2, t3, sums, gain, w_mine, w_theirs, out, w, acc):
-    zl, core, turn, x_here = where[0], where[1], where[2], where[3]
+    sums = columns.T[: 2 * NZH]
+    for target in range(NZL * NY):
+        out[target, 0:8] = sums
+        out[target, 8:11] = ln_gain[...].astype(jnp.float32)
+        out[target, 11:13] = q_gain[...]
+        out[target, 13:15] = k_gain[...]
+        out[target, 15:16] = jnp.zeros((1, 128), jnp.float32)
+
+
+def partial_kernel(where, t0, t1, t2, t3, shared, w_mine, w_theirs, out, w, acc):
+    zl, core, turn, x_here, y_here = (where[i] for i in range(5))
     half = w_mine.shape[2]
     for step in range(NX):
         x = lax.rem(x_here + step, NX)
@@ -89,13 +95,17 @@
             w[x, pl.ds(pl.multiple_of((1 - core) * half, half), half), cols] = w_theirs[step, s]
     tokens = (t0, t1, t2, t3)
 
+    sums = shared[0, 0:8]
+    for group in range(1, NZL * NY):
+        sums += shared[group, 0:8]
     center = sums[:NZH] / FEATURES
     scale = lax.rsqrt(sums[NZH:] / FEATURES - center * center + EPSILON)
     stats = jnp.concatenate([center, scale], axis=0).T
 
     for slot in range(NZL):
         part = lax.rem(zl + slot, NZL)
-        row_gain = gain[part]
+        rows = shared[part * NY + y_here, 8:11]
+        row_gain = jnp.concatenate([rows[0:1], rows[1:2], rows[2:3]], axis=1)
         normed = []
         for quarter in range(NZH):
             x = tokens[slot][quarter].astype(jnp.float32)
@@ -121,7 +131,12 @@
                 out[core_to, y_to, :, s * DH : s * DH + DH] = acc[rows, cols].astype(jnp.bfloat16)
 
 
-def heads_kernel(part, head_gain, q_out, kv_out):
+def heads_kernel(where, part, shared, q_out, kv_out):
+    rows = shared[where[5], 11:15]
+    high = where[6] > 0
+    q_row = jnp.where(high, rows[1:2], rows[0:1])
+    k_row = jnp.where(high, rows[3:4], rows[2:3])
+
     def head_norm(values, row):
         mid = jnp.mean(values, axis=1, keepdims=True)
         var = jnp.mean(values * values, axis=1, keepdims=True) - mid * mid
@@ -130,8 +145,8 @@
     for source in range(2):
         rows = slice(source * 128, source * 128 + 128)
         acc = sum(part[source, y].astype(jnp.float32) for y in range(NY))
-        q_out[rows] = head_norm(acc[:, :DH], head_gain[0])
-        key = head_norm(acc[:, DH : 2 * DH], head_gain[1])
+        q_out[rows] = head_norm(acc[:, :DH], q_row)
+        key = head_norm(acc[:, DH : 2 * DH], k_row)
         value = acc[:, 2 * DH :].astype(jnp.bfloat16)
         for target in range(NX * 2):
             kv_out[target, 0, rows] = key
@@ -183,7 +198,9 @@
     turn = (zh + zl + (zl >= 2)) % NZH
     head_zl = (zl + 2) % NZL
     head_y = (zh + NY - jnp.where(head_zl == 1, 1, jnp.where(head_zl == 3, 2, 0))) % NY
-    where = jnp.stack([zl, core, turn, lax.axis_index("x")]).astype(jnp.int32)
+    where = jnp.stack(
+        [zl, core, turn, lax.axis_index("x"), y_here, head_zl * NY + head_y, y_high]
+    ).astype(jnp.int32)
 
     with jax.named_scope("weights"):
         w_moved = to_plane(jnp.transpose(w_qkv, (1, 0, 2)))
@@ -206,28 +223,18 @@
         t2 = along_z_two(t0)
 
     with jax.named_scope("norm"):
-        own = kernel_call(sums_kernel, jax.ShapeDtypeStruct((2 * NZH, 128), jnp.float32), (t0,))
-        shared = spread(
-            jnp.concatenate([own.reshape(-1), ln_gain.astype(jnp.float32), q_gain, k_gain])[None],
-            ("zl",) + Y,
-            NZL * NY,
-        )[:, 0]
-        sums = jnp.sum(shared[:, :1024], axis=0).reshape(2 * NZH, 128)
-        gain = lax.dynamic_index_in_dim(
-            shared[:, 1024:1408].reshape(NZL, NY, 1, 384), y_here, 1, keepdims=False
-        )
-        head_gain = lax.dynamic_index_in_dim(
-            shared[:, 1408:], head_zl * NY + head_y, 0, keepdims=False
-        )
-        head_gain = lax.dynamic_index_in_dim(
-            head_gain.reshape(2, 2, 1, DH), y_high, 1, keepdims=False
-        )
+        shared = kernel_call(
+            share_kernel,
+            jax.ShapeDtypeStruct((NZL * NY, 16, 128), jnp.float32),
+            (t0, ln_gain.reshape(3, 128), q_gain.reshape(2, 128), k_gain.reshape(2, 128)),
+        )
+        shared = lax.all_to_all(shared, ("zl",) + Y, 0, 0)
 
     with jax.named_scope("project"):
         part = kernel_call(
             partial_kernel,
             jax.ShapeDtypeStruct((CORES, NY, 128, 3 * DH), jnp.bfloat16),
-            (where, t0, t1, t2, t3, sums, gain, w_mine, w_theirs),
+            (where, t0, t1, t2, t3, shared, w_mine, w_theirs),
             scalars=1,
             scratch=[
                 pltpu.VMEM((NX, 384, 768), jnp.bfloat16),
@@ -242,7 +249,8 @@
                 jax.ShapeDtypeStruct((256, DH), jnp.bfloat16),
                 jax.ShapeDtypeStruct((NX * 2, 2, 256, DH), jnp.bfloat16),
             ),
-            (part, head_gain),
+            (where, part, shared),
+            scalars=1,
         )
 
     with jax.named_scope("keys"):

time: 169 us -> 168 us (level)
  blocking collectives: 19.2 us -> 36.1 us
  starting transfers between devices: 76.8 us -> 71.1 us
  local copies, waits for them, and re-layouts: 7.46 us -> 1.77 us
  waiting for transfers between devices: 55.9 us -> 50.3 us
    all_to_all x0 -> x1, blocking collectives: none -> 17 us  [body(): lax.all_to_all(part, ('core',) + Y, 0, 0).reshape(CORES, NY, 128, 3 * DH)]
    all_to_all x1, waiting for transfers between devices: 10.6 us -> 0.01 us  [body(): shared = lax.all_to_all(shared, ('zl',) + Y, 0, 0)]
    ppermute x11, waiting for transfers between devices: 42.2 us -> 47.2 us  [shift(): return lax.ppermute(values, axes, pairs)]
    all_to_all x2 -> x1, starting transfers between devices: 23.9 us -> 19.9 us  [spread(): lax.all_to_all(jnp.broadcast_to(values[None], (count,) + values.shape), a...]
    all_to_all x1, starting transfers between devices: 5.87 us -> 3.56 us  [body(): shared = lax.all_to_all(shared, ('zl',) + Y, 0, 0)]
  transfers between devices with their start and end apart: 14 -> 13, of which waited for: 10 -> 10; matrix products, arithmetic and copies ran while one was open for 4% -> 0% of each run, Pallas kernels for 0% -> 1%
where the time goes in v14:
time: 168 us
  starting transfers between devices  71.1 us (42%)
  waiting for transfers between devices  50.3 us (30%)
  blocking collectives  36.1 us (21%)
  Pallas kernels  7.35 us (4%)
  local copies, waits for them, and re-layouts  1.77 us (1%)
    ppermute x11, starting transfers between devices, shift(): return lax.ppermute(values, axes, pairs)  47.7 us
    ppermute x11, waiting for transfers between devices, shift(): return lax.ppermute(values, axes, pairs)  47.2 us
    all_to_all x1, starting transfers between devices, spread(): lax.all_to_all(jnp.broadcast_to(values[None], (count,) + values.shape), a...  19.9 us
    all_to_all x1, blocking collectives, body(): kv_mine = lax.all_to_all(kv, ('x', 'yl'), 0, 0)  19.1 us
    all_to_all x1, blocking collectives, body(): lax.all_to_all(part, ('core',) + Y, 0, 0).reshape(CORES, NY, 128, 3 * DH)  17 us
    pallas_call x4, Pallas kernels, kernel_call(): pl.pallas_call(kernel, out_shape=out_shape, in_specs=[smem] * scalars + [...  7.35 us
    all_to_all x1, starting transfers between devices, body(): shared = lax.all_to_all(shared, ('zl',) + Y, 0, 0)  3.56 us
  transfers between devices with their start and end apart: 13, of which 10 were waited for; matrix products, arithmetic and copies ran while one was open for 0% of the time, Pallas kernels for 1%

profile of v14, /device:TPU:9, one launch (start us, length us, event | category | flops | bytes accessed | tf_op | source)
XLA Modules:
  0.0 167.7 jit_solution(12952577300509607238)
XLA Ops:
  0.0 11.4 %collective-permute-start = (bf16[3,192,256]{2,1,0:T(8,128)(2,1)}, bf16[3,192,256]{2,1,0:T(8,128)(2,1)S(1)}, u32[]{:S(2)}, u32[]{:S(2)}) collective-permute-start(bf16[3,192,256]{2,1,0:T(8,128)(2,1)} %bitcast.26), channel_id=1, source_target_pairs={{0,8},{1,40},{2,72},{3,104},{4,44},{5,76},{6,108},{7,12},{8,0},{9,... | collective-permute-start | bytes 884744 | tf_op jit(solution)/shard_map/weights/ppermute | solution.py:26
  11.4 12.4 %collective-permute-done = bf16[3,192,256]{2,1,0:T(8,128)(2,1)S(1)} collective-permute-done((bf16[3,192,256]{2,1,0:T(8,128)(2,1)}, bf16[3,192,256]{2,1,0:T(8,128)(2,1)S(1)}, u32[]{:S(2)}, u32[]{:S(2)}) %collective-permute-start) | collective-permute-done | bytes 294944 | tf_op jit(solution)/shard_map/weights/ppermute | solution.py:26
  23.8 1.7 broadcast_in_dim.2
  25.4 19.9 %all-to-all-start = ((bf16[4,128,384]{2,1,0:T(8,128)(2,1)}), bf16[4,128,384]{2,1,0:T(8,128)(2,1)S(1)}, u32[]{:S(2)}, u32[]{:S(2)}) async-start(bf16[4,128,384]{2,1,0:T(8,128)(2,1)} %broadcast_in_dim.2), calls=%async_computation | async-start | bytes 786432 | tf_op jit(solution)/shard_map/tokens/all_to_all | solution.py:68
  45.3 3.1 %collective-permute-start.3 = (bf16[3,192,256]{2,1,0:T(8,128)(2,1)S(1)}, bf16[3,192,256]{2,1,0:T(8,128)(2,1)S(1)}, u32[]{:S(2)}, u32[]{:S(2)}) collective-permute-start(bf16[3,192,256]{2,1,0:T(8,128)(2,1)S(1)} %collective-permute-done), channel_id=1, source_target_pairs={{0,128},{128,256},{256,384},{384,0},{1,129},{129,257},{257,385},{3... | collective-permute-start | bytes 884744 | tf_op jit(solution)/shard_map/weights/ppermute | solution.py:26
  48.4 4.4 %collective-permute-start.2 = (bf16[3,192,256]{2,1,0:T(8,128)(2,1)S(1)}, bf16[3,192,256]{2,1,0:T(8,128)(2,1)S(1)}, u32[]{:S(2)}, u32[]{:S(2)}) collective-permute-start(bf16[3,192,256]{2,1,0:T(8,128)(2,1)S(1)} %collective-permute-done), channel_id=1, source_target_pairs={{0,256},{128,384},{256,0},{384,128},{1,257},{129,385},{257,1},{385... | collective-permute-start | bytes 884744 | tf_op jit(solution)/shard_map/weights/ppermute | solution.py:26
  52.8 3.1 %collective-permute-start.1 = (bf16[3,192,256]{2,1,0:T(8,128)(2,1)S(1)}, bf16[3,192,256]{2,1,0:T(8,128)(2,1)S(1)}, u32[]{:S(2)}, u32[]{:S(2)}) collective-permute-start(bf16[3,192,256]{2,1,0:T(8,128)(2,1)S(1)} %collective-permute-done), channel_id=1, source_target_pairs={{0,384},{128,0},{256,128},{384,256},{1,385},{129,1},{257,129},{385... | collective-permute-start | bytes 884744 | tf_op jit(solution)/shard_map/weights/ppermute | solution.py:26
  55.9 6.4 %collective-permute-done.2 = bf16[3,192,256]{2,1,0:T(8,128)(2,1)S(1)} collective-permute-done((bf16[3,192,256]{2,1,0:T(8,128)(2,1)S(1)}, bf16[3,192,256]{2,1,0:T(8,128)(2,1)S(1)}, u32[]{:S(2)}, u32[]{:S(2)}) %collective-permute-start.2) | collective-permute-done | bytes 294944 | tf_op jit(solution)/shard_map/weights/ppermute | solution.py:26
  62.3 1.4 collective-permute-done.1
  63.8 3.1 %all-to-all-done.tokens.t0 = bf16[4,128,384]{2,1,0:T(8,128)(2,1)S(1)} async-done(((bf16[4,128,384]{2,1,0:T(8,128)(2,1)}), bf16[4,128,384]{2,1,0:T(8,128)(2,1)S(1)}, u32[]{:S(2)}, u32[]{:S(2)}) %all-to-all-start) | async-done | bytes 393248 | tf_op jit(solution)/shard_map/tokens/all_to_all | solution.py:68
  66.9 0.1 pad_maximum_fusion.w_mine
  67.0 2.9 %collective-permute-start.7 = (bf16[4,3,192,256]{3,2,1,0:T(8,128)(2,1)S(1)}, bf16[4,3,192,256]{3,2,1,0:T(8,128)(2,1)S(1)}, u32[]{:S(2)}, u32[]{:S(2)}) collective-permute-start(bf16[4,3,192,256]{3,2,1,0:T(8,128)(2,1)S(1)} %pad_maximum_fusion.w_mine), channel_id=1, source_target_pairs={{0,16},{16,0},{1,17},{17,1},{2,18},{18,2},{3,19},{19,3},{4,20},{20... | collective-permute-start | bytes 3538952 | tf_op jit(solution)/shard_map/weights/ppermute | solution.py:26
  70.0 0.9 norm.1
  70.9 3.6 %all-to-all-start.1 = ((f32[16,16,128]{2,1,0:T(8,128)}), f32[16,16,128]{2,1,0:T(8,128)S(1)}, u32[]{:S(2)}, u32[]{:S(2)}) async-start(f32[16,16,128]{2,1,0:T(8,128)} %norm.1), calls=%async_computation.1 | async-start | bytes 262144 | tf_op jit(solution)/shard_map/norm/all_to_all | solution.py:231
  74.4 3.1 %collective-permute-start.6 = (bf16[4,128,384]{2,1,0:T(8,128)(2,1)S(1)}, bf16[4,128,384]{2,1,0:T(8,128)(2,1)S(1)}, u32[]{:S(2)}, u32[]{:S(2)}) collective-permute-start(bf16[4,128,384]{2,1,0:T(8,128)(2,1)S(1)} %all-to-all-done.tokens.t0), channel_id=1, source_target_pairs={{0,4},{4,8},{8,12},{12,32},{32,36},{36,40},{40,44},{44,64},{64,68}... | collective-permute-start | bytes 1179656 | tf_op jit(solution)/shard_map/tokens/ppermute | solution.py:26
  77.5 4.0 %collective-permute-start.5 = (bf16[4,128,384]{2,1,0:T(8,128)(2,1)S(1)}, bf16[4,128,384]{2,1,0:T(8,128)(2,1)}, u32[]{:S(2)}, u32[]{:S(2)}) collective-permute-start(bf16[4,128,384]{2,1,0:T(8,128)(2,1)S(1)} %all-to-all-done.tokens.t0), channel_id=1, source_target_pairs={{0,8},{4,108},{8,32},{12,4},{32,40},{36,12},{40,64},{44,36},{64,72... | collective-permute-start | bytes 1179656 | tf_op jit(solution)/shard_map/tokens/ppermute | solution.py:26
  81.5 5.4 %collective-permute-start.4 = (bf16[4,128,384]{2,1,0:T(8,128)(2,1)S(1)}, bf16[4,128,384]{2,1,0:T(8,128)(2,1)}, u32[]{:S(2)}, u32[]{:S(2)}) collective-permute-start(bf16[4,128,384]{2,1,0:T(8,128)(2,1)S(1)} %all-to-all-done.tokens.t0), channel_id=1, source_target_pairs={{0,108},{4,0},{8,4},{12,8},{32,12},{36,32},{40,36},{44,40},{64,44}... | collective-permute-start | bytes 1179656 | tf_op jit(solution)/shard_map/tokens/ppermute | solution.py:26
  87.1 3.5 %collective-permute-done.6.t3 = bf16[4,128,384]{2,1,0:T(8,128)(2,1)S(1)} collective-permute-done((bf16[4,128,384]{2,1,0:T(8,128)(2,1)S(1)}, bf16[4,128,384]{2,1,0:T(8,128)(2,1)S(1)}, u32[]{:S(2)}, u32[]{:S(2)}) %collective-permute-start.6) | collective-permute-done | bytes 393248 | tf_op jit(solution)/shard_map/tokens/ppermute | solution.py:26
  90.6 9.4 %collective-permute-done.5.t2 = bf16[4,128,384]{2,1,0:T(8,128)(2,1)} collective-permute-done((bf16[4,128,384]{2,1,0:T(8,128)(2,1)S(1)}, bf16[4,128,384]{2,1,0:T(8,128)(2,1)}, u32[]{:S(2)}, u32[]{:S(2)}) %collective-permute-start.5) | collective-permute-done | bytes 393248 | tf_op jit(solution)/shard_map/tokens/ppermute | solution.py:26
  100.0 2.0 %collective-permute-done.4.t1 = bf16[4,128,384]{2,1,0:T(8,128)(2,1)} collective-permute-done((bf16[4,128,384]{2,1,0:T(8,128)(2,1)S(1)}, bf16[4,128,384]{2,1,0:T(8,128)(2,1)}, u32[]{:S(2)}, u32[]{:S(2)}) %collective-permute-start.4) | collective-permute-done | bytes 393248 | tf_op jit(solution)/shard_map/tokens/ppermute | solution.py:26
  101.9 3.4 %project.2 = bf16[2,4,128,384]{3,2,1,0:T(8,128)(2,1)S(1)} custom-call(s32[7]{0:T(128)S(1)} %stack.46.where, bf16[4,128,384]{2,1,0:T(8,128)(2,1)S(1)} %all-to-all-done.tokens.t0, bf16[4,128,384]{2,1,0:T(8,128)(2,1)} %collective-permute-done.4.t1, bf16[4,128,384]{2,1,0:T(8,128)(2,1)} %collective-permute-done.5.t2, ...), custom_call_target="tpu_custom_call" | custom-call | tf_op jit(solution)/shard_map/project/pallas_call | solution.py:182
  105.4 17.0 %all_to_all.20 = bf16[8,128,384]{2,1,0:T(8,128)(2,1)S(1)} all-to-all(bf16[8,128,384]{2,1,0:T(8,128)(2,1)S(1)} %bitcast.17), channel_id=1, replica_groups=mesh['x'=4,'zh'=4,'core'=2,'zl'=4,'yh'=2,'yl'=2] {'core','yh','yl'}, dimensions={0} | all-to-all | bytes 1572864 | tf_op jit(solution)/shard_map/project/all_to_all | solution.py:245
  122.4 0.8 project.3
  123.2 19.1 %all_to_all.21.kv_mine = bf16[8,2,256,128]{3,2,1,0:T(8,128)(2,1)S(1)} all-to-all(bf16[8,2,256,128]{3,2,1,0:T(8,128)(2,1)S(1)} %get-tuple-element.20), channel_id=1, replica_groups=mesh['x'=4,'zh'=4,'core'=2,'zl'=4,'yh'=2,'yl'=2] {'x','yl'}, dimensions={0} | all-to-all | bytes 2097152 | tf_op jit(solution)/shard_map/keys/all_to_all | solution.py:257
  142.3 3.6 %collective-permute-start.8 = (bf16[8,2,256,128]{3,2,1,0:T(8,128)(2,1)S(1)}, bf16[8,2,256,128]{3,2,1,0:T(8,128)(2,1)S(1)}, u32[]{:S(2)}, u32[]{:S(2)}) collective-permute-start(bf16[8,2,256,128]{3,2,1,0:T(8,128)(2,1)S(1)} %all_to_all.21.kv_mine), channel_id=1, source_target_pairs={{0,16},{16,0},{1,17},{17,1},{2,18},{18,2},{3,19},{19,3},{4,20},{20... | collective-permute-start | bytes 3145736 | tf_op jit(solution)/shard_map/keys/ppermute | solution.py:26
  145.9 2.3 %collective-permute-done.8.kv_theirs = bf16[8,2,256,128]{3,2,1,0:T(8,128)(2,1)S(1)} collective-permute-done((bf16[8,2,256,128]{3,2,1,0:T(8,128)(2,1)S(1)}, bf16[8,2,256,128]{3,2,1,0:T(8,128)(2,1)S(1)}, u32[]{:S(2)}, u32[]{:S(2)}) %collective-permute-start.8) | collective-permute-done | bytes 1048608 | tf_op jit(solution)/shard_map/keys/ppermute | solution.py:26
  148.2 2.2 %attend.1 = bf16[256,128]{1,0:T(8,128)(2,1)S(1)} custom-call(bf16[256,128]{1,0:T(8,128)(2,1)S(1)} %get-tuple-element.19.q, bf16[8,2,256,128]{3,2,1,0:T(8,128)(2,1)S(1)} %all_to_all.21.kv_mine, bf16[8,2,256,128]{3,2,1,0:T(8,128)(2,1)S(1)} %collective-permute-done.8.kv_theirs), custom_call_target="tpu_custom_call" | custom-call | tf_op jit(solution)/shard_map/attend/pallas_call | solution.py:182
  150.4 3.6 %collective-permute-start.9 = (bf16[256,128]{1,0:T(8,128)(2,1)S(1)}, bf16[256,128]{1,0:T(8,128)(2,1)S(1)}, u32[]{:S(2)}, u32[]{:S(2)}) collective-permute-start(bf16[256,128]{1,0:T(8,128)(2,1)S(1)} %attend.1), channel_id=1, source_target_pairs={{0,8},{1,40},{2,72},{3,104},{4,46},{5,78},{6,110},{7,14},{8,96},{9... | collective-permute-start | bytes 196616 | tf_op jit(solution)/shard_map/home/ppermute | solution.py:26
  154.0 9.0 %collective-permute-done.9 = bf16[256,128]{1,0:T(8,128)(2,1)S(1)} collective-permute-done((bf16[256,128]{1,0:T(8,128)(2,1)S(1)}, bf16[256,128]{1,0:T(8,128)(2,1)S(1)}, u32[]{:S(2)}, u32[]{:S(2)}) %collective-permute-start.9) | collective-permute-done | bytes 65568 | tf_op jit(solution)/shard_map/home/ppermute | solution.py:26
  163.1 3.1 %collective-permute-start.10 = (bf16[128,128]{1,0:T(8,128)(2,1)S(1)}, bf16[128,128]{1,0:T(8,128)(2,1)S(1)}, u32[]{:S(2)}, u32[]{:S(2)}) collective-permute-start(bf16[128,128]{1,0:T(8,128)(2,1)S(1)} %get-tuple-element.22), channel_id=1, source_target_pairs={{0,16},{16,0},{1,17},{17,1},{2,18},{18,2},{3,19},{19,3},{4,20},{20... | collective-permute-start | bytes 98312 | tf_op jit(solution)/shard_map/home/ppermute | solution.py:26
  166.2 0.8 collective-permute-done.10
  167.0 0.6 maximum_select_fusion
  (11 shorter events, 0.1 us)
Async XLA Ops:
  0.0 23.8 %collective-permute-start = (bf16[3,192,256]{2,1,0:T(8,128)(2,1)}, bf16[3,192,256]{2,1,0:T(8,128)(2,1)S(1)}, u32[]{:S(2)}, u32[]{:S(2)}) collective-permute-start(bf16[3,192,256]{2,1,0:T(8,128)(2,1)} %bitcast.26), channel_id=1, source_target_pairs={{0,8},{1,40},{2,72},{3,104},{4,44},{5,76},{6,108},{7,12},{8,0},{9,... | collective-permute-start | bytes 884744 | tf_op jit(solution)/shard_map/weights/ppermute | solution.py:26
  25.4 41.4 %all-to-all-start = ((bf16[4,128,384]{2,1,0:T(8,128)(2,1)}), bf16[4,128,384]{2,1,0:T(8,128)(2,1)S(1)}, u32[]{:S(2)}, u32[]{:S(2)}) async-start(bf16[4,128,384]{2,1,0:T(8,128)(2,1)} %broadcast_in_dim.2), calls=%async_computation | async-start | bytes 786432 | tf_op jit(solution)/shard_map/tokens/all_to_all | solution.py:68
  45.3 10.6 %collective-permute-start.3 = (bf16[3,192,256]{2,1,0:T(8,128)(2,1)S(1)}, bf16[3,192,256]{2,1,0:T(8,128)(2,1)S(1)}, u32[]{:S(2)}, u32[]{:S(2)}) collective-permute-start(bf16[3,192,256]{2,1,0:T(8,128)(2,1)S(1)} %collective-permute-done), channel_id=1, source_target_pairs={{0,128},{128,256},{256,384},{384,0},{1,129},{129,257},{257,385},{3... | collective-permute-start | bytes 884744 | tf_op jit(solution)/shard_map/weights/ppermute | solution.py:26
  48.4 13.9 %collective-permute-start.2 = (bf16[3,192,256]{2,1,0:T(8,128)(2,1)S(1)}, bf16[3,192,256]{2,1,0:T(8,128)(2,1)S(1)}, u32[]{:S(2)}, u32[]{:S(2)}) collective-permute-start(bf16[3,192,256]{2,1,0:T(8,128)(2,1)S(1)} %collective-permute-done), channel_id=1, source_target_pairs={{0,256},{128,384},{256,0},{384,128},{1,257},{129,385},{257,1},{385... | collective-permute-start | bytes 884744 | tf_op jit(solution)/shard_map/weights/ppermute | solution.py:26
  52.8 10.9 %collective-permute-start.1 = (bf16[3,192,256]{2,1,0:T(8,128)(2,1)S(1)}, bf16[3,192,256]{2,1,0:T(8,128)(2,1)S(1)}, u32[]{:S(2)}, u32[]{:S(2)}) collective-permute-start(bf16[3,192,256]{2,1,0:T(8,128)(2,1)S(1)} %collective-permute-done), channel_id=1, source_target_pairs={{0,384},{128,0},{256,128},{384,256},{1,385},{129,1},{257,129},{385... | collective-permute-start | bytes 884744 | tf_op jit(solution)/shard_map/weights/ppermute | solution.py:26
  66.9 3.1 %copy-start = (bf16[384]{0:T(512)(128)(2,1)S(1)}, bf16[384]{0:T(512)(128)(2,1)}, u32[]{:S(2)}) copy-start(bf16[384]{0:T(512)(128)(2,1)} %param.6) | copy-start | bytes 2308
  66.9 3.1 %copy-start.1 = (f32[256]{0:T(256)S(1)}, f32[256]{0:T(256)}, u32[]{:S(2)}) copy-start(f32[256]{0:T(256)} %param.8) | copy-start | bytes 3076
  66.9 3.1 %copy-start.2 = (f32[256]{0:T(256)S(1)}, f32[256]{0:T(256)}, u32[]{:S(2)}) copy-start(f32[256]{0:T(256)} %param.9) | copy-start | bytes 3076
  67.0 34.9 %collective-permute-start.7 = (bf16[4,3,192,256]{3,2,1,0:T(8,128)(2,1)S(1)}, bf16[4,3,192,256]{3,2,1,0:T(8,128)(2,1)S(1)}, u32[]{:S(2)}, u32[]{:S(2)}) collective-permute-start(bf16[4,3,192,256]{3,2,1,0:T(8,128)(2,1)S(1)} %pad_maximum_fusion.w_mine), channel_id=1, source_target_pairs={{0,16},{16,0},{1,17},{17,1},{2,18},{18,2},{3,19},{19,3},{4,20},{20... | collective-permute-start | bytes 3538952 | tf_op jit(solution)/shard_map/weights/ppermute | solution.py:26
  70.9 31.1 %all-to-all-start.1 = ((f32[16,16,128]{2,1,0:T(8,128)}), f32[16,16,128]{2,1,0:T(8,128)S(1)}, u32[]{:S(2)}, u32[]{:S(2)}) async-start(f32[16,16,128]{2,1,0:T(8,128)} %norm.1), calls=%async_computation.1 | async-start | bytes 262144 | tf_op jit(solution)/shard_map/norm/all_to_all | solution.py:231
  74.4 16.1 %collective-permute-start.6 = (bf16[4,128,384]{2,1,0:T(8,128)(2,1)S(1)}, bf16[4,128,384]{2,1,0:T(8,128)(2,1)S(1)}, u32[]{:S(2)}, u32[]{:S(2)}) collective-permute-start(bf16[4,128,384]{2,1,0:T(8,128)(2,1)S(1)} %all-to-all-done.tokens.t0), channel_id=1, source_target_pairs={{0,4},{4,8},{8,12},{12,32},{32,36},{36,40},{40,44},{44,64},{64,68}... | collective-permute-start | bytes 1179656 | tf_op jit(solution)/shard_map/tokens/ppermute | solution.py:26
  77.5 22.4 %collective-permute-start.5 = (bf16[4,128,384]{2,1,0:T(8,128)(2,1)S(1)}, bf16[4,128,384]{2,1,0:T(8,128)(2,1)}, u32[]{:S(2)}, u32[]{:S(2)}) collective-permute-start(bf16[4,128,384]{2,1,0:T(8,128)(2,1)S(1)} %all-to-all-done.tokens.t0), channel_id=1, source_target_pairs={{0,8},{4,108},{8,32},{12,4},{32,40},{36,12},{40,64},{44,36},{64,72... | collective-permute-start | bytes 1179656 | tf_op jit(solution)/shard_map/tokens/ppermute | solution.py:26
  81.5 20.4 %collective-permute-start.4 = (bf16[4,128,384]{2,1,0:T(8,128)(2,1)S(1)}, bf16[4,128,384]{2,1,0:T(8,128)(2,1)}, u32[]{:S(2)}, u32[]{:S(2)}) collective-permute-start(bf16[4,128,384]{2,1,0:T(8,128)(2,1)S(1)} %all-to-all-done.tokens.t0), channel_id=1, source_target_pairs={{0,108},{4,0},{8,4},{12,8},{32,12},{36,32},{40,36},{44,40},{64,44}... | collective-permute-start | bytes 1179656 | tf_op jit(solution)/shard_map/tokens/ppermute | solution.py:26
  142.3 5.9 %collective-permute-start.8 = (bf16[8,2,256,128]{3,2,1,0:T(8,128)(2,1)S(1)}, bf16[8,2,256,128]{3,2,1,0:T(8,128)(2,1)S(1)}, u32[]{:S(2)}, u32[]{:S(2)}) collective-permute-start(bf16[8,2,256,128]{3,2,1,0:T(8,128)(2,1)S(1)} %all_to_all.21.kv_mine), channel_id=1, source_target_pairs={{0,16},{16,0},{1,17},{17,1},{2,18},{18,2},{3,19},{19,3},{4,20},{20... | collective-permute-start | bytes 3145736 | tf_op jit(solution)/shard_map/keys/ppermute | solution.py:26
  150.4 12.6 %collective-permute-start.9 = (bf16[256,128]{1,0:T(8,128)(2,1)S(1)}, bf16[256,128]{1,0:T(8,128)(2,1)S(1)}, u32[]{:S(2)}, u32[]{:S(2)}) collective-permute-start(bf16[256,128]{1,0:T(8,128)(2,1)S(1)} %attend.1), channel_id=1, source_target_pairs={{0,8},{1,40},{2,72},{3,104},{4,46},{5,78},{6,110},{7,14},{8,96},{9... | collective-permute-start | bytes 196616 | tf_op jit(solution)/shard_map/home/ppermute | solution.py:26
  163.1 4.0 %collective-permute-start.10 = (bf16[128,128]{1,0:T(8,128)(2,1)S(1)}, bf16[128,128]{1,0:T(8,128)(2,1)S(1)}, u32[]{:S(2)}, u32[]{:S(2)}) collective-permute-start(bf16[128,128]{1,0:T(8,128)(2,1)S(1)} %get-tuple-element.22), channel_id=1, source_target_pairs={{0,16},{16,0},{1,17},{17,1},{2,18},{18,2},{3,19},{19,3},{4,20},{20... | collective-permute-start | bytes 98312 | tf_op jit(solution)/shard_map/home/ppermute | solution.py:26

commit v15 on v14

--- a/solution.py
+++ b/solution.py
@@ -68,7 +68,7 @@
     return lax.all_to_all(jnp.broadcast_to(values[None], (count,) + values.shape), axes, 0, 0)
 
 
-def share_kernel(tokens, ln_gain, q_gain, k_gain, out):
+def share_kernel(tokens, ln_gain, out):
     lane = lax.broadcasted_iota(jnp.int32, (128, 128), 1)
     columns = jnp.zeros((128, 128), jnp.float32)
     for quarter in range(NZH):
@@ -79,9 +79,6 @@
     for target in range(NZL * NY):
         out[target, 0:8] = sums
         out[target, 8:11] = ln_gain[...].astype(jnp.float32)
-        out[target, 11:13] = q_gain[...]
-        out[target, 13:15] = k_gain[...]
-        out[target, 15:16] = jnp.zeros((1, 128), jnp.float32)
 
 
 def partial_kernel(where, t0, t1, t2, t3, shared, w_mine, w_theirs, out, w, acc):
@@ -131,11 +128,10 @@
                 out[core_to, y_to, :, s * DH : s * DH + DH] = acc[rows, cols].astype(jnp.bfloat16)
 
 
-def heads_kernel(where, part, shared, q_out, kv_out):
-    rows = shared[where[5], 11:15]
-    high = where[6] > 0
-    q_row = jnp.where(high, rows[1:2], rows[0:1])
-    k_row = jnp.where(high, rows[3:4], rows[2:3])
+def heads_kernel(where, part, head_gain, q_out, kv_out):
+    high = where[5] > 0
+    q_row = jnp.where(high, head_gain[1:2], head_gain[0:1])
+    k_row = jnp.where(high, head_gain[3:4], head_gain[2:3])
 
     def head_norm(values, row):
         mid = jnp.mean(values, axis=1, keepdims=True)
@@ -196,17 +192,16 @@
     y_high = lax.axis_index("yh")
     y_here = y_high * 2 + lax.axis_index("yl")
     turn = (zh + zl + (zl >= 2)) % NZH
-    head_zl = (zl + 2) % NZL
-    head_y = (zh + NY - jnp.where(head_zl == 1, 1, jnp.where(head_zl == 3, 2, 0))) % NY
     where = jnp.stack(
-        [zl, core, turn, lax.axis_index("x"), y_here, head_zl * NY + head_y, y_high]
+        [zl, core, turn, lax.axis_index("x"), y_here, y_high]
     ).astype(jnp.int32)
 
     with jax.named_scope("weights"):
         w_moved = to_plane(jnp.transpose(w_qkv, (1, 0, 2)))
+        head_gain = to_plane(jnp.concatenate([q_gain, k_gain]).reshape(4, DH))
 
     with jax.named_scope("tokens"):
-        tokens, w_moved = lax.optimization_barrier((tokens, w_moved))
+        tokens, w_moved, head_gain = lax.optimization_barrier((tokens, w_moved, head_gain))
         t0 = spread(tokens, "zh", NZH)
 
     with jax.named_scope("weights"):
@@ -225,8 +220,8 @@
     with jax.named_scope("norm"):
         shared = kernel_call(
             share_kernel,
-            jax.ShapeDtypeStruct((NZL * NY, 16, 128), jnp.float32),
-            (t0, ln_gain.reshape(3, 128), q_gain.reshape(2, 128), k_gain.reshape(2, 128)),
+            jax.ShapeDtypeStruct((NZL * NY, 11, 128), jnp.float32),
+            (t0, ln_gain.reshape(3, 128)),
         )
         shared = lax.all_to_all(shared, ("zl",) + Y, 0, 0)
 
@@ -249,7 +244,7 @@
                 jax.ShapeDtypeStruct((256, DH), jnp.bfloat16),
                 jax.ShapeDtypeStruct((NX * 2, 2, 256, DH), jnp.bfloat16),
             ),
-            (where, part, shared),
+            (where, part, head_gain),
             scalars=1,
         )
 

time: 168 us -> 166 us (0.988)
  the two profiles are of different devices: /device:TPU:9 before, /device:TPU:33 now
where the time goes in v15:
time: 166 us; the launch traced here: 165 us
  starting transfers between devices  85.5 us (52%)
  blocking collectives  34.7 us (21%)
  waiting for transfers between devices  33.9 us (20%)
  Pallas kernels  7.36 us (4%)
  local copies, waits for them, and re-layouts  1.77 us (1%)
    ppermute x12, starting transfers between devices, shift(): return lax.ppermute(values, axes, pairs)  61.1 us
    ppermute x12, waiting for transfers between devices, shift(): return lax.ppermute(values, axes, pairs)  21.9 us
    all_to_all x1, blocking collectives, body(): kv_mine = lax.all_to_all(kv, ('x', 'yl'), 0, 0)  18.4 us
    all_to_all x1, starting transfers between devices, spread(): lax.all_to_all(jnp.broadcast_to(values[None], (count,) + values.shape), a...  16.3 us
    all_to_all x1, blocking collectives, body(): lax.all_to_all(part, ('core',) + Y, 0, 0).reshape(CORES, NY, 128, 3 * DH)  16.3 us
    all_to_all x1, waiting for transfers between devices, body(): shared = lax.all_to_all(shared, ('zl',) + Y, 0, 0)  12.1 us
    all_to_all x1, starting transfers between devices, body(): shared = lax.all_to_all(shared, ('zl',) + Y, 0, 0)  8.06 us
    pallas_call x4, Pallas kernels, kernel_call(): pl.pallas_call(kernel, out_shape=out_shape, in_specs=[smem] * scalars + [...  7.36 us
  transfers between devices with their start and end apart: 14, of which 7 were waited for; matrix products, arithmetic and copies ran while one was open for 0% of the time, Pallas kernels for 1%

profile of v15, /device:TPU:33, one launch (start us, length us, event | category | flops | bytes accessed | tf_op | source)
XLA Modules:
  0.0 164.9 jit_solution(11786594720941558563)
XLA Ops:
  0.0 11.5 %collective-permute-start = (bf16[3,192,256]{2,1,0:T(8,128)(2,1)}, bf16[3,192,256]{2,1,0:T(8,128)(2,1)S(1)}, u32[]{:S(2)}, u32[]{:S(2)}) collective-permute-start(bf16[3,192,256]{2,1,0:T(8,128)(2,1)} %bitcast.25), channel_id=1, source_target_pairs={{0,8},{1,40},{2,72},{3,104},{4,44},{5,76},{6,108},{7,12},{8,0},{9,... | collective-permute-start | bytes 884744 | tf_op jit(solution)/shard_map/weights/ppermute | solution.py:26
  11.5 0.7 pad_maximum_fusion.1
  12.2 6.2 %collective-permute-start.1 = (f32[4,128]{1,0:T(4,128)S(1)}, f32[4,128]{1,0:T(4,128)S(1)}, u32[]{:S(2)}, u32[]{:S(2)}) collective-permute-start(f32[4,128]{1,0:T(4,128)S(1)} %pad_maximum_fusion.1), channel_id=1, source_target_pairs={{0,8},{1,40},{2,72},{3,104},{4,44},{5,76},{6,108},{7,12},{8,0},{9,... | collective-permute-start | bytes 6152 | tf_op jit(solution)/shard_map/weights/ppermute | solution.py:26
  18.4 2.6 %collective-permute-done.1.head_gain = f32[4,128]{1,0:T(4,128)S(1)} collective-permute-done((f32[4,128]{1,0:T(4,128)S(1)}, f32[4,128]{1,0:T(4,128)S(1)}, u32[]{:S(2)}, u32[]{:S(2)}) %collective-permute-start.1) | collective-permute-done | bytes 2080 | tf_op jit(solution)/shard_map/weights/ppermute | solution.py:26
  21.1 1.7 %broadcast_in_dim.2 = bf16[4,128,384]{2,1,0:T(8,128)(2,1)} broadcast(bf16[128,384]{1,0:T(8,128)(2,1)} %param.5), dimensions={1,2} | broadcast | bytes 491520 | tf_op jit(solution)/shard_map/tokens/broadcast_in_dim | solution.py:68
  22.8 16.3 %all-to-all-start = ((bf16[4,128,384]{2,1,0:T(8,128)(2,1)}), bf16[4,128,384]{2,1,0:T(8,128)(2,1)S(1)}, u32[]{:S(2)}, u32[]{:S(2)}) async-start(bf16[4,128,384]{2,1,0:T(8,128)(2,1)} %broadcast_in_dim.2), calls=%async_computation | async-start | bytes 786432 | tf_op jit(solution)/shard_map/tokens/all_to_all | solution.py:68
  39.1 3.1 %collective-permute-start.4 = (bf16[3,192,256]{2,1,0:T(8,128)(2,1)S(1)}, bf16[3,192,256]{2,1,0:T(8,128)(2,1)S(1)}, u32[]{:S(2)}, u32[]{:S(2)}) collective-permute-start(bf16[3,192,256]{2,1,0:T(8,128)(2,1)S(1)} %collective-permute-done), channel_id=1, source_target_pairs={{0,128},{128,256},{256,384},{384,0},{1,129},{129,257},{257,385},{3... | collective-permute-start | bytes 884744 | tf_op jit(solution)/shard_map/weights/ppermute | solution.py:26
  42.2 4.4 %collective-permute-start.3 = (bf16[3,192,256]{2,1,0:T(8,128)(2,1)S(1)}, bf16[3,192,256]{2,1,0:T(8,128)(2,1)S(1)}, u32[]{:S(2)}, u32[]{:S(2)}) collective-permute-start(bf16[3,192,256]{2,1,0:T(8,128)(2,1)S(1)} %collective-permute-done), channel_id=1, source_target_pairs={{0,256},{128,384},{256,0},{384,128},{1,257},{129,385},{257,1},{385... | collective-permute-start | bytes 884744 | tf_op jit(solution)/shard_map/weights/ppermute | solution.py:26
  46.6 3.1 %collective-permute-start.2 = (bf16[3,192,256]{2,1,0:T(8,128)(2,1)S(1)}, bf16[3,192,256]{2,1,0:T(8,128)(2,1)S(1)}, u32[]{:S(2)}, u32[]{:S(2)}) collective-permute-start(bf16[3,192,256]{2,1,0:T(8,128)(2,1)S(1)} %collective-permute-done), channel_id=1, source_target_pairs={{0,384},{128,0},{256,128},{384,256},{1,385},{129,1},{257,129},{385... | collective-permute-start | bytes 884744 | tf_op jit(solution)/shard_map/weights/ppermute | solution.py:26
  49.7 6.3 %collective-permute-done.3 = bf16[3,192,256]{2,1,0:T(8,128)(2,1)S(1)} collective-permute-done((bf16[3,192,256]{2,1,0:T(8,128)(2,1)S(1)}, bf16[3,192,256]{2,1,0:T(8,128)(2,1)S(1)}, u32[]{:S(2)}, u32[]{:S(2)}) %collective-permute-start.3) | collective-permute-done | bytes 294944 | tf_op jit(solution)/shard_map/weights/ppermute | solution.py:26
  56.0 1.5 collective-permute-done.2
  57.5 0.1 pad_maximum_fusion.w_mine
  57.7 4.8 %collective-permute-start.8 = (bf16[4,3,192,256]{3,2,1,0:T(8,128)(2,1)S(1)}, bf16[4,3,192,256]{3,2,1,0:T(8,128)(2,1)S(1)}, u32[]{:S(2)}, u32[]{:S(2)}) collective-permute-start(bf16[4,3,192,256]{3,2,1,0:T(8,128)(2,1)S(1)} %pad_maximum_fusion.w_mine), channel_id=1, source_target_pairs={{0,16},{16,0},{1,17},{17,1},{2,18},{18,2},{3,19},{19,3},{4,20},{20... | collective-permute-start | bytes 3538952 | tf_op jit(solution)/shard_map/weights/ppermute | solution.py:26
  62.5 9.7 %collective-permute-start.7 = (bf16[4,128,384]{2,1,0:T(8,128)(2,1)S(1)}, bf16[4,128,384]{2,1,0:T(8,128)(2,1)S(1)}, u32[]{:S(2)}, u32[]{:S(2)}) collective-permute-start(bf16[4,128,384]{2,1,0:T(8,128)(2,1)S(1)} %all-to-all-done.tokens.t0), channel_id=1, source_target_pairs={{0,4},{4,8},{8,12},{12,32},{32,36},{36,40},{40,44},{44,64},{64,68}... | collective-permute-start | bytes 1179656 | tf_op jit(solution)/shard_map/tokens/ppermute | solution.py:26
  72.2 1.9 %collective-permute-start.6 = (bf16[4,128,384]{2,1,0:T(8,128)(2,1)S(1)}, bf16[4,128,384]{2,1,0:T(8,128)(2,1)}, u32[]{:S(2)}, u32[]{:S(2)}) collective-permute-start(bf16[4,128,384]{2,1,0:T(8,128)(2,1)S(1)} %all-to-all-done.tokens.t0), channel_id=1, source_target_pairs={{0,8},{4,108},{8,32},{12,4},{32,40},{36,12},{40,64},{44,36},{64,72... | collective-permute-start | bytes 1179656 | tf_op jit(solution)/shard_map/tokens/ppermute | solution.py:26
  74.2 3.1 %collective-permute-start.5 = (bf16[4,128,384]{2,1,0:T(8,128)(2,1)S(1)}, bf16[4,128,384]{2,1,0:T(8,128)(2,1)}, u32[]{:S(2)}, u32[]{:S(2)}) collective-permute-start(bf16[4,128,384]{2,1,0:T(8,128)(2,1)S(1)} %all-to-all-done.tokens.t0), channel_id=1, source_target_pairs={{0,108},{4,0},{8,4},{12,8},{32,12},{36,32},{40,36},{44,40},{64,44}... | collective-permute-start | bytes 1179656 | tf_op jit(solution)/shard_map/tokens/ppermute | solution.py:26
  77.3 0.9 norm.1
  78.2 8.1 %all-to-all-start.1 = ((f32[16,11,128]{2,1,0:T(8,128)}), f32[16,11,128]{2,1,0:T(8,128)S(1)}, u32[]{:S(2)}, u32[]{:S(2)}) async-start(f32[16,11,128]{2,1,0:T(8,128)} %norm.1), calls=%async_computation.1 | async-start | bytes 262144 | tf_op jit(solution)/shard_map/norm/all_to_all | solution.py:226
  86.2 0.1 stack.42.where
  86.3 12.1 %all-to-all-done.1.shared = f32[16,11,128]{2,1,0:T(8,128)S(1)} async-done(((f32[16,11,128]{2,1,0:T(8,128)}), f32[16,11,128]{2,1,0:T(8,128)S(1)}, u32[]{:S(2)}, u32[]{:S(2)}) %all-to-all-start.1) | async-done | bytes 90144 | tf_op jit(solution)/shard_map/norm/all_to_all | solution.py:226
  98.4 3.4 %project.2 = bf16[2,4,128,384]{3,2,1,0:T(8,128)(2,1)S(1)} custom-call(s32[6]{0:T(128)S(1)} %stack.42.where, bf16[4,128,384]{2,1,0:T(8,128)(2,1)S(1)} %all-to-all-done.tokens.t0, bf16[4,128,384]{2,1,0:T(8,128)(2,1)} %collective-permute-done.5.t1, bf16[4,128,384]{2,1,0:T(8,128)(2,1)} %collective-permute-done.6.t2, ...), custom_call_target="tpu_custom_call" | custom-call | tf_op jit(solution)/shard_map/project/pallas_call | solution.py:178
  101.8 16.3 %all_to_all.20 = bf16[8,128,384]{2,1,0:T(8,128)(2,1)S(1)} all-to-all(bf16[8,128,384]{2,1,0:T(8,128)(2,1)S(1)} %bitcast.16), channel_id=1, replica_groups=mesh['x'=4,'zh'=4,'core'=2,'zl'=4,'yh'=2,'yl'=2] {'core','yh','yl'}, dimensions={0} | all-to-all | bytes 1572864 | tf_op jit(solution)/shard_map/project/all_to_all | solution.py:240
  118.1 0.8 project.3
  118.9 18.4 %all_to_all.21.kv_mine = bf16[8,2,256,128]{3,2,1,0:T(8,128)(2,1)S(1)} all-to-all(bf16[8,2,256,128]{3,2,1,0:T(8,128)(2,1)S(1)} %get-tuple-element.22), channel_id=1, replica_groups=mesh['x'=4,'zh'=4,'core'=2,'zl'=4,'yh'=2,'yl'=2] {'x','yl'}, dimensions={0} | all-to-all | bytes 2097152 | tf_op jit(solution)/shard_map/keys/all_to_all | solution.py:252
  137.4 3.9 %collective-permute-start.9 = (bf16[8,2,256,128]{3,2,1,0:T(8,128)(2,1)S(1)}, bf16[8,2,256,128]{3,2,1,0:T(8,128)(2,1)S(1)}, u32[]{:S(2)}, u32[]{:S(2)}) collective-permute-start(bf16[8,2,256,128]{3,2,1,0:T(8,128)(2,1)S(1)} %all_to_all.21.kv_mine), channel_id=1, source_target_pairs={{0,16},{16,0},{1,17},{17,1},{2,18},{18,2},{3,19},{19,3},{4,20},{20... | collective-permute-start | bytes 3145736 | tf_op jit(solution)/shard_map/keys/ppermute | solution.py:26
  141.3 2.3 %collective-permute-done.9.kv_theirs = bf16[8,2,256,128]{3,2,1,0:T(8,128)(2,1)S(1)} collective-permute-done((bf16[8,2,256,128]{3,2,1,0:T(8,128)(2,1)S(1)}, bf16[8,2,256,128]{3,2,1,0:T(8,128)(2,1)S(1)}, u32[]{:S(2)}, u32[]{:S(2)}) %collective-permute-start.9) | collective-permute-done | bytes 1048608 | tf_op jit(solution)/shard_map/keys/ppermute | solution.py:26
  143.6 2.2 %attend.1 = bf16[256,128]{1,0:T(8,128)(2,1)S(1)} custom-call(bf16[256,128]{1,0:T(8,128)(2,1)S(1)} %get-tuple-element.21.q, bf16[8,2,256,128]{3,2,1,0:T(8,128)(2,1)S(1)} %all_to_all.21.kv_mine, bf16[8,2,256,128]{3,2,1,0:T(8,128)(2,1)S(1)} %collective-permute-done.9.kv_theirs), custom_call_target="tpu_custom_call" | custom-call | tf_op jit(solution)/shard_map/attend/pallas_call | solution.py:178
  145.8 3.5 %collective-permute-start.10 = (bf16[256,128]{1,0:T(8,128)(2,1)S(1)}, bf16[256,128]{1,0:T(8,128)(2,1)S(1)}, u32[]{:S(2)}, u32[]{:S(2)}) collective-permute-start(bf16[256,128]{1,0:T(8,128)(2,1)S(1)} %attend.1), channel_id=1, source_target_pairs={{0,8},{1,40},{2,72},{3,104},{4,46},{5,78},{6,110},{7,14},{8,96},{9... | collective-permute-start | bytes 196616 | tf_op jit(solution)/shard_map/home/ppermute | solution.py:26
  149.3 8.3 %collective-permute-done.10 = bf16[256,128]{1,0:T(8,128)(2,1)S(1)} collective-permute-done((bf16[256,128]{1,0:T(8,128)(2,1)S(1)}, bf16[256,128]{1,0:T(8,128)(2,1)S(1)}, u32[]{:S(2)}, u32[]{:S(2)}) %collective-permute-start.10) | collective-permute-done | bytes 65568 | tf_op jit(solution)/shard_map/home/ppermute | solution.py:26
  157.6 5.8 %collective-permute-start.11 = (bf16[128,128]{1,0:T(8,128)(2,1)S(1)}, bf16[128,128]{1,0:T(8,128)(2,1)S(1)}, u32[]{:S(2)}, u32[]{:S(2)}) collective-permute-start(bf16[128,128]{1,0:T(8,128)(2,1)S(1)} %get-tuple-element.24), channel_id=1, source_target_pairs={{0,16},{16,0},{1,17},{17,1},{2,18},{18,2},{3,19},{19,3},{4,20},{20... | collective-permute-start | bytes 98312 | tf_op jit(solution)/shard_map/home/ppermute | solution.py:26
  163.5 0.8 collective-permute-done.11
  164.3 0.6 maximum_select_fusion
  (10 shorter events, 0.0 us)
Async XLA Ops:
  0.0 21.1 %collective-permute-start = (bf16[3,192,256]{2,1,0:T(8,128)(2,1)}, bf16[3,192,256]{2,1,0:T(8,128)(2,1)S(1)}, u32[]{:S(2)}, u32[]{:S(2)}) collective-permute-start(bf16[3,192,256]{2,1,0:T(8,128)(2,1)} %bitcast.25), channel_id=1, source_target_pairs={{0,8},{1,40},{2,72},{3,104},{4,44},{5,76},{6,108},{7,12},{8,0},{9,... | collective-permute-start | bytes 884744 | tf_op jit(solution)/shard_map/weights/ppermute | solution.py:26
  12.2 8.8 %collective-permute-start.1 = (f32[4,128]{1,0:T(4,128)S(1)}, f32[4,128]{1,0:T(4,128)S(1)}, u32[]{:S(2)}, u32[]{:S(2)}) collective-permute-start(f32[4,128]{1,0:T(4,128)S(1)} %pad_maximum_fusion.1), channel_id=1, source_target_pairs={{0,8},{1,40},{2,72},{3,104},{4,44},{5,76},{6,108},{7,12},{8,0},{9,... | collective-permute-start | bytes 6152 | tf_op jit(solution)/shard_map/weights/ppermute | solution.py:26
  22.8 34.8 %all-to-all-start = ((bf16[4,128,384]{2,1,0:T(8,128)(2,1)}), bf16[4,128,384]{2,1,0:T(8,128)(2,1)S(1)}, u32[]{:S(2)}, u32[]{:S(2)}) async-start(bf16[4,128,384]{2,1,0:T(8,128)(2,1)} %broadcast_in_dim.2), calls=%async_computation | async-start | bytes 786432 | tf_op jit(solution)/shard_map/tokens/all_to_all | solution.py:68
  39.1 10.6 %collective-permute-start.4 = (bf16[3,192,256]{2,1,0:T(8,128)(2,1)S(1)}, bf16[3,192,256]{2,1,0:T(8,128)(2,1)S(1)}, u32[]{:S(2)}, u32[]{:S(2)}) collective-permute-start(bf16[3,192,256]{2,1,0:T(8,128)(2,1)S(1)} %collective-permute-done), channel_id=1, source_target_pairs={{0,128},{128,256},{256,384},{384,0},{1,129},{129,257},{257,385},{3... | collective-permute-start | bytes 884744 | tf_op jit(solution)/shard_map/weights/ppermute | solution.py:26
  42.2 13.8 %collective-permute-start.3 = (bf16[3,192,256]{2,1,0:T(8,128)(2,1)S(1)}, bf16[3,192,256]{2,1,0:T(8,128)(2,1)S(1)}, u32[]{:S(2)}, u32[]{:S(2)}) collective-permute-start(bf16[3,192,256]{2,1,0:T(8,128)(2,1)S(1)} %collective-permute-done), channel_id=1, source_target_pairs={{0,256},{128,384},{256,0},{384,128},{1,257},{129,385},{257,1},{385... | collective-permute-start | bytes 884744 | tf_op jit(solution)/shard_map/weights/ppermute | solution.py:26
  46.6 10.9 %collective-permute-start.2 = (bf16[3,192,256]{2,1,0:T(8,128)(2,1)S(1)}, bf16[3,192,256]{2,1,0:T(8,128)(2,1)S(1)}, u32[]{:S(2)}, u32[]{:S(2)}) collective-permute-start(bf16[3,192,256]{2,1,0:T(8,128)(2,1)S(1)} %collective-permute-done), channel_id=1, source_target_pairs={{0,384},{128,0},{256,128},{384,256},{1,385},{129,1},{257,129},{385... | collective-permute-start | bytes 884744 | tf_op jit(solution)/shard_map/weights/ppermute | solution.py:26
  57.5 19.7 %copy-start = (bf16[384]{0:T(512)(128)(2,1)S(1)}, bf16[384]{0:T(512)(128)(2,1)}, u32[]{:S(2)}) copy-start(bf16[384]{0:T(512)(128)(2,1)} %param.6) | copy-start | bytes 2308
  57.7 40.7 %collective-permute-start.8 = (bf16[4,3,192,256]{3,2,1,0:T(8,128)(2,1)S(1)}, bf16[4,3,192,256]{3,2,1,0:T(8,128)(2,1)S(1)}, u32[]{:S(2)}, u32[]{:S(2)}) collective-permute-start(bf16[4,3,192,256]{3,2,1,0:T(8,128)(2,1)S(1)} %pad_maximum_fusion.w_mine), channel_id=1, source_target_pairs={{0,16},{16,0},{1,17},{17,1},{2,18},{18,2},{3,19},{19,3},{4,20},{20... | collective-permute-start | bytes 3538952 | tf_op jit(solution)/shard_map/weights/ppermute | solution.py:26
  62.5 35.9 %collective-permute-start.7 = (bf16[4,128,384]{2,1,0:T(8,128)(2,1)S(1)}, bf16[4,128,384]{2,1,0:T(8,128)(2,1)S(1)}, u32[]{:S(2)}, u32[]{:S(2)}) collective-permute-start(bf16[4,128,384]{2,1,0:T(8,128)(2,1)S(1)} %all-to-all-done.tokens.t0), channel_id=1, source_target_pairs={{0,4},{4,8},{8,12},{12,32},{32,36},{36,40},{40,44},{44,64},{64,68}... | collective-permute-start | bytes 1179656 | tf_op jit(solution)/shard_map/tokens/ppermute | solution.py:26
  72.2 26.2 %collective-permute-start.6 = (bf16[4,128,384]{2,1,0:T(8,128)(2,1)S(1)}, bf16[4,128,384]{2,1,0:T(8,128)(2,1)}, u32[]{:S(2)}, u32[]{:S(2)}) collective-permute-start(bf16[4,128,384]{2,1,0:T(8,128)(2,1)S(1)} %all-to-all-done.tokens.t0), channel_id=1, source_target_pairs={{0,8},{4,108},{8,32},{12,4},{32,40},{36,12},{40,64},{44,36},{64,72... | collective-permute-start | bytes 1179656 | tf_op jit(solution)/shard_map/tokens/ppermute | solution.py:26
  74.2 24.2 %collective-permute-start.5 = (bf16[4,128,384]{2,1,0:T(8,128)(2,1)S(1)}, bf16[4,128,384]{2,1,0:T(8,128)(2,1)}, u32[]{:S(2)}, u32[]{:S(2)}) collective-permute-start(bf16[4,128,384]{2,1,0:T(8,128)(2,1)S(1)} %all-to-all-done.tokens.t0), channel_id=1, source_target_pairs={{0,108},{4,0},{8,4},{12,8},{32,12},{36,32},{40,36},{44,40},{64,44}... | collective-permute-start | bytes 1179656 | tf_op jit(solution)/shard_map/tokens/ppermute | solution.py:26
  78.2 20.2 %all-to-all-start.1 = ((f32[16,11,128]{2,1,0:T(8,128)}), f32[16,11,128]{2,1,0:T(8,128)S(1)}, u32[]{:S(2)}, u32[]{:S(2)}) async-start(f32[16,11,128]{2,1,0:T(8,128)} %norm.1), calls=%async_computation.1 | async-start | bytes 262144 | tf_op jit(solution)/shard_map/norm/all_to_all | solution.py:226
  137.4 6.2 %collective-permute-start.9 = (bf16[8,2,256,128]{3,2,1,0:T(8,128)(2,1)S(1)}, bf16[8,2,256,128]{3,2,1,0:T(8,128)(2,1)S(1)}, u32[]{:S(2)}, u32[]{:S(2)}) collective-permute-start(bf16[8,2,256,128]{3,2,1,0:T(8,128)(2,1)S(1)} %all_to_all.21.kv_mine), channel_id=1, source_target_pairs={{0,16},{16,0},{1,17},{17,1},{2,18},{18,2},{3,19},{19,3},{4,20},{20... | collective-permute-start | bytes 3145736 | tf_op jit(solution)/shard_map/keys/ppermute | solution.py:26
  145.8 11.8 %collective-permute-start.10 = (bf16[256,128]{1,0:T(8,128)(2,1)S(1)}, bf16[256,128]{1,0:T(8,128)(2,1)S(1)}, u32[]{:S(2)}, u32[]{:S(2)}) collective-permute-start(bf16[256,128]{1,0:T(8,128)(2,1)S(1)} %attend.1), channel_id=1, source_target_pairs={{0,8},{1,40},{2,72},{3,104},{4,46},{5,78},{6,110},{7,14},{8,96},{9... | collective-permute-start | bytes 196616 | tf_op jit(solution)/shard_map/home/ppermute | solution.py:26
  157.6 6.7 %collective-permute-start.11 = (bf16[128,128]{1,0:T(8,128)(2,1)S(1)}, bf16[128,128]{1,0:T(8,128)(2,1)S(1)}, u32[]{:S(2)}, u32[]{:S(2)}) collective-permute-start(bf16[128,128]{1,0:T(8,128)(2,1)S(1)} %get-tuple-element.24), channel_id=1, source_target_pairs={{0,16},{16,0},{1,17},{17,1},{2,18},{18,2},{3,19},{19,3},{4,20},{20... | collective-permute-start | bytes 98312 | tf_op jit(solution)/shard_map/home/ppermute | solution.py:26

commit v16 on v15

--- a/solution.py
+++ b/solution.py
@@ -125,7 +125,7 @@
             head = y_to // 2
             for s in range(3):
                 cols = slice(s * 256 + head * DH, s * 256 + head * DH + DH)
-                out[core_to, y_to, :, s * DH : s * DH + DH] = acc[rows, cols].astype(jnp.bfloat16)
+                out[core_to, y_to, :, s * DH : s * DH + DH] = acc[rows, cols]
 
 
 def heads_kernel(where, part, head_gain, q_out, kv_out):
@@ -228,7 +228,7 @@
     with jax.named_scope("project"):
         part = kernel_call(
             partial_kernel,
-            jax.ShapeDtypeStruct((CORES, NY, 128, 3 * DH), jnp.bfloat16),
+            jax.ShapeDtypeStruct((CORES, NY, 128, 3 * DH), jnp.float32),
             (where, t0, t1, t2, t3, shared, w_mine, w_theirs),
             scalars=1,
             scratch=[

time: 166 us -> 174 us (1.048)
  blocking collectives: 34.7 us -> 43.1 us
    all_to_all x1, blocking collectives: 16.3 us -> 24.7 us  [body(): lax.all_to_all(part, ('core',) + Y, 0, 0).reshape(CORES, NY, 128, 3 * DH)]
where the time goes in v16:
time: 174 us; the launch traced here: 173 us
  starting transfers between devices  85.5 us (49%)
  blocking collectives  43.1 us (25%)
  waiting for transfers between devices  33.9 us (19%)
  Pallas kernels  7.26 us (4%)
  local copies, waits for them, and re-layouts  1.77 us (1%)
    ppermute x12, starting transfers between devices, shift(): return lax.ppermute(values, axes, pairs)  61 us
    all_to_all x1, blocking collectives, body(): lax.all_to_all(part, ('core',) + Y, 0, 0).reshape(CORES, NY, 128, 3 * DH)  24.7 us
    ppermute x12, waiting for transfers between devices, shift(): return lax.ppermute(values, axes, pairs)  21.9 us
    all_to_all x1, blocking collectives, body(): kv_mine = lax.all_to_all(kv, ('x', 'yl'), 0, 0)  18.4 us
    all_to_all x1, starting transfers between devices, spread(): lax.all_to_all(jnp.broadcast_to(values[None], (count,) + values.shape), a...  16.3 us
    all_to_all x1, waiting for transfers between devices, body(): shared = lax.all_to_all(shared, ('zl',) + Y, 0, 0)  12.1 us
    all_to_all x1, starting transfers between devices, body(): shared = lax.all_to_all(shared, ('zl',) + Y, 0, 0)  8.06 us
    pallas_call x4, Pallas kernels, kernel_call(): pl.pallas_call(kernel, out_shape=out_shape, in_specs=[smem] * scalars + [...  7.26 us
  transfers between devices with their start and end apart: 14, of which 7 were waited for; matrix products, arithmetic and copies ran while one was open for 0% of the time, Pallas kernels for 1%

profile of v16, /device:TPU:33, one launch (start us, length us, event | category | flops | bytes accessed | tf_op | source)
XLA Modules:
  0.0 173.3 jit_solution(14424419150936846065)
XLA Ops:
  0.0 11.5 %collective-permute-start = (bf16[3,192,256]{2,1,0:T(8,128)(2,1)}, bf16[3,192,256]{2,1,0:T(8,128)(2,1)S(1)}, u32[]{:S(2)}, u32[]{:S(2)}) collective-permute-start(bf16[3,192,256]{2,1,0:T(8,128)(2,1)} %bitcast.25), channel_id=1, source_target_pairs={{0,8},{1,40},{2,72},{3,104},{4,44},{5,76},{6,108},{7,12},{8,0},{9,... | collective-permute-start | bytes 884744 | tf_op jit(solution)/shard_map/weights/ppermute | solution.py:26
  11.5 0.7 pad_maximum_fusion.1
  12.2 6.2 %collective-permute-start.1 = (f32[4,128]{1,0:T(4,128)S(1)}, f32[4,128]{1,0:T(4,128)S(1)}, u32[]{:S(2)}, u32[]{:S(2)}) collective-permute-start(f32[4,128]{1,0:T(4,128)S(1)} %pad_maximum_fusion.1), channel_id=1, source_target_pairs={{0,8},{1,40},{2,72},{3,104},{4,44},{5,76},{6,108},{7,12},{8,0},{9,... | collective-permute-start | bytes 6152 | tf_op jit(solution)/shard_map/weights/ppermute | solution.py:26
  18.4 2.6 %collective-permute-done.1.head_gain = f32[4,128]{1,0:T(4,128)S(1)} collective-permute-done((f32[4,128]{1,0:T(4,128)S(1)}, f32[4,128]{1,0:T(4,128)S(1)}, u32[]{:S(2)}, u32[]{:S(2)}) %collective-permute-start.1) | collective-permute-done | bytes 2080 | tf_op jit(solution)/shard_map/weights/ppermute | solution.py:26
  21.1 1.7 broadcast_in_dim.2
  22.8 16.3 %all-to-all-start = ((bf16[4,128,384]{2,1,0:T(8,128)(2,1)}), bf16[4,128,384]{2,1,0:T(8,128)(2,1)S(1)}, u32[]{:S(2)}, u32[]{:S(2)}) async-start(bf16[4,128,384]{2,1,0:T(8,128)(2,1)} %broadcast_in_dim.2), calls=%async_computation | async-start | bytes 786432 | tf_op jit(solution)/shard_map/tokens/all_to_all | solution.py:68
  39.1 3.1 %collective-permute-start.4 = (bf16[3,192,256]{2,1,0:T(8,128)(2,1)S(1)}, bf16[3,192,256]{2,1,0:T(8,128)(2,1)S(1)}, u32[]{:S(2)}, u32[]{:S(2)}) collective-permute-start(bf16[3,192,256]{2,1,0:T(8,128)(2,1)S(1)} %collective-permute-done), channel_id=1, source_target_pairs={{0,128},{128,256},{256,384},{384,0},{1,129},{129,257},{257,385},{3... | collective-permute-start | bytes 884744 | tf_op jit(solution)/shard_map/weights/ppermute | solution.py:26
  42.2 4.4 %collective-permute-start.3 = (bf16[3,192,256]{2,1,0:T(8,128)(2,1)S(1)}, bf16[3,192,256]{2,1,0:T(8,128)(2,1)S(1)}, u32[]{:S(2)}, u32[]{:S(2)}) collective-permute-start(bf16[3,192,256]{2,1,0:T(8,128)(2,1)S(1)} %collective-permute-done), channel_id=1, source_target_pairs={{0,256},{128,384},{256,0},{384,128},{1,257},{129,385},{257,1},{385... | collective-permute-start | bytes 884744 | tf_op jit(solution)/shard_map/weights/ppermute | solution.py:26
  46.6 3.1 %collective-permute-start.2 = (bf16[3,192,256]{2,1,0:T(8,128)(2,1)S(1)}, bf16[3,192,256]{2,1,0:T(8,128)(2,1)S(1)}, u32[]{:S(2)}, u32[]{:S(2)}) collective-permute-start(bf16[3,192,256]{2,1,0:T(8,128)(2,1)S(1)} %collective-permute-done), channel_id=1, source_target_pairs={{0,384},{128,0},{256,128},{384,256},{1,385},{129,1},{257,129},{385... | collective-permute-start | bytes 884744 | tf_op jit(solution)/shard_map/weights/ppermute | solution.py:26
  49.7 6.3 %collective-permute-done.3 = bf16[3,192,256]{2,1,0:T(8,128)(2,1)S(1)} collective-permute-done((bf16[3,192,256]{2,1,0:T(8,128)(2,1)S(1)}, bf16[3,192,256]{2,1,0:T(8,128)(2,1)S(1)}, u32[]{:S(2)}, u32[]{:S(2)}) %collective-permute-start.3) | collective-permute-done | bytes 294944 | tf_op jit(solution)/shard_map/weights/ppermute | solution.py:26
  56.0 1.5 collective-permute-done.2
  57.5 0.1 pad_maximum_fusion.w_mine
  57.7 4.8 %collective-permute-start.8 = (bf16[4,3,192,256]{3,2,1,0:T(8,128)(2,1)S(1)}, bf16[4,3,192,256]{3,2,1,0:T(8,128)(2,1)S(1)}, u32[]{:S(2)}, u32[]{:S(2)}) collective-permute-start(bf16[4,3,192,256]{3,2,1,0:T(8,128)(2,1)S(1)} %pad_maximum_fusion.w_mine), channel_id=1, source_target_pairs={{0,16},{16,0},{1,17},{17,1},{2,18},{18,2},{3,19},{19,3},{4,20},{20... | collective-permute-start | bytes 3538952 | tf_op jit(solution)/shard_map/weights/ppermute | solution.py:26
  62.5 9.7 %collective-permute-start.7 = (bf16[4,128,384]{2,1,0:T(8,128)(2,1)S(1)}, bf16[4,128,384]{2,1,0:T(8,128)(2,1)S(1)}, u32[]{:S(2)}, u32[]{:S(2)}) collective-permute-start(bf16[4,128,384]{2,1,0:T(8,128)(2,1)S(1)} %all-to-all-done.tokens.t0), channel_id=1, source_target_pairs={{0,4},{4,8},{8,12},{12,32},{32,36},{36,40},{40,44},{44,64},{64,68}... | collective-permute-start | bytes 1179656 | tf_op jit(solution)/shard_map/tokens/ppermute | solution.py:26
  72.2 1.9 %collective-permute-start.6 = (bf16[4,128,384]{2,1,0:T(8,128)(2,1)S(1)}, bf16[4,128,384]{2,1,0:T(8,128)(2,1)}, u32[]{:S(2)}, u32[]{:S(2)}) collective-permute-start(bf16[4,128,384]{2,1,0:T(8,128)(2,1)S(1)} %all-to-all-done.tokens.t0), channel_id=1, source_target_pairs={{0,8},{4,108},{8,32},{12,4},{32,40},{36,12},{40,64},{44,36},{64,72... | collective-permute-start | bytes 1179656 | tf_op jit(solution)/shard_map/tokens/ppermute | solution.py:26
  74.2 3.1 %collective-permute-start.5 = (bf16[4,128,384]{2,1,0:T(8,128)(2,1)S(1)}, bf16[4,128,384]{2,1,0:T(8,128)(2,1)}, u32[]{:S(2)}, u32[]{:S(2)}) collective-permute-start(bf16[4,128,384]{2,1,0:T(8,128)(2,1)S(1)} %all-to-all-done.tokens.t0), channel_id=1, source_target_pairs={{0,108},{4,0},{8,4},{12,8},{32,12},{36,32},{40,36},{44,40},{64,44}... | collective-permute-start | bytes 1179656 | tf_op jit(solution)/shard_map/tokens/ppermute | solution.py:26
  77.3 0.9 norm.1
  78.2 8.1 %all-to-all-start.1 = ((f32[16,11,128]{2,1,0:T(8,128)}), f32[16,11,128]{2,1,0:T(8,128)S(1)}, u32[]{:S(2)}, u32[]{:S(2)}) async-start(f32[16,11,128]{2,1,0:T(8,128)} %norm.1), calls=%async_computation.1 | async-start | bytes 262144 | tf_op jit(solution)/shard_map/norm/all_to_all | solution.py:226
  86.2 0.1 stack.42.where
  86.3 12.1 %all-to-all-done.1.shared = f32[16,11,128]{2,1,0:T(8,128)S(1)} async-done(((f32[16,11,128]{2,1,0:T(8,128)}), f32[16,11,128]{2,1,0:T(8,128)S(1)}, u32[]{:S(2)}, u32[]{:S(2)}) %all-to-all-start.1) | async-done | bytes 90144 | tf_op jit(solution)/shard_map/norm/all_to_all | solution.py:226
  98.4 3.4 %project.2 = f32[2,4,128,384]{3,2,1,0:T(8,128)S(1)} custom-call(s32[6]{0:T(128)S(1)} %stack.42.where, bf16[4,128,384]{2,1,0:T(8,128)(2,1)S(1)} %all-to-all-done.tokens.t0, bf16[4,128,384]{2,1,0:T(8,128)(2,1)} %collective-permute-done.5.t1, bf16[4,128,384]{2,1,0:T(8,128)(2,1)} %collective-permute-done.6.t2, ...), custom_call_target="tpu_custom_call" | custom-call | tf_op jit(solution)/shard_map/project/pallas_call | solution.py:178
  101.8 24.7 %all_to_all.20 = f32[8,128,384]{2,1,0:T(8,128)S(1)} all-to-all(f32[8,128,384]{2,1,0:T(8,128)S(1)} %bitcast.17), channel_id=1, replica_groups=mesh['x'=4,'zh'=4,'core'=2,'zl'=4,'yh'=2,'yl'=2] {'core','yh','yl'}, dimensions={0} | all-to-all | bytes 3145728 | tf_op jit(solution)/shard_map/project/all_to_all | solution.py:240
  126.5 0.8 project.3
  127.3 18.4 %all_to_all.21.kv_mine = bf16[8,2,256,128]{3,2,1,0:T(8,128)(2,1)S(1)} all-to-all(bf16[8,2,256,128]{3,2,1,0:T(8,128)(2,1)S(1)} %get-tuple-element.22), channel_id=1, replica_groups=mesh['x'=4,'zh'=4,'core'=2,'zl'=4,'yh'=2,'yl'=2] {'x','yl'}, dimensions={0} | all-to-all | bytes 2097152 | tf_op jit(solution)/shard_map/keys/all_to_all | solution.py:252
  145.7 3.9 %collective-permute-start.9 = (bf16[8,2,256,128]{3,2,1,0:T(8,128)(2,1)S(1)}, bf16[8,2,256,128]{3,2,1,0:T(8,128)(2,1)S(1)}, u32[]{:S(2)}, u32[]{:S(2)}) collective-permute-start(bf16[8,2,256,128]{3,2,1,0:T(8,128)(2,1)S(1)} %all_to_all.21.kv_mine), channel_id=1, source_target_pairs={{0,16},{16,0},{1,17},{17,1},{2,18},{18,2},{3,19},{19,3},{4,20},{20... | collective-permute-start | bytes 3145736 | tf_op jit(solution)/shard_map/keys/ppermute | solution.py:26
  149.6 2.3 %collective-permute-done.9.kv_theirs = bf16[8,2,256,128]{3,2,1,0:T(8,128)(2,1)S(1)} collective-permute-done((bf16[8,2,256,128]{3,2,1,0:T(8,128)(2,1)S(1)}, bf16[8,2,256,128]{3,2,1,0:T(8,128)(2,1)S(1)}, u32[]{:S(2)}, u32[]{:S(2)}) %collective-permute-start.9) | collective-permute-done | bytes 1048608 | tf_op jit(solution)/shard_map/keys/ppermute | solution.py:26
  151.9 2.2 %attend.1 = bf16[256,128]{1,0:T(8,128)(2,1)S(1)} custom-call(bf16[256,128]{1,0:T(8,128)(2,1)S(1)} %get-tuple-element.21.q, bf16[8,2,256,128]{3,2,1,0:T(8,128)(2,1)S(1)} %all_to_all.21.kv_mine, bf16[8,2,256,128]{3,2,1,0:T(8,128)(2,1)S(1)} %collective-permute-done.9.kv_theirs), custom_call_target="tpu_custom_call" | custom-call | tf_op jit(solution)/shard_map/attend/pallas_call | solution.py:178
  154.1 3.5 %collective-permute-start.10 = (bf16[256,128]{1,0:T(8,128)(2,1)S(1)}, bf16[256,128]{1,0:T(8,128)(2,1)S(1)}, u32[]{:S(2)}, u32[]{:S(2)}) collective-permute-start(bf16[256,128]{1,0:T(8,128)(2,1)S(1)} %attend.1), channel_id=1, source_target_pairs={{0,8},{1,40},{2,72},{3,104},{4,46},{5,78},{6,110},{7,14},{8,96},{9... | collective-permute-start | bytes 196616 | tf_op jit(solution)/shard_map/home/ppermute | solution.py:26
  157.6 8.3 %collective-permute-done.10 = bf16[256,128]{1,0:T(8,128)(2,1)S(1)} collective-permute-done((bf16[256,128]{1,0:T(8,128)(2,1)S(1)}, bf16[256,128]{1,0:T(8,128)(2,1)S(1)}, u32[]{:S(2)}, u32[]{:S(2)}) %collective-permute-start.10) | collective-permute-done | bytes 65568 | tf_op jit(solution)/shard_map/home/ppermute | solution.py:26
  165.9 5.8 %collective-permute-start.11 = (bf16[128,128]{1,0:T(8,128)(2,1)S(1)}, bf16[128,128]{1,0:T(8,128)(2,1)S(1)}, u32[]{:S(2)}, u32[]{:S(2)}) collective-permute-start(bf16[128,128]{1,0:T(8,128)(2,1)S(1)} %get-tuple-element.24), channel_id=1, source_target_pairs={{0,16},{16,0},{1,17},{17,1},{2,18},{18,2},{3,19},{19,3},{4,20},{20... | collective-permute-start | bytes 98312 | tf_op jit(solution)/shard_map/home/ppermute | solution.py:26
  171.8 0.8 collective-permute-done.11
  172.6 0.6 maximum_select_fusion
  (10 shorter events, 0.0 us)
Async XLA Ops:
  0.0 21.1 %collective-permute-start = (bf16[3,192,256]{2,1,0:T(8,128)(2,1)}, bf16[3,192,256]{2,1,0:T(8,128)(2,1)S(1)}, u32[]{:S(2)}, u32[]{:S(2)}) collective-permute-start(bf16[3,192,256]{2,1,0:T(8,128)(2,1)} %bitcast.25), channel_id=1, source_target_pairs={{0,8},{1,40},{2,72},{3,104},{4,44},{5,76},{6,108},{7,12},{8,0},{9,... | collective-permute-start | bytes 884744 | tf_op jit(solution)/shard_map/weights/ppermute | solution.py:26
  12.2 8.8 %collective-permute-start.1 = (f32[4,128]{1,0:T(4,128)S(1)}, f32[4,128]{1,0:T(4,128)S(1)}, u32[]{:S(2)}, u32[]{:S(2)}) collective-permute-start(f32[4,128]{1,0:T(4,128)S(1)} %pad_maximum_fusion.1), channel_id=1, source_target_pairs={{0,8},{1,40},{2,72},{3,104},{4,44},{5,76},{6,108},{7,12},{8,0},{9,... | collective-permute-start | bytes 6152 | tf_op jit(solution)/shard_map/weights/ppermute | solution.py:26
  22.8 34.8 %all-to-all-start = ((bf16[4,128,384]{2,1,0:T(8,128)(2,1)}), bf16[4,128,384]{2,1,0:T(8,128)(2,1)S(1)}, u32[]{:S(2)}, u32[]{:S(2)}) async-start(bf16[4,128,384]{2,1,0:T(8,128)(2,1)} %broadcast_in_dim.2), calls=%async_computation | async-start | bytes 786432 | tf_op jit(solution)/shard_map/tokens/all_to_all | solution.py:68
  39.1 10.6 %collective-permute-start.4 = (bf16[3,192,256]{2,1,0:T(8,128)(2,1)S(1)}, bf16[3,192,256]{2,1,0:T(8,128)(2,1)S(1)}, u32[]{:S(2)}, u32[]{:S(2)}) collective-permute-start(bf16[3,192,256]{2,1,0:T(8,128)(2,1)S(1)} %collective-permute-done), channel_id=1, source_target_pairs={{0,128},{128,256},{256,384},{384,0},{1,129},{129,257},{257,385},{3... | collective-permute-start | bytes 884744 | tf_op jit(solution)/shard_map/weights/ppermute | solution.py:26
  42.2 13.8 %collective-permute-start.3 = (bf16[3,192,256]{2,1,0:T(8,128)(2,1)S(1)}, bf16[3,192,256]{2,1,0:T(8,128)(2,1)S(1)}, u32[]{:S(2)}, u32[]{:S(2)}) collective-permute-start(bf16[3,192,256]{2,1,0:T(8,128)(2,1)S(1)} %collective-permute-done), channel_id=1, source_target_pairs={{0,256},{128,384},{256,0},{384,128},{1,257},{129,385},{257,1},{385... | collective-permute-start | bytes 884744 | tf_op jit(solution)/shard_map/weights/ppermute | solution.py:26
  46.6 10.9 %collective-permute-start.2 = (bf16[3,192,256]{2,1,0:T(8,128)(2,1)S(1)}, bf16[3,192,256]{2,1,0:T(8,128)(2,1)S(1)}, u32[]{:S(2)}, u32[]{:S(2)}) collective-permute-start(bf16[3,192,256]{2,1,0:T(8,128)(2,1)S(1)} %collective-permute-done), channel_id=1, source_target_pairs={{0,384},{128,0},{256,128},{384,256},{1,385},{129,1},{257,129},{385... | collective-permute-start | bytes 884744 | tf_op jit(solution)/shard_map/weights/ppermute | solution.py:26
  57.5 19.7 %copy-start = (bf16[384]{0:T(512)(128)(2,1)S(1)}, bf16[384]{0:T(512)(128)(2,1)}, u32[]{:S(2)}) copy-start(bf16[384]{0:T(512)(128)(2,1)} %param.6) | copy-start | bytes 2308
  57.7 40.7 %collective-permute-start.8 = (bf16[4,3,192,256]{3,2,1,0:T(8,128)(2,1)S(1)}, bf16[4,3,192,256]{3,2,1,0:T(8,128)(2,1)S(1)}, u32[]{:S(2)}, u32[]{:S(2)}) collective-permute-start(bf16[4,3,192,256]{3,2,1,0:T(8,128)(2,1)S(1)} %pad_maximum_fusion.w_mine), channel_id=1, source_target_pairs={{0,16},{16,0},{1,17},{17,1},{2,18},{18,2},{3,19},{19,3},{4,20},{20... | collective-permute-start | bytes 3538952 | tf_op jit(solution)/shard_map/weights/ppermute | solution.py:26
  62.5 35.9 %collective-permute-start.7 = (bf16[4,128,384]{2,1,0:T(8,128)(2,1)S(1)}, bf16[4,128,384]{2,1,0:T(8,128)(2,1)S(1)}, u32[]{:S(2)}, u32[]{:S(2)}) collective-permute-start(bf16[4,128,384]{2,1,0:T(8,128)(2,1)S(1)} %all-to-all-done.tokens.t0), channel_id=1, source_target_pairs={{0,4},{4,8},{8,12},{12,32},{32,36},{36,40},{40,44},{44,64},{64,68}... | collective-permute-start | bytes 1179656 | tf_op jit(solution)/shard_map/tokens/ppermute | solution.py:26
  72.2 26.2 %collective-permute-start.6 = (bf16[4,128,384]{2,1,0:T(8,128)(2,1)S(1)}, bf16[4,128,384]{2,1,0:T(8,128)(2,1)}, u32[]{:S(2)}, u32[]{:S(2)}) collective-permute-start(bf16[4,128,384]{2,1,0:T(8,128)(2,1)S(1)} %all-to-all-done.tokens.t0), channel_id=1, source_target_pairs={{0,8},{4,108},{8,32},{12,4},{32,40},{36,12},{40,64},{44,36},{64,72... | collective-permute-start | bytes 1179656 | tf_op jit(solution)/shard_map/tokens/ppermute | solution.py:26
  74.2 24.2 %collective-permute-start.5 = (bf16[4,128,384]{2,1,0:T(8,128)(2,1)S(1)}, bf16[4,128,384]{2,1,0:T(8,128)(2,1)}, u32[]{:S(2)}, u32[]{:S(2)}) collective-permute-start(bf16[4,128,384]{2,1,0:T(8,128)(2,1)S(1)} %all-to-all-done.tokens.t0), channel_id=1, source_target_pairs={{0,108},{4,0},{8,4},{12,8},{32,12},{36,32},{40,36},{44,40},{64,44}... | collective-permute-start | bytes 1179656 | tf_op jit(solution)/shard_map/tokens/ppermute | solution.py:26
  78.2 20.2 %all-to-all-start.1 = ((f32[16,11,128]{2,1,0:T(8,128)}), f32[16,11,128]{2,1,0:T(8,128)S(1)}, u32[]{:S(2)}, u32[]{:S(2)}) async-start(f32[16,11,128]{2,1,0:T(8,128)} %norm.1), calls=%async_computation.1 | async-start | bytes 262144 | tf_op jit(solution)/shard_map/norm/all_to_all | solution.py:226
  145.7 6.2 %collective-permute-start.9 = (bf16[8,2,256,128]{3,2,1,0:T(8,128)(2,1)S(1)}, bf16[8,2,256,128]{3,2,1,0:T(8,128)(2,1)S(1)}, u32[]{:S(2)}, u32[]{:S(2)}) collective-permute-start(bf16[8,2,256,128]{3,2,1,0:T(8,128)(2,1)S(1)} %all_to_all.21.kv_mine), channel_id=1, source_target_pairs={{0,16},{16,0},{1,17},{17,1},{2,18},{18,2},{3,19},{19,3},{4,20},{20... | collective-permute-start | bytes 3145736 | tf_op jit(solution)/shard_map/keys/ppermute | solution.py:26
  154.1 11.8 %collective-permute-start.10 = (bf16[256,128]{1,0:T(8,128)(2,1)S(1)}, bf16[256,128]{1,0:T(8,128)(2,1)S(1)}, u32[]{:S(2)}, u32[]{:S(2)}) collective-permute-start(bf16[256,128]{1,0:T(8,128)(2,1)S(1)} %attend.1), channel_id=1, source_target_pairs={{0,8},{1,40},{2,72},{3,104},{4,46},{5,78},{6,110},{7,14},{8,96},{9... | collective-permute-start | bytes 196616 | tf_op jit(solution)/shard_map/home/ppermute | solution.py:26
  165.9 6.7 %collective-permute-start.11 = (bf16[128,128]{1,0:T(8,128)(2,1)S(1)}, bf16[128,128]{1,0:T(8,128)(2,1)S(1)}, u32[]{:S(2)}, u32[]{:S(2)}) collective-permute-start(bf16[128,128]{1,0:T(8,128)(2,1)S(1)} %get-tuple-element.24), channel_id=1, source_target_pairs={{0,16},{16,0},{1,17},{17,1},{2,18},{18,2},{3,19},{19,3},{4,20},{20... | collective-permute-start | bytes 98312 | tf_op jit(solution)/shard_map/home/ppermute | solution.py:26

commit v17 on v15

--- a/solution.py
+++ b/solution.py
@@ -81,8 +81,8 @@
         out[target, 8:11] = ln_gain[...].astype(jnp.float32)
 
 
-def partial_kernel(where, t0, t1, t2, t3, shared, w_mine, w_theirs, out, w, acc):
-    zl, core, turn, x_here, y_here = (where[i] for i in range(5))
+def layout_kernel(where, w_mine, w_theirs, w):
+    core, x_here = where[1], where[3]
     half = w_mine.shape[2]
     for step in range(NX):
         x = lax.rem(x_here + step, NX)
@@ -90,6 +90,10 @@
             cols = slice(s * 256, s * 256 + 256)
             w[x, pl.ds(pl.multiple_of(core * half, half), half), cols] = w_mine[step, s]
             w[x, pl.ds(pl.multiple_of((1 - core) * half, half), half), cols] = w_theirs[step, s]
+
+
+def partial_kernel(where, t0, t1, t2, t3, shared, w, out, acc):
+    zl, turn, y_here = where[0], where[2], where[4]
     tokens = (t0, t1, t2, t3)
 
     sums = shared[0, 0:8]
@@ -149,27 +153,39 @@
             kv_out[target, 1, rows] = value
 
 
-def attend_kernel(q, kv_mine, kv_theirs, out):
-    scores = [
-        lax.dot_general(
-            q[...],
-            kv[:, 0].reshape(-1, DH),
-            (((1,), (1,)), ((), ())),
-            preferred_element_type=jnp.float32,
-        )
-        * (DH ** -0.5)
-        for kv in (kv_mine, kv_theirs)
-    ]
-    top = jnp.maximum(*[jnp.max(part, axis=1, keepdims=True) for part in scores])
-    weights = [jnp.exp(part - top) for part in scores]
-    total = sum(jnp.sum(part, axis=1, keepdims=True) for part in weights)
-    mixed = sum(
-        jnp.dot(
-            part.astype(jnp.bfloat16), kv[:, 1].reshape(-1, DH), preferred_element_type=jnp.float32
-        )
-        for part, kv in zip(weights, (kv_mine, kv_theirs))
+def head_scores(q, kv):
+    keys = kv[:, 0].reshape(-1, DH)
+    return lax.dot_general(
+        q[...], keys, (((1,), (1,)), ((), ())), preferred_element_type=jnp.float32
+    ) * (DH ** -0.5)
+
+
+def attend_first_kernel(q, kv, mixed, extremes):
+    scores = head_scores(q, kv)
+    top = jnp.max(scores, axis=1, keepdims=True)
+    weights = jnp.exp(scores - top)
+    total = jnp.sum(weights, axis=1, keepdims=True)
+    lane = lax.broadcasted_iota(jnp.int32, extremes.shape, 1)
+    extremes[...] = jnp.where(lane == 0, top, total)
+    mixed[...] = jnp.dot(
+        weights.astype(jnp.bfloat16), kv[:, 1].reshape(-1, DH), preferred_element_type=jnp.float32
     )
-    out[...] = (mixed / total).astype(jnp.bfloat16)
+
+
+def attend_second_kernel(where, q, kv, mixed, extremes, out):
+    scores = head_scores(q, kv)
+    top_before = extremes[:, 0:1]
+    top = jnp.maximum(top_before, jnp.max(scores, axis=1, keepdims=True))
+    scale = jnp.exp(top_before - top)
+    weights = jnp.exp(scores - top)
+    total = extremes[:, 1:2] * scale + jnp.sum(weights, axis=1, keepdims=True)
+    both = mixed[...] * scale + jnp.dot(
+        weights.astype(jnp.bfloat16), kv[:, 1].reshape(-1, DH), preferred_element_type=jnp.float32
+    )
+    rows = (both / total).astype(jnp.bfloat16)
+    for half in range(2):
+        place = lax.rem(where[1] + half, 2)
+        out[pl.ds(pl.multiple_of(place * 128, 128), 128)] = rows[half * 128 : half * 128 + 128]
 
 
 def kernel_call(kernel, out_shape, args, scalars=0, scratch=()):
@@ -226,13 +242,18 @@
         shared = lax.all_to_all(shared, ("zl",) + Y, 0, 0)
 
     with jax.named_scope("project"):
+        w = kernel_call(
+            layout_kernel,
+            jax.ShapeDtypeStruct((NX, 384, 768), jnp.bfloat16),
+            (where, w_mine, w_theirs),
+            scalars=1,
+        )
         part = kernel_call(
             partial_kernel,
             jax.ShapeDtypeStruct((CORES, NY, 128, 3 * DH), jnp.bfloat16),
-            (where, t0, t1, t2, t3, shared, w_mine, w_theirs),
+            (where, t0, t1, t2, t3, shared, w),
             scalars=1,
             scratch=[
-                pltpu.VMEM((NX, 384, 768), jnp.bfloat16),
                 pltpu.VMEM((512, 768), jnp.float32),
             ],
         )
@@ -253,14 +274,25 @@
         kv_theirs = swap_cores(kv_mine)
 
     with jax.named_scope("attend"):
+        partial = kernel_call(
+            attend_first_kernel,
+            (
+                jax.ShapeDtypeStruct((256, DH), jnp.float32),
+                jax.ShapeDtypeStruct((256, DH), jnp.float32),
+            ),
+            (q, kv_mine),
+        )
         out = kernel_call(
-            attend_kernel, jax.ShapeDtypeStruct((256, DH), jnp.bfloat16), (q, kv_mine, kv_theirs)
+            attend_second_kernel,
+            jax.ShapeDtypeStruct((256, DH), jnp.bfloat16),
+            (where, q, kv_theirs, *partial),
+            scalars=1,
         )
 
     with jax.named_scope("home"):
         arrived = to_home(out)
-        same = lax.dynamic_slice_in_dim(arrived, core * 128, 128)
-        cross = swap_cores(lax.dynamic_slice_in_dim(arrived, (1 - core) * 128, 128))
+        same = arrived[:128]
+        cross = swap_cores(arrived[128:])
         zl_from = (zl + 2) % NZL
         zh_from = y_here + jnp.where(zl == 1, 1, jnp.where(zl == 3, 2, 0))
         y_from = zh + 4 * NY - zh_from - zl_from - (zl_from >= 2) - 2 * core

time: 166 us -> 163 us (0.982)
  the two profiles are of different devices: /device:TPU:33 before, /device:TPU:16 now
where the time goes in v17:
time: 163 us; the launch traced here: 162 us
  starting transfers between devices  79.6 us (49%)
  blocking collectives  33.8 us (21%)
  waiting for transfers between devices  33.1 us (20%)
  Pallas kernels  10.1 us (6%)
  local copies, waits for them, and re-layouts  4.08 us (3%)
    ppermute x12, starting transfers between devices, shift(): return lax.ppermute(values, axes, pairs)  60.2 us
    ppermute x12, waiting for transfers between devices, shift(): return lax.ppermute(values, axes, pairs)  29.8 us
    all_to_all x1, blocking collectives, body(): kv_mine = lax.all_to_all(kv, ('x', 'yl'), 0, 0)  18.6 us
    all_to_all x1, blocking collectives, body(): lax.all_to_all(part, ('core',) + Y, 0, 0).reshape(CORES, NY, 128, 3 * DH)  15.2 us
    all_to_all x1, starting transfers between devices, body(): shared = lax.all_to_all(shared, ('zl',) + Y, 0, 0)  11.3 us
    pallas_call x6, Pallas kernels, kernel_call(): pl.pallas_call(kernel, out_shape=out_shape, in_specs=[smem] * scalars + [...  10.1 us
    all_to_all x1, starting transfers between devices, spread(): lax.all_to_all(jnp.broadcast_to(values[None], (count,) + values.shape), a...  8.12 us
    all_to_all x1, waiting for transfers between devices, body(): shared = lax.all_to_all(shared, ('zl',) + Y, 0, 0)  3.3 us
  transfers between devices with their start and end apart: 14, of which 8 were waited for; matrix products, arithmetic and copies ran while one was open for 0% of the time, Pallas kernels for 2%

profile of v17, /device:TPU:16, one launch (start us, length us, event | category | flops | bytes accessed | tf_op | source)
XLA Modules:
  0.0 162.3 jit_solution(5527125750408006783)
XLA Ops:
  0.0 14.6 %collective-permute-start = (bf16[3,192,256]{2,1,0:T(8,128)(2,1)}, bf16[3,192,256]{2,1,0:T(8,128)(2,1)S(1)}, u32[]{:S(2)}, u32[]{:S(2)}) collective-permute-start(bf16[3,192,256]{2,1,0:T(8,128)(2,1)} %bitcast.25), channel_id=1, source_target_pairs={{0,8},{1,40},{2,72},{3,104},{4,44},{5,76},{6,108},{7,12},{8,0},{9,... | collective-permute-start | bytes 884744 | tf_op jit(solution)/shard_map/weights/ppermute | solution.py:26
  15.3 1.9 %collective-permute-start.1 = (f32[4,128]{1,0:T(4,128)S(1)}, f32[4,128]{1,0:T(4,128)S(1)}, u32[]{:S(2)}, u32[]{:S(2)}) collective-permute-start(f32[4,128]{1,0:T(4,128)S(1)} %pad_maximum_fusion.1), channel_id=1, source_target_pairs={{0,8},{1,40},{2,72},{3,104},{4,44},{5,76},{6,108},{7,12},{8,0},{9,... | collective-permute-start | bytes 6152 | tf_op jit(solution)/shard_map/weights/ppermute | solution.py:26
  17.2 14.2 %collective-permute-done.1.head_gain = f32[4,128]{1,0:T(4,128)S(1)} collective-permute-done((f32[4,128]{1,0:T(4,128)S(1)}, f32[4,128]{1,0:T(4,128)S(1)}, u32[]{:S(2)}, u32[]{:S(2)}) %collective-permute-start.1) | collective-permute-done | bytes 2080 | tf_op jit(solution)/shard_map/weights/ppermute | solution.py:26
  31.4 1.7 %broadcast_in_dim.2 = bf16[4,128,384]{2,1,0:T(8,128)(2,1)} broadcast(bf16[128,384]{1,0:T(8,128)(2,1)} %param.5), dimensions={1,2} | broadcast | bytes 491520 | tf_op jit(solution)/shard_map/tokens/broadcast_in_dim | solution.py:68
  33.1 8.1 %all-to-all-start = ((bf16[4,128,384]{2,1,0:T(8,128)(2,1)}), bf16[4,128,384]{2,1,0:T(8,128)(2,1)}, u32[]{:S(2)}, u32[]{:S(2)}) async-start(bf16[4,128,384]{2,1,0:T(8,128)(2,1)} %broadcast_in_dim.2), calls=%async_computation | async-start | bytes 786432 | tf_op jit(solution)/shard_map/tokens/all_to_all | solution.py:68
  41.2 4.7 %collective-permute-start.2 = (bf16[3,192,256]{2,1,0:T(8,128)(2,1)S(1)}, bf16[3,192,256]{2,1,0:T(8,128)(2,1)S(1)}, u32[]{:S(2)}, u32[]{:S(2)}) collective-permute-start(bf16[3,192,256]{2,1,0:T(8,128)(2,1)S(1)} %collective-permute-done), channel_id=1, source_target_pairs={{0,384},{128,0},{256,128},{384,256},{1,385},{129,1},{257,129},{385... | collective-permute-start | bytes 884744 | tf_op jit(solution)/shard_map/weights/ppermute | solution.py:26
  45.8 2.7 %collective-permute-start.3 = (bf16[3,192,256]{2,1,0:T(8,128)(2,1)S(1)}, bf16[3,192,256]{2,1,0:T(8,128)(2,1)S(1)}, u32[]{:S(2)}, u32[]{:S(2)}) collective-permute-start(bf16[3,192,256]{2,1,0:T(8,128)(2,1)S(1)} %collective-permute-done), channel_id=1, source_target_pairs={{0,256},{128,384},{256,0},{384,128},{1,257},{129,385},{257,1},{385... | collective-permute-start | bytes 884744 | tf_op jit(solution)/shard_map/weights/ppermute | solution.py:26
  48.6 2.8 %collective-permute-start.4 = (bf16[3,192,256]{2,1,0:T(8,128)(2,1)S(1)}, bf16[3,192,256]{2,1,0:T(8,128)(2,1)S(1)}, u32[]{:S(2)}, u32[]{:S(2)}) collective-permute-start(bf16[3,192,256]{2,1,0:T(8,128)(2,1)S(1)} %collective-permute-done), channel_id=1, source_target_pairs={{0,128},{128,256},{256,384},{384,0},{1,129},{129,257},{257,385},{3... | collective-permute-start | bytes 884744 | tf_op jit(solution)/shard_map/weights/ppermute | solution.py:26
  51.4 5.1 %collective-permute-done.2 = bf16[3,192,256]{2,1,0:T(8,128)(2,1)S(1)} collective-permute-done((bf16[3,192,256]{2,1,0:T(8,128)(2,1)S(1)}, bf16[3,192,256]{2,1,0:T(8,128)(2,1)S(1)}, u32[]{:S(2)}, u32[]{:S(2)}) %collective-permute-start.2) | collective-permute-done | bytes 294944 | tf_op jit(solution)/shard_map/weights/ppermute | solution.py:26
  56.5 2.5 %collective-permute-done.3 = bf16[3,192,256]{2,1,0:T(8,128)(2,1)S(1)} collective-permute-done((bf16[3,192,256]{2,1,0:T(8,128)(2,1)S(1)}, bf16[3,192,256]{2,1,0:T(8,128)(2,1)S(1)}, u32[]{:S(2)}, u32[]{:S(2)}) %collective-permute-start.3) | collective-permute-done | bytes 294944 | tf_op jit(solution)/shard_map/weights/ppermute | solution.py:26
  59.0 3.1 %collective-permute-done.4 = bf16[3,192,256]{2,1,0:T(8,128)(2,1)S(1)} collective-permute-done((bf16[3,192,256]{2,1,0:T(8,128)(2,1)S(1)}, bf16[3,192,256]{2,1,0:T(8,128)(2,1)S(1)}, u32[]{:S(2)}, u32[]{:S(2)}) %collective-permute-start.4) | collective-permute-done | bytes 294944 | tf_op jit(solution)/shard_map/weights/ppermute | solution.py:26
  62.3 1.9 %collective-permute-start.8 = (bf16[4,3,192,256]{3,2,1,0:T(8,128)(2,1)S(1)}, bf16[4,3,192,256]{3,2,1,0:T(8,128)(2,1)S(1)}, u32[]{:S(2)}, u32[]{:S(2)}) collective-permute-start(bf16[4,3,192,256]{3,2,1,0:T(8,128)(2,1)S(1)} %pad_maximum_fusion.w_mine), channel_id=1, source_target_pairs={{0,16},{16,0},{1,17},{17,1},{2,18},{18,2},{3,19},{19,3},{4,20},{20... | collective-permute-start | bytes 3538952 | tf_op jit(solution)/shard_map/weights/ppermute | solution.py:26
  64.2 7.6 %collective-permute-start.5 = (bf16[4,128,384]{2,1,0:T(8,128)(2,1)}, bf16[4,128,384]{2,1,0:T(8,128)(2,1)}, u32[]{:S(2)}, u32[]{:S(2)}) collective-permute-start(bf16[4,128,384]{2,1,0:T(8,128)(2,1)} %all-to-all-done.tokens.t0), channel_id=1, source_target_pairs={{0,108},{4,0},{8,4},{12,8},{32,12},{36,32},{40,36},{44,40},{64,44}... | collective-permute-start | bytes 1179656 | tf_op jit(solution)/shard_map/tokens/ppermute | solution.py:26
  71.8 3.5 %collective-permute-start.6 = (bf16[4,128,384]{2,1,0:T(8,128)(2,1)}, bf16[4,128,384]{2,1,0:T(8,128)(2,1)}, u32[]{:S(2)}, u32[]{:S(2)}) collective-permute-start(bf16[4,128,384]{2,1,0:T(8,128)(2,1)} %all-to-all-done.tokens.t0), channel_id=1, source_target_pairs={{0,8},{4,108},{8,32},{12,4},{32,40},{36,12},{40,64},{44,36},{64,72... | collective-permute-start | bytes 1179656 | tf_op jit(solution)/shard_map/tokens/ppermute | solution.py:26
  75.3 2.2 %collective-permute-start.7 = (bf16[4,128,384]{2,1,0:T(8,128)(2,1)}, bf16[4,128,384]{2,1,0:T(8,128)(2,1)}, u32[]{:S(2)}, u32[]{:S(2)}) collective-permute-start(bf16[4,128,384]{2,1,0:T(8,128)(2,1)} %all-to-all-done.tokens.t0), channel_id=1, source_target_pairs={{0,4},{4,8},{8,12},{12,32},{32,36},{36,40},{40,44},{44,64},{64,68}... | collective-permute-start | bytes 1179656 | tf_op jit(solution)/shard_map/tokens/ppermute | solution.py:26
  77.5 1.9 %norm.1 = f32[16,11,128]{2,1,0:T(8,128)} custom-call(bf16[4,128,384]{2,1,0:T(8,128)(2,1)} %all-to-all-done.tokens.t0, bf16[3,128]{1,0:T(4,128)(2,1)S(1)} %bitcast.18), custom_call_target="tpu_custom_call" | custom-call | tf_op jit(solution)/shard_map/norm/pallas_call | solution.py:194
  79.4 11.3 %all-to-all-start.1 = ((f32[16,11,128]{2,1,0:T(8,128)}), f32[16,11,128]{2,1,0:T(8,128)}, u32[]{:S(2)}, u32[]{:S(2)}) async-start(f32[16,11,128]{2,1,0:T(8,128)} %norm.1), calls=%async_computation.1 | async-start | bytes 262144 | tf_op jit(solution)/shard_map/norm/all_to_all | solution.py:242
  90.8 1.0 copy-done
  91.8 1.3 copy-done.1
  93.8 3.3 %all-to-all-done.1.shared = f32[16,11,128]{2,1,0:T(8,128)} async-done(((f32[16,11,128]{2,1,0:T(8,128)}), f32[16,11,128]{2,1,0:T(8,128)}, u32[]{:S(2)}, u32[]{:S(2)}) %all-to-all-start.1) | async-done | bytes 90144 | tf_op jit(solution)/shard_map/norm/all_to_all | solution.py:242
  97.1 3.6 %project.4 = bf16[2,4,128,384]{3,2,1,0:T(8,128)(2,1)S(1)} custom-call(s32[6]{0:T(128)S(1)} %stack.42.where, bf16[4,128,384]{2,1,0:T(8,128)(2,1)} %all-to-all-done.tokens.t0, bf16[4,128,384]{2,1,0:T(8,128)(2,1)} %collective-permute-done.5.t1, bf16[4,128,384]{2,1,0:T(8,128)(2,1)} %collective-permute-done.6.t2, bf16[4,128,384]{2,1,0:T(8,128)(2,1)} %collective-permute-done.7.t3, ...), custom_call_target="tpu_custom_call" | custom-call | tf_op jit(solution)/shard_map/project/pallas_call | solution.py:194
  100.8 15.2 %all_to_all.20 = bf16[8,128,384]{2,1,0:T(8,128)(2,1)S(1)} all-to-all(bf16[8,128,384]{2,1,0:T(8,128)(2,1)S(1)} %bitcast.16), channel_id=1, replica_groups=mesh['x'=4,'zh'=4,'core'=2,'zl'=4,'yh'=2,'yl'=2] {'core','yh','yl'}, dimensions={0} | all-to-all | bytes 1572864 | tf_op jit(solution)/shard_map/project/all_to_all | solution.py:261
  116.0 0.8 project.5
  116.8 18.6 %all_to_all.21.kv = bf16[8,2,256,128]{3,2,1,0:T(8,128)(2,1)S(1)} all-to-all(bf16[8,2,256,128]{3,2,1,0:T(8,128)(2,1)S(1)} %get-tuple-element.24), channel_id=1, replica_groups=mesh['x'=4,'zh'=4,'core'=2,'zl'=4,'yh'=2,'yl'=2] {'x','yl'}, dimensions={0} | all-to-all | bytes 2097152 | tf_op jit(solution)/shard_map/keys/all_to_all | solution.py:273
  135.3 1.9 %collective-permute-start.9 = (bf16[8,2,256,128]{3,2,1,0:T(8,128)(2,1)S(1)}, bf16[8,2,256,128]{3,2,1,0:T(8,128)(2,1)S(1)}, u32[]{:S(2)}, u32[]{:S(2)}) collective-permute-start(bf16[8,2,256,128]{3,2,1,0:T(8,128)(2,1)S(1)} %all_to_all.21.kv), channel_id=1, source_target_pairs={{0,16},{16,0},{1,17},{17,1},{2,18},{18,2},{3,19},{19,3},{4,20},{20... | collective-permute-start | bytes 3145736 | tf_op jit(solution)/shard_map/keys/ppermute | solution.py:26
  137.3 1.1 attend.2
  138.4 1.5 collective-permute-done.9.kv
  139.9 1.8 %attend.3 = bf16[256,128]{1,0:T(8,128)(2,1)S(1)} custom-call(s32[6]{0:T(128)S(1)} %stack.42.where, bf16[256,128]{1,0:T(8,128)(2,1)S(1)} %get-tuple-element.23.q, bf16[8,2,256,128]{3,2,1,0:T(8,128)(2,1)S(1)} %collective-permute-done.9.kv, f32[256,128]{1,0:T(8,128)S(1)} %get-tuple-element.25.mixed, f32[256,128]{1,0:T(8,128)S(1)} %get-tuple-element.26.extremes), custom_call_target="tpu_custom_call" | custom-call | tf_op jit(solution)/shard_map/attend/pallas_call | solution.py:194
  141.7 14.5 %collective-permute-start.10 = (bf16[256,128]{1,0:T(8,128)(2,1)S(1)}, bf16[256,128]{1,0:T(8,128)(2,1)S(1)}, u32[]{:S(2)}, u32[]{:S(2)}) collective-permute-start(bf16[256,128]{1,0:T(8,128)(2,1)S(1)} %attend.3), channel_id=1, source_target_pairs={{0,8},{1,40},{2,72},{3,104},{4,46},{5,78},{6,110},{7,14},{8,96},{9... | collective-permute-start | bytes 196616 | tf_op jit(solution)/shard_map/home/ppermute | solution.py:26
  156.3 2.3 %collective-permute-done.10 = bf16[256,128]{1,0:T(8,128)(2,1)S(1)} collective-permute-done((bf16[256,128]{1,0:T(8,128)(2,1)S(1)}, bf16[256,128]{1,0:T(8,128)(2,1)S(1)}, u32[]{:S(2)}, u32[]{:S(2)}) %collective-permute-start.10) | collective-permute-done | bytes 65568 | tf_op jit(solution)/shard_map/home/ppermute | solution.py:26
  158.6 1.9 %collective-permute-start.11 = (bf16[128,128]{1,0:T(8,128)(2,1)S(1)}, bf16[128,128]{1,0:T(8,128)(2,1)S(1)}, u32[]{:S(2)}, u32[]{:S(2)}) collective-permute-start(bf16[128,128]{1,0:T(8,128)(2,1)S(1)} %get-tuple-element.28), channel_id=1, source_target_pairs={{0,16},{16,0},{1,17},{17,1},{2,18},{18,2},{3,19},{19,3},{4,20},{20... | collective-permute-start | bytes 98312 | tf_op jit(solution)/shard_map/home/ppermute | solution.py:26
  160.5 1.1 collective-permute-done.11
  (16 shorter events, 2.3 us)
Async XLA Ops:
  0.0 31.4 %collective-permute-start = (bf16[3,192,256]{2,1,0:T(8,128)(2,1)}, bf16[3,192,256]{2,1,0:T(8,128)(2,1)S(1)}, u32[]{:S(2)}, u32[]{:S(2)}) collective-permute-start(bf16[3,192,256]{2,1,0:T(8,128)(2,1)} %bitcast.25), channel_id=1, source_target_pairs={{0,8},{1,40},{2,72},{3,104},{4,44},{5,76},{6,108},{7,12},{8,0},{9,... | collective-permute-start | bytes 884744 | tf_op jit(solution)/shard_map/weights/ppermute | solution.py:26
  15.3 16.1 %collective-permute-start.1 = (f32[4,128]{1,0:T(4,128)S(1)}, f32[4,128]{1,0:T(4,128)S(1)}, u32[]{:S(2)}, u32[]{:S(2)}) collective-permute-start(f32[4,128]{1,0:T(4,128)S(1)} %pad_maximum_fusion.1), channel_id=1, source_target_pairs={{0,8},{1,40},{2,72},{3,104},{4,44},{5,76},{6,108},{7,12},{8,0},{9,... | collective-permute-start | bytes 6152 | tf_op jit(solution)/shard_map/weights/ppermute | solution.py:26
  33.1 29.0 %all-to-all-start = ((bf16[4,128,384]{2,1,0:T(8,128)(2,1)}), bf16[4,128,384]{2,1,0:T(8,128)(2,1)}, u32[]{:S(2)}, u32[]{:S(2)}) async-start(bf16[4,128,384]{2,1,0:T(8,128)(2,1)} %broadcast_in_dim.2), calls=%async_computation | async-start | bytes 786432 | tf_op jit(solution)/shard_map/tokens/all_to_all | solution.py:68
  41.2 15.3 %collective-permute-start.2 = (bf16[3,192,256]{2,1,0:T(8,128)(2,1)S(1)}, bf16[3,192,256]{2,1,0:T(8,128)(2,1)S(1)}, u32[]{:S(2)}, u32[]{:S(2)}) collective-permute-start(bf16[3,192,256]{2,1,0:T(8,128)(2,1)S(1)} %collective-permute-done), channel_id=1, source_target_pairs={{0,384},{128,0},{256,128},{384,256},{1,385},{129,1},{257,129},{385... | collective-permute-start | bytes 884744 | tf_op jit(solution)/shard_map/weights/ppermute | solution.py:26
  45.8 13.1 %collective-permute-start.3 = (bf16[3,192,256]{2,1,0:T(8,128)(2,1)S(1)}, bf16[3,192,256]{2,1,0:T(8,128)(2,1)S(1)}, u32[]{:S(2)}, u32[]{:S(2)}) collective-permute-start(bf16[3,192,256]{2,1,0:T(8,128)(2,1)S(1)} %collective-permute-done), channel_id=1, source_target_pairs={{0,256},{128,384},{256,0},{384,128},{1,257},{129,385},{257,1},{385... | collective-permute-start | bytes 884744 | tf_op jit(solution)/shard_map/weights/ppermute | solution.py:26
  48.6 13.5 %collective-permute-start.4 = (bf16[3,192,256]{2,1,0:T(8,128)(2,1)S(1)}, bf16[3,192,256]{2,1,0:T(8,128)(2,1)S(1)}, u32[]{:S(2)}, u32[]{:S(2)}) collective-permute-start(bf16[3,192,256]{2,1,0:T(8,128)(2,1)S(1)} %collective-permute-done), channel_id=1, source_target_pairs={{0,128},{128,256},{256,384},{384,0},{1,129},{129,257},{257,385},{3... | collective-permute-start | bytes 884744 | tf_op jit(solution)/shard_map/weights/ppermute | solution.py:26
  62.1 15.4 %copy-start.2 = (bf16[384]{0:T(512)(128)(2,1)S(1)}, bf16[384]{0:T(512)(128)(2,1)}, u32[]{:S(2)}) copy-start(bf16[384]{0:T(512)(128)(2,1)} %param.6) | copy-start | bytes 2308
  62.3 28.5 %collective-permute-start.8 = (bf16[4,3,192,256]{3,2,1,0:T(8,128)(2,1)S(1)}, bf16[4,3,192,256]{3,2,1,0:T(8,128)(2,1)S(1)}, u32[]{:S(2)}, u32[]{:S(2)}) collective-permute-start(bf16[4,3,192,256]{3,2,1,0:T(8,128)(2,1)S(1)} %pad_maximum_fusion.w_mine), channel_id=1, source_target_pairs={{0,16},{16,0},{1,17},{17,1},{2,18},{18,2},{3,19},{19,3},{4,20},{20... | collective-permute-start | bytes 3538952 | tf_op jit(solution)/shard_map/weights/ppermute | solution.py:26
  64.2 32.9 %collective-permute-start.5 = (bf16[4,128,384]{2,1,0:T(8,128)(2,1)}, bf16[4,128,384]{2,1,0:T(8,128)(2,1)}, u32[]{:S(2)}, u32[]{:S(2)}) collective-permute-start(bf16[4,128,384]{2,1,0:T(8,128)(2,1)} %all-to-all-done.tokens.t0), channel_id=1, source_target_pairs={{0,108},{4,0},{8,4},{12,8},{32,12},{36,32},{40,36},{44,40},{64,44}... | collective-permute-start | bytes 1179656 | tf_op jit(solution)/shard_map/tokens/ppermute | solution.py:26
  71.8 25.4 %collective-permute-start.6 = (bf16[4,128,384]{2,1,0:T(8,128)(2,1)}, bf16[4,128,384]{2,1,0:T(8,128)(2,1)}, u32[]{:S(2)}, u32[]{:S(2)}) collective-permute-start(bf16[4,128,384]{2,1,0:T(8,128)(2,1)} %all-to-all-done.tokens.t0), channel_id=1, source_target_pairs={{0,8},{4,108},{8,32},{12,4},{32,40},{36,12},{40,64},{44,36},{64,72... | collective-permute-start | bytes 1179656 | tf_op jit(solution)/shard_map/tokens/ppermute | solution.py:26
  75.3 21.8 %collective-permute-start.7 = (bf16[4,128,384]{2,1,0:T(8,128)(2,1)}, bf16[4,128,384]{2,1,0:T(8,128)(2,1)}, u32[]{:S(2)}, u32[]{:S(2)}) collective-permute-start(bf16[4,128,384]{2,1,0:T(8,128)(2,1)} %all-to-all-done.tokens.t0), channel_id=1, source_target_pairs={{0,4},{4,8},{8,12},{12,32},{32,36},{36,40},{40,44},{44,64},{64,68}... | collective-permute-start | bytes 1179656 | tf_op jit(solution)/shard_map/tokens/ppermute | solution.py:26
  79.4 17.7 %all-to-all-start.1 = ((f32[16,11,128]{2,1,0:T(8,128)}), f32[16,11,128]{2,1,0:T(8,128)}, u32[]{:S(2)}, u32[]{:S(2)}) async-start(f32[16,11,128]{2,1,0:T(8,128)} %norm.1), calls=%async_computation.1 | async-start | bytes 262144 | tf_op jit(solution)/shard_map/norm/all_to_all | solution.py:242
  90.8 1.0 copy-start
  91.8 1.3 copy-start.1
  135.3 4.5 %collective-permute-start.9 = (bf16[8,2,256,128]{3,2,1,0:T(8,128)(2,1)S(1)}, bf16[8,2,256,128]{3,2,1,0:T(8,128)(2,1)S(1)}, u32[]{:S(2)}, u32[]{:S(2)}) collective-permute-start(bf16[8,2,256,128]{3,2,1,0:T(8,128)(2,1)S(1)} %all_to_all.21.kv), channel_id=1, source_target_pairs={{0,16},{16,0},{1,17},{17,1},{2,18},{18,2},{3,19},{19,3},{4,20},{20... | collective-permute-start | bytes 3145736 | tf_op jit(solution)/shard_map/keys/ppermute | solution.py:26
  141.7 16.8 %collective-permute-start.10 = (bf16[256,128]{1,0:T(8,128)(2,1)S(1)}, bf16[256,128]{1,0:T(8,128)(2,1)S(1)}, u32[]{:S(2)}, u32[]{:S(2)}) collective-permute-start(bf16[256,128]{1,0:T(8,128)(2,1)S(1)} %attend.3), channel_id=1, source_target_pairs={{0,8},{1,40},{2,72},{3,104},{4,46},{5,78},{6,110},{7,14},{8,96},{9... | collective-permute-start | bytes 196616 | tf_op jit(solution)/shard_map/home/ppermute | solution.py:26
  158.6 3.1 %collective-permute-start.11 = (bf16[128,128]{1,0:T(8,128)(2,1)S(1)}, bf16[128,128]{1,0:T(8,128)(2,1)S(1)}, u32[]{:S(2)}, u32[]{:S(2)}) collective-permute-start(bf16[128,128]{1,0:T(8,128)(2,1)S(1)} %get-tuple-element.28), channel_id=1, source_target_pairs={{0,16},{16,0},{1,17},{17,1},{2,18},{18,2},{3,19},{19,3},{4,20},{20... | collective-permute-start | bytes 98312 | tf_op jit(solution)/shard_map/home/ppermute | solution.py:26

commit v18 on v17

--- a/solution.py
+++ b/solution.py
@@ -66,6 +66,11 @@
 
 def spread(values, axes, count):
     return lax.all_to_all(jnp.broadcast_to(values[None], (count,) + values.shape), axes, 0, 0)
+
+
+def copies_kernel(tokens, out):
+    for target in range(NZH):
+        out[target] = tokens[...]
 
 
 def share_kernel(tokens, ln_gain, out):
@@ -217,8 +222,13 @@
         head_gain = to_plane(jnp.concatenate([q_gain, k_gain]).reshape(4, DH))
 
     with jax.named_scope("tokens"):
-        tokens, w_moved, head_gain = lax.optimization_barrier((tokens, w_moved, head_gain))
-        t0 = spread(tokens, "zh", NZH)
+        copies = kernel_call(
+            copies_kernel,
+            jax.ShapeDtypeStruct((NZH,) + tokens.shape, jnp.bfloat16),
+            (tokens,),
+        )
+        copies, w_moved, head_gain = lax.optimization_barrier((copies, w_moved, head_gain))
+        t0 = lax.all_to_all(copies, "zh", 0, 0)
 
     with jax.named_scope("weights"):
         along_x = [

time: 163 us -> 162 us (level)
  waiting for transfers between devices: 33.1 us -> 31.4 us
    ppermute x12, waiting for transfers between devices: 29.8 us -> 28.1 us  [shift(): return lax.ppermute(values, axes, pairs)]
    broadcast_in_dim x1 -> x0, local copies, waits for them, and re-layouts: 1.68 us -> none  [spread(): jnp.broadcast_to(values[None], (count,) + values.shape)]
    pallas_call x6 -> x7, Pallas kernels: 10.1 us -> 10.8 us  [kernel_call(): pl.pallas_call(kernel, out_shape=out_shape, in_specs=[smem] * scalars + [...]
  transfers between devices with their start and end apart: 14 -> 14, of which waited for: 8 -> 8; matrix products, arithmetic and copies ran while one was open for 0% -> 0% of each run, Pallas kernels for 2% -> 3%
where the time goes in v18:
time: 162 us; the launch traced here: 161 us
  starting transfers between devices  79.6 us (49%)
  blocking collectives  33.7 us (21%)
  waiting for transfers between devices  31.4 us (19%)
  Pallas kernels  10.8 us (7%)
  local copies, waits for them, and re-layouts  3.29 us (2%)
    ppermute x12, starting transfers between devices, shift(): return lax.ppermute(values, axes, pairs)  60.2 us
    ppermute x12, waiting for transfers between devices, shift(): return lax.ppermute(values, axes, pairs)  28.1 us
    all_to_all x1, blocking collectives, body(): kv_mine = lax.all_to_all(kv, ('x', 'yl'), 0, 0)  18.6 us
    all_to_all x1, blocking collectives, body(): lax.all_to_all(part, ('core',) + Y, 0, 0).reshape(CORES, NY, 128, 3 * DH)  15.2 us
    all_to_all x1, starting transfers between devices, body(): shared = lax.all_to_all(shared, ('zl',) + Y, 0, 0)  11.3 us
    pallas_call x7, Pallas kernels, kernel_call(): pl.pallas_call(kernel, out_shape=out_shape, in_specs=[smem] * scalars + [...  10.8 us
    all_to_all x1, starting transfers between devices, body(): t0 = lax.all_to_all(copies, 'zh', 0, 0)  8.12 us
    all_to_all x1, waiting for transfers between devices, body(): shared = lax.all_to_all(shared, ('zl',) + Y, 0, 0)  3.3 us
  transfers between devices with their start and end apart: 14, of which 8 were waited for; matrix products, arithmetic and copies ran while one was open for 0% of the time, Pallas kernels for 3%

profile of v18, /device:TPU:16, one launch (start us, length us, event | category | flops | bytes accessed | tf_op | source)
XLA Modules:
  0.0 160.6 jit_solution(17585616439558113775)
XLA Ops:
  0.0 14.6 %collective-permute-start = (bf16[3,192,256]{2,1,0:T(8,128)(2,1)}, bf16[3,192,256]{2,1,0:T(8,128)(2,1)S(1)}, u32[]{:S(2)}, u32[]{:S(2)}) collective-permute-start(bf16[3,192,256]{2,1,0:T(8,128)(2,1)} %bitcast.25), channel_id=1, source_target_pairs={{0,8},{1,40},{2,72},{3,104},{4,44},{5,76},{6,108},{7,12},{8,0},{9,... | collective-permute-start | bytes 884744 | tf_op jit(solution)/shard_map/weights/ppermute | solution.py:26
  15.3 1.9 %collective-permute-start.1 = (f32[4,128]{1,0:T(4,128)S(1)}, f32[4,128]{1,0:T(4,128)S(1)}, u32[]{:S(2)}, u32[]{:S(2)}) collective-permute-start(f32[4,128]{1,0:T(4,128)S(1)} %pad_maximum_fusion.1), channel_id=1, source_target_pairs={{0,8},{1,40},{2,72},{3,104},{4,44},{5,76},{6,108},{7,12},{8,0},{9,... | collective-permute-start | bytes 6152 | tf_op jit(solution)/shard_map/weights/ppermute | solution.py:26
  17.2 0.9 copy-done.2
  18.9 12.5 %collective-permute-done.1.head_gain = f32[4,128]{1,0:T(4,128)S(1)} collective-permute-done((f32[4,128]{1,0:T(4,128)S(1)}, f32[4,128]{1,0:T(4,128)S(1)}, u32[]{:S(2)}, u32[]{:S(2)}) %collective-permute-start.1) | collective-permute-done | bytes 2080 | tf_op jit(solution)/shard_map/weights/ppermute | solution.py:26
  31.4 8.1 %all-to-all-start = ((bf16[4,128,384]{2,1,0:T(8,128)(2,1)}), bf16[4,128,384]{2,1,0:T(8,128)(2,1)}, u32[]{:S(2)}, u32[]{:S(2)}) async-start(bf16[4,128,384]{2,1,0:T(8,128)(2,1)} %tokens.2), calls=%async_computation | async-start | bytes 786432 | tf_op jit(solution)/shard_map/tokens/all_to_all | solution.py:231
  39.5 4.7 %collective-permute-start.2 = (bf16[3,192,256]{2,1,0:T(8,128)(2,1)S(1)}, bf16[3,192,256]{2,1,0:T(8,128)(2,1)S(1)}, u32[]{:S(2)}, u32[]{:S(2)}) collective-permute-start(bf16[3,192,256]{2,1,0:T(8,128)(2,1)S(1)} %collective-permute-done), channel_id=1, source_target_pairs={{0,384},{128,0},{256,128},{384,256},{1,385},{129,1},{257,129},{385... | collective-permute-start | bytes 884744 | tf_op jit(solution)/shard_map/weights/ppermute | solution.py:26
  44.2 2.7 %collective-permute-start.3 = (bf16[3,192,256]{2,1,0:T(8,128)(2,1)S(1)}, bf16[3,192,256]{2,1,0:T(8,128)(2,1)S(1)}, u32[]{:S(2)}, u32[]{:S(2)}) collective-permute-start(bf16[3,192,256]{2,1,0:T(8,128)(2,1)S(1)} %collective-permute-done), channel_id=1, source_target_pairs={{0,256},{128,384},{256,0},{384,128},{1,257},{129,385},{257,1},{385... | collective-permute-start | bytes 884744 | tf_op jit(solution)/shard_map/weights/ppermute | solution.py:26
  46.9 2.8 %collective-permute-start.4 = (bf16[3,192,256]{2,1,0:T(8,128)(2,1)S(1)}, bf16[3,192,256]{2,1,0:T(8,128)(2,1)S(1)}, u32[]{:S(2)}, u32[]{:S(2)}) collective-permute-start(bf16[3,192,256]{2,1,0:T(8,128)(2,1)S(1)} %collective-permute-done), channel_id=1, source_target_pairs={{0,128},{128,256},{256,384},{384,0},{1,129},{129,257},{257,385},{3... | collective-permute-start | bytes 884744 | tf_op jit(solution)/shard_map/weights/ppermute | solution.py:26
  49.7 5.1 %collective-permute-done.2 = bf16[3,192,256]{2,1,0:T(8,128)(2,1)S(1)} collective-permute-done((bf16[3,192,256]{2,1,0:T(8,128)(2,1)S(1)}, bf16[3,192,256]{2,1,0:T(8,128)(2,1)S(1)}, u32[]{:S(2)}, u32[]{:S(2)}) %collective-permute-start.2) | collective-permute-done | bytes 294944 | tf_op jit(solution)/shard_map/weights/ppermute | solution.py:26
  54.8 2.5 %collective-permute-done.3 = bf16[3,192,256]{2,1,0:T(8,128)(2,1)S(1)} collective-permute-done((bf16[3,192,256]{2,1,0:T(8,128)(2,1)S(1)}, bf16[3,192,256]{2,1,0:T(8,128)(2,1)S(1)}, u32[]{:S(2)}, u32[]{:S(2)}) %collective-permute-start.3) | collective-permute-done | bytes 294944 | tf_op jit(solution)/shard_map/weights/ppermute | solution.py:26
  57.3 3.1 %collective-permute-done.4 = bf16[3,192,256]{2,1,0:T(8,128)(2,1)S(1)} collective-permute-done((bf16[3,192,256]{2,1,0:T(8,128)(2,1)S(1)}, bf16[3,192,256]{2,1,0:T(8,128)(2,1)S(1)}, u32[]{:S(2)}, u32[]{:S(2)}) %collective-permute-start.4) | collective-permute-done | bytes 294944 | tf_op jit(solution)/shard_map/weights/ppermute | solution.py:26
  60.6 1.9 %collective-permute-start.8 = (bf16[4,3,192,256]{3,2,1,0:T(8,128)(2,1)S(1)}, bf16[4,3,192,256]{3,2,1,0:T(8,128)(2,1)S(1)}, u32[]{:S(2)}, u32[]{:S(2)}) collective-permute-start(bf16[4,3,192,256]{3,2,1,0:T(8,128)(2,1)S(1)} %pad_maximum_fusion.w_mine), channel_id=1, source_target_pairs={{0,16},{16,0},{1,17},{17,1},{2,18},{18,2},{3,19},{19,3},{4,20},{20... | collective-permute-start | bytes 3538952 | tf_op jit(solution)/shard_map/weights/ppermute | solution.py:26
  62.5 7.6 %collective-permute-start.5 = (bf16[4,128,384]{2,1,0:T(8,128)(2,1)}, bf16[4,128,384]{2,1,0:T(8,128)(2,1)}, u32[]{:S(2)}, u32[]{:S(2)}) collective-permute-start(bf16[4,128,384]{2,1,0:T(8,128)(2,1)} %all-to-all-done.tokens.t0), channel_id=1, source_target_pairs={{0,108},{4,0},{8,4},{12,8},{32,12},{36,32},{40,36},{44,40},{64,44}... | collective-permute-start | bytes 1179656 | tf_op jit(solution)/shard_map/tokens/ppermute | solution.py:26
  70.1 3.5 %collective-permute-start.6 = (bf16[4,128,384]{2,1,0:T(8,128)(2,1)}, bf16[4,128,384]{2,1,0:T(8,128)(2,1)}, u32[]{:S(2)}, u32[]{:S(2)}) collective-permute-start(bf16[4,128,384]{2,1,0:T(8,128)(2,1)} %all-to-all-done.tokens.t0), channel_id=1, source_target_pairs={{0,8},{4,108},{8,32},{12,4},{32,40},{36,12},{40,64},{44,36},{64,72... | collective-permute-start | bytes 1179656 | tf_op jit(solution)/shard_map/tokens/ppermute | solution.py:26
  73.6 2.2 %collective-permute-start.7 = (bf16[4,128,384]{2,1,0:T(8,128)(2,1)}, bf16[4,128,384]{2,1,0:T(8,128)(2,1)}, u32[]{:S(2)}, u32[]{:S(2)}) collective-permute-start(bf16[4,128,384]{2,1,0:T(8,128)(2,1)} %all-to-all-done.tokens.t0), channel_id=1, source_target_pairs={{0,4},{4,8},{8,12},{12,32},{32,36},{36,40},{40,44},{44,64},{64,68}... | collective-permute-start | bytes 1179656 | tf_op jit(solution)/shard_map/tokens/ppermute | solution.py:26
  75.8 1.9 %norm.1 = f32[16,11,128]{2,1,0:T(8,128)} custom-call(bf16[4,128,384]{2,1,0:T(8,128)(2,1)} %all-to-all-done.tokens.t0, bf16[3,128]{1,0:T(4,128)(2,1)S(1)} %bitcast.18), custom_call_target="tpu_custom_call" | custom-call | tf_op jit(solution)/shard_map/norm/pallas_call | solution.py:199
  77.7 11.3 %all-to-all-start.1 = ((f32[16,11,128]{2,1,0:T(8,128)}), f32[16,11,128]{2,1,0:T(8,128)}, u32[]{:S(2)}, u32[]{:S(2)}) async-start(f32[16,11,128]{2,1,0:T(8,128)} %norm.1), calls=%async_computation.1 | async-start | bytes 262144 | tf_op jit(solution)/shard_map/norm/all_to_all | solution.py:252
  89.1 1.0 copy-done
  90.1 1.3 copy-done.1
  92.1 3.3 %all-to-all-done.1.shared = f32[16,11,128]{2,1,0:T(8,128)} async-done(((f32[16,11,128]{2,1,0:T(8,128)}), f32[16,11,128]{2,1,0:T(8,128)}, u32[]{:S(2)}, u32[]{:S(2)}) %all-to-all-start.1) | async-done | bytes 90144 | tf_op jit(solution)/shard_map/norm/all_to_all | solution.py:252
  95.4 3.7 %project.4 = bf16[2,4,128,384]{3,2,1,0:T(8,128)(2,1)S(1)} custom-call(s32[6]{0:T(128)S(1)} %stack.42.where, bf16[4,128,384]{2,1,0:T(8,128)(2,1)} %all-to-all-done.tokens.t0, bf16[4,128,384]{2,1,0:T(8,128)(2,1)} %collective-permute-done.5.t1, bf16[4,128,384]{2,1,0:T(8,128)(2,1)} %collective-permute-done.6.t2, bf16[4,128,384]{2,1,0:T(8,128)(2,1)} %collective-permute-done.7.t3, ...), custom_call_target="tpu_custom_call" | custom-call | tf_op jit(solution)/shard_map/project/pallas_call | solution.py:199
  99.1 15.2 %all_to_all.20 = bf16[8,128,384]{2,1,0:T(8,128)(2,1)S(1)} all-to-all(bf16[8,128,384]{2,1,0:T(8,128)(2,1)S(1)} %bitcast.16), channel_id=1, replica_groups=mesh['x'=4,'zh'=4,'core'=2,'zl'=4,'yh'=2,'yl'=2] {'core','yh','yl'}, dimensions={0} | all-to-all | bytes 1572864 | tf_op jit(solution)/shard_map/project/all_to_all | solution.py:271
  114.3 0.8 project.5
  115.1 18.6 %all_to_all.21.kv = bf16[8,2,256,128]{3,2,1,0:T(8,128)(2,1)S(1)} all-to-all(bf16[8,2,256,128]{3,2,1,0:T(8,128)(2,1)S(1)} %get-tuple-element.24), channel_id=1, replica_groups=mesh['x'=4,'zh'=4,'core'=2,'zl'=4,'yh'=2,'yl'=2] {'x','yl'}, dimensions={0} | all-to-all | bytes 2097152 | tf_op jit(solution)/shard_map/keys/all_to_all | solution.py:283
  133.7 1.9 %collective-permute-start.9 = (bf16[8,2,256,128]{3,2,1,0:T(8,128)(2,1)S(1)}, bf16[8,2,256,128]{3,2,1,0:T(8,128)(2,1)S(1)}, u32[]{:S(2)}, u32[]{:S(2)}) collective-permute-start(bf16[8,2,256,128]{3,2,1,0:T(8,128)(2,1)S(1)} %all_to_all.21.kv), channel_id=1, source_target_pairs={{0,16},{16,0},{1,17},{17,1},{2,18},{18,2},{3,19},{19,3},{4,20},{20... | collective-permute-start | bytes 3145736 | tf_op jit(solution)/shard_map/keys/ppermute | solution.py:26
  135.6 1.1 attend.2
  136.7 1.5 collective-permute-done.9.kv
  138.2 1.8 %attend.3 = bf16[256,128]{1,0:T(8,128)(2,1)S(1)} custom-call(s32[6]{0:T(128)S(1)} %stack.42.where, bf16[256,128]{1,0:T(8,128)(2,1)S(1)} %get-tuple-element.23.q, bf16[8,2,256,128]{3,2,1,0:T(8,128)(2,1)S(1)} %collective-permute-done.9.kv, f32[256,128]{1,0:T(8,128)S(1)} %get-tuple-element.25.mixed, f32[256,128]{1,0:T(8,128)S(1)} %get-tuple-element.26.extremes), custom_call_target="tpu_custom_call" | custom-call | tf_op jit(solution)/shard_map/attend/pallas_call | solution.py:199
  140.0 14.5 %collective-permute-start.10 = (bf16[256,128]{1,0:T(8,128)(2,1)S(1)}, bf16[256,128]{1,0:T(8,128)(2,1)S(1)}, u32[]{:S(2)}, u32[]{:S(2)}) collective-permute-start(bf16[256,128]{1,0:T(8,128)(2,1)S(1)} %attend.3), channel_id=1, source_target_pairs={{0,8},{1,40},{2,72},{3,104},{4,46},{5,78},{6,110},{7,14},{8,96},{9... | collective-permute-start | bytes 196616 | tf_op jit(solution)/shard_map/home/ppermute | solution.py:26
  154.6 2.3 %collective-permute-done.10 = bf16[256,128]{1,0:T(8,128)(2,1)S(1)} collective-permute-done((bf16[256,128]{1,0:T(8,128)(2,1)S(1)}, bf16[256,128]{1,0:T(8,128)(2,1)S(1)}, u32[]{:S(2)}, u32[]{:S(2)}) %collective-permute-start.10) | collective-permute-done | bytes 65568 | tf_op jit(solution)/shard_map/home/ppermute | solution.py:26
  156.9 1.9 %collective-permute-start.11 = (bf16[128,128]{1,0:T(8,128)(2,1)S(1)}, bf16[128,128]{1,0:T(8,128)(2,1)S(1)}, u32[]{:S(2)}, u32[]{:S(2)}) collective-permute-start(bf16[128,128]{1,0:T(8,128)(2,1)S(1)} %get-tuple-element.28), channel_id=1, source_target_pairs={{0,16},{16,0},{1,17},{17,1},{2,18},{18,2},{3,19},{19,3},{4,20},{20... | collective-permute-start | bytes 98312 | tf_op jit(solution)/shard_map/home/ppermute | solution.py:26
  158.9 1.1 collective-permute-done.11
  (18 shorter events, 3.1 us)
Async XLA Ops:
  0.0 31.4 %collective-permute-start = (bf16[3,192,256]{2,1,0:T(8,128)(2,1)}, bf16[3,192,256]{2,1,0:T(8,128)(2,1)S(1)}, u32[]{:S(2)}, u32[]{:S(2)}) collective-permute-start(bf16[3,192,256]{2,1,0:T(8,128)(2,1)} %bitcast.25), channel_id=1, source_target_pairs={{0,8},{1,40},{2,72},{3,104},{4,44},{5,76},{6,108},{7,12},{8,0},{9,... | collective-permute-start | bytes 884744 | tf_op jit(solution)/shard_map/weights/ppermute | solution.py:26
  15.3 16.1 %collective-permute-start.1 = (f32[4,128]{1,0:T(4,128)S(1)}, f32[4,128]{1,0:T(4,128)S(1)}, u32[]{:S(2)}, u32[]{:S(2)}) collective-permute-start(f32[4,128]{1,0:T(4,128)S(1)} %pad_maximum_fusion.1), channel_id=1, source_target_pairs={{0,8},{1,40},{2,72},{3,104},{4,44},{5,76},{6,108},{7,12},{8,0},{9,... | collective-permute-start | bytes 6152 | tf_op jit(solution)/shard_map/weights/ppermute | solution.py:26
  17.2 0.9 copy-start.2
  31.4 29.0 %all-to-all-start = ((bf16[4,128,384]{2,1,0:T(8,128)(2,1)}), bf16[4,128,384]{2,1,0:T(8,128)(2,1)}, u32[]{:S(2)}, u32[]{:S(2)}) async-start(bf16[4,128,384]{2,1,0:T(8,128)(2,1)} %tokens.2), calls=%async_computation | async-start | bytes 786432 | tf_op jit(solution)/shard_map/tokens/all_to_all | solution.py:231
  39.5 15.3 %collective-permute-start.2 = (bf16[3,192,256]{2,1,0:T(8,128)(2,1)S(1)}, bf16[3,192,256]{2,1,0:T(8,128)(2,1)S(1)}, u32[]{:S(2)}, u32[]{:S(2)}) collective-permute-start(bf16[3,192,256]{2,1,0:T(8,128)(2,1)S(1)} %collective-permute-done), channel_id=1, source_target_pairs={{0,384},{128,0},{256,128},{384,256},{1,385},{129,1},{257,129},{385... | collective-permute-start | bytes 884744 | tf_op jit(solution)/shard_map/weights/ppermute | solution.py:26
  44.2 13.1 %collective-permute-start.3 = (bf16[3,192,256]{2,1,0:T(8,128)(2,1)S(1)}, bf16[3,192,256]{2,1,0:T(8,128)(2,1)S(1)}, u32[]{:S(2)}, u32[]{:S(2)}) collective-permute-start(bf16[3,192,256]{2,1,0:T(8,128)(2,1)S(1)} %collective-permute-done), channel_id=1, source_target_pairs={{0,256},{128,384},{256,0},{384,128},{1,257},{129,385},{257,1},{385... | collective-permute-start | bytes 884744 | tf_op jit(solution)/shard_map/weights/ppermute | solution.py:26
  46.9 13.5 %collective-permute-start.4 = (bf16[3,192,256]{2,1,0:T(8,128)(2,1)S(1)}, bf16[3,192,256]{2,1,0:T(8,128)(2,1)S(1)}, u32[]{:S(2)}, u32[]{:S(2)}) collective-permute-start(bf16[3,192,256]{2,1,0:T(8,128)(2,1)S(1)} %collective-permute-done), channel_id=1, source_target_pairs={{0,128},{128,256},{256,384},{384,0},{1,129},{129,257},{257,385},{3... | collective-permute-start | bytes 884744 | tf_op jit(solution)/shard_map/weights/ppermute | solution.py:26
  60.4 15.4 %copy-start.3 = (bf16[384]{0:T(512)(128)(2,1)S(1)}, bf16[384]{0:T(512)(128)(2,1)}, u32[]{:S(2)}) copy-start(bf16[384]{0:T(512)(128)(2,1)} %param.6) | copy-start | bytes 2308
  60.6 28.5 %collective-permute-start.8 = (bf16[4,3,192,256]{3,2,1,0:T(8,128)(2,1)S(1)}, bf16[4,3,192,256]{3,2,1,0:T(8,128)(2,1)S(1)}, u32[]{:S(2)}, u32[]{:S(2)}) collective-permute-start(bf16[4,3,192,256]{3,2,1,0:T(8,128)(2,1)S(1)} %pad_maximum_fusion.w_mine), channel_id=1, source_target_pairs={{0,16},{16,0},{1,17},{17,1},{2,18},{18,2},{3,19},{19,3},{4,20},{20... | collective-permute-start | bytes 3538952 | tf_op jit(solution)/shard_map/weights/ppermute | solution.py:26
  62.5 32.9 %collective-permute-start.5 = (bf16[4,128,384]{2,1,0:T(8,128)(2,1)}, bf16[4,128,384]{2,1,0:T(8,128)(2,1)}, u32[]{:S(2)}, u32[]{:S(2)}) collective-permute-start(bf16[4,128,384]{2,1,0:T(8,128)(2,1)} %all-to-all-done.tokens.t0), channel_id=1, source_target_pairs={{0,108},{4,0},{8,4},{12,8},{32,12},{36,32},{40,36},{44,40},{64,44}... | collective-permute-start | bytes 1179656 | tf_op jit(solution)/shard_map/tokens/ppermute | solution.py:26
  70.1 25.4 %collective-permute-start.6 = (bf16[4,128,384]{2,1,0:T(8,128)(2,1)}, bf16[4,128,384]{2,1,0:T(8,128)(2,1)}, u32[]{:S(2)}, u32[]{:S(2)}) collective-permute-start(bf16[4,128,384]{2,1,0:T(8,128)(2,1)} %all-to-all-done.tokens.t0), channel_id=1, source_target_pairs={{0,8},{4,108},{8,32},{12,4},{32,40},{36,12},{40,64},{44,36},{64,72... | collective-permute-start | bytes 1179656 | tf_op jit(solution)/shard_map/tokens/ppermute | solution.py:26
  73.6 21.8 %collective-permute-start.7 = (bf16[4,128,384]{2,1,0:T(8,128)(2,1)}, bf16[4,128,384]{2,1,0:T(8,128)(2,1)}, u32[]{:S(2)}, u32[]{:S(2)}) collective-permute-start(bf16[4,128,384]{2,1,0:T(8,128)(2,1)} %all-to-all-done.tokens.t0), channel_id=1, source_target_pairs={{0,4},{4,8},{8,12},{12,32},{32,36},{36,40},{40,44},{44,64},{64,68}... | collective-permute-start | bytes 1179656 | tf_op jit(solution)/shard_map/tokens/ppermute | solution.py:26
  77.7 17.7 %all-to-all-start.1 = ((f32[16,11,128]{2,1,0:T(8,128)}), f32[16,11,128]{2,1,0:T(8,128)}, u32[]{:S(2)}, u32[]{:S(2)}) async-start(f32[16,11,128]{2,1,0:T(8,128)} %norm.1), calls=%async_computation.1 | async-start | bytes 262144 | tf_op jit(solution)/shard_map/norm/all_to_all | solution.py:252
  89.1 1.0 copy-start
  90.1 1.3 copy-start.1
  133.7 4.5 %collective-permute-start.9 = (bf16[8,2,256,128]{3,2,1,0:T(8,128)(2,1)S(1)}, bf16[8,2,256,128]{3,2,1,0:T(8,128)(2,1)S(1)}, u32[]{:S(2)}, u32[]{:S(2)}) collective-permute-start(bf16[8,2,256,128]{3,2,1,0:T(8,128)(2,1)S(1)} %all_to_all.21.kv), channel_id=1, source_target_pairs={{0,16},{16,0},{1,17},{17,1},{2,18},{18,2},{3,19},{19,3},{4,20},{20... | collective-permute-start | bytes 3145736 | tf_op jit(solution)/shard_map/keys/ppermute | solution.py:26
  140.0 16.8 %collective-permute-start.10 = (bf16[256,128]{1,0:T(8,128)(2,1)S(1)}, bf16[256,128]{1,0:T(8,128)(2,1)S(1)}, u32[]{:S(2)}, u32[]{:S(2)}) collective-permute-start(bf16[256,128]{1,0:T(8,128)(2,1)S(1)} %attend.3), channel_id=1, source_target_pairs={{0,8},{1,40},{2,72},{3,104},{4,46},{5,78},{6,110},{7,14},{8,96},{9... | collective-permute-start | bytes 196616 | tf_op jit(solution)/shard_map/home/ppermute | solution.py:26
  156.9 3.1 %collective-permute-start.11 = (bf16[128,128]{1,0:T(8,128)(2,1)S(1)}, bf16[128,128]{1,0:T(8,128)(2,1)S(1)}, u32[]{:S(2)}, u32[]{:S(2)}) collective-permute-start(bf16[128,128]{1,0:T(8,128)(2,1)S(1)} %get-tuple-element.28), channel_id=1, source_target_pairs={{0,16},{16,0},{1,17},{17,1},{2,18},{18,2},{3,19},{19,3},{4,20},{20... | collective-permute-start | bytes 98312 | tf_op jit(solution)/shard_map/home/ppermute | solution.py:26

commit v19 on v18

--- a/solution.py
+++ b/solution.py
@@ -134,7 +134,7 @@
             head = y_to // 2
             for s in range(3):
                 cols = slice(s * 256 + head * DH, s * 256 + head * DH + DH)
-                out[core_to, y_to, :, s * DH : s * DH + DH] = acc[rows, cols].astype(jnp.bfloat16)
+                out[core_to, y_to, :, s * DH : s * DH + DH] = acc[rows, cols]
 
 
 def heads_kernel(where, part, head_gain, q_out, kv_out):
@@ -260,7 +260,7 @@
         )
         part = kernel_call(
             partial_kernel,
-            jax.ShapeDtypeStruct((CORES, NY, 128, 3 * DH), jnp.bfloat16),
+            jax.ShapeDtypeStruct((CORES, NY, 128, 3 * DH), jnp.float32),
             (where, t0, t1, t2, t3, shared, w),
             scalars=1,
             scratch=[

time: 162 us -> 170 us (1.049)
  blocking collectives: 33.7 us -> 42.2 us
    all_to_all x1, blocking collectives: 15.2 us -> 23.6 us  [body(): lax.all_to_all(part, ('core',) + Y, 0, 0).reshape(CORES, NY, 128, 3 * DH)]
where the time goes in v19:
time: 170 us; the launch traced here: 169 us
  starting transfers between devices  79.6 us (47%)
  blocking collectives  42.2 us (25%)
  waiting for transfers between devices  31.4 us (18%)
  Pallas kernels  10.7 us (6%)
  local copies, waits for them, and re-layouts  3.29 us (2%)
    ppermute x12, starting transfers between devices, shift(): return lax.ppermute(values, axes, pairs)  60.2 us
    ppermute x12, waiting for transfers between devices, shift(): return lax.ppermute(values, axes, pairs)  28.1 us
    all_to_all x1, blocking collectives, body(): lax.all_to_all(part, ('core',) + Y, 0, 0).reshape(CORES, NY, 128, 3 * DH)  23.6 us
    all_to_all x1, blocking collectives, body(): kv_mine = lax.all_to_all(kv, ('x', 'yl'), 0, 0)  18.6 us
    all_to_all x1, starting transfers between devices, body(): shared = lax.all_to_all(shared, ('zl',) + Y, 0, 0)  11.3 us
    pallas_call x7, Pallas kernels, kernel_call(): pl.pallas_call(kernel, out_shape=out_shape, in_specs=[smem] * scalars + [...  10.7 us
    all_to_all x1, starting transfers between devices, body(): t0 = lax.all_to_all(copies, 'zh', 0, 0)  8.12 us
  transfers between devices with their start and end apart: 14, of which 8 were waited for; matrix products, arithmetic and copies ran while one was open for 0% of the time, Pallas kernels for 3%

profile of v19, /device:TPU:16, one launch (start us, length us, event | category | flops | bytes accessed | tf_op | source)
XLA Modules:
  0.0 168.9 jit_solution(2563143132927147651)
XLA Ops:
  0.0 14.6 %collective-permute-start = (bf16[3,192,256]{2,1,0:T(8,128)(2,1)}, bf16[3,192,256]{2,1,0:T(8,128)(2,1)S(1)}, u32[]{:S(2)}, u32[]{:S(2)}) collective-permute-start(bf16[3,192,256]{2,1,0:T(8,128)(2,1)} %bitcast.25), channel_id=1, source_target_pairs={{0,8},{1,40},{2,72},{3,104},{4,44},{5,76},{6,108},{7,12},{8,0},{9,... | collective-permute-start | bytes 884744 | tf_op jit(solution)/shard_map/weights/ppermute | solution.py:26
  15.3 1.9 %collective-permute-start.1 = (f32[4,128]{1,0:T(4,128)S(1)}, f32[4,128]{1,0:T(4,128)S(1)}, u32[]{:S(2)}, u32[]{:S(2)}) collective-permute-start(f32[4,128]{1,0:T(4,128)S(1)} %pad_maximum_fusion.1), channel_id=1, source_target_pairs={{0,8},{1,40},{2,72},{3,104},{4,44},{5,76},{6,108},{7,12},{8,0},{9,... | collective-permute-start | bytes 6152 | tf_op jit(solution)/shard_map/weights/ppermute | solution.py:26
  17.2 0.9 copy-done.2
  18.1 0.8 tokens.2
  18.9 12.5 %collective-permute-done.1.head_gain = f32[4,128]{1,0:T(4,128)S(1)} collective-permute-done((f32[4,128]{1,0:T(4,128)S(1)}, f32[4,128]{1,0:T(4,128)S(1)}, u32[]{:S(2)}, u32[]{:S(2)}) %collective-permute-start.1) | collective-permute-done | bytes 2080 | tf_op jit(solution)/shard_map/weights/ppermute | solution.py:26
  31.4 8.1 %all-to-all-start = ((bf16[4,128,384]{2,1,0:T(8,128)(2,1)}), bf16[4,128,384]{2,1,0:T(8,128)(2,1)}, u32[]{:S(2)}, u32[]{:S(2)}) async-start(bf16[4,128,384]{2,1,0:T(8,128)(2,1)} %tokens.2), calls=%async_computation | async-start | bytes 786432 | tf_op jit(solution)/shard_map/tokens/all_to_all | solution.py:231
  39.5 4.7 %collective-permute-start.2 = (bf16[3,192,256]{2,1,0:T(8,128)(2,1)S(1)}, bf16[3,192,256]{2,1,0:T(8,128)(2,1)S(1)}, u32[]{:S(2)}, u32[]{:S(2)}) collective-permute-start(bf16[3,192,256]{2,1,0:T(8,128)(2,1)S(1)} %collective-permute-done), channel_id=1, source_target_pairs={{0,384},{128,0},{256,128},{384,256},{1,385},{129,1},{257,129},{385... | collective-permute-start | bytes 884744 | tf_op jit(solution)/shard_map/weights/ppermute | solution.py:26
  44.2 2.7 %collective-permute-start.3 = (bf16[3,192,256]{2,1,0:T(8,128)(2,1)S(1)}, bf16[3,192,256]{2,1,0:T(8,128)(2,1)S(1)}, u32[]{:S(2)}, u32[]{:S(2)}) collective-permute-start(bf16[3,192,256]{2,1,0:T(8,128)(2,1)S(1)} %collective-permute-done), channel_id=1, source_target_pairs={{0,256},{128,384},{256,0},{384,128},{1,257},{129,385},{257,1},{385... | collective-permute-start | bytes 884744 | tf_op jit(solution)/shard_map/weights/ppermute | solution.py:26
  46.9 2.8 %collective-permute-start.4 = (bf16[3,192,256]{2,1,0:T(8,128)(2,1)S(1)}, bf16[3,192,256]{2,1,0:T(8,128)(2,1)S(1)}, u32[]{:S(2)}, u32[]{:S(2)}) collective-permute-start(bf16[3,192,256]{2,1,0:T(8,128)(2,1)S(1)} %collective-permute-done), channel_id=1, source_target_pairs={{0,128},{128,256},{256,384},{384,0},{1,129},{129,257},{257,385},{3... | collective-permute-start | bytes 884744 | tf_op jit(solution)/shard_map/weights/ppermute | solution.py:26
  49.7 5.1 %collective-permute-done.2 = bf16[3,192,256]{2,1,0:T(8,128)(2,1)S(1)} collective-permute-done((bf16[3,192,256]{2,1,0:T(8,128)(2,1)S(1)}, bf16[3,192,256]{2,1,0:T(8,128)(2,1)S(1)}, u32[]{:S(2)}, u32[]{:S(2)}) %collective-permute-start.2) | collective-permute-done | bytes 294944 | tf_op jit(solution)/shard_map/weights/ppermute | solution.py:26
  54.8 2.5 %collective-permute-done.3 = bf16[3,192,256]{2,1,0:T(8,128)(2,1)S(1)} collective-permute-done((bf16[3,192,256]{2,1,0:T(8,128)(2,1)S(1)}, bf16[3,192,256]{2,1,0:T(8,128)(2,1)S(1)}, u32[]{:S(2)}, u32[]{:S(2)}) %collective-permute-start.3) | collective-permute-done | bytes 294944 | tf_op jit(solution)/shard_map/weights/ppermute | solution.py:26
  57.3 3.1 %collective-permute-done.4 = bf16[3,192,256]{2,1,0:T(8,128)(2,1)S(1)} collective-permute-done((bf16[3,192,256]{2,1,0:T(8,128)(2,1)S(1)}, bf16[3,192,256]{2,1,0:T(8,128)(2,1)S(1)}, u32[]{:S(2)}, u32[]{:S(2)}) %collective-permute-start.4) | collective-permute-done | bytes 294944 | tf_op jit(solution)/shard_map/weights/ppermute | solution.py:26
  60.6 1.9 %collective-permute-start.8 = (bf16[4,3,192,256]{3,2,1,0:T(8,128)(2,1)S(1)}, bf16[4,3,192,256]{3,2,1,0:T(8,128)(2,1)S(1)}, u32[]{:S(2)}, u32[]{:S(2)}) collective-permute-start(bf16[4,3,192,256]{3,2,1,0:T(8,128)(2,1)S(1)} %pad_maximum_fusion.w_mine), channel_id=1, source_target_pairs={{0,16},{16,0},{1,17},{17,1},{2,18},{18,2},{3,19},{19,3},{4,20},{20... | collective-permute-start | bytes 3538952 | tf_op jit(solution)/shard_map/weights/ppermute | solution.py:26
  62.5 7.6 %collective-permute-start.5 = (bf16[4,128,384]{2,1,0:T(8,128)(2,1)}, bf16[4,128,384]{2,1,0:T(8,128)(2,1)}, u32[]{:S(2)}, u32[]{:S(2)}) collective-permute-start(bf16[4,128,384]{2,1,0:T(8,128)(2,1)} %all-to-all-done.tokens.t0), channel_id=1, source_target_pairs={{0,108},{4,0},{8,4},{12,8},{32,12},{36,32},{40,36},{44,40},{64,44}... | collective-permute-start | bytes 1179656 | tf_op jit(solution)/shard_map/tokens/ppermute | solution.py:26
  70.1 3.5 %collective-permute-start.6 = (bf16[4,128,384]{2,1,0:T(8,128)(2,1)}, bf16[4,128,384]{2,1,0:T(8,128)(2,1)}, u32[]{:S(2)}, u32[]{:S(2)}) collective-permute-start(bf16[4,128,384]{2,1,0:T(8,128)(2,1)} %all-to-all-done.tokens.t0), channel_id=1, source_target_pairs={{0,8},{4,108},{8,32},{12,4},{32,40},{36,12},{40,64},{44,36},{64,72... | collective-permute-start | bytes 1179656 | tf_op jit(solution)/shard_map/tokens/ppermute | solution.py:26
  73.6 2.2 %collective-permute-start.7 = (bf16[4,128,384]{2,1,0:T(8,128)(2,1)}, bf16[4,128,384]{2,1,0:T(8,128)(2,1)}, u32[]{:S(2)}, u32[]{:S(2)}) collective-permute-start(bf16[4,128,384]{2,1,0:T(8,128)(2,1)} %all-to-all-done.tokens.t0), channel_id=1, source_target_pairs={{0,4},{4,8},{8,12},{12,32},{32,36},{36,40},{40,44},{44,64},{64,68}... | collective-permute-start | bytes 1179656 | tf_op jit(solution)/shard_map/tokens/ppermute | solution.py:26
  75.8 1.9 %norm.1 = f32[16,11,128]{2,1,0:T(8,128)} custom-call(bf16[4,128,384]{2,1,0:T(8,128)(2,1)} %all-to-all-done.tokens.t0, bf16[3,128]{1,0:T(4,128)(2,1)S(1)} %bitcast.18), custom_call_target="tpu_custom_call" | custom-call | tf_op jit(solution)/shard_map/norm/pallas_call | solution.py:199
  77.7 11.3 %all-to-all-start.1 = ((f32[16,11,128]{2,1,0:T(8,128)}), f32[16,11,128]{2,1,0:T(8,128)}, u32[]{:S(2)}, u32[]{:S(2)}) async-start(f32[16,11,128]{2,1,0:T(8,128)} %norm.1), calls=%async_computation.1 | async-start | bytes 262144 | tf_op jit(solution)/shard_map/norm/all_to_all | solution.py:252
  89.1 1.0 copy-done
  90.1 1.3 copy-done.1
  92.1 3.3 %all-to-all-done.1.shared = f32[16,11,128]{2,1,0:T(8,128)} async-done(((f32[16,11,128]{2,1,0:T(8,128)}), f32[16,11,128]{2,1,0:T(8,128)}, u32[]{:S(2)}, u32[]{:S(2)}) %all-to-all-start.1) | async-done | bytes 90144 | tf_op jit(solution)/shard_map/norm/all_to_all | solution.py:252
  95.4 3.6 %project.4 = f32[2,4,128,384]{3,2,1,0:T(8,128)S(1)} custom-call(s32[6]{0:T(128)S(1)} %stack.42.where, bf16[4,128,384]{2,1,0:T(8,128)(2,1)} %all-to-all-done.tokens.t0, bf16[4,128,384]{2,1,0:T(8,128)(2,1)} %collective-permute-done.5.t1, bf16[4,128,384]{2,1,0:T(8,128)(2,1)} %collective-permute-done.6.t2, bf16[4,128,384]{2,1,0:T(8,128)(2,1)} %collective-permute-done.7.t3, ...), custom_call_target="tpu_custom_call" | custom-call | tf_op jit(solution)/shard_map/project/pallas_call | solution.py:199
  99.0 23.6 %all_to_all.20 = f32[8,128,384]{2,1,0:T(8,128)S(1)} all-to-all(f32[8,128,384]{2,1,0:T(8,128)S(1)} %bitcast.17), channel_id=1, replica_groups=mesh['x'=4,'zh'=4,'core'=2,'zl'=4,'yh'=2,'yl'=2] {'core','yh','yl'}, dimensions={0} | all-to-all | bytes 3145728 | tf_op jit(solution)/shard_map/project/all_to_all | solution.py:271
  123.4 18.6 %all_to_all.21.kv = bf16[8,2,256,128]{3,2,1,0:T(8,128)(2,1)S(1)} all-to-all(bf16[8,2,256,128]{3,2,1,0:T(8,128)(2,1)S(1)} %get-tuple-element.24), channel_id=1, replica_groups=mesh['x'=4,'zh'=4,'core'=2,'zl'=4,'yh'=2,'yl'=2] {'x','yl'}, dimensions={0} | all-to-all | bytes 2097152 | tf_op jit(solution)/shard_map/keys/all_to_all | solution.py:283
  142.0 1.9 %collective-permute-start.9 = (bf16[8,2,256,128]{3,2,1,0:T(8,128)(2,1)S(1)}, bf16[8,2,256,128]{3,2,1,0:T(8,128)(2,1)S(1)}, u32[]{:S(2)}, u32[]{:S(2)}) collective-permute-start(bf16[8,2,256,128]{3,2,1,0:T(8,128)(2,1)S(1)} %all_to_all.21.kv), channel_id=1, source_target_pairs={{0,16},{16,0},{1,17},{17,1},{2,18},{18,2},{3,19},{19,3},{4,20},{20... | collective-permute-start | bytes 3145736 | tf_op jit(solution)/shard_map/keys/ppermute | solution.py:26
  143.9 1.1 attend.2
  145.1 1.5 collective-permute-done.9.kv
  146.5 1.8 %attend.3 = bf16[256,128]{1,0:T(8,128)(2,1)S(1)} custom-call(s32[6]{0:T(128)S(1)} %stack.42.where, bf16[256,128]{1,0:T(8,128)(2,1)S(1)} %get-tuple-element.23.q, bf16[8,2,256,128]{3,2,1,0:T(8,128)(2,1)S(1)} %collective-permute-done.9.kv, f32[256,128]{1,0:T(8,128)S(1)} %get-tuple-element.25.mixed, f32[256,128]{1,0:T(8,128)S(1)} %get-tuple-element.26.extremes), custom_call_target="tpu_custom_call" | custom-call | tf_op jit(solution)/shard_map/attend/pallas_call | solution.py:199
  148.4 14.5 %collective-permute-start.10 = (bf16[256,128]{1,0:T(8,128)(2,1)S(1)}, bf16[256,128]{1,0:T(8,128)(2,1)S(1)}, u32[]{:S(2)}, u32[]{:S(2)}) collective-permute-start(bf16[256,128]{1,0:T(8,128)(2,1)S(1)} %attend.3), channel_id=1, source_target_pairs={{0,8},{1,40},{2,72},{3,104},{4,46},{5,78},{6,110},{7,14},{8,96},{9... | collective-permute-start | bytes 196616 | tf_op jit(solution)/shard_map/home/ppermute | solution.py:26
  162.9 2.3 %collective-permute-done.10 = bf16[256,128]{1,0:T(8,128)(2,1)S(1)} collective-permute-done((bf16[256,128]{1,0:T(8,128)(2,1)S(1)}, bf16[256,128]{1,0:T(8,128)(2,1)S(1)}, u32[]{:S(2)}, u32[]{:S(2)}) %collective-permute-start.10) | collective-permute-done | bytes 65568 | tf_op jit(solution)/shard_map/home/ppermute | solution.py:26
  165.2 1.9 %collective-permute-start.11 = (bf16[128,128]{1,0:T(8,128)(2,1)S(1)}, bf16[128,128]{1,0:T(8,128)(2,1)S(1)}, u32[]{:S(2)}, u32[]{:S(2)}) collective-permute-start(bf16[128,128]{1,0:T(8,128)(2,1)S(1)} %get-tuple-element.28), channel_id=1, source_target_pairs={{0,16},{16,0},{1,17},{17,1},{2,18},{18,2},{3,19},{19,3},{4,20},{20... | collective-permute-start | bytes 98312 | tf_op jit(solution)/shard_map/home/ppermute | solution.py:26
  167.2 1.1 collective-permute-done.11
  (18 shorter events, 3.1 us)
Async XLA Ops:
  0.0 31.4 %collective-permute-start = (bf16[3,192,256]{2,1,0:T(8,128)(2,1)}, bf16[3,192,256]{2,1,0:T(8,128)(2,1)S(1)}, u32[]{:S(2)}, u32[]{:S(2)}) collective-permute-start(bf16[3,192,256]{2,1,0:T(8,128)(2,1)} %bitcast.25), channel_id=1, source_target_pairs={{0,8},{1,40},{2,72},{3,104},{4,44},{5,76},{6,108},{7,12},{8,0},{9,... | collective-permute-start | bytes 884744 | tf_op jit(solution)/shard_map/weights/ppermute | solution.py:26
  15.3 16.1 %collective-permute-start.1 = (f32[4,128]{1,0:T(4,128)S(1)}, f32[4,128]{1,0:T(4,128)S(1)}, u32[]{:S(2)}, u32[]{:S(2)}) collective-permute-start(f32[4,128]{1,0:T(4,128)S(1)} %pad_maximum_fusion.1), channel_id=1, source_target_pairs={{0,8},{1,40},{2,72},{3,104},{4,44},{5,76},{6,108},{7,12},{8,0},{9,... | collective-permute-start | bytes 6152 | tf_op jit(solution)/shard_map/weights/ppermute | solution.py:26
  17.2 0.9 copy-start.2
  31.4 29.0 %all-to-all-start = ((bf16[4,128,384]{2,1,0:T(8,128)(2,1)}), bf16[4,128,384]{2,1,0:T(8,128)(2,1)}, u32[]{:S(2)}, u32[]{:S(2)}) async-start(bf16[4,128,384]{2,1,0:T(8,128)(2,1)} %tokens.2), calls=%async_computation | async-start | bytes 786432 | tf_op jit(solution)/shard_map/tokens/all_to_all | solution.py:231
  39.5 15.3 %collective-permute-start.2 = (bf16[3,192,256]{2,1,0:T(8,128)(2,1)S(1)}, bf16[3,192,256]{2,1,0:T(8,128)(2,1)S(1)}, u32[]{:S(2)}, u32[]{:S(2)}) collective-permute-start(bf16[3,192,256]{2,1,0:T(8,128)(2,1)S(1)} %collective-permute-done), channel_id=1, source_target_pairs={{0,384},{128,0},{256,128},{384,256},{1,385},{129,1},{257,129},{385... | collective-permute-start | bytes 884744 | tf_op jit(solution)/shard_map/weights/ppermute | solution.py:26
  44.2 13.1 %collective-permute-start.3 = (bf16[3,192,256]{2,1,0:T(8,128)(2,1)S(1)}, bf16[3,192,256]{2,1,0:T(8,128)(2,1)S(1)}, u32[]{:S(2)}, u32[]{:S(2)}) collective-permute-start(bf16[3,192,256]{2,1,0:T(8,128)(2,1)S(1)} %collective-permute-done), channel_id=1, source_target_pairs={{0,256},{128,384},{256,0},{384,128},{1,257},{129,385},{257,1},{385... | collective-permute-start | bytes 884744 | tf_op jit(solution)/shard_map/weights/ppermute | solution.py:26
  46.9 13.5 %collective-permute-start.4 = (bf16[3,192,256]{2,1,0:T(8,128)(2,1)S(1)}, bf16[3,192,256]{2,1,0:T(8,128)(2,1)S(1)}, u32[]{:S(2)}, u32[]{:S(2)}) collective-permute-start(bf16[3,192,256]{2,1,0:T(8,128)(2,1)S(1)} %collective-permute-done), channel_id=1, source_target_pairs={{0,128},{128,256},{256,384},{384,0},{1,129},{129,257},{257,385},{3... | collective-permute-start | bytes 884744 | tf_op jit(solution)/shard_map/weights/ppermute | solution.py:26
  60.4 15.4 %copy-start.3 = (bf16[384]{0:T(512)(128)(2,1)S(1)}, bf16[384]{0:T(512)(128)(2,1)}, u32[]{:S(2)}) copy-start(bf16[384]{0:T(512)(128)(2,1)} %param.6) | copy-start | bytes 2308
  60.6 28.5 %collective-permute-start.8 = (bf16[4,3,192,256]{3,2,1,0:T(8,128)(2,1)S(1)}, bf16[4,3,192,256]{3,2,1,0:T(8,128)(2,1)S(1)}, u32[]{:S(2)}, u32[]{:S(2)}) collective-permute-start(bf16[4,3,192,256]{3,2,1,0:T(8,128)(2,1)S(1)} %pad_maximum_fusion.w_mine), channel_id=1, source_target_pairs={{0,16},{16,0},{1,17},{17,1},{2,18},{18,2},{3,19},{19,3},{4,20},{20... | collective-permute-start | bytes 3538952 | tf_op jit(solution)/shard_map/weights/ppermute | solution.py:26
  62.5 32.9 %collective-permute-start.5 = (bf16[4,128,384]{2,1,0:T(8,128)(2,1)}, bf16[4,128,384]{2,1,0:T(8,128)(2,1)}, u32[]{:S(2)}, u32[]{:S(2)}) collective-permute-start(bf16[4,128,384]{2,1,0:T(8,128)(2,1)} %all-to-all-done.tokens.t0), channel_id=1, source_target_pairs={{0,108},{4,0},{8,4},{12,8},{32,12},{36,32},{40,36},{44,40},{64,44}... | collective-permute-start | bytes 1179656 | tf_op jit(solution)/shard_map/tokens/ppermute | solution.py:26
  70.1 25.4 %collective-permute-start.6 = (bf16[4,128,384]{2,1,0:T(8,128)(2,1)}, bf16[4,128,384]{2,1,0:T(8,128)(2,1)}, u32[]{:S(2)}, u32[]{:S(2)}) collective-permute-start(bf16[4,128,384]{2,1,0:T(8,128)(2,1)} %all-to-all-done.tokens.t0), channel_id=1, source_target_pairs={{0,8},{4,108},{8,32},{12,4},{32,40},{36,12},{40,64},{44,36},{64,72... | collective-permute-start | bytes 1179656 | tf_op jit(solution)/shard_map/tokens/ppermute | solution.py:26
  73.6 21.8 %collective-permute-start.7 = (bf16[4,128,384]{2,1,0:T(8,128)(2,1)}, bf16[4,128,384]{2,1,0:T(8,128)(2,1)}, u32[]{:S(2)}, u32[]{:S(2)}) collective-permute-start(bf16[4,128,384]{2,1,0:T(8,128)(2,1)} %all-to-all-done.tokens.t0), channel_id=1, source_target_pairs={{0,4},{4,8},{8,12},{12,32},{32,36},{36,40},{40,44},{44,64},{64,68}... | collective-permute-start | bytes 1179656 | tf_op jit(solution)/shard_map/tokens/ppermute | solution.py:26
  77.7 17.7 %all-to-all-start.1 = ((f32[16,11,128]{2,1,0:T(8,128)}), f32[16,11,128]{2,1,0:T(8,128)}, u32[]{:S(2)}, u32[]{:S(2)}) async-start(f32[16,11,128]{2,1,0:T(8,128)} %norm.1), calls=%async_computation.1 | async-start | bytes 262144 | tf_op jit(solution)/shard_map/norm/all_to_all | solution.py:252
  89.1 1.0 copy-start
  90.1 1.3 copy-start.1
  142.0 4.5 %collective-permute-start.9 = (bf16[8,2,256,128]{3,2,1,0:T(8,128)(2,1)S(1)}, bf16[8,2,256,128]{3,2,1,0:T(8,128)(2,1)S(1)}, u32[]{:S(2)}, u32[]{:S(2)}) collective-permute-start(bf16[8,2,256,128]{3,2,1,0:T(8,128)(2,1)S(1)} %all_to_all.21.kv), channel_id=1, source_target_pairs={{0,16},{16,0},{1,17},{17,1},{2,18},{18,2},{3,19},{19,3},{4,20},{20... | collective-permute-start | bytes 3145736 | tf_op jit(solution)/shard_map/keys/ppermute | solution.py:26
  148.4 16.8 %collective-permute-start.10 = (bf16[256,128]{1,0:T(8,128)(2,1)S(1)}, bf16[256,128]{1,0:T(8,128)(2,1)S(1)}, u32[]{:S(2)}, u32[]{:S(2)}) collective-permute-start(bf16[256,128]{1,0:T(8,128)(2,1)S(1)} %attend.3), channel_id=1, source_target_pairs={{0,8},{1,40},{2,72},{3,104},{4,46},{5,78},{6,110},{7,14},{8,96},{9... | collective-permute-start | bytes 196616 | tf_op jit(solution)/shard_map/home/ppermute | solution.py:26
  165.2 3.1 %collective-permute-start.11 = (bf16[128,128]{1,0:T(8,128)(2,1)S(1)}, bf16[128,128]{1,0:T(8,128)(2,1)S(1)}, u32[]{:S(2)}, u32[]{:S(2)}) collective-permute-start(bf16[128,128]{1,0:T(8,128)(2,1)S(1)} %get-tuple-element.28), channel_id=1, source_target_pairs={{0,16},{16,0},{1,17},{17,1},{2,18},{18,2},{3,19},{19,3},{4,20},{20... | collective-permute-start | bytes 98312 | tf_op jit(solution)/shard_map/home/ppermute | solution.py:26

commit v20 on v18

--- a/solution.py
+++ b/solution.py
@@ -9,6 +9,7 @@
 DH = 128
 EPSILON = 1e-06
 FEATURES = 6144
+SCORE_SCALE = DH ** -0.5 * 1.4426950408889634
 NX = NZH = NZL = NY = 4
 CORES = 2
 AXES = ("x", "zh", "core", "zl", "yh", "yl")
@@ -162,13 +163,13 @@
     keys = kv[:, 0].reshape(-1, DH)
     return lax.dot_general(
         q[...], keys, (((1,), (1,)), ((), ())), preferred_element_type=jnp.float32
-    ) * (DH ** -0.5)
+    )
 
 
 def attend_first_kernel(q, kv, mixed, extremes):
     scores = head_scores(q, kv)
     top = jnp.max(scores, axis=1, keepdims=True)
-    weights = jnp.exp(scores - top)
+    weights = jnp.exp2((scores - top) * SCORE_SCALE)
     total = jnp.sum(weights, axis=1, keepdims=True)
     lane = lax.broadcasted_iota(jnp.int32, extremes.shape, 1)
     extremes[...] = jnp.where(lane == 0, top, total)
@@ -181,8 +182,8 @@
     scores = head_scores(q, kv)
     top_before = extremes[:, 0:1]
     top = jnp.maximum(top_before, jnp.max(scores, axis=1, keepdims=True))
-    scale = jnp.exp(top_before - top)
-    weights = jnp.exp(scores - top)
+    scale = jnp.exp2((top_before - top) * SCORE_SCALE)
+    weights = jnp.exp2((scores - top) * SCORE_SCALE)
     total = extremes[:, 1:2] * scale + jnp.sum(weights, axis=1, keepdims=True)
     both = mixed[...] * scale + jnp.dot(
         weights.astype(jnp.bfloat16), kv[:, 1].reshape(-1, DH), preferred_element_type=jnp.float32

time: 162 us -> 162 us (level)
  no operation moved by 1% of the time
where the time goes in v20:
time: 162 us; the launch traced here: 161 us
  starting transfers between devices  79.6 us (49%)
  blocking collectives  33.7 us (21%)
  waiting for transfers between devices  31.5 us (19%)
  Pallas kernels  10.7 us (7%)
  local copies, waits for them, and re-layouts  3.29 us (2%)
    ppermute x12, starting transfers between devices, shift(): return lax.ppermute(values, axes, pairs)  60.2 us
    ppermute x12, waiting for transfers between devices, shift(): return lax.ppermute(values, axes, pairs)  28.2 us
    all_to_all x1, blocking collectives, body(): kv_mine = lax.all_to_all(kv, ('x', 'yl'), 0, 0)  18.6 us
    all_to_all x1, blocking collectives, body(): lax.all_to_all(part, ('core',) + Y, 0, 0).reshape(CORES, NY, 128, 3 * DH)  15.2 us
    all_to_all x1, starting transfers between devices, body(): shared = lax.all_to_all(shared, ('zl',) + Y, 0, 0)  11.3 us
    pallas_call x7, Pallas kernels, kernel_call(): pl.pallas_call(kernel, out_shape=out_shape, in_specs=[smem] * scalars + [...  10.7 us
    all_to_all x1, starting transfers between devices, body(): t0 = lax.all_to_all(copies, 'zh', 0, 0)  8.12 us
    all_to_all x1, waiting for transfers between devices, body(): shared = lax.all_to_all(shared, ('zl',) + Y, 0, 0)  3.3 us
  transfers between devices with their start and end apart: 14, of which 8 were waited for; matrix products, arithmetic and copies ran while one was open for 0% of the time, Pallas kernels for 3%

profile of v20, /device:TPU:16, one launch (start us, length us, event | category | flops | bytes accessed | tf_op | source)
XLA Modules:
  0.0 160.6 jit_solution(10307082816043272469)
XLA Ops:
  0.0 14.6 %collective-permute-start = (bf16[3,192,256]{2,1,0:T(8,128)(2,1)}, bf16[3,192,256]{2,1,0:T(8,128)(2,1)S(1)}, u32[]{:S(2)}, u32[]{:S(2)}) collective-permute-start(bf16[3,192,256]{2,1,0:T(8,128)(2,1)} %bitcast.25), channel_id=1, source_target_pairs={{0,8},{1,40},{2,72},{3,104},{4,44},{5,76},{6,108},{7,12},{8,0},{9,... | collective-permute-start | bytes 884744 | tf_op jit(solution)/shard_map/weights/ppermute | solution.py:27
  15.3 1.9 %collective-permute-start.1 = (f32[4,128]{1,0:T(4,128)S(1)}, f32[4,128]{1,0:T(4,128)S(1)}, u32[]{:S(2)}, u32[]{:S(2)}) collective-permute-start(f32[4,128]{1,0:T(4,128)S(1)} %pad_maximum_fusion.1), channel_id=1, source_target_pairs={{0,8},{1,40},{2,72},{3,104},{4,44},{5,76},{6,108},{7,12},{8,0},{9,... | collective-permute-start | bytes 6152 | tf_op jit(solution)/shard_map/weights/ppermute | solution.py:27
  17.2 0.9 copy-done.2
  18.9 12.5 %collective-permute-done.1.head_gain = f32[4,128]{1,0:T(4,128)S(1)} collective-permute-done((f32[4,128]{1,0:T(4,128)S(1)}, f32[4,128]{1,0:T(4,128)S(1)}, u32[]{:S(2)}, u32[]{:S(2)}) %collective-permute-start.1) | collective-permute-done | bytes 2080 | tf_op jit(solution)/shard_map/weights/ppermute | solution.py:27
  31.4 8.1 %all-to-all-start = ((bf16[4,128,384]{2,1,0:T(8,128)(2,1)}), bf16[4,128,384]{2,1,0:T(8,128)(2,1)}, u32[]{:S(2)}, u32[]{:S(2)}) async-start(bf16[4,128,384]{2,1,0:T(8,128)(2,1)} %tokens.2), calls=%async_computation | async-start | bytes 786432 | tf_op jit(solution)/shard_map/tokens/all_to_all | solution.py:232
  39.5 4.7 %collective-permute-start.2 = (bf16[3,192,256]{2,1,0:T(8,128)(2,1)S(1)}, bf16[3,192,256]{2,1,0:T(8,128)(2,1)S(1)}, u32[]{:S(2)}, u32[]{:S(2)}) collective-permute-start(bf16[3,192,256]{2,1,0:T(8,128)(2,1)S(1)} %collective-permute-done), channel_id=1, source_target_pairs={{0,384},{128,0},{256,128},{384,256},{1,385},{129,1},{257,129},{385... | collective-permute-start | bytes 884744 | tf_op jit(solution)/shard_map/weights/ppermute | solution.py:27
  44.2 2.7 %collective-permute-start.3 = (bf16[3,192,256]{2,1,0:T(8,128)(2,1)S(1)}, bf16[3,192,256]{2,1,0:T(8,128)(2,1)S(1)}, u32[]{:S(2)}, u32[]{:S(2)}) collective-permute-start(bf16[3,192,256]{2,1,0:T(8,128)(2,1)S(1)} %collective-permute-done), channel_id=1, source_target_pairs={{0,256},{128,384},{256,0},{384,128},{1,257},{129,385},{257,1},{385... | collective-permute-start | bytes 884744 | tf_op jit(solution)/shard_map/weights/ppermute | solution.py:27
  46.9 2.8 %collective-permute-start.4 = (bf16[3,192,256]{2,1,0:T(8,128)(2,1)S(1)}, bf16[3,192,256]{2,1,0:T(8,128)(2,1)S(1)}, u32[]{:S(2)}, u32[]{:S(2)}) collective-permute-start(bf16[3,192,256]{2,1,0:T(8,128)(2,1)S(1)} %collective-permute-done), channel_id=1, source_target_pairs={{0,128},{128,256},{256,384},{384,0},{1,129},{129,257},{257,385},{3... | collective-permute-start | bytes 884744 | tf_op jit(solution)/shard_map/weights/ppermute | solution.py:27
  49.7 5.1 %collective-permute-done.2 = bf16[3,192,256]{2,1,0:T(8,128)(2,1)S(1)} collective-permute-done((bf16[3,192,256]{2,1,0:T(8,128)(2,1)S(1)}, bf16[3,192,256]{2,1,0:T(8,128)(2,1)S(1)}, u32[]{:S(2)}, u32[]{:S(2)}) %collective-permute-start.2) | collective-permute-done | bytes 294944 | tf_op jit(solution)/shard_map/weights/ppermute | solution.py:27
  54.8 2.5 %collective-permute-done.3 = bf16[3,192,256]{2,1,0:T(8,128)(2,1)S(1)} collective-permute-done((bf16[3,192,256]{2,1,0:T(8,128)(2,1)S(1)}, bf16[3,192,256]{2,1,0:T(8,128)(2,1)S(1)}, u32[]{:S(2)}, u32[]{:S(2)}) %collective-permute-start.3) | collective-permute-done | bytes 294944 | tf_op jit(solution)/shard_map/weights/ppermute | solution.py:27
  57.3 3.1 %collective-permute-done.4 = bf16[3,192,256]{2,1,0:T(8,128)(2,1)S(1)} collective-permute-done((bf16[3,192,256]{2,1,0:T(8,128)(2,1)S(1)}, bf16[3,192,256]{2,1,0:T(8,128)(2,1)S(1)}, u32[]{:S(2)}, u32[]{:S(2)}) %collective-permute-start.4) | collective-permute-done | bytes 294944 | tf_op jit(solution)/shard_map/weights/ppermute | solution.py:27
  60.6 1.9 %collective-permute-start.8 = (bf16[4,3,192,256]{3,2,1,0:T(8,128)(2,1)S(1)}, bf16[4,3,192,256]{3,2,1,0:T(8,128)(2,1)S(1)}, u32[]{:S(2)}, u32[]{:S(2)}) collective-permute-start(bf16[4,3,192,256]{3,2,1,0:T(8,128)(2,1)S(1)} %pad_maximum_fusion.w_mine), channel_id=1, source_target_pairs={{0,16},{16,0},{1,17},{17,1},{2,18},{18,2},{3,19},{19,3},{4,20},{20... | collective-permute-start | bytes 3538952 | tf_op jit(solution)/shard_map/weights/ppermute | solution.py:27
  62.5 7.6 %collective-permute-start.5 = (bf16[4,128,384]{2,1,0:T(8,128)(2,1)}, bf16[4,128,384]{2,1,0:T(8,128)(2,1)}, u32[]{:S(2)}, u32[]{:S(2)}) collective-permute-start(bf16[4,128,384]{2,1,0:T(8,128)(2,1)} %all-to-all-done.tokens.t0), channel_id=1, source_target_pairs={{0,108},{4,0},{8,4},{12,8},{32,12},{36,32},{40,36},{44,40},{64,44}... | collective-permute-start | bytes 1179656 | tf_op jit(solution)/shard_map/tokens/ppermute | solution.py:27
  70.1 3.5 %collective-permute-start.6 = (bf16[4,128,384]{2,1,0:T(8,128)(2,1)}, bf16[4,128,384]{2,1,0:T(8,128)(2,1)}, u32[]{:S(2)}, u32[]{:S(2)}) collective-permute-start(bf16[4,128,384]{2,1,0:T(8,128)(2,1)} %all-to-all-done.tokens.t0), channel_id=1, source_target_pairs={{0,8},{4,108},{8,32},{12,4},{32,40},{36,12},{40,64},{44,36},{64,72... | collective-permute-start | bytes 1179656 | tf_op jit(solution)/shard_map/tokens/ppermute | solution.py:27
  73.6 2.2 %collective-permute-start.7 = (bf16[4,128,384]{2,1,0:T(8,128)(2,1)}, bf16[4,128,384]{2,1,0:T(8,128)(2,1)}, u32[]{:S(2)}, u32[]{:S(2)}) collective-permute-start(bf16[4,128,384]{2,1,0:T(8,128)(2,1)} %all-to-all-done.tokens.t0), channel_id=1, source_target_pairs={{0,4},{4,8},{8,12},{12,32},{32,36},{36,40},{40,44},{44,64},{64,68}... | collective-permute-start | bytes 1179656 | tf_op jit(solution)/shard_map/tokens/ppermute | solution.py:27
  75.8 1.9 %norm.1 = f32[16,11,128]{2,1,0:T(8,128)} custom-call(bf16[4,128,384]{2,1,0:T(8,128)(2,1)} %all-to-all-done.tokens.t0, bf16[3,128]{1,0:T(4,128)(2,1)S(1)} %bitcast.18), custom_call_target="tpu_custom_call" | custom-call | tf_op jit(solution)/shard_map/norm/pallas_call | solution.py:200
  77.7 11.3 %all-to-all-start.1 = ((f32[16,11,128]{2,1,0:T(8,128)}), f32[16,11,128]{2,1,0:T(8,128)}, u32[]{:S(2)}, u32[]{:S(2)}) async-start(f32[16,11,128]{2,1,0:T(8,128)} %norm.1), calls=%async_computation.1 | async-start | bytes 262144 | tf_op jit(solution)/shard_map/norm/all_to_all | solution.py:253
  89.1 1.0 copy-done
  90.1 1.3 copy-done.1
  92.1 3.3 %all-to-all-done.1.shared = f32[16,11,128]{2,1,0:T(8,128)} async-done(((f32[16,11,128]{2,1,0:T(8,128)}), f32[16,11,128]{2,1,0:T(8,128)}, u32[]{:S(2)}, u32[]{:S(2)}) %all-to-all-start.1) | async-done | bytes 90144 | tf_op jit(solution)/shard_map/norm/all_to_all | solution.py:253
  95.4 3.7 %project.4 = bf16[2,4,128,384]{3,2,1,0:T(8,128)(2,1)S(1)} custom-call(s32[6]{0:T(128)S(1)} %stack.42.where, bf16[4,128,384]{2,1,0:T(8,128)(2,1)} %all-to-all-done.tokens.t0, bf16[4,128,384]{2,1,0:T(8,128)(2,1)} %collective-permute-done.5.t1, bf16[4,128,384]{2,1,0:T(8,128)(2,1)} %collective-permute-done.6.t2, bf16[4,128,384]{2,1,0:T(8,128)(2,1)} %collective-permute-done.7.t3, ...), custom_call_target="tpu_custom_call" | custom-call | tf_op jit(solution)/shard_map/project/pallas_call | solution.py:200
  99.1 15.2 %all_to_all.20 = bf16[8,128,384]{2,1,0:T(8,128)(2,1)S(1)} all-to-all(bf16[8,128,384]{2,1,0:T(8,128)(2,1)S(1)} %bitcast.16), channel_id=1, replica_groups=mesh['x'=4,'zh'=4,'core'=2,'zl'=4,'yh'=2,'yl'=2] {'core','yh','yl'}, dimensions={0} | all-to-all | bytes 1572864 | tf_op jit(solution)/shard_map/project/all_to_all | solution.py:272
  114.3 0.8 project.5
  115.1 18.6 %all_to_all.21.kv = bf16[8,2,256,128]{3,2,1,0:T(8,128)(2,1)S(1)} all-to-all(bf16[8,2,256,128]{3,2,1,0:T(8,128)(2,1)S(1)} %get-tuple-element.24), channel_id=1, replica_groups=mesh['x'=4,'zh'=4,'core'=2,'zl'=4,'yh'=2,'yl'=2] {'x','yl'}, dimensions={0} | all-to-all | bytes 2097152 | tf_op jit(solution)/shard_map/keys/all_to_all | solution.py:284
  133.7 1.9 %collective-permute-start.9 = (bf16[8,2,256,128]{3,2,1,0:T(8,128)(2,1)S(1)}, bf16[8,2,256,128]{3,2,1,0:T(8,128)(2,1)S(1)}, u32[]{:S(2)}, u32[]{:S(2)}) collective-permute-start(bf16[8,2,256,128]{3,2,1,0:T(8,128)(2,1)S(1)} %all_to_all.21.kv), channel_id=1, source_target_pairs={{0,16},{16,0},{1,17},{17,1},{2,18},{18,2},{3,19},{19,3},{4,20},{20... | collective-permute-start | bytes 3145736 | tf_op jit(solution)/shard_map/keys/ppermute | solution.py:27
  135.6 1.1 attend.2
  136.6 1.6 collective-permute-done.9.kv
  138.2 1.8 %attend.3 = bf16[256,128]{1,0:T(8,128)(2,1)S(1)} custom-call(s32[6]{0:T(128)S(1)} %stack.42.where, bf16[256,128]{1,0:T(8,128)(2,1)S(1)} %get-tuple-element.23.q, bf16[8,2,256,128]{3,2,1,0:T(8,128)(2,1)S(1)} %collective-permute-done.9.kv, f32[256,128]{1,0:T(8,128)S(1)} %get-tuple-element.25.mixed, f32[256,128]{1,0:T(8,128)S(1)} %get-tuple-element.26.extremes), custom_call_target="tpu_custom_call" | custom-call | tf_op jit(solution)/shard_map/attend/pallas_call | solution.py:200
  140.0 14.5 %collective-permute-start.10 = (bf16[256,128]{1,0:T(8,128)(2,1)S(1)}, bf16[256,128]{1,0:T(8,128)(2,1)S(1)}, u32[]{:S(2)}, u32[]{:S(2)}) collective-permute-start(bf16[256,128]{1,0:T(8,128)(2,1)S(1)} %attend.3), channel_id=1, source_target_pairs={{0,8},{1,40},{2,72},{3,104},{4,46},{5,78},{6,110},{7,14},{8,96},{9... | collective-permute-start | bytes 196616 | tf_op jit(solution)/shard_map/home/ppermute | solution.py:27
  154.5 2.3 %collective-permute-done.10 = bf16[256,128]{1,0:T(8,128)(2,1)S(1)} collective-permute-done((bf16[256,128]{1,0:T(8,128)(2,1)S(1)}, bf16[256,128]{1,0:T(8,128)(2,1)S(1)}, u32[]{:S(2)}, u32[]{:S(2)}) %collective-permute-start.10) | collective-permute-done | bytes 65568 | tf_op jit(solution)/shard_map/home/ppermute | solution.py:27
  156.8 1.9 %collective-permute-start.11 = (bf16[128,128]{1,0:T(8,128)(2,1)S(1)}, bf16[128,128]{1,0:T(8,128)(2,1)S(1)}, u32[]{:S(2)}, u32[]{:S(2)}) collective-permute-start(bf16[128,128]{1,0:T(8,128)(2,1)S(1)} %get-tuple-element.28), channel_id=1, source_target_pairs={{0,16},{16,0},{1,17},{17,1},{2,18},{18,2},{3,19},{19,3},{4,20},{20... | collective-permute-start | bytes 98312 | tf_op jit(solution)/shard_map/home/ppermute | solution.py:27
  158.8 1.1 collective-permute-done.11
  (18 shorter events, 3.1 us)
Async XLA Ops:
  0.0 31.4 %collective-permute-start = (bf16[3,192,256]{2,1,0:T(8,128)(2,1)}, bf16[3,192,256]{2,1,0:T(8,128)(2,1)S(1)}, u32[]{:S(2)}, u32[]{:S(2)}) collective-permute-start(bf16[3,192,256]{2,1,0:T(8,128)(2,1)} %bitcast.25), channel_id=1, source_target_pairs={{0,8},{1,40},{2,72},{3,104},{4,44},{5,76},{6,108},{7,12},{8,0},{9,... | collective-permute-start | bytes 884744 | tf_op jit(solution)/shard_map/weights/ppermute | solution.py:27
  15.3 16.1 %collective-permute-start.1 = (f32[4,128]{1,0:T(4,128)S(1)}, f32[4,128]{1,0:T(4,128)S(1)}, u32[]{:S(2)}, u32[]{:S(2)}) collective-permute-start(f32[4,128]{1,0:T(4,128)S(1)} %pad_maximum_fusion.1), channel_id=1, source_target_pairs={{0,8},{1,40},{2,72},{3,104},{4,44},{5,76},{6,108},{7,12},{8,0},{9,... | collective-permute-start | bytes 6152 | tf_op jit(solution)/shard_map/weights/ppermute | solution.py:27
  17.2 0.9 copy-start.2
  31.4 29.0 %all-to-all-start = ((bf16[4,128,384]{2,1,0:T(8,128)(2,1)}), bf16[4,128,384]{2,1,0:T(8,128)(2,1)}, u32[]{:S(2)}, u32[]{:S(2)}) async-start(bf16[4,128,384]{2,1,0:T(8,128)(2,1)} %tokens.2), calls=%async_computation | async-start | bytes 786432 | tf_op jit(solution)/shard_map/tokens/all_to_all | solution.py:232
  39.5 15.3 %collective-permute-start.2 = (bf16[3,192,256]{2,1,0:T(8,128)(2,1)S(1)}, bf16[3,192,256]{2,1,0:T(8,128)(2,1)S(1)}, u32[]{:S(2)}, u32[]{:S(2)}) collective-permute-start(bf16[3,192,256]{2,1,0:T(8,128)(2,1)S(1)} %collective-permute-done), channel_id=1, source_target_pairs={{0,384},{128,0},{256,128},{384,256},{1,385},{129,1},{257,129},{385... | collective-permute-start | bytes 884744 | tf_op jit(solution)/shard_map/weights/ppermute | solution.py:27
  44.2 13.1 %collective-permute-start.3 = (bf16[3,192,256]{2,1,0:T(8,128)(2,1)S(1)}, bf16[3,192,256]{2,1,0:T(8,128)(2,1)S(1)}, u32[]{:S(2)}, u32[]{:S(2)}) collective-permute-start(bf16[3,192,256]{2,1,0:T(8,128)(2,1)S(1)} %collective-permute-done), channel_id=1, source_target_pairs={{0,256},{128,384},{256,0},{384,128},{1,257},{129,385},{257,1},{385... | collective-permute-start | bytes 884744 | tf_op jit(solution)/shard_map/weights/ppermute | solution.py:27
  46.9 13.5 %collective-permute-start.4 = (bf16[3,192,256]{2,1,0:T(8,128)(2,1)S(1)}, bf16[3,192,256]{2,1,0:T(8,128)(2,1)S(1)}, u32[]{:S(2)}, u32[]{:S(2)}) collective-permute-start(bf16[3,192,256]{2,1,0:T(8,128)(2,1)S(1)} %collective-permute-done), channel_id=1, source_target_pairs={{0,128},{128,256},{256,384},{384,0},{1,129},{129,257},{257,385},{3... | collective-permute-start | bytes 884744 | tf_op jit(solution)/shard_map/weights/ppermute | solution.py:27
  60.4 15.4 %copy-start.3 = (bf16[384]{0:T(512)(128)(2,1)S(1)}, bf16[384]{0:T(512)(128)(2,1)}, u32[]{:S(2)}) copy-start(bf16[384]{0:T(512)(128)(2,1)} %param.6) | copy-start | bytes 2308
  60.6 28.5 %collective-permute-start.8 = (bf16[4,3,192,256]{3,2,1,0:T(8,128)(2,1)S(1)}, bf16[4,3,192,256]{3,2,1,0:T(8,128)(2,1)S(1)}, u32[]{:S(2)}, u32[]{:S(2)}) collective-permute-start(bf16[4,3,192,256]{3,2,1,0:T(8,128)(2,1)S(1)} %pad_maximum_fusion.w_mine), channel_id=1, source_target_pairs={{0,16},{16,0},{1,17},{17,1},{2,18},{18,2},{3,19},{19,3},{4,20},{20... | collective-permute-start | bytes 3538952 | tf_op jit(solution)/shard_map/weights/ppermute | solution.py:27
  62.5 32.9 %collective-permute-start.5 = (bf16[4,128,384]{2,1,0:T(8,128)(2,1)}, bf16[4,128,384]{2,1,0:T(8,128)(2,1)}, u32[]{:S(2)}, u32[]{:S(2)}) collective-permute-start(bf16[4,128,384]{2,1,0:T(8,128)(2,1)} %all-to-all-done.tokens.t0), channel_id=1, source_target_pairs={{0,108},{4,0},{8,4},{12,8},{32,12},{36,32},{40,36},{44,40},{64,44}... | collective-permute-start | bytes 1179656 | tf_op jit(solution)/shard_map/tokens/ppermute | solution.py:27
  70.1 25.4 %collective-permute-start.6 = (bf16[4,128,384]{2,1,0:T(8,128)(2,1)}, bf16[4,128,384]{2,1,0:T(8,128)(2,1)}, u32[]{:S(2)}, u32[]{:S(2)}) collective-permute-start(bf16[4,128,384]{2,1,0:T(8,128)(2,1)} %all-to-all-done.tokens.t0), channel_id=1, source_target_pairs={{0,8},{4,108},{8,32},{12,4},{32,40},{36,12},{40,64},{44,36},{64,72... | collective-permute-start | bytes 1179656 | tf_op jit(solution)/shard_map/tokens/ppermute | solution.py:27
  73.6 21.8 %collective-permute-start.7 = (bf16[4,128,384]{2,1,0:T(8,128)(2,1)}, bf16[4,128,384]{2,1,0:T(8,128)(2,1)}, u32[]{:S(2)}, u32[]{:S(2)}) collective-permute-start(bf16[4,128,384]{2,1,0:T(8,128)(2,1)} %all-to-all-done.tokens.t0), channel_id=1, source_target_pairs={{0,4},{4,8},{8,12},{12,32},{32,36},{36,40},{40,44},{44,64},{64,68}... | collective-permute-start | bytes 1179656 | tf_op jit(solution)/shard_map/tokens/ppermute | solution.py:27
  77.7 17.7 %all-to-all-start.1 = ((f32[16,11,128]{2,1,0:T(8,128)}), f32[16,11,128]{2,1,0:T(8,128)}, u32[]{:S(2)}, u32[]{:S(2)}) async-start(f32[16,11,128]{2,1,0:T(8,128)} %norm.1), calls=%async_computation.1 | async-start | bytes 262144 | tf_op jit(solution)/shard_map/norm/all_to_all | solution.py:253
  89.1 1.0 copy-start
  90.1 1.3 copy-start.1
  133.7 4.5 %collective-permute-start.9 = (bf16[8,2,256,128]{3,2,1,0:T(8,128)(2,1)S(1)}, bf16[8,2,256,128]{3,2,1,0:T(8,128)(2,1)S(1)}, u32[]{:S(2)}, u32[]{:S(2)}) collective-permute-start(bf16[8,2,256,128]{3,2,1,0:T(8,128)(2,1)S(1)} %all_to_all.21.kv), channel_id=1, source_target_pairs={{0,16},{16,0},{1,17},{17,1},{2,18},{18,2},{3,19},{19,3},{4,20},{20... | collective-permute-start | bytes 3145736 | tf_op jit(solution)/shard_map/keys/ppermute | solution.py:27
  140.0 16.8 %collective-permute-start.10 = (bf16[256,128]{1,0:T(8,128)(2,1)S(1)}, bf16[256,128]{1,0:T(8,128)(2,1)S(1)}, u32[]{:S(2)}, u32[]{:S(2)}) collective-permute-start(bf16[256,128]{1,0:T(8,128)(2,1)S(1)} %attend.3), channel_id=1, source_target_pairs={{0,8},{1,40},{2,72},{3,104},{4,46},{5,78},{6,110},{7,14},{8,96},{9... | collective-permute-start | bytes 196616 | tf_op jit(solution)/shard_map/home/ppermute | solution.py:27
  156.8 3.1 %collective-permute-start.11 = (bf16[128,128]{1,0:T(8,128)(2,1)S(1)}, bf16[128,128]{1,0:T(8,128)(2,1)S(1)}, u32[]{:S(2)}, u32[]{:S(2)}) collective-permute-start(bf16[128,128]{1,0:T(8,128)(2,1)S(1)} %get-tuple-element.28), channel_id=1, source_target_pairs={{0,16},{16,0},{1,17},{17,1},{2,18},{18,2},{3,19},{19,3},{4,20},{20... | collective-permute-start | bytes 98312 | tf_op jit(solution)/shard_map/home/ppermute | solution.py:27
